TPU v7x, 256 devices: a whole 4x4x8 slice. The times are simulated.
256 devices in a mesh: lon: 16 (over x_hi, z), lat: 16 (over y, x_lo, core).
Axes of the slice: x: 4 (x_hi: 2, x_lo: 2; x = x_hi * 2 + x_lo), y: 4, z: 8, core: 2. Of those that a mesh axis runs over, the one named last changes fastest.
Arguments:
- fields: bfloat16 [4, 192, 96, 512], P(None, 'lat', 'lon'), may hold values from -6 to 6
- cotangent: bfloat16 [4, 192, 96, 512], P(None, 'lat', 'lon'), may hold values from -6 to 6
- land_ids: int32 [192, 96], replicated, may hold values from 0 to 2
- gain_a: float32 [512], replicated, may hold values from 0.1 to 1.9
- table_a: float32 [16, 3, 3], replicated, may hold values from -3 to 300
- qkv_weight_a: bfloat16 [512, 1536], replicated, may hold values from -0.25 to 0.25
- out_weight_a: bfloat16 [512, 512], replicated, may hold values from -0.25 to 0.25
- gain_b: float32 [512], replicated, may hold values from 0.1 to 1.9
- table_b: float32 [16, 3, 3], replicated, may hold values from -3 to 300
- qkv_weight_b: bfloat16 [512, 1536], replicated, may hold values from -0.25 to 0.25
- out_weight_b: bfloat16 [512, 512], replicated, may hold values from -0.25 to 0.25
Outputs:
- advanced: bfloat16 [4, 192, 96, 512], P(None, 'lat', 'lon')
- grad_fields: bfloat16 [4, 192, 96, 512], P(None, 'lat', 'lon')
- grad_qkv_a: float32 [512, 1536], P('lat', 'lon')
- grad_out_a: float32 [512, 512], P('lat', 'lon')
- grad_qkv_b: float32 [512, 1536], P('lat', 'lon')
- grad_out_b: float32 [512, 512], P('lat', 'lon')
Inputs may be any that keep to these rules, and one draw needn't show every extreme that they name: `land_ids`: class of each grid column: 0 sea, 1 land, 2 polar ice.
All inputs are finite; a program needn't handle non-finite values.
Results may differ from a plain program's by a relative error of at most 0.035.
Values may be sent and summed in bfloat16 or wider, within the bound.
No kernel may reach another device: no remote copies, remote signals or barrier semaphores. Data moves between devices by JAX's collectives and lax.ppermute only.
A program may use at most 128 MiB of HBM per device.

v0:
```python
import jax
import jax.numpy as jnp
import numpy as np
from jax import lax
from jax.experimental import pallas as pl
from jax.experimental.pallas import tpu as pltpu
from jax.sharding import PartitionSpec as P

WINDOWS = 2
LENGTH = 144
QUARTER = 36
TOKENS = WINDOWS * LENGTH
PIECE = WINDOWS * QUARTER
WIDTH = 512
HEADS = 16
HEAD = 32
GROUP = 128
GROUPS = WIDTH // GROUP
PER_GROUP = GROUP // HEAD
ROOT = HEAD**0.5
EPS = 1e-05
NEG = -1000000000.0
VMEM_LIMIT = 24 * 1024 * 1024
F32 = jnp.float32
BF16 = jnp.bfloat16


def _tables():
    place = np.zeros((TOKENS, TOKENS), np.float32)
    sort = np.zeros((TOKENS, TOKENS), np.float32)
    where = np.zeros((LENGTH, 8), np.int32)
    for window in range(WINDOWS):
        for quadrant in range(4):
            for level in range(2):
                for row in range(6):
                    for column in range(3):
                        inner = level * 18 + row * 3 + column
                        at = quadrant * QUARTER + inner
                        token = window * LENGTH + at
                        lat = quadrant // 2 * 6 + row
                        lon = quadrant % 2 * 3 + column
                        source = (lat * 6 + lon) * 4 + 2 * window + level
                        place[token, source] = 1
                        sort[quadrant * PIECE + window * QUARTER + inner, token] = 1
                        where[at, 0] = lat
                        where[at, 1] = lon
    return place, sort, where


PLACE, SORT, WHERE = _tables()


def mm(left, right):
    return jnp.dot(left, right, preferred_element_type=F32)


def mm_t(left, right):
    return lax.dot_general(left, right, (((1,), (1,)), ((), ())), preferred_element_type=F32)


def normalise(inputs):
    centre = inputs - jnp.mean(inputs, axis=-1, keepdims=True)
    spread = jnp.mean(centre * centre, axis=-1, keepdims=True)
    scale = lax.rsqrt(spread + EPS)
    return centre * scale, scale


def lanes(shape):
    return lax.broadcasted_iota(jnp.int32, shape, 1)


def head_masks():
    lane = lanes((1, GROUP))
    return [
        ((lane >= h * HEAD) & (lane < (h + 1) * HEAD)).astype(F32).astype(BF16)
        for h in range(PER_GROUP)
    ]


def bias_features(ids_ref, where_ref, table_ref, spare_ref, shift, last):
    lat_at = lax.axis_index("lat")
    lon_at = lax.axis_index("lon")
    rows, columns = ids_ref.shape
    row = where_ref[:, 0:1]
    column = where_ref[:, 1:2] + (lon_at * 6 + shift // 2)
    at = row + (lat_at * 12 + shift)
    at = jnp.where(at >= rows, at - rows, at)
    column = jnp.where(column >= columns, column - columns, column)
    pick = (lanes((LENGTH, rows)) == at).astype(F32).astype(BF16)
    found = mm(pick, ids_ref[...].astype(F32).astype(BF16))
    found = jnp.where(lanes((LENGTH, columns)) == column, found, 0.0)
    kind = jnp.sum(found, axis=1, keepdims=True).astype(jnp.int32)
    lane = lanes((LENGTH, GROUP))
    third = (lane >= 3).astype(jnp.int32) + (lane >= 6).astype(jnp.int32)
    query = ((lane < 9) & (third == kind)).astype(F32)
    key = ((lane < 3) & (lane == kind)).astype(F32)
    if last:
        flag = ((row >= 6) & (lat_at == lax.axis_size("lat") - 1)).astype(F32)
        query = jnp.where(lane == 9, flag, jnp.where(lane == 10, 1.0 - flag, query))
        key = jnp.where(lane == 3, 1.0 - flag, jnp.where(lane == 4, flag, key))
    small = (16, GROUP)
    lane = lanes(small)
    sub = lax.broadcasted_iota(jnp.int32, small, 0)
    third = (lane >= 3).astype(jnp.int32) + (lane >= 6).astype(jnp.int32)
    part = lane - 3 * third
    spots = {
        (first, second): (lane < 9) & (third == first) & (sub == second)
        for first in range(3)
        for second in range(3)
    }
    fixed = jnp.where(((sub == 3) & (lane == 9)) | ((sub == 4) & (lane == 10)), NEG * ROOT, 0.0)
    for head in range(HEADS):
        entry = fixed
        for (first, second), spot in spots.items():
            entry = jnp.where(spot, table_ref[first, second, head] * ROOT, entry)
        high = entry.astype(BF16).astype(F32)
        middle = (entry - high).astype(BF16).astype(F32)
        low = entry - high - middle
        entry = jnp.where(part == 0, high, jnp.where(part == 1, middle, low))
        entry = jnp.where(lane >= 9, high, entry)
        spare_ref[:, head * GROUP : (head + 1) * GROUP] = entry.astype(BF16)
    features = mm(key.astype(BF16)[:, :16], spare_ref[...])
    return query.astype(BF16), features.astype(BF16)


def forward_core(
    inputs, gain, qkv_ref, out_ref, query_features, key_ref, packed_ref, probs_ref, mixed_t_ref, scores_ref
):
    hat, _ = normalise(inputs)
    normed = (hat * gain).astype(BF16)
    packed_ref[...] = mm(normed, qkv_ref[...]).astype(BF16)
    masks = head_masks()
    factor = F32(1.0 / ROOT * np.log2(np.e))
    for window, group, rows, at in sections():
        query = packed_ref[rows, at : at + GROUP]
        keys = packed_ref[rows, WIDTH + at : WIDTH + at + GROUP]
        for h in range(PER_GROUP):
            head = group * PER_GROUP + h
            left = jnp.concatenate([keys, key_ref[:, head * GROUP : (head + 1) * GROUP]], axis=1)
            right = jnp.concatenate([query * masks[h], query_features], axis=1)
            scores_ref[window * HEADS + head] = mm_t(left, right)
    for item in range(WINDOWS * HEADS):
        scores = scores_ref[item]
        top = jnp.max(scores, axis=0, keepdims=True)
        raised = jnp.exp2((scores - top) * factor)
        total = jnp.sum(raised, axis=0, keepdims=True)
        probs_ref[item] = (raised * (1.0 / total)).astype(BF16)
    for window, group, rows, at in sections():
        values_t = packed_ref[rows, 2 * WIDTH + at : 2 * WIDTH + at + GROUP].T
        for h in range(PER_GROUP):
            head = group * PER_GROUP + h
            mixed = mm(values_t[h * HEAD : (h + 1) * HEAD], probs_ref[window * HEADS + head])
            mixed_t_ref[window, head * HEAD : (head + 1) * HEAD, :] = mixed.astype(BF16)
    parts = [mm(mixed_t_ref[window].T, out_ref[...]) for window in range(WINDOWS)]
    return normed, jnp.concatenate(parts, axis=0)


def sections():
    for window in range(WINDOWS):
        for group in range(GROUPS):
            rows = slice(window * LENGTH, (window + 1) * LENGTH)
            yield window, group, rows, group * GROUP


def backward_core(
    upstream, out_ref, packed_ref, probs_ref, mixed_t_ref, d_packed_ref, d_probs_ref, d_scores_ref
):
    masks = head_masks()
    d_mixed = mm_t(upstream, out_ref[...]).astype(BF16)
    for window, group, rows, at in sections():
        values = packed_ref[rows, 2 * WIDTH + at : 2 * WIDTH + at + GROUP]
        up = d_mixed[rows, at : at + GROUP]
        for h in range(PER_GROUP):
            d_probs_ref[window * HEADS + group * PER_GROUP + h] = mm_t(values, up * masks[h])
    for window in range(WINDOWS):
        here = upstream[window * LENGTH : (window + 1) * LENGTH]
        d_mixed_t = mm_t(out_ref[...], here).astype(BF16)
        dots = d_mixed_t.astype(F32) * mixed_t_ref[window].astype(F32)
        for head in range(HEADS):
            item = window * HEADS + head
            inner = jnp.sum(dots[head * HEAD : (head + 1) * HEAD], axis=0, keepdims=True)
            d_scores = (d_probs_ref[item] - inner) * F32(1.0 / ROOT)
            d_scores_ref[item] = (probs_ref[item].astype(F32) * d_scores).astype(BF16)
    for window, group, rows, at in sections():
        query = packed_ref[rows, at : at + GROUP]
        keys_t = packed_ref[rows, WIDTH + at : WIDTH + at + GROUP].T
        up = d_mixed[rows, at : at + GROUP]
        d_values = None
        d_keys = None
        d_query = []
        for h in range(PER_GROUP):
            item = window * HEADS + group * PER_GROUP + h
            d_value = mm(probs_ref[item], up * masks[h])
            d_key = mm(d_scores_ref[item], query * masks[h])
            d_values = d_value if d_values is None else d_values + d_value
            d_keys = d_key if d_keys is None else d_keys + d_key
            d_query.append(mm(keys_t[h * HEAD : (h + 1) * HEAD], d_scores_ref[item]))
        d_query = jnp.concatenate(d_query, axis=0).T
        d_packed_ref[rows, at : at + GROUP] = d_query.astype(BF16)
        d_packed_ref[rows, WIDTH + at : WIDTH + at + GROUP] = d_keys.astype(BF16)
        d_packed_ref[rows, 2 * WIDTH + at : 2 * WIDTH + at + GROUP] = d_values.astype(BF16)


def norm_backward(inputs, gain, d_packed, qkv_ref):
    d_normed = mm_t(d_packed, qkv_ref[...]).astype(BF16).astype(F32)
    hat, scale = normalise(inputs)
    d_hat = d_normed * gain
    mean = jnp.mean(d_hat, axis=-1, keepdims=True)
    along = jnp.mean(d_hat * hat, axis=-1, keepdims=True)
    return scale * (d_hat - mean - hat * along)


def grads_half(half, normed_t_ref, mixed_t_ref, upstream, d_packed_ref, result_ref):
    def blocks(ref, *first):
        return [
            ref[(*first, pl.ds(pl.multiple_of((2 * block + half) * 32, 32), 32), slice(None))]
            for block in range(8)
        ]

    left = jnp.concatenate(blocks(normed_t_ref), axis=0)
    result_ref[:, : 3 * WIDTH] = mm(left, d_packed_ref[...]).astype(BF16)
    total = None
    for window in range(WINDOWS):
        left = jnp.concatenate(blocks(mixed_t_ref, window), axis=0)
        part = mm(left, upstream[window * LENGTH : (window + 1) * LENGTH])
        total = part if total is None else total + part
    result_ref[:, 3 * WIDTH :] = total.astype(BF16)


def load_grid(ref, place, spare_ref):
    for row in range(12):
        for column in range(6):
            at = (row * 6 + column) * 4
            spare_ref[at : at + 4, :] = ref[row, column].astype(F32)
    return mm(place, spare_ref[...].astype(BF16))


def store_grid(ref, place_t, tokens):
    spread = mm(place_t, tokens)
    for row in range(12):
        for column in range(6):
            at = (row * 6 + column) * 4
            ref[row, column] = spread[at : at + 4].astype(BF16)


def split_pieces(sort, tokens, refs):
    tokens = mm(sort, tokens)
    for at, ref in enumerate(refs):
        ref[...] = tokens[at * PIECE : (at + 1) * PIECE].astype(BF16)


def join_pieces(sort_t, refs):
    tokens = jnp.concatenate([ref[...].astype(F32) for ref in refs], axis=0)
    return mm(sort_t, tokens.astype(BF16))


def fetch(pairs, sems):
    copies = [
        pltpu.make_async_copy(source, target, sems.at[at])
        for at, (source, target) in enumerate(pairs)
    ]
    for copy in copies:
        copy.start()
    return copies


def kernel_forward_a(
    fields_hbm, ids_hbm, gain_hbm, table, qkv_hbm, out_hbm, place_hbm, sort_hbm, where_hbm,
    piece0, piece1, piece2, piece3, inputs_out, middle_out, normed_out, packed, probs, mixed_t,
    fields, ids, gain, qkv, out, place, sort, where, grid, spare, key_features, scores, sems,
):
    ids_in, where_in, fields_in, place_in, gain_in, qkv_in, out_in, sort_in = fetch(
        (
            (ids_hbm, ids), (where_hbm, where), (fields_hbm, fields), (place_hbm, place),
            (gain_hbm, gain), (qkv_hbm, qkv), (out_hbm, out), (sort_hbm, sort),
        ),
        sems,
    )
    ids_in.wait()
    where_in.wait()
    query_features, features = bias_features(ids, where, table, spare, 0, False)
    key_features[...] = features
    fields_in.wait()
    place_in.wait()
    inputs = load_grid(fields, place[...], grid)
    inputs_out[...] = inputs.astype(BF16)
    gain_in.wait()
    qkv_in.wait()
    out_in.wait()
    normed, delta = forward_core(
        inputs, gain[...].reshape(1, WIDTH), qkv, out, query_features, key_features,
        packed, probs, mixed_t, scores,
    )
    normed_out[...] = normed
    middle = (inputs + delta).astype(BF16)
    middle_out[...] = middle
    sort_in.wait()
    split_pieces(sort[...], middle, (piece0, piece1, piece2, piece3))


def kernel_cotangent(
    cotangent_hbm, place, sort, normed, ids, table, where,
    piece0, piece1, piece2, piece3, upstream_out, normed_t, query_out, key_out,
    cotangent, grid, spare, sems,
):
    (cotangent_in,) = fetch(((cotangent_hbm, cotangent),), sems)
    normed_t[...] = normed[...].T
    query, keys = bias_features(ids, where, table, spare, 6, True)
    query_out[...] = query
    key_out[...] = keys
    cotangent_in.wait()
    upstream = load_grid(cotangent, place[...], grid).astype(BF16)
    upstream_out[...] = upstream
    split_pieces(sort[...], upstream, (piece0, piece1, piece2, piece3))


def kernel_forward_b(
    piece0, piece1, piece2, piece3, query_features, key_features, gain, qkv, out, sort, sort_t,
    back0, back1, back2, back3, inputs_out, normed_out, packed, probs, mixed_t,
    scores,
):
    inputs = join_pieces(sort_t[...], (piece0, piece1, piece2, piece3))
    inputs_out[...] = inputs.astype(BF16)
    normed, delta = forward_core(
        inputs, gain[...].reshape(1, WIDTH), qkv, out, query_features[...], key_features,
        packed, probs, mixed_t, scores,
    )
    normed_out[...] = normed
    split_pieces(sort[...], delta.astype(BF16), (back0, back1, back2, back3))


def kernel_backward_b(
    piece0, piece1, piece2, piece3, inputs, gain, qkv, out, packed, probs, mixed_t, sort, sort_t,
    back0, back1, back2, back3, upstream_out, d_packed,
    d_probs, d_scores,
):
    upstream = join_pieces(sort_t[...], (piece0, piece1, piece2, piece3)).astype(BF16)
    upstream_out[...] = upstream
    backward_core(upstream, out, packed, probs, mixed_t, d_packed, d_probs, d_scores)
    d_inputs = norm_backward(
        inputs[...].astype(F32), gain[...].reshape(1, WIDTH), d_packed[...], qkv
    )
    split_pieces(sort[...], d_inputs.astype(BF16), (back0, back1, back2, back3))


def kernel_grads_b(normed, mixed_t, upstream, d_packed, send, keep, normed_t):
    normed_t[...] = normed[...].T
    core = lax.axis_index("lat") % 2
    grads_half(1 - core, normed_t, mixed_t, upstream[...], d_packed, send)
    grads_half(core, normed_t, mixed_t, upstream[...], d_packed, keep)


def kernel_backward_a(
    back0, back1, back2, back3, upstream, out, packed, probs, mixed_t, normed_t, sort_t,
    grad_middle_out, d_packed, send,
    d_probs, d_scores,
):
    d_inputs = join_pieces(sort_t[...], (back0, back1, back2, back3))
    grad_middle = (upstream[...].astype(F32) + d_inputs).astype(BF16)
    grad_middle_out[...] = grad_middle
    backward_core(grad_middle, out, packed, probs, mixed_t, d_packed, d_probs, d_scores)
    core = lax.axis_index("lat") % 2
    grads_half(1 - core, normed_t, mixed_t, grad_middle, d_packed, send)


def kernel_finish_a(
    back0, back1, back2, back3, inputs, middle, grad_middle, gain, qkv, d_packed, normed_t,
    mixed_t, place_t, sort_t,
    keep, advanced, grad_fields,
):
    core = lax.axis_index("lat") % 2
    grads_half(core, normed_t, mixed_t, grad_middle[...], d_packed, keep)
    delta = join_pieces(sort_t[...], (back0, back1, back2, back3))
    store_grid(advanced, place_t[...], (middle[...].astype(F32) + delta).astype(BF16))
    d_inputs = norm_backward(
        inputs[...].astype(F32), gain[...].reshape(1, WIDTH), d_packed[...], qkv
    )
    total = (grad_middle[...].astype(F32) + d_inputs).astype(BF16)
    store_grid(grad_fields, place_t[...], total)


def kernel_columns(keep_a, got_a, keep_b, got_b, result):
    for at, (keep, got) in enumerate(((keep_a, got_a), (keep_b, got_b))):
        total = keep[...].astype(F32) + got[...].astype(F32)
        for block in range(16):
            qkv = total[:, block * 96 : (block + 1) * 96]
            out = total[:, 3 * WIDTH + block * 32 : 3 * WIDTH + (block + 1) * 32]
            result[block, at] = jnp.concatenate([qkv, out], axis=1).astype(BF16)


def kernel_total(parts, qkv_a, out_a, qkv_b, out_b):
    total = parts[0].astype(F32)
    for at in range(1, 16):
        total = total + parts[at].astype(F32)
    for at, (qkv, out) in enumerate(((qkv_a, out_a), (qkv_b, out_b))):
        qkv[...] = total[at, :, :96]
        out[...] = total[at, :, 96:]


def call(kernel, outs, scratch, args, smem=(), hbm=(), copies=0, cost=None):
    def space(at):
        return pltpu.SMEM if at in smem else pl.ANY if at in hbm else pltpu.VMEM

    shapes = [pltpu.VMEM(shape, kind) for shape, kind in scratch]
    if copies:
        shapes.append(pltpu.SemaphoreType.DMA((copies,)))
    return pl.pallas_call(
        kernel,
        out_shape=tuple(jax.ShapeDtypeStruct(shape, kind) for shape, kind in outs),
        in_specs=[pl.BlockSpec(memory_space=space(at)) for at in range(len(args))],
        out_specs=tuple(pl.BlockSpec(memory_space=pltpu.VMEM) for _ in outs),
        scratch_shapes=shapes,
        cost_estimate=cost,
        compiler_params=pltpu.CompilerParams(vmem_limit_bytes=VMEM_LIMIT),
    )(*args)


def permute(array, axis, target):
    length = lax.axis_size(axis)
    return lax.ppermute(array, axis, [(i, target(i) % length) for i in range(length)])


def permute_both(array, by):
    lons, lats = lax.axis_size("lon"), lax.axis_size("lat")
    pairs = [
        (lon * lats + lat, (lon + by) % lons * lats + (lat + by) % lats)
        for lon in range(lons)
        for lat in range(lats)
    ]
    return lax.ppermute(array, ("lon", "lat"), pairs)


def pick(array, at):
    return lax.dynamic_index_in_dim(array, at, 0, keepdims=False)


def add(*parts):
    return sum(part.astype(F32) for part in parts).astype(BF16)


def reduce_rows(send, keep):
    y = lax.axis_index("lat") // 4
    whole = add(keep, permute(send, "lat", lambda i: i ^ 1)).reshape(4, 2, 32, 4 * WIDTH)
    half = 2 * WIDTH
    one, two = whole[..., :half], whole[..., half:]
    got_one = permute(jnp.stack([pick(one, y ^ 1), pick(one, y ^ 2)]), "lat", lambda i: i ^ 4)
    got_two = permute(jnp.stack([pick(two, y ^ 3), pick(two, y ^ 2)]), "lat", lambda i: i ^ 12)
    keep_one = add(pick(one, y), got_one[0])
    send_one = add(pick(one, y ^ 3), got_one[1])
    keep_two = add(pick(two, y), got_two[0])
    send_two = add(pick(two, y ^ 1), got_two[1])
    last_one = permute(send_one, "lat", lambda i: i ^ 12)
    last_two = permute(send_two, "lat", lambda i: i ^ 4)
    both = jnp.concatenate([add(keep_one, last_one), add(keep_two, last_two)], axis=-1)
    near = lax.axis_index("lat") // 2 % 2
    return pick(both, near), permute(pick(both, 1 - near), "lat", lambda i: i ^ 2)


def body(
    fields, cotangent, land_ids, gain_a, table_a, qkv_weight_a, out_weight_a,
    gain_b, table_b, qkv_weight_b, out_weight_b,
):
    place = jnp.asarray(PLACE, BF16)
    place_t = jnp.asarray(PLACE.T, BF16)
    sort = jnp.asarray(SORT, BF16)
    sort_t = jnp.asarray(SORT.T, BF16)
    where = jnp.asarray(WHERE)
    fields = fields.transpose(1, 2, 0, 3)
    cotangent = cotangent.transpose(1, 2, 0, 3)
    table_a = table_a.transpose(1, 2, 0)
    table_b = table_b.transpose(1, 2, 0)
    grid = (fields.shape, BF16)
    piece = ((PIECE, WIDTH), BF16)
    token = ((TOKENS, WIDTH), BF16)
    token_wide = ((TOKENS, WIDTH), F32)
    packed = ((TOKENS, 3 * WIDTH), BF16)
    probs = ((WINDOWS * HEADS, LENGTH, LENGTH), BF16)
    scores = ((WINDOWS * HEADS, LENGTH, LENGTH), F32)
    mixed_t = ((WINDOWS, WIDTH, LENGTH), BF16)
    half_grads = ((WIDTH // 2, 4 * WIDTH), BF16)
    normed_t = ((WIDTH, TOKENS), BF16)
    square = ((TOKENS, TOKENS), BF16)
    spare = ((16, HEADS * GROUP), BF16)
    query = ((LENGTH, GROUP), BF16)
    keys = ((LENGTH, HEADS * GROUP), BF16)
    ids = (land_ids.shape, jnp.int32)
    place_of = (where.shape, jnp.int32)
    vector = ((WIDTH,), F32)
    qkv_shape = ((WIDTH, 3 * WIDTH), BF16)
    out_shape = ((WIDTH, WIDTH), BF16)

    p0, p1, p2, p3, inputs_a, middle_a, normed_a, packed_a, probs_a, mixed_a = call(
        kernel_forward_a,
        [piece] * 4 + [token] * 3 + [packed, probs, mixed_t],
        [grid, ids, vector, qkv_shape, out_shape, square, square, place_of, token_wide, spare, keys, scores],
        (fields, land_ids, gain_a, table_a, qkv_weight_a, out_weight_a, place, sort, where),
        smem=(3,), hbm=(0, 1, 2, 4, 5, 6, 7, 8), copies=8,
    )
    diagonal = permute_both(p0, -1)
    below = permute(p1, "lat", lambda i: i - 1)
    eastern = permute(p2, "lon", lambda i: i - 1)
    c0, c1, c2, c3, upstream_a, normed_a_t, query_b, keys_b = call(
        kernel_cotangent,
        [piece] * 4 + [token, normed_t, query, keys],
        [grid, token_wide, spare],
        (cotangent, place, sort, normed_a, land_ids, table_b, where),
        smem=(5,), hbm=(0,), copies=1,
    )
    c_diagonal = permute_both(c0, -1)
    c_below = permute(c1, "lat", lambda i: i - 1)
    c_eastern = permute(c2, "lon", lambda i: i - 1)
    b0, b1, b2, b3, inputs_b, normed_b, packed_b, probs_b, mixed_b = call(
        kernel_forward_b,
        [piece] * 4 + [token] * 2 + [packed, probs, mixed_t],
        [scores],
        (p3, eastern, below, diagonal, query_b, keys_b, gain_b, qkv_weight_b, out_weight_b, sort, sort_t),
    )
    delta_diagonal = permute_both(b3, 1)
    delta_above = permute(b2, "lat", lambda i: i + 1)
    delta_western = permute(b1, "lon", lambda i: i + 1)
    d0, d1, d2, d3, upstream_b, d_packed_b = call(
        kernel_backward_b,
        [piece] * 4 + [token, packed],
        [scores, probs],
        (
            c3, c_eastern, c_below, c_diagonal, inputs_b, gain_b, qkv_weight_b, out_weight_b,
            packed_b, probs_b, mixed_b, sort, sort_t,
        ),
    )
    d_diagonal = permute_both(d3, 1)
    d_above = permute(d2, "lat", lambda i: i + 1)
    d_western = permute(d1, "lon", lambda i: i + 1)
    send_b, keep_b = call(
        kernel_grads_b, [half_grads] * 2, [normed_t], (normed_b, mixed_b, upstream_b, d_packed_b)
    )
    grad_middle, d_packed_a, send_a = call(
        kernel_backward_a,
        [token, packed, half_grads],
        [scores, probs],
        (
            d_diagonal, d_above, d_western, d0, upstream_a, out_weight_a, packed_a, probs_a,
            mixed_a, normed_a_t, sort_t,
        ),
    )
    keep_a, advanced, grad_fields = call(
        kernel_finish_a,
        [half_grads, grid, grid],
        [],
        (
            delta_diagonal, delta_above, delta_western, b0, inputs_a, middle_a, grad_middle,
            gain_a, qkv_weight_a, d_packed_a, normed_a_t, mixed_a, place_t, sort_t,
        ),
    )
    blocks = call(
        kernel_columns,
        [((16, 2, 32, GROUP), BF16)],
        [],
        reduce_rows(send_a, keep_a) + reduce_rows(send_b, keep_b),
    )[0]
    blocks = lax.all_to_all(blocks, "lon", 0, 0, tiled=True)
    grads = call(
        kernel_total,
        [((32, 96), F32), ((32, 32), F32)] * 2,
        [],
        (blocks,),
    )
    return (advanced.transpose(2, 0, 1, 3), grad_fields.transpose(2, 0, 1, 3), *grads)


def solution(mesh):
    grid = P(None, "lat", "lon", None)
    return jax.shard_map(
        body,
        mesh=mesh,
        in_specs=(grid, grid) + (P(),) * 9,
        out_specs=(grid, grid) + (P("lat", "lon"),) * 4,
        check_vma=False,
    )
```

profile of v0, /device:TPU:6, one launch (start us, length us, event | category | flops | bytes accessed | tf_op | source)
XLA Modules:
  0.0 125.4 jit_solution(18386716730957362941)
XLA Ops:
  0.6 1.4 %copy-done.1 = bf16[512,1536]{1,0:T(8,128)(2,1)S(1)} copy-done((bf16[512,1536]{1,0:T(8,128)(2,1)S(1)}, bf16[512,1536]{1,0:T(8,128)(2,1)}, u32[]{:S(2)}) %copy-start.1) | copy-done | bytes 1572888
  2.0 0.9 copy-done.3
  3.0 1.0 copy-done.7
  4.0 0.9 copy-done.11
  5.0 0.9 copy-done.15
  5.9 1.0 copy-done.16
  6.8 0.9 copy-done.19
  7.7 0.7 copy-done.25
  8.4 0.7 copy-done.28
  9.1 6.3 %shard_map.199 = (bf16[72,512]{1,0:T(8,128)(2,1)S(1)}, bf16[72,512]{1,0:T(8,128)(2,1)S(1)}, bf16[72,512]{1,0:T(8,128)(2,1)S(1)}, bf16[72,512]{1,0:T(8,128)(2,1)S...) custom-call(bf16[12,6,4,512]{3,2,1,0:T(4,128)(2,1)S(1)} %bitcast.44,, ...), custom_call_target="tpu_custom_call" | custom-call | tf_op jit(solution)/shard_map/pallas_call | solution.py:407
  15.5 6.8 %collective-permute-start = (bf16[72,512]{1,0:T(8,128)(2,1)S(1)}, bf16[72,512]{1,0:T(8,128)(2,1)S(1)}, u32[]{:S(2)}, u32[]{:S(2)}) collective-permute-start(bf16[72,512]{1,0:T(8,128)(2,1)S(1)} %get-tuple-element.52), channel_id=1, source_target_pairs={{0,240},{16,0},{32,16},{48,32},{64,48},{80,64},{96,80},{112,96},{1... | collective-permute-start | bytes 221192 | tf_op jit(solution)/shard_map/ppermute | solution.py:420
  22.2 0.2 collective-permute-start.2
  22.5 1.0 copy-done.20
  23.4 2.0 %shard_map.200 = (bf16[72,512]{1,0:T(8,128)(2,1)S(1)}, bf16[72,512]{1,0:T(8,128)(2,1)S(1)}, bf16[72,512]{1,0:T(8,128)(2,1)S(1)}, bf16[72,512]{1,0:T(8,128)(2,1)S...) custom-call(bf16[12,6,4,512]{3,2,1,0:T(4,128)(2,1)S(1)} %bitcast.45,, ...), custom_call_target="tpu_custom_call" | custom-call | tf_op jit(solution)/shard_map/pallas_call | solution.py:407
  25.5 2.0 %collective-permute-start.6 = (bf16[72,512]{1,0:T(8,128)(2,1)S(1)}, bf16[72,512]{1,0:T(8,128)(2,1)S(1)}, u32[]{:S(2)}, u32[]{:S(2)}) collective-permute-start(bf16[72,512]{1,0:T(8,128)(2,1)S(1)} %get-tuple-element.65), channel_id=1, source_target_pairs={{0,240},{16,0},{32,16},{48,32},{64,48},{80,64},{96,80},{112,96},{1... | collective-permute-start | bytes 221192 | tf_op jit(solution)/shard_map/ppermute | solution.py:420
  27.4 2.4 %collective-permute-start.7 = (bf16[72,512]{1,0:T(8,128)(2,1)S(1)}, bf16[72,512]{1,0:T(8,128)(2,1)S(1)}, u32[]{:S(2)}, u32[]{:S(2)}) collective-permute-start(bf16[72,512]{1,0:T(8,128)(2,1)S(1)} %get-tuple-element.66), channel_id=1, source_target_pairs={{0,15},{1,0},{2,1},{3,2},{4,3},{5,4},{6,5},{7,6},{8,7},{9,8},{10,9... | collective-permute-start | bytes 221192 | tf_op jit(solution)/shard_map/ppermute | solution.py:420
  29.8 1.2 collective-permute-start.8
  31.1 4.4 %shard_map.201 = (bf16[72,512]{1,0:T(8,128)(2,1)S(1)}, bf16[72,512]{1,0:T(8,128)(2,1)}, bf16[72,512]{1,0:T(8,128)(2,1)}, bf16[72,512]{1,0:T(8,128)(2,1)}, bf16[2...) custom-call(bf16[72,512]{1,0:T(8,128)(2,1)S(1)} %get-tuple-element.5, ...), custom_call_target="tpu_custom_call" | custom-call | tf_op jit(solution)/shard_map/pallas_call | solution.py:407
  35.5 4.5 %shard_map.202 = (bf16[72,512]{1,0:T(8,128)(2,1)S(1)}, bf16[72,512]{1,0:T(8,128)(2,1)S(1)}, bf16[72,512]{1,0:T(8,128)(2,1)S(1)}, bf16[72,512]{1,0:T(8,128)(2,1)S...) custom-call(bf16[72,512]{1,0:T(8,128)(2,1)S(1)} %get-tuple-element.64.piece0, ...), custom_call_target="tpu_custom_call" | custom-call | tf_op jit(solution)/shard_map/pallas_call | solution.py:407
  40.1 2.2 %shard_map.205 = (bf16[256,2048]{1,0:T(8,128)(2,1)}, bf16[256,2048]{1,0:T(8,128)(2,1)S(1)}) custom-call(bf16[288,512]{1,0:T(8,128)(2,1)S(1)} %get-tuple-element.87.normed, bf16[2,512,144]{2,1,0:T(8,128)(2,1)S(1)} %get-tuple-element.71.mixed_t, bf16[288,512]{1,0:T(8,128)(2,1)S(1)} %get-tuple-element.88.upstream, bf16[288,1536]{1,0:T(8,128)(2,1)S(1)} %get-tuple-element.89.d_packed), custom_call_target="tpu_custom_call" | custom-call | tf_op jit(solution)/shard_map/pallas_call | solution.py:407
  42.2 1.0 copy-done.9
  43.2 0.5 collective-permute-start.18
  43.8 1.3 %collective-permute-start.11 = (bf16[72,512]{1,0:T(8,128)(2,1)S(1)}, bf16[72,512]{1,0:T(8,128)(2,1)S(1)}, u32[]{:S(2)}, u32[]{:S(2)}) collective-permute-start(bf16[72,512]{1,0:T(8,128)(2,1)S(1)} %get-tuple-element.74), channel_id=1, source_target_pairs={{0,16},{16,32},{32,48},{48,64},{64,80},{80,96},{96,112},{112,128},... | collective-permute-start | bytes 221192 | tf_op jit(solution)/shard_map/ppermute | solution.py:420
  45.1 2.4 %collective-permute-done.10.back1 = bf16[72,512]{1,0:T(8,128)(2,1)S(1)} collective-permute-done((bf16[72,512]{1,0:T(8,128)(2,1)S(1)}, bf16[72,512]{1,0:T(8,128)(2,1)S(1)}, u32[]{:S(2)}, u32[]{:S(2)}) %collective-permute-start.10) | collective-permute-done | bytes 73760 | tf_op jit(solution)/shard_map/ppermute | solution.py:420
  47.5 5.0 %collective-permute-done.11.back2 = bf16[72,512]{1,0:T(8,128)(2,1)S(1)} collective-permute-done((bf16[72,512]{1,0:T(8,128)(2,1)S(1)}, bf16[72,512]{1,0:T(8,128)(2,1)S(1)}, u32[]{:S(2)}, u32[]{:S(2)}) %collective-permute-start.11) | collective-permute-done | bytes 73760 | tf_op jit(solution)/shard_map/ppermute | solution.py:420
  52.6 1.3 %collective-permute-done.9.back0 = bf16[72,512]{1,0:T(8,128)(2,1)S(1)} collective-permute-done((bf16[72,512]{1,0:T(8,128)(2,1)S(1)}, bf16[72,512]{1,0:T(8,128)(2,1)S(1)}, u32[]{:S(2)}, u32[]{:S(2)}) %collective-permute-start.9) | collective-permute-done | bytes 73760 | tf_op jit(solution)/shard_map/ppermute | solution.py:430
  53.9 5.2 %shard_map.203 = (bf16[288,512]{1,0:T(8,128)(2,1)S(1)}, bf16[288,1536]{1,0:T(8,128)(2,1)S(1)}, bf16[256,2048]{1,0:T(8,128)(2,1)}) custom-call(bf16[72,512]{1,0:T(8,128)(2,1)S(1)} %collective-permute-done.9.back0, bf16[72,512]{1,0:T(8,128)(2,1)S(1)} %collective-permute-done.10.back1, bf16[72,512]{1,0:T(8,128)(2,1)S(1)} %collective-permute-done.11.back2, ...), custom_call_target="tpu_custom_call" | custom-call | tf_op jit(solution)/shard_map/pallas_call | solution.py:407
  59.1 0.9 copy-done.13
  60.0 0.7 copy-done.17
  60.8 0.5 collective-permute-start.4
  61.3 6.9 %collective-permute-done.3.back0 = bf16[72,512]{1,0:T(8,128)(2,1)} collective-permute-done((bf16[72,512]{1,0:T(8,128)(2,1)}, bf16[72,512]{1,0:T(8,128)(2,1)}, u32[]{:S(2)}, u32[]{:S(2)}) %collective-permute-start.3) | collective-permute-done | bytes 73760 | tf_op jit(solution)/shard_map/ppermute | solution.py:430
  68.2 2.6 %collective-permute-done.5.back2 = bf16[72,512]{1,0:T(8,128)(2,1)} collective-permute-done((bf16[72,512]{1,0:T(8,128)(2,1)}, bf16[72,512]{1,0:T(8,128)(2,1)}, u32[]{:S(2)}, u32[]{:S(2)}) %collective-permute-start.5) | collective-permute-done | bytes 73760 | tf_op jit(solution)/shard_map/ppermute | solution.py:420
  70.7 1.2 copy-done.14
  71.9 1.0 copy-done.18
  72.9 0.9 copy-done.23
  73.8 3.9 %shard_map.204 = (bf16[256,2048]{1,0:T(8,128)(2,1)S(1)}, bf16[12,6,4,512]{3,2,1,0:T(4,128)(2,1)}, bf16[12,6,4,512]{3,2,1,0:T(4,128)(2,1)}) custom-call(bf16[72,512]{1,0:T(8,128)(2,1)} %collective-permute-done.3.back0, bf16[72,512]{1,0:T(8,128)(2,1)} %collective-permute-done.4.back1, bf16[72,512]{1,0:T(8,128)(2,1)} %collective-permute-done.5.back2, ...), custom_call_target="tpu_custom_call" | custom-call | tf_op jit(solution)/shard_map/pallas_call | solution.py:407
  77.6 1.6 %add_convert_fusion = bf16[256,2048]{1,0:T(8,128)(2,1)S(1)} fusion(bf16[256,2048]{1,0:T(8,128)(2,1)} %collective-permute-done.18, bf16[256,2048]{1,0:T(8,128)(2,1)S(1)} %copy-done.10), kind=kLoop, calls=%fused_computation | loop fusion | flops 2097152 | bytes 3145728 | tf_op jit(solution)/shard_map/convert_element_type | solution.py:438
  79.3 0.1 fusion.20
  79.4 1.6 %add_convert_fusion.1 = bf16[256,2048]{1,0:T(8,128)(2,1)S(1)} fusion(bf16[256,2048]{1,0:T(8,128)(2,1)} %collective-permute-done.12, bf16[256,2048]{1,0:T(8,128)(2,1)S(1)} %get-tuple-element.85), kind=kLoop, calls=%fused_computation.1 | loop fusion | flops 2097152 | bytes 3145728 | tf_op jit(solution)/shard_map/convert_element_type | solution.py:438
  81.0 0.1 fusion.21
  81.2 3.1 %collective-permute-start.21 = (bf16[2,2,32,1024]{3,2,1,0:T(8,128)(2,1)S(1)}, bf16[2,2,32,1024]{3,2,1,0:T(8,128)(2,1)S(1)}, u32[]{:S(2)}, u32[]{:S(2)}) collective-permute-start(bf16[2,2,32,1024]{3,2,1,0:T(8,128)(2,1)S(1)} %pad_maximum_fusion.3), channel_id=1, source_target_pairs={{0,12},{1,13},{2,14},{3,15},{4,8},{5,9},{6,10},{7,11},{8,4},{9,5},... | collective-permute-start | bytes 786440 | tf_op jit(solution)/shard_map/ppermute | solution.py:420
  84.3 0.4 collective-permute-start.19
  84.8 1.1 collective-permute-start.15
  85.9 0.7 collective-permute-start.13
  86.7 4.9 %collective-permute-done.21 = bf16[2,2,32,1024]{3,2,1,0:T(8,128)(2,1)S(1)} collective-permute-done((bf16[2,2,32,1024]{3,2,1,0:T(8,128)(2,1)S(1)}, bf16[2,2,32,1024]{3,2,1,0:T(8,128)(2,1)S(1)}, u32[]{:S(2)}, u32[]{:S(2)}) %collective-permute-start.21) | collective-permute-done | bytes 262176 | tf_op jit(solution)/shard_map/ppermute | solution.py:420
  91.6 0.7 collective-permute-start.22
  92.3 1.2 collective-permute-done.19
  93.6 1.5 %collective-permute-start.20 = (bf16[2,32,1024]{2,1,0:T(8,128)(2,1)S(1)}, bf16[2,32,1024]{2,1,0:T(8,128)(2,1)S(1)}, u32[]{:S(2)}, u32[]{:S(2)}) collective-permute-start(bf16[2,32,1024]{2,1,0:T(8,128)(2,1)S(1)} %fusion.9), channel_id=1, source_target_pairs={{0,12},{1,13},{2,14},{3,15},{4,8},{5,9},{6,10},{7,11},{8,4},{9,5},... | collective-permute-start | bytes 393224 | tf_op jit(solution)/shard_map/ppermute | solution.py:420
  95.1 2.1 %collective-permute-done.15 = bf16[2,2,32,1024]{3,2,1,0:T(8,128)(2,1)S(1)} collective-permute-done((bf16[2,2,32,1024]{3,2,1,0:T(8,128)(2,1)S(1)}, bf16[2,2,32,1024]{3,2,1,0:T(8,128)(2,1)S(1)}, u32[]{:S(2)}, u32[]{:S(2)}) %collective-permute-start.15) | collective-permute-done | bytes 262176 | tf_op jit(solution)/shard_map/ppermute | solution.py:420
  97.3 0.2 collective-permute-start.16
  97.4 1.8 %collective-permute-done.13 = bf16[2,2,32,1024]{3,2,1,0:T(8,128)(2,1)S(1)} collective-permute-done((bf16[2,2,32,1024]{3,2,1,0:T(8,128)(2,1)S(1)}, bf16[2,2,32,1024]{3,2,1,0:T(8,128)(2,1)S(1)}, u32[]{:S(2)}, u32[]{:S(2)}) %collective-permute-start.13) | collective-permute-done | bytes 262176 | tf_op jit(solution)/shard_map/ppermute | solution.py:420
  99.2 1.3 %collective-permute-start.14 = (bf16[2,32,1024]{2,1,0:T(8,128)(2,1)S(1)}, bf16[2,32,1024]{2,1,0:T(8,128)(2,1)S(1)}, u32[]{:S(2)}, u32[]{:S(2)}) collective-permute-start(bf16[2,32,1024]{2,1,0:T(8,128)(2,1)S(1)} %fusion.5), channel_id=1, source_target_pairs={{0,12},{1,13},{2,14},{3,15},{4,8},{5,9},{6,10},{7,11},{8,4},{9,5},... | collective-permute-start | bytes 393224 | tf_op jit(solution)/shard_map/ppermute | solution.py:420
  100.5 1.5 %collective-permute-done.22 = bf16[2,32,1024]{2,1,0:T(8,128)(2,1)S(1)} collective-permute-done((bf16[2,32,1024]{2,1,0:T(8,128)(2,1)S(1)}, bf16[2,32,1024]{2,1,0:T(8,128)(2,1)S(1)}, u32[]{:S(2)}, u32[]{:S(2)}) %collective-permute-start.22) | collective-permute-done | bytes 131104 | tf_op jit(solution)/shard_map/ppermute | solution.py:420
  102.1 0.1 fusion.1
  102.2 0.3 collective-permute-start.23
  102.5 1.2 collective-permute-done.16
  103.7 0.1 fusion.2
  103.7 1.7 %collective-permute-done.14 = bf16[2,32,1024]{2,1,0:T(8,128)(2,1)S(1)} collective-permute-done((bf16[2,32,1024]{2,1,0:T(8,128)(2,1)S(1)}, bf16[2,32,1024]{2,1,0:T(8,128)(2,1)S(1)}, u32[]{:S(2)}, u32[]{:S(2)}) %collective-permute-start.14) | collective-permute-done | bytes 131104 | tf_op jit(solution)/shard_map/ppermute | solution.py:420
  105.6 0.3 collective-permute-start.17
  105.9 2.5 %collective-permute-done.23.got_b = bf16[32,2048]{1,0:T(8,128)(2,1)S(1)} collective-permute-done((bf16[32,2048]{1,0:T(8,128)(2,1)S(1)}, bf16[32,2048]{1,0:T(8,128)(2,1)S(1)}, u32[]{:S(2)}, u32[]{:S(2)}) %collective-permute-start.23) | collective-permute-done | bytes 131104 | tf_op jit(solution)/shard_map/ppermute | solution.py:420
  108.4 2.3 %collective-permute-done.17.got_a = bf16[32,2048]{1,0:T(8,128)(2,1)S(1)} collective-permute-done((bf16[32,2048]{1,0:T(8,128)(2,1)S(1)}, bf16[32,2048]{1,0:T(8,128)(2,1)S(1)}, u32[]{:S(2)}, u32[]{:S(2)}) %collective-permute-start.17) | collective-permute-done | bytes 131104 | tf_op jit(solution)/shard_map/ppermute | solution.py:420
  110.6 0.2 shard_map.206
  110.8 13.8 %all_to_all.5.parts = bf16[16,2,32,128]{3,2,1,0:T(8,128)(2,1)S(1)} all-to-all(bf16[16,2,32,128]{3,2,1,0:T(8,128)(2,1)S(1)} %shard_map.206), channel_id=1, replica_groups=mesh['lon'=16,'lat'=16] {'lon'}, dimensions={0} | all-to-all | bytes 524288 | tf_op jit(solution)/shard_map/all_to_all | solution.py:560
  124.7 0.7 shard_map.207
  (72 shorter events, 0.7 us)
Async XLA Ops:
  0.6 1.4 %copy-start.1 = (bf16[512,1536]{1,0:T(8,128)(2,1)S(1)}, bf16[512,1536]{1,0:T(8,128)(2,1)}, u32[]{:S(2)}) copy-start(bf16[512,1536]{1,0:T(8,128)(2,1)} %qkv.5) | copy-start | bytes 4718596
  2.0 0.9 copy-start.3
  3.0 1.0 copy-start.7
  4.0 0.9 copy-start.11
  5.0 0.9 copy-start.15
  5.9 1.0 copy-start.16
  6.8 0.9 copy-start.19
  7.7 0.7 copy-start.25
  8.4 0.7 copy-start.28
  9.1 13.4 %copy-start.4 = (bf16[288,288]{1,0:T(8,128)(2,1)S(1)}, bf16[288,288]{1,0:T(8,128)(2,1)}, u32[]{:S(2)}) copy-start(bf16[288,288]{1,0:T(8,128)(2,1)} %constant.104.clone.sort_hbm.sort) | copy-start | bytes 497668
  9.1 13.4 %copy-start.12 = (bf16[288,288]{1,0:T(8,128)(2,1)S(1)}, bf16[288,288]{1,0:T(8,128)(2,1)}, u32[]{:S(2)}) copy-start(bf16[288,288]{1,0:T(8,128)(2,1)} %constant.102.clone.place_hbm.place) | copy-start | bytes 497668
  9.1 13.4 %copy-start.27 = (f32[16,3,3]{0,2,1:T(4,128)S(1)}, f32[16,3,3]{0,2,1:T(4,128)}, u32[]{:S(2)}) copy-start(f32[16,3,3]{0,2,1:T(4,128)} %param.24) | copy-start | bytes 1732
  9.1 22.0 %copy-start = (bf16[512,1536]{1,0:T(8,128)(2,1)S(1)}, bf16[512,1536]{1,0:T(8,128)(2,1)}, u32[]{:S(2)}) copy-start(bf16[512,1536]{1,0:T(8,128)(2,1)} %qkv.4) | copy-start | bytes 4718596
  9.1 22.0 %copy-start.5 = (bf16[288,288]{1,0:T(8,128)(2,1)S(1)}, bf16[288,288]{1,0:T(8,128)(2,1)}, u32[]{:S(2)}) copy-start(bf16[288,288]{1,0:T(8,128)(2,1)} %constant.105.clone.sort_t) | copy-start | bytes 497668
  9.1 22.0 %copy-start.6 = (bf16[512,512]{1,0:T(8,128)(2,1)S(1)}, bf16[512,512]{1,0:T(8,128)(2,1)}, u32[]{:S(2)}) copy-start(bf16[512,512]{1,0:T(8,128)(2,1)} %out.4) | copy-start | bytes 1572868
  9.1 22.0 %copy-start.24 = (f32[512]{0:T(512)S(1)}, f32[512]{0:T(512)}, u32[]{:S(2)}) copy-start(f32[512]{0:T(512)} %gain.4) | copy-start | bytes 6148
  15.5 14.4 %collective-permute-start = (bf16[72,512]{1,0:T(8,128)(2,1)S(1)}, bf16[72,512]{1,0:T(8,128)(2,1)S(1)}, u32[]{:S(2)}, u32[]{:S(2)}) collective-permute-start(bf16[72,512]{1,0:T(8,128)(2,1)S(1)} %get-tuple-element.52), channel_id=1, source_target_pairs={{0,240},{16,0},{32,16},{48,32},{64,48},{80,64},{96,80},{112,96},{1... | collective-permute-start | bytes 221192 | tf_op jit(solution)/shard_map/ppermute | solution.py:420
  22.2 8.8 %collective-permute-start.1 = (bf16[72,512]{1,0:T(8,128)(2,1)S(1)}, bf16[72,512]{1,0:T(8,128)(2,1)S(1)}, u32[]{:S(2)}, u32[]{:S(2)}) collective-permute-start(bf16[72,512]{1,0:T(8,128)(2,1)S(1)} %get-tuple-element.53), channel_id=1, source_target_pairs={{0,15},{1,0},{2,1},{3,2},{4,3},{5,4},{6,5},{7,6},{8,7},{9,8},{10,9... | collective-permute-start | bytes 221192 | tf_op jit(solution)/shard_map/ppermute | solution.py:420
  22.2 8.8 %collective-permute-start.2 = (bf16[72,512]{1,0:T(8,128)(2,1)S(1)}, bf16[72,512]{1,0:T(8,128)(2,1)S(1)}, u32[]{:S(2)}, u32[]{:S(2)}) collective-permute-start(bf16[72,512]{1,0:T(8,128)(2,1)S(1)} %get-tuple-element.54), channel_id=1, source_target_pairs={{0,255},{1,240},{2,241},{3,242},{4,243},{5,244},{6,245},{7,246},{8... | collective-permute-start | bytes 221192 | tf_op jit(solution)/shard_map/ppermute | solution.py:430
  22.4 1.0 copy-start.20
  25.5 10.1 %collective-permute-start.6 = (bf16[72,512]{1,0:T(8,128)(2,1)S(1)}, bf16[72,512]{1,0:T(8,128)(2,1)S(1)}, u32[]{:S(2)}, u32[]{:S(2)}) collective-permute-start(bf16[72,512]{1,0:T(8,128)(2,1)S(1)} %get-tuple-element.65), channel_id=1, source_target_pairs={{0,240},{16,0},{32,16},{48,32},{64,48},{80,64},{96,80},{112,96},{1... | collective-permute-start | bytes 221192 | tf_op jit(solution)/shard_map/ppermute | solution.py:420
  27.4 8.1 %collective-permute-start.7 = (bf16[72,512]{1,0:T(8,128)(2,1)S(1)}, bf16[72,512]{1,0:T(8,128)(2,1)S(1)}, u32[]{:S(2)}, u32[]{:S(2)}) collective-permute-start(bf16[72,512]{1,0:T(8,128)(2,1)S(1)} %get-tuple-element.66), channel_id=1, source_target_pairs={{0,15},{1,0},{2,1},{3,2},{4,3},{5,4},{6,5},{7,6},{8,7},{9,8},{10,9... | collective-permute-start | bytes 221192 | tf_op jit(solution)/shard_map/ppermute | solution.py:420
  29.8 5.7 %collective-permute-start.8 = (bf16[72,512]{1,0:T(8,128)(2,1)S(1)}, bf16[72,512]{1,0:T(8,128)(2,1)S(1)}, u32[]{:S(2)}, u32[]{:S(2)}) collective-permute-start(bf16[72,512]{1,0:T(8,128)(2,1)S(1)} %get-tuple-element.67), channel_id=1, source_target_pairs={{0,255},{1,240},{2,241},{3,242},{4,243},{5,244},{6,245},{7,246},{8... | collective-permute-start | bytes 221192 | tf_op jit(solution)/shard_map/ppermute | solution.py:430
  35.5 4.5 %copy-start.22 = (bf16[72,512]{1,0:T(8,128)(2,1)}, bf16[72,512]{1,0:T(8,128)(2,1)S(1)}, u32[]{:S(2)}) copy-start(bf16[72,512]{1,0:T(8,128)(2,1)S(1)} %get-tuple-element.61.back3) | copy-start | bytes 221188
  40.0 13.8 %copy-start.8 = (bf16[512,512]{1,0:T(8,128)(2,1)S(1)}, bf16[512,512]{1,0:T(8,128)(2,1)}, u32[]{:S(2)}) copy-start(bf16[512,512]{1,0:T(8,128)(2,1)} %out.5) | copy-start | bytes 1572868
  42.2 1.0 copy-start.9
  43.2 34.4 %collective-permute-start.18 = (bf16[256,2048]{1,0:T(8,128)(2,1)}, bf16[256,2048]{1,0:T(8,128)(2,1)}, u32[]{:S(2)}, u32[]{:S(2)}) collective-permute-start(bf16[256,2048]{1,0:T(8,128)(2,1)} %get-tuple-element.91), channel_id=1, source_target_pairs={{0,1},{1,0},{2,3},{3,2},{4,5},{5,4},{6,7},{7,6},{8,9},{9,8},{10,11... | collective-permute-start | bytes 3145736 | tf_op jit(solution)/shard_map/ppermute | solution.py:420
  43.8 3.8 %collective-permute-start.10 = (bf16[72,512]{1,0:T(8,128)(2,1)S(1)}, bf16[72,512]{1,0:T(8,128)(2,1)S(1)}, u32[]{:S(2)}, u32[]{:S(2)}) collective-permute-start(bf16[72,512]{1,0:T(8,128)(2,1)S(1)} %get-tuple-element.73), channel_id=1, source_target_pairs={{0,1},{1,2},{2,3},{3,4},{4,5},{5,6},{6,7},{7,8},{8,9},{9,10},{10,1... | collective-permute-start | bytes 221192 | tf_op jit(solution)/shard_map/ppermute | solution.py:420
  43.8 8.8 %collective-permute-start.11 = (bf16[72,512]{1,0:T(8,128)(2,1)S(1)}, bf16[72,512]{1,0:T(8,128)(2,1)S(1)}, u32[]{:S(2)}, u32[]{:S(2)}) collective-permute-start(bf16[72,512]{1,0:T(8,128)(2,1)S(1)} %get-tuple-element.74), channel_id=1, source_target_pairs={{0,16},{16,32},{32,48},{48,64},{64,80},{80,96},{96,112},{112,128},... | collective-permute-start | bytes 221192 | tf_op jit(solution)/shard_map/ppermute | solution.py:420
  45.1 8.8 %collective-permute-start.9 = (bf16[72,512]{1,0:T(8,128)(2,1)S(1)}, bf16[72,512]{1,0:T(8,128)(2,1)S(1)}, u32[]{:S(2)}, u32[]{:S(2)}) collective-permute-start(bf16[72,512]{1,0:T(8,128)(2,1)S(1)} %get-tuple-element.72), channel_id=1, source_target_pairs={{0,17},{1,18},{2,19},{3,20},{4,21},{5,22},{6,23},{7,24},{8,25},{9,... | collective-permute-start | bytes 221192 | tf_op jit(solution)/shard_map/ppermute | solution.py:430
  53.9 16.9 %copy-start.2 = (bf16[512,1536]{1,0:T(8,128)(2,1)S(1)}, bf16[512,1536]{1,0:T(8,128)(2,1)}, u32[]{:S(2)}) copy-start(bf16[512,1536]{1,0:T(8,128)(2,1)} %qkv.5) | copy-start | bytes 4718596
  53.9 16.9 %copy-start.21 = (bf16[288,288]{1,0:T(8,128)(2,1)S(1)}, bf16[288,288]{1,0:T(8,128)(2,1)}, u32[]{:S(2)}) copy-start(bf16[288,288]{1,0:T(8,128)(2,1)} %constant.103.clone.place_t) | copy-start | bytes 497668
  53.9 16.9 %copy-start.26 = (f32[512]{0:T(512)S(1)}, f32[512]{0:T(512)}, u32[]{:S(2)}) copy-start(f32[512]{0:T(512)} %gain.5) | copy-start | bytes 6148
  59.1 0.9 copy-start.13
  60.0 0.7 copy-start.17
  60.7 18.6 %collective-permute-start.12 = (bf16[256,2048]{1,0:T(8,128)(2,1)}, bf16[256,2048]{1,0:T(8,128)(2,1)}, u32[]{:S(2)}, u32[]{:S(2)}) collective-permute-start(bf16[256,2048]{1,0:T(8,128)(2,1)} %get-tuple-element.86), channel_id=1, source_target_pairs={{0,1},{1,0},{2,3},{3,2},{4,5},{5,4},{6,7},{7,6},{8,9},{9,8},{10,11... | collective-permute-start | bytes 3145736 | tf_op jit(solution)/shard_map/ppermute | solution.py:420
  60.8 7.4 %collective-permute-start.3 = (bf16[72,512]{1,0:T(8,128)(2,1)}, bf16[72,512]{1,0:T(8,128)(2,1)}, u32[]{:S(2)}, u32[]{:S(2)}) collective-permute-start(bf16[72,512]{1,0:T(8,128)(2,1)} %get-tuple-element.58), channel_id=1, source_target_pairs={{0,17},{1,18},{2,19},{3,20},{4,21},{5,22},{6,23},{7,24},{8,25},{9,... | collective-permute-start | bytes 221192 | tf_op jit(solution)/shard_map/ppermute | solution.py:430
  60.8 7.4 %collective-permute-start.4 = (bf16[72,512]{1,0:T(8,128)(2,1)}, bf16[72,512]{1,0:T(8,128)(2,1)}, u32[]{:S(2)}, u32[]{:S(2)}) collective-permute-start(bf16[72,512]{1,0:T(8,128)(2,1)} %get-tuple-element.59), channel_id=1, source_target_pairs={{0,1},{1,2},{2,3},{3,4},{4,5},{5,6},{6,7},{7,8},{8,9},{9,10},{10,1... | collective-permute-start | bytes 221192 | tf_op jit(solution)/shard_map/ppermute | solution.py:420
  61.3 9.5 %collective-permute-start.5 = (bf16[72,512]{1,0:T(8,128)(2,1)}, bf16[72,512]{1,0:T(8,128)(2,1)}, u32[]{:S(2)}, u32[]{:S(2)}) collective-permute-start(bf16[72,512]{1,0:T(8,128)(2,1)} %get-tuple-element.60), channel_id=1, source_target_pairs={{0,16},{16,32},{32,48},{48,64},{64,80},{80,96},{96,112},{112,128},... | collective-permute-start | bytes 221192 | tf_op jit(solution)/shard_map/ppermute | solution.py:420
  70.7 1.2 copy-start.14
  71.9 1.0 copy-start.18
  72.9 0.9 copy-start.23
  73.8 3.9 %copy-start.10 = (bf16[256,2048]{1,0:T(8,128)(2,1)S(1)}, bf16[256,2048]{1,0:T(8,128)(2,1)}, u32[]{:S(2)}) copy-start(bf16[256,2048]{1,0:T(8,128)(2,1)} %copy-done.9) | copy-start | bytes 3145732
  81.2 10.4 %collective-permute-start.21 = (bf16[2,2,32,1024]{3,2,1,0:T(8,128)(2,1)S(1)}, bf16[2,2,32,1024]{3,2,1,0:T(8,128)(2,1)S(1)}, u32[]{:S(2)}, u32[]{:S(2)}) collective-permute-start(bf16[2,2,32,1024]{3,2,1,0:T(8,128)(2,1)S(1)} %pad_maximum_fusion.3), channel_id=1, source_target_pairs={{0,12},{1,13},{2,14},{3,15},{4,8},{5,9},{6,10},{7,11},{8,4},{9,5},... | collective-permute-start | bytes 786440 | tf_op jit(solution)/shard_map/ppermute | solution.py:420
  84.3 9.3 %collective-permute-start.19 = (bf16[2,2,32,1024]{3,2,1,0:T(8,128)(2,1)S(1)}, bf16[2,2,32,1024]{3,2,1,0:T(8,128)(2,1)S(1)}, u32[]{:S(2)}, u32[]{:S(2)}) collective-permute-start(bf16[2,2,32,1024]{3,2,1,0:T(8,128)(2,1)S(1)} %pad_maximum_fusion.2), channel_id=1, source_target_pairs={{0,4},{1,5},{2,6},{3,7},{4,0},{5,1},{6,2},{7,3},{8,12},{9,13},{10,... | collective-permute-start | bytes 786440 | tf_op jit(solution)/shard_map/ppermute | solution.py:420
  84.8 12.5 %collective-permute-start.15 = (bf16[2,2,32,1024]{3,2,1,0:T(8,128)(2,1)S(1)}, bf16[2,2,32,1024]{3,2,1,0:T(8,128)(2,1)S(1)}, u32[]{:S(2)}, u32[]{:S(2)}) collective-permute-start(bf16[2,2,32,1024]{3,2,1,0:T(8,128)(2,1)S(1)} %pad_maximum_fusion.1), channel_id=1, source_target_pairs={{0,12},{1,13},{2,14},{3,15},{4,8},{5,9},{6,10},{7,11},{8,4},{9,5},... | collective-permute-start | bytes 786440 | tf_op jit(solution)/shard_map/ppermute | solution.py:420
  85.9 13.2 %collective-permute-start.13 = (bf16[2,2,32,1024]{3,2,1,0:T(8,128)(2,1)S(1)}, bf16[2,2,32,1024]{3,2,1,0:T(8,128)(2,1)S(1)}, u32[]{:S(2)}, u32[]{:S(2)}) collective-permute-start(bf16[2,2,32,1024]{3,2,1,0:T(8,128)(2,1)S(1)} %pad_maximum_fusion), channel_id=1, source_target_pairs={{0,4},{1,5},{2,6},{3,7},{4,0},{5,1},{6,2},{7,3},{8,12},{9,13},{10,... | collective-permute-start | bytes 786440 | tf_op jit(solution)/shard_map/ppermute | solution.py:420
  91.6 10.4 %collective-permute-start.22 = (bf16[2,32,1024]{2,1,0:T(8,128)(2,1)S(1)}, bf16[2,32,1024]{2,1,0:T(8,128)(2,1)S(1)}, u32[]{:S(2)}, u32[]{:S(2)}) collective-permute-start(bf16[2,32,1024]{2,1,0:T(8,128)(2,1)S(1)} %fusion.11), channel_id=1, source_target_pairs={{0,4},{1,5},{2,6},{3,7},{4,0},{5,1},{6,2},{7,3},{8,12},{9,13},{10,... | collective-permute-start | bytes 393224 | tf_op jit(solution)/shard_map/ppermute | solution.py:420
  93.6 8.4 %collective-permute-start.20 = (bf16[2,32,1024]{2,1,0:T(8,128)(2,1)S(1)}, bf16[2,32,1024]{2,1,0:T(8,128)(2,1)S(1)}, u32[]{:S(2)}, u32[]{:S(2)}) collective-permute-start(bf16[2,32,1024]{2,1,0:T(8,128)(2,1)S(1)} %fusion.9), channel_id=1, source_target_pairs={{0,12},{1,13},{2,14},{3,15},{4,8},{5,9},{6,10},{7,11},{8,4},{9,5},... | collective-permute-start | bytes 393224 | tf_op jit(solution)/shard_map/ppermute | solution.py:420
  97.3 6.4 %collective-permute-start.16 = (bf16[2,32,1024]{2,1,0:T(8,128)(2,1)S(1)}, bf16[2,32,1024]{2,1,0:T(8,128)(2,1)S(1)}, u32[]{:S(2)}, u32[]{:S(2)}) collective-permute-start(bf16[2,32,1024]{2,1,0:T(8,128)(2,1)S(1)} %fusion.7), channel_id=1, source_target_pairs={{0,4},{1,5},{2,6},{3,7},{4,0},{5,1},{6,2},{7,3},{8,12},{9,13},{10,... | collective-permute-start | bytes 393224 | tf_op jit(solution)/shard_map/ppermute | solution.py:420
  99.2 6.3 %collective-permute-start.14 = (bf16[2,32,1024]{2,1,0:T(8,128)(2,1)S(1)}, bf16[2,32,1024]{2,1,0:T(8,128)(2,1)S(1)}, u32[]{:S(2)}, u32[]{:S(2)}) collective-permute-start(bf16[2,32,1024]{2,1,0:T(8,128)(2,1)S(1)} %fusion.5), channel_id=1, source_target_pairs={{0,12},{1,13},{2,14},{3,15},{4,8},{5,9},{6,10},{7,11},{8,4},{9,5},... | collective-permute-start | bytes 393224 | tf_op jit(solution)/shard_map/ppermute | solution.py:420
  102.2 6.2 %collective-permute-start.23 = (bf16[32,2048]{1,0:T(8,128)(2,1)S(1)}, bf16[32,2048]{1,0:T(8,128)(2,1)S(1)}, u32[]{:S(2)}, u32[]{:S(2)}) collective-permute-start(bf16[32,2048]{1,0:T(8,128)(2,1)S(1)} %get-tuple-element.108), channel_id=1, source_target_pairs={{0,2},{1,3},{2,0},{3,1},{4,6},{5,7},{6,4},{7,5},{8,10},{9,11},{10,... | collective-permute-start | bytes 393224 | tf_op jit(solution)/shard_map/ppermute | solution.py:420
  105.6 5.1 %collective-permute-start.17 = (bf16[32,2048]{1,0:T(8,128)(2,1)S(1)}, bf16[32,2048]{1,0:T(8,128)(2,1)S(1)}, u32[]{:S(2)}, u32[]{:S(2)}) collective-permute-start(bf16[32,2048]{1,0:T(8,128)(2,1)S(1)} %get-tuple-element.110), channel_id=1, source_target_pairs={{0,2},{1,3},{2,0},{3,1},{4,6},{5,7},{6,4},{7,5},{8,10},{9,11},{10,... | collective-permute-start | bytes 393224 | tf_op jit(solution)/shard_map/ppermute | solution.py:420
where the time goes:
time: 128 us; the launch traced here: 125 us
  waiting for transfers between devices  37.5 us (29%)
  Pallas kernels  29.5 us (23%)
  starting transfers between devices  24.6 us (19%)
  local copies, waits for them, and re-layouts  15.3 us (12%)
  blocking collectives  13.8 us (11%)
  other arithmetic  3.76 us (3%)
    pallas_call x9, Pallas kernels, call(): pl.pallas_call(kernel, out_shape=tuple((jax.ShapeDtypeStruct(shape, kind)...  29.5 us
    ppermute x20, waiting for transfers between devices, permute(): lax.ppermute(array, axis, [(i, target(i) % length) for i in range(length)])  29.3 us
    ppermute x20, starting transfers between devices, permute(): lax.ppermute(array, axis, [(i, target(i) % length) for i in range(length)])  23.1 us
    unnamed x58, local copies, waits for them, and re-layouts  15.1 us
    all_to_all x1, blocking collectives, body(): blocks = lax.all_to_all(blocks, 'lon', 0, 0, tiled=True)  13.8 us
    ppermute x4, waiting for transfers between devices, permute_both(): return lax.ppermute(array, ('lon', 'lat'), pairs)  8.19 us
    convert_element_type x10, other arithmetic, add(): return sum((part.astype(F32) for part in parts)).astype(BF16)  3.6 us
  transfers between devices with their start and end apart: 24, of which 14 were waited for; matrix products, arithmetic and copies ran while one was open for 2% of the time, Pallas kernels for 12%

commit v1 on v0

--- a/solution.py
+++ b/solution.py
@@ -364,19 +364,59 @@
 
 
 def kernel_finish_a(
-    back0, back1, back2, back3, inputs, middle, grad_middle, gain, qkv, d_packed, normed_t,
-    mixed_t, place_t, sort_t,
-    keep, advanced, grad_fields,
-):
+    inputs, grad_middle, gain, qkv_hbm, d_packed, normed_t, mixed_t, place_t,
+    keep, grad_fields,
+    qkv, sems,
+):
+    (qkv_in,) = fetch(((qkv_hbm, qkv),), sems)
     core = lax.axis_index("lat") % 2
     grads_half(core, normed_t, mixed_t, grad_middle[...], d_packed, keep)
+    qkv_in.wait()
+    d_inputs = norm_backward(
+        inputs[...].astype(F32), gain[...].reshape(1, WIDTH), d_packed[...], qkv
+    )
+    total = (grad_middle[...].astype(F32) + d_inputs).astype(BF16)
+    store_grid(grad_fields, place_t[...], total)
+
+
+def kernel_advanced(back0, back1, back2, back3, middle, place_t, sort_t, advanced):
     delta = join_pieces(sort_t[...], (back0, back1, back2, back3))
     store_grid(advanced, place_t[...], (middle[...].astype(F32) + delta).astype(BF16))
-    d_inputs = norm_backward(
-        inputs[...].astype(F32), gain[...].reshape(1, WIDTH), d_packed[...], qkv
-    )
-    total = (grad_middle[...].astype(F32) + d_inputs).astype(BF16)
-    store_grid(grad_fields, place_t[...], total)
+
+
+def kernel_first_sum(keep, got, send_one, send_two, keep_one, keep_two):
+    y = lax.axis_index("lat") // 4
+    half = 2 * WIDTH
+
+    def put(target, place, block, columns):
+        rows = pl.ds(pl.multiple_of(block * 64, 64), 64)
+        target[place] = keep[rows, columns] + got[rows, columns]
+
+    one, two = slice(0, half), slice(half, 2 * half)
+    put(send_one, 0, y ^ 1, one)
+    put(send_one, 1, y ^ 2, one)
+    put(send_two, 0, y ^ 3, two)
+    put(send_two, 1, y ^ 2, two)
+    put(keep_one, 0, y, one)
+    put(keep_one, 1, y ^ 3, one)
+    put(keep_two, 0, y, two)
+    put(keep_two, 1, y ^ 1, two)
+
+
+def kernel_second_sum(keep_one, got_one, keep_two, got_two, send_one, send_two, held_one, held_two):
+    send_one[...] = keep_one[1] + got_one[1]
+    send_two[...] = keep_two[1] + got_two[1]
+    held_one[...] = keep_one[0] + got_one[0]
+    held_two[...] = keep_two[0] + got_two[0]
+
+
+def kernel_third_sum(held_one, got_one, held_two, got_two, send, keep):
+    near = lax.axis_index("lat") // 2 % 2
+    half = 2 * WIDTH
+    for target, place in ((send, 1 - near), (keep, near)):
+        rows = pl.ds(pl.multiple_of(place * 32, 32), 32)
+        target[:, :half] = held_one[rows] + got_one[rows]
+        target[:, half:] = held_two[rows] + got_two[rows]
 
 
 def kernel_columns(keep_a, got_a, keep_b, got_b, result):
@@ -397,16 +437,24 @@
         out[...] = total[at, :, 96:]
 
 
-def call(kernel, outs, scratch, args, smem=(), hbm=(), copies=0, cost=None):
+def call(kernel, outs, scratch, args, smem=(), hbm=(), copies=0, flops=0, final=()):
     def space(at):
-        return pltpu.SMEM if at in smem else pl.ANY if at in hbm else pltpu.VMEM
-
+        return pltpu.SMEM if at in smem else pltpu.HBM if at in hbm else pltpu.VMEM
+
+    cost = pl.CostEstimate(flops=flops, bytes_accessed=1 << 20, transcendentals=0) if flops else None
+    args = [
+        pltpu.with_memory_space_constraint(arg, pltpu.HBM) if at in hbm or at in smem else arg
+        for at, arg in enumerate(args)
+    ]
     shapes = [pltpu.VMEM(shape, kind) for shape, kind in scratch]
     if copies:
         shapes.append(pltpu.SemaphoreType.DMA((copies,)))
     return pl.pallas_call(
         kernel,
-        out_shape=tuple(jax.ShapeDtypeStruct(shape, kind) for shape, kind in outs),
+        out_shape=tuple(
+            jax.ShapeDtypeStruct(shape, kind) if at in final else pltpu.VMEM(shape, kind)
+            for at, (shape, kind) in enumerate(outs)
+        ),
         in_specs=[pl.BlockSpec(memory_space=space(at)) for at in range(len(args))],
         out_specs=tuple(pl.BlockSpec(memory_space=pltpu.VMEM) for _ in outs),
         scratch_shapes=shapes,
@@ -430,30 +478,34 @@
     return lax.ppermute(array, ("lon", "lat"), pairs)
 
 
-def pick(array, at):
-    return lax.dynamic_index_in_dim(array, at, 0, keepdims=False)
-
-
-def add(*parts):
-    return sum(part.astype(F32) for part in parts).astype(BF16)
-
-
-def reduce_rows(send, keep):
-    y = lax.axis_index("lat") // 4
-    whole = add(keep, permute(send, "lat", lambda i: i ^ 1)).reshape(4, 2, 32, 4 * WIDTH)
-    half = 2 * WIDTH
-    one, two = whole[..., :half], whole[..., half:]
-    got_one = permute(jnp.stack([pick(one, y ^ 1), pick(one, y ^ 2)]), "lat", lambda i: i ^ 4)
-    got_two = permute(jnp.stack([pick(two, y ^ 3), pick(two, y ^ 2)]), "lat", lambda i: i ^ 12)
-    keep_one = add(pick(one, y), got_one[0])
-    send_one = add(pick(one, y ^ 3), got_one[1])
-    keep_two = add(pick(two, y), got_two[0])
-    send_two = add(pick(two, y ^ 1), got_two[1])
-    last_one = permute(send_one, "lat", lambda i: i ^ 12)
-    last_two = permute(send_two, "lat", lambda i: i ^ 4)
-    both = jnp.concatenate([add(keep_one, last_one), add(keep_two, last_two)], axis=-1)
-    near = lax.axis_index("lat") // 2 % 2
-    return pick(both, near), permute(pick(both, 1 - near), "lat", lambda i: i ^ 2)
+def first_round(send, keep):
+    return keep, permute(send, "lat", lambda i: i ^ 1)
+
+
+def first_sum(keep, got):
+    return call(kernel_first_sum, [((2, 64, 2 * WIDTH), BF16)] * 4, [], (keep, got))
+
+
+def second_round(send_one, send_two, keep_one, keep_two):
+    got_one = permute(send_one, "lat", lambda i: i ^ 4)
+    got_two = permute(send_two, "lat", lambda i: i ^ 12)
+    return keep_one, got_one, keep_two, got_two
+
+
+def second_sum(*parts):
+    return call(kernel_second_sum, [((64, 2 * WIDTH), BF16)] * 4, [], parts)
+
+
+def third_round(send_one, send_two, held_one, held_two):
+    got_one = permute(send_one, "lat", lambda i: i ^ 12)
+    got_two = permute(send_two, "lat", lambda i: i ^ 4)
+    return held_one, got_one, held_two, got_two
+
+
+def fourth_round(*parts):
+    rows = ((32, 4 * WIDTH), BF16)
+    send, keep = call(kernel_third_sum, [rows] * 2, [], parts)
+    return keep, permute(send, "lat", lambda i: i ^ 2)
 
 
 def body(
@@ -494,7 +546,7 @@
         [piece] * 4 + [token] * 3 + [packed, probs, mixed_t],
         [grid, ids, vector, qkv_shape, out_shape, square, square, place_of, token_wide, spare, keys, scores],
         (fields, land_ids, gain_a, table_a, qkv_weight_a, out_weight_a, place, sort, where),
-        smem=(3,), hbm=(0, 1, 2, 4, 5, 6, 7, 8), copies=8,
+        smem=(3,), hbm=(0, 1, 2, 4, 5, 6, 7, 8), copies=8, flops=7 * 10**9,
     )
     diagonal = permute_both(p0, -1)
     below = permute(p1, "lat", lambda i: i - 1)
@@ -504,7 +556,7 @@
         [piece] * 4 + [token, normed_t, query, keys],
         [grid, token_wide, spare],
         (cotangent, place, sort, normed_a, land_ids, table_b, where),
-        smem=(5,), hbm=(0,), copies=1,
+        smem=(5,), hbm=(0,), copies=1, flops=2 * 10**9,
     )
     c_diagonal = permute_both(c0, -1)
     c_below = permute(c1, "lat", lambda i: i - 1)
@@ -514,10 +566,8 @@
         [piece] * 4 + [token] * 2 + [packed, probs, mixed_t],
         [scores],
         (p3, eastern, below, diagonal, query_b, keys_b, gain_b, qkv_weight_b, out_weight_b, sort, sort_t),
-    )
-    delta_diagonal = permute_both(b3, 1)
-    delta_above = permute(b2, "lat", lambda i: i + 1)
-    delta_western = permute(b1, "lon", lambda i: i + 1)
+        flops=5 * 10**9,
+    )
     d0, d1, d2, d3, upstream_b, d_packed_b = call(
         kernel_backward_b,
         [piece] * 4 + [token, packed],
@@ -526,13 +576,17 @@
             c3, c_eastern, c_below, c_diagonal, inputs_b, gain_b, qkv_weight_b, out_weight_b,
             packed_b, probs_b, mixed_b, sort, sort_t,
         ),
+        flops=5 * 10**9,
     )
     d_diagonal = permute_both(d3, 1)
     d_above = permute(d2, "lat", lambda i: i + 1)
     d_western = permute(d1, "lon", lambda i: i + 1)
     send_b, keep_b = call(
-        kernel_grads_b, [half_grads] * 2, [normed_t], (normed_b, mixed_b, upstream_b, d_packed_b)
-    )
+        kernel_grads_b, [half_grads] * 2, [normed_t], (normed_b, mixed_b, upstream_b, d_packed_b),
+        flops=2 * 10**9,
+    )
+    sums_b = first_sum(*first_round(send_b, keep_b))
+    rounds_b = second_round(*sums_b)
     grad_middle, d_packed_a, send_a = call(
         kernel_backward_a,
         [token, packed, half_grads],
@@ -541,21 +595,36 @@
             d_diagonal, d_above, d_western, d0, upstream_a, out_weight_a, packed_a, probs_a,
             mixed_a, normed_a_t, sort_t,
         ),
-    )
-    keep_a, advanced, grad_fields = call(
+        flops=5 * 10**9,
+    )
+    sums_b = second_sum(*rounds_b)
+    rounds_b = third_round(*sums_b)
+    keep_a, grad_fields = call(
         kernel_finish_a,
-        [half_grads, grid, grid],
+        [half_grads, grid],
+        [qkv_shape],
+        (inputs_a, grad_middle, gain_a, qkv_weight_a, d_packed_a, normed_a_t, mixed_a, place_t),
+        hbm=(3,), copies=1, flops=4 * 10**9, final=(1,),
+    )
+    sums_a = first_sum(*first_round(send_a, keep_a))
+    sums_a, b1, b2, b3 = lax.optimization_barrier((sums_a, b1, b2, b3))
+    rounds_a = second_round(*sums_a)
+    delta_diagonal = permute_both(b3, 1)
+    delta_above = permute(b2, "lat", lambda i: i + 1)
+    delta_western = permute(b1, "lon", lambda i: i + 1)
+    rounds_b = fourth_round(*rounds_b)
+    sums_a = second_sum(*rounds_a)
+    sums_a, b0 = lax.optimization_barrier((sums_a, b0))
+    advanced = call(
+        kernel_advanced,
+        [grid],
         [],
-        (
-            delta_diagonal, delta_above, delta_western, b0, inputs_a, middle_a, grad_middle,
-            gain_a, qkv_weight_a, d_packed_a, normed_a_t, mixed_a, place_t, sort_t,
-        ),
-    )
+        (delta_diagonal, delta_above, delta_western, b0, middle_a, place_t, sort_t),
+        flops=10**9, final=(0,),
+    )[0]
+    rounds_a = fourth_round(*third_round(*sums_a))
     blocks = call(
-        kernel_columns,
-        [((16, 2, 32, GROUP), BF16)],
-        [],
-        reduce_rows(send_a, keep_a) + reduce_rows(send_b, keep_b),
+        kernel_columns, [((16, 2, 32, GROUP), BF16)], [], rounds_a + rounds_b, final=(0,)
     )[0]
     blocks = lax.all_to_all(blocks, "lon", 0, 0, tiled=True)
     grads = call(
@@ -563,6 +632,7 @@
         [((32, 96), F32), ((32, 32), F32)] * 2,
         [],
         (blocks,),
+        final=(0, 1, 2, 3),
     )
     return (advanced.transpose(2, 0, 1, 3), grad_fields.transpose(2, 0, 1, 3), *grads)
 

time: 128 us -> 99.2 us (0.78)
  local copies, waits for them, and re-layouts: 15.3 us -> 0.06 us
  blocking collectives: 13.8 us -> 0 us
  starting transfers between devices: 24.6 us -> 32.5 us
  other arithmetic: 3.76 us -> 0 us
  waiting for transfers between devices: 37.5 us -> 34.1 us
    unnamed x58 -> x22, local copies, waits for them, and re-layouts: 15.1 us -> 0.06 us
    all_to_all x1 -> x0, blocking collectives: 13.8 us -> none  [body(): blocks = lax.all_to_all(blocks, 'lon', 0, 0, tiled=True)]
    all_to_all x0 -> x1, starting transfers between devices: none -> 5.95 us  [body(): blocks = lax.all_to_all(blocks, 'lon', 0, 0, tiled=True)]
    ppermute x20, waiting for transfers between devices: 29.3 us -> 23.6 us  [permute(): lax.ppermute(array, axis, [(i, target(i) % length) for i in range(length)])]
    convert_element_type x10 -> x0, other arithmetic: 3.6 us -> none  [add(): return sum((part.astype(F32) for part in parts)).astype(BF16)]
    ppermute x4, waiting for transfers between devices: 8.19 us -> 10.4 us  [permute_both(): return lax.ppermute(array, ('lon', 'lat'), pairs)]
    ppermute x20, starting transfers between devices: 23.1 us -> 24.5 us  [permute(): lax.ppermute(array, axis, [(i, target(i) % length) for i in range(length)])]
    pallas_call x9 -> x16, Pallas kernels: 29.5 us -> 29.9 us  [call(): pl.pallas_call(kernel, out_shape=tuple((jax.ShapeDtypeStruct(shape, kind)...]
  transfers between devices with their start and end apart: 24 -> 25, of which waited for: 14 -> 12; matrix products, arithmetic and copies ran while one was open for 2% -> 0% of each run, Pallas kernels for 12% -> 18%
where the time goes in v1:
time: 99.2 us; the launch traced here: 97.4 us
  waiting for transfers between devices  34.1 us (34%)
  starting transfers between devices  32.5 us (33%)
  Pallas kernels  29.9 us (30%)
    pallas_call x16, Pallas kernels, call(): pl.pallas_call(kernel, out_shape=tuple((jax.ShapeDtypeStruct(shape, kind)...  29.9 us
    ppermute x20, starting transfers between devices, permute(): lax.ppermute(array, axis, [(i, target(i) % length) for i in range(length)])  24.5 us
    ppermute x20, waiting for transfers between devices, permute(): lax.ppermute(array, axis, [(i, target(i) % length) for i in range(length)])  23.6 us
    ppermute x4, waiting for transfers between devices, permute_both(): return lax.ppermute(array, ('lon', 'lat'), pairs)  10.4 us
    all_to_all x1, starting transfers between devices, body(): blocks = lax.all_to_all(blocks, 'lon', 0, 0, tiled=True)  5.95 us
    ppermute x4, starting transfers between devices, permute_both(): return lax.ppermute(array, ('lon', 'lat'), pairs)  2.03 us
  transfers between devices with their start and end apart: 25, of which 12 were waited for; matrix products, arithmetic and copies ran while one was open for 0% of the time, Pallas kernels for 18%

profile of v1, /device:TPU:6, one launch (start us, length us, event | category | flops | bytes accessed | tf_op | source)
XLA Modules:
  0.0 97.4 jit_solution(12579066180182024507)
XLA Ops:
  0.6 0.0 copy-start.8
  0.7 0.0 copy-start.9
  0.7 0.0 copy-start.10
  0.7 6.4 %shard_map.199 = (bf16[72,512]{1,0:T(8,128)(2,1)S(1)}, bf16[72,512]{1,0:T(8,128)(2,1)S(1)}, bf16[72,512]{1,0:T(8,128)(2,1)S(1)}, bf16[72,512]{1,0:T(8,128)(2,1)S...) custom-call(bf16[12,6,4,512]{3,2,1,0:T(4,128)(2,1)} %bitcast.6, ...), custom_call_target="tpu_custom_call" | custom-call | flops 7000000000 | bytes 1048576 | tf_op jit(solution)/shard_map/pallas_call | solution.py:452
  7.1 6.8 %collective-permute-start.3 = (bf16[72,512]{1,0:T(8,128)(2,1)S(1)}, bf16[72,512]{1,0:T(8,128)(2,1)S(1)}, u32[]{:S(2)}, u32[]{:S(2)}) collective-permute-start(bf16[72,512]{1,0:T(8,128)(2,1)S(1)} %get-tuple-element.89), channel_id=1, source_target_pairs={{0,240},{16,0},{32,16},{48,32},{64,48},{80,64},{96,80},{112,96},{1... | collective-permute-start | bytes 221192 | tf_op jit(solution)/shard_map/ppermute | solution.py:468
  13.9 0.0 collective-permute-start.4
  13.9 0.2 collective-permute-start.5
  14.1 0.0 copy-start
  14.1 0.0 copy-start.1
  14.1 0.0 copy-start.4
  14.1 0.0 copy-start.6
  14.1 2.9 %shard_map.200 = (bf16[72,512]{1,0:T(8,128)(2,1)S(1)}, bf16[72,512]{1,0:T(8,128)(2,1)S(1)}, bf16[72,512]{1,0:T(8,128)(2,1)S(1)}, bf16[72,512]{1,0:T(8,128)(2,1)S...) custom-call(bf16[12,6,4,512]{3,2,1,0:T(4,128)(2,1)} %bitcast.7, ...), custom_call_target="tpu_custom_call" | custom-call | flops 2000000000 | bytes 1048576 | tf_op jit(solution)/shard_map/pallas_call | solution.py:452
  17.1 2.0 %collective-permute-start = (bf16[72,512]{1,0:T(8,128)(2,1)S(1)}, bf16[72,512]{1,0:T(8,128)(2,1)S(1)}, u32[]{:S(2)}, u32[]{:S(2)}) collective-permute-start(bf16[72,512]{1,0:T(8,128)(2,1)S(1)} %get-tuple-element.85), channel_id=1, source_target_pairs={{0,240},{16,0},{32,16},{48,32},{64,48},{80,64},{96,80},{112,96},{1... | collective-permute-start | bytes 221192 | tf_op jit(solution)/shard_map/ppermute | solution.py:468
  19.0 2.4 %collective-permute-start.1 = (bf16[72,512]{1,0:T(8,128)(2,1)S(1)}, bf16[72,512]{1,0:T(8,128)(2,1)S(1)}, u32[]{:S(2)}, u32[]{:S(2)}) collective-permute-start(bf16[72,512]{1,0:T(8,128)(2,1)S(1)} %get-tuple-element.86), channel_id=1, source_target_pairs={{0,15},{1,0},{2,1},{3,2},{4,3},{5,4},{6,5},{7,6},{8,7},{9,8},{10,9... | collective-permute-start | bytes 221192 | tf_op jit(solution)/shard_map/ppermute | solution.py:468
  21.4 1.2 %collective-permute-start.2 = (bf16[72,512]{1,0:T(8,128)(2,1)S(1)}, bf16[72,512]{1,0:T(8,128)(2,1)S(1)}, u32[]{:S(2)}, u32[]{:S(2)}) collective-permute-start(bf16[72,512]{1,0:T(8,128)(2,1)S(1)} %get-tuple-element.87), channel_id=1, source_target_pairs={{0,255},{1,240},{2,241},{3,242},{4,243},{5,244},{6,245},{7,246},{8... | collective-permute-start | bytes 221192 | tf_op jit(solution)/shard_map/ppermute | solution.py:478
  22.6 0.0 collective-permute-done.4.piece2
  22.6 0.0 collective-permute-done.5.piece3
  22.7 3.7 %shard_map.201 = (bf16[72,512]{1,0:T(8,128)(2,1)S(1)}, bf16[72,512]{1,0:T(8,128)(2,1)S(1)}, bf16[72,512]{1,0:T(8,128)(2,1)S(1)}, bf16[72,512]{1,0:T(8,128)(2,1)S...) custom-call(bf16[72,512]{1,0:T(8,128)(2,1)S(1)} %get-tuple-element.8, ...), custom_call_target="tpu_custom_call" | custom-call | flops 5000000000 | bytes 1048576 | tf_op jit(solution)/shard_map/pallas_call | solution.py:452
  26.4 0.0 collective-permute-done.1.piece2
  26.5 0.0 collective-permute-done.2.piece3
  26.5 4.4 %shard_map.202 = (bf16[72,512]{1,0:T(8,128)(2,1)S(1)}, bf16[72,512]{1,0:T(8,128)(2,1)S(1)}, bf16[72,512]{1,0:T(8,128)(2,1)S(1)}, bf16[72,512]{1,0:T(8,128)(2,1)S...) custom-call(bf16[72,512]{1,0:T(8,128)(2,1)S(1)} %get-tuple-element.84.piece0, ...), custom_call_target="tpu_custom_call" | custom-call | flops 5000000000 | bytes 1048576 | tf_op jit(solution)/shard_map/pallas_call | solution.py:452
  30.8 0.6 collective-permute-start.6
  31.4 0.1 collective-permute-start.7
  31.5 1.0 collective-permute-start.8
  32.5 1.3 %shard_map.209 = (bf16[256,2048]{1,0:T(8,128)(2,1)S(1)}, bf16[256,2048]{1,0:T(8,128)(2,1)S(1)}) custom-call(bf16[288,512]{1,0:T(8,128)(2,1)S(1)} %get-tuple-element.139.normed, bf16[2,512,144]{2,1,0:T(8,128)(2,1)S(1)} %get-tuple-element.97.mixed_t, bf16[288,512]{1,0:T(8,128)(2,1)S(1)} %get-tuple-element.140.upstream, ...), custom_call_target="tpu_custom_call" | custom-call | flops 2000000000 | bytes 1048576 | tf_op jit(solution)/shard_map/pallas_call | solution.py:452
  33.8 0.4 collective-permute-start.18
  34.2 4.0 %collective-permute-done.6.back0 = bf16[72,512]{1,0:T(8,128)(2,1)S(1)} collective-permute-done((bf16[72,512]{1,0:T(8,128)(2,1)S(1)}, bf16[72,512]{1,0:T(8,128)(2,1)S(1)}, u32[]{:S(2)}, u32[]{:S(2)}) %collective-permute-start.6) | collective-permute-done | bytes 73760 | tf_op jit(solution)/shard_map/ppermute | solution.py:478
  38.2 2.2 %collective-permute-done.8.back2 = bf16[72,512]{1,0:T(8,128)(2,1)S(1)} collective-permute-done((bf16[72,512]{1,0:T(8,128)(2,1)S(1)}, bf16[72,512]{1,0:T(8,128)(2,1)S(1)}, u32[]{:S(2)}, u32[]{:S(2)}) %collective-permute-start.8) | collective-permute-done | bytes 73760 | tf_op jit(solution)/shard_map/ppermute | solution.py:468
  40.4 4.0 %shard_map.203 = (bf16[288,512]{1,0:T(8,128)(2,1)S(1)}, bf16[288,1536]{1,0:T(8,128)(2,1)S(1)}, bf16[256,2048]{1,0:T(8,128)(2,1)S(1)}) custom-call(bf16[72,512]{1,0:T(8,128)(2,1)S(1)} %collective-permute-done.6.back0, bf16[72,512]{1,0:T(8,128)(2,1)S(1)} %collective-permute-done.7.back1, bf16[72,512]{1,0:T(8,128)(2,1)S(1)} %collective-permute-done.8.back2, ...), custom_call_target="tpu_custom_call" | custom-call | flops 5000000000 | bytes 1048576 | tf_op jit(solution)/shard_map/pallas_call | solution.py:452
  44.5 0.1 collective-permute-start.9
  44.6 3.8 %shard_map.204 = (bf16[256,2048]{1,0:T(8,128)(2,1)S(1)}, bf16[12,6,4,512]{3,2,1,0:T(4,128)(2,1)}) custom-call(bf16[288,512]{1,0:T(8,128)(2,1)S(1)} %get-tuple-element.82.inputs, bf16[288,512]{1,0:T(8,128)(2,1)S(1)} %get-tuple-element.107.grad_middle, f32[512]{0:T(512)S(1)} %copy-done.5, bf16[512,1536]{1,0:T(8,128)(2,1)} %qkv_hbm.3, ...), custom_call_target="tpu_custom_call" | custom-call | flops 4000000000 | bytes 1048576 | tf_op jit(solution)/shard_map/pallas_call | solution.py:452
  48.4 0.1 shard_map.210
  48.5 1.6 %collective-permute-start.19 = (bf16[2,64,1024]{2,1,0:T(8,128)(2,1)S(1)}, bf16[2,64,1024]{2,1,0:T(8,128)(2,1)S(1)}, u32[]{:S(2)}, u32[]{:S(2)}) collective-permute-start(bf16[2,64,1024]{2,1,0:T(8,128)(2,1)S(1)} %get-tuple-element.145), channel_id=1, source_target_pairs={{0,4},{1,5},{2,6},{3,7},{4,0},{5,1},{6,2},{7,3},{8,12},{9,13},{10,... | collective-permute-start | bytes 786440 | tf_op jit(solution)/shard_map/ppermute | solution.py:468
  50.1 1.9 %collective-permute-start.20 = (bf16[2,64,1024]{2,1,0:T(8,128)(2,1)S(1)}, bf16[2,64,1024]{2,1,0:T(8,128)(2,1)S(1)}, u32[]{:S(2)}, u32[]{:S(2)}) collective-permute-start(bf16[2,64,1024]{2,1,0:T(8,128)(2,1)S(1)} %get-tuple-element.147), channel_id=1, source_target_pairs={{0,12},{1,13},{2,14},{3,15},{4,8},{5,9},{6,10},{7,11},{8,4},{9,5},... | collective-permute-start | bytes 786440 | tf_op jit(solution)/shard_map/ppermute | solution.py:468
  52.0 0.0 collective-permute-done.9.got
  52.0 0.1 shard_map.205
  52.1 1.3 %collective-permute-start.13 = (bf16[2,64,1024]{2,1,0:T(8,128)(2,1)S(1)}, bf16[2,64,1024]{2,1,0:T(8,128)(2,1)S(1)}, u32[]{:S(2)}, u32[]{:S(2)}) collective-permute-start(bf16[2,64,1024]{2,1,0:T(8,128)(2,1)S(1)} %get-tuple-element.122), channel_id=1, source_target_pairs={{0,4},{1,5},{2,6},{3,7},{4,0},{5,1},{6,2},{7,3},{8,12},{9,13},{10,... | collective-permute-start | bytes 786440 | tf_op jit(solution)/shard_map/ppermute | solution.py:468
  53.4 0.6 collective-permute-start.14
  54.0 3.7 %collective-permute-done.19.got_one = bf16[2,64,1024]{2,1,0:T(8,128)(2,1)S(1)} collective-permute-done((bf16[2,64,1024]{2,1,0:T(8,128)(2,1)S(1)}, bf16[2,64,1024]{2,1,0:T(8,128)(2,1)S(1)}, u32[]{:S(2)}, u32[]{:S(2)}) %collective-permute-start.19) | collective-permute-done | bytes 262176 | tf_op jit(solution)/shard_map/ppermute | solution.py:468
  57.7 2.8 %collective-permute-done.20.got_two = bf16[2,64,1024]{2,1,0:T(8,128)(2,1)S(1)} collective-permute-done((bf16[2,64,1024]{2,1,0:T(8,128)(2,1)S(1)}, bf16[2,64,1024]{2,1,0:T(8,128)(2,1)S(1)}, u32[]{:S(2)}, u32[]{:S(2)}) %collective-permute-start.20) | collective-permute-done | bytes 262176 | tf_op jit(solution)/shard_map/ppermute | solution.py:468
  60.5 0.1 shard_map.211
  60.5 1.9 %collective-permute-start.21 = (bf16[64,1024]{1,0:T(8,128)(2,1)S(1)}, bf16[64,1024]{1,0:T(8,128)(2,1)S(1)}, u32[]{:S(2)}, u32[]{:S(2)}) collective-permute-start(bf16[64,1024]{1,0:T(8,128)(2,1)S(1)} %get-tuple-element.149), channel_id=1, source_target_pairs={{0,12},{1,13},{2,14},{3,15},{4,8},{5,9},{6,10},{7,11},{8,4},{9,5},... | collective-permute-start | bytes 393224 | tf_op jit(solution)/shard_map/ppermute | solution.py:468
  62.5 0.4 collective-permute-done.13.got_one
  62.9 3.2 %collective-permute-done.14.got_two = bf16[2,64,1024]{2,1,0:T(8,128)(2,1)S(1)} collective-permute-done((bf16[2,64,1024]{2,1,0:T(8,128)(2,1)S(1)}, bf16[2,64,1024]{2,1,0:T(8,128)(2,1)S(1)}, u32[]{:S(2)}, u32[]{:S(2)}) %collective-permute-start.14) | collective-permute-done | bytes 262176 | tf_op jit(solution)/shard_map/ppermute | solution.py:468
  66.1 0.1 shard_map.206
  66.2 1.9 %collective-permute-start.15 = (bf16[64,1024]{1,0:T(8,128)(2,1)S(1)}, bf16[64,1024]{1,0:T(8,128)(2,1)S(1)}, u32[]{:S(2)}, u32[]{:S(2)}) collective-permute-start(bf16[64,1024]{1,0:T(8,128)(2,1)S(1)} %get-tuple-element.134), channel_id=1, source_target_pairs={{0,12},{1,13},{2,14},{3,15},{4,8},{5,9},{6,10},{7,11},{8,4},{9,5},... | collective-permute-start | bytes 393224 | tf_op jit(solution)/shard_map/ppermute | solution.py:468
  68.1 0.0 collective-permute-start.16
  68.1 0.1 collective-permute-done.21.got_one
  68.2 0.0 collective-permute-done.22.got_two
  68.2 0.3 collective-permute-start.23
  68.5 3.9 %collective-permute-done.15.got_one = bf16[64,1024]{1,0:T(8,128)(2,1)S(1)} collective-permute-done((bf16[64,1024]{1,0:T(8,128)(2,1)S(1)}, bf16[64,1024]{1,0:T(8,128)(2,1)S(1)}, u32[]{:S(2)}, u32[]{:S(2)}) %collective-permute-start.15) | collective-permute-done | bytes 131104 | tf_op jit(solution)/shard_map/ppermute | solution.py:468
  72.4 0.6 collective-permute-done.16.got_two
  73.1 0.3 collective-permute-start.17
  73.3 0.0 collective-permute-done.23.got_b
  73.3 4.8 %collective-permute-done.17.got_a = bf16[32,2048]{1,0:T(8,128)(2,1)S(1)} collective-permute-done((bf16[32,2048]{1,0:T(8,128)(2,1)S(1)}, bf16[32,2048]{1,0:T(8,128)(2,1)S(1)}, u32[]{:S(2)}, u32[]{:S(2)}) %collective-permute-start.17) | collective-permute-done | bytes 131104 | tf_op jit(solution)/shard_map/ppermute | solution.py:468
  78.2 0.9 shard_map.213
  79.1 6.0 %all-to-all-start = ((bf16[16,2,32,128]{3,2,1,0:T(8,128)(2,1)}), bf16[16,2,32,128]{3,2,1,0:T(8,128)(2,1)S(1)}, u32[]{:S(2)}, u32[]{:S(2)}) async-start(bf16[16,2,32,128]{3,2,1,0:T(8,128)(2,1)} %shard_map.213), calls=%async_computation | async-start | bytes 524288 | tf_op jit(solution)/shard_map/all_to_all | solution.py:629
  85.0 0.6 collective-permute-start.11
  85.6 1.5 %collective-permute-start.12 = (bf16[72,512]{1,0:T(8,128)(2,1)S(1)}, bf16[72,512]{1,0:T(8,128)(2,1)S(1)}, u32[]{:S(2)}, u32[]{:S(2)}) collective-permute-start(bf16[72,512]{1,0:T(8,128)(2,1)S(1)} %get-tuple-element.120), channel_id=1, source_target_pairs={{0,16},{16,32},{32,48},{48,64},{64,80},{80,96},{96,112},{112,128},... | collective-permute-start | bytes 221192 | tf_op jit(solution)/shard_map/ppermute | solution.py:468
  87.1 6.4 %collective-permute-done.10.back0 = bf16[72,512]{1,0:T(8,128)(2,1)S(1)} collective-permute-done((bf16[72,512]{1,0:T(8,128)(2,1)S(1)}, bf16[72,512]{1,0:T(8,128)(2,1)S(1)}, u32[]{:S(2)}, u32[]{:S(2)}) %collective-permute-start.10) | collective-permute-done | bytes 73760 | tf_op jit(solution)/shard_map/ppermute | solution.py:478
  93.5 1.9 %collective-permute-done.12.back2 = bf16[72,512]{1,0:T(8,128)(2,1)S(1)} collective-permute-done((bf16[72,512]{1,0:T(8,128)(2,1)S(1)}, bf16[72,512]{1,0:T(8,128)(2,1)S(1)}, u32[]{:S(2)}, u32[]{:S(2)}) %collective-permute-start.12) | collective-permute-done | bytes 73760 | tf_op jit(solution)/shard_map/ppermute | solution.py:468
  95.4 1.3 %shard_map.207 = bf16[12,6,4,512]{3,2,1,0:T(4,128)(2,1)} custom-call(bf16[72,512]{1,0:T(8,128)(2,1)S(1)} %collective-permute-done.10.back0, bf16[72,512]{1,0:T(8,128)(2,1)S(1)} %collective-permute-done.11.back1, bf16[72,512]{1,0:T(8,128)(2,1)S(1)} %collective-permute-done.12.back2, bf16[72,512]{1,0:T(8,128)(2,1)S(1)} %get-tuple-element.130.back3, ...), custom_call_target="tpu_custom_call" | custom-call | flops 1000000000 | bytes 1048576 | tf_op jit(solution)/shard_map/pallas_call | solution.py:452
  96.7 0.0 all-to-all-done.parts
  96.7 0.7 shard_map.214
  (24 shorter events, 0.1 us)
Async XLA Ops:
  0.6 13.4 %copy-start.3 = (s32[192,96]{1,0:T(8,128)S(1)}, s32[192,96]{1,0:T(8,128)}, u32[]{:S(2)}) copy-start(s32[192,96]{1,0:T(8,128)} %ids.1) | copy-start | bytes 221188
  0.6 13.4 %copy-start.8 = (bf16[288,288]{1,0:T(8,128)(2,1)S(1)}, bf16[288,288]{1,0:T(8,128)(2,1)}, u32[]{:S(2)}) copy-start(bf16[288,288]{1,0:T(8,128)(2,1)} %constant.12.clone.sort_hbm.sort) | copy-start | bytes 497668
  0.7 13.4 %copy-start.9 = (bf16[288,288]{1,0:T(8,128)(2,1)S(1)}, bf16[288,288]{1,0:T(8,128)(2,1)}, u32[]{:S(2)}) copy-start(bf16[288,288]{1,0:T(8,128)(2,1)} %constant.10.clone.place_hbm.place) | copy-start | bytes 497668
  0.7 13.4 %copy-start.10 = (s32[144,8]{1,0:T(8,128)S(1)}, s32[144,8]{1,0:T(8,128)}, u32[]{:S(2)}) copy-start(s32[144,8]{1,0:T(8,128)} %constant.14.clone.where_hbm.where) | copy-start | bytes 13828
  7.1 14.3 %collective-permute-start.3 = (bf16[72,512]{1,0:T(8,128)(2,1)S(1)}, bf16[72,512]{1,0:T(8,128)(2,1)S(1)}, u32[]{:S(2)}, u32[]{:S(2)}) collective-permute-start(bf16[72,512]{1,0:T(8,128)(2,1)S(1)} %get-tuple-element.89), channel_id=1, source_target_pairs={{0,240},{16,0},{32,16},{48,32},{64,48},{80,64},{96,80},{112,96},{1... | collective-permute-start | bytes 221192 | tf_op jit(solution)/shard_map/ppermute | solution.py:468
  13.9 8.8 %collective-permute-start.4 = (bf16[72,512]{1,0:T(8,128)(2,1)S(1)}, bf16[72,512]{1,0:T(8,128)(2,1)S(1)}, u32[]{:S(2)}, u32[]{:S(2)}) collective-permute-start(bf16[72,512]{1,0:T(8,128)(2,1)S(1)} %get-tuple-element.90), channel_id=1, source_target_pairs={{0,15},{1,0},{2,1},{3,2},{4,3},{5,4},{6,5},{7,6},{8,7},{9,8},{10,9... | collective-permute-start | bytes 221192 | tf_op jit(solution)/shard_map/ppermute | solution.py:468
  13.9 8.8 %collective-permute-start.5 = (bf16[72,512]{1,0:T(8,128)(2,1)S(1)}, bf16[72,512]{1,0:T(8,128)(2,1)S(1)}, u32[]{:S(2)}, u32[]{:S(2)}) collective-permute-start(bf16[72,512]{1,0:T(8,128)(2,1)S(1)} %get-tuple-element.91), channel_id=1, source_target_pairs={{0,255},{1,240},{2,241},{3,242},{4,243},{5,244},{6,245},{7,246},{8... | collective-permute-start | bytes 221192 | tf_op jit(solution)/shard_map/ppermute | solution.py:478
  14.1 8.6 %copy-start = (bf16[512,1536]{1,0:T(8,128)(2,1)S(1)}, bf16[512,1536]{1,0:T(8,128)(2,1)}, u32[]{:S(2)}) copy-start(bf16[512,1536]{1,0:T(8,128)(2,1)} %qkv.3) | copy-start | bytes 4718596
  14.1 8.6 %copy-start.1 = (bf16[512,512]{1,0:T(8,128)(2,1)S(1)}, bf16[512,512]{1,0:T(8,128)(2,1)}, u32[]{:S(2)}) copy-start(bf16[512,512]{1,0:T(8,128)(2,1)} %out.4) | copy-start | bytes 1572868
  14.1 8.6 %copy-start.4 = (f32[512]{0:T(512)S(1)}, f32[512]{0:T(512)}, u32[]{:S(2)}) copy-start(f32[512]{0:T(512)} %gain.4) | copy-start | bytes 6148
  14.1 8.6 %copy-start.6 = (bf16[288,288]{1,0:T(8,128)(2,1)S(1)}, bf16[288,288]{1,0:T(8,128)(2,1)}, u32[]{:S(2)}) copy-start(bf16[288,288]{1,0:T(8,128)(2,1)} %constant.13.clone.sort_t) | copy-start | bytes 497668
  17.1 9.4 %collective-permute-start = (bf16[72,512]{1,0:T(8,128)(2,1)S(1)}, bf16[72,512]{1,0:T(8,128)(2,1)S(1)}, u32[]{:S(2)}, u32[]{:S(2)}) collective-permute-start(bf16[72,512]{1,0:T(8,128)(2,1)S(1)} %get-tuple-element.85), channel_id=1, source_target_pairs={{0,240},{16,0},{32,16},{48,32},{64,48},{80,64},{96,80},{112,96},{1... | collective-permute-start | bytes 221192 | tf_op jit(solution)/shard_map/ppermute | solution.py:468
  19.0 7.4 %collective-permute-start.1 = (bf16[72,512]{1,0:T(8,128)(2,1)S(1)}, bf16[72,512]{1,0:T(8,128)(2,1)S(1)}, u32[]{:S(2)}, u32[]{:S(2)}) collective-permute-start(bf16[72,512]{1,0:T(8,128)(2,1)S(1)} %get-tuple-element.86), channel_id=1, source_target_pairs={{0,15},{1,0},{2,1},{3,2},{4,3},{5,4},{6,5},{7,6},{8,7},{9,8},{10,9... | collective-permute-start | bytes 221192 | tf_op jit(solution)/shard_map/ppermute | solution.py:468
  21.4 5.0 %collective-permute-start.2 = (bf16[72,512]{1,0:T(8,128)(2,1)S(1)}, bf16[72,512]{1,0:T(8,128)(2,1)S(1)}, u32[]{:S(2)}, u32[]{:S(2)}) collective-permute-start(bf16[72,512]{1,0:T(8,128)(2,1)S(1)} %get-tuple-element.87), channel_id=1, source_target_pairs={{0,255},{1,240},{2,241},{3,242},{4,243},{5,244},{6,245},{7,246},{8... | collective-permute-start | bytes 221192 | tf_op jit(solution)/shard_map/ppermute | solution.py:478
  30.8 7.4 %collective-permute-start.6 = (bf16[72,512]{1,0:T(8,128)(2,1)S(1)}, bf16[72,512]{1,0:T(8,128)(2,1)S(1)}, u32[]{:S(2)}, u32[]{:S(2)}) collective-permute-start(bf16[72,512]{1,0:T(8,128)(2,1)S(1)} %get-tuple-element.98), channel_id=1, source_target_pairs={{0,17},{1,18},{2,19},{3,20},{4,21},{5,22},{6,23},{7,24},{8,25},{9,... | collective-permute-start | bytes 221192 | tf_op jit(solution)/shard_map/ppermute | solution.py:478
  31.4 6.8 %collective-permute-start.7 = (bf16[72,512]{1,0:T(8,128)(2,1)S(1)}, bf16[72,512]{1,0:T(8,128)(2,1)S(1)}, u32[]{:S(2)}, u32[]{:S(2)}) collective-permute-start(bf16[72,512]{1,0:T(8,128)(2,1)S(1)} %get-tuple-element.99), channel_id=1, source_target_pairs={{0,1},{1,2},{2,3},{3,4},{4,5},{5,6},{6,7},{7,8},{8,9},{9,10},{10,1... | collective-permute-start | bytes 221192 | tf_op jit(solution)/shard_map/ppermute | solution.py:468
  31.5 8.9 %collective-permute-start.8 = (bf16[72,512]{1,0:T(8,128)(2,1)S(1)}, bf16[72,512]{1,0:T(8,128)(2,1)S(1)}, u32[]{:S(2)}, u32[]{:S(2)}) collective-permute-start(bf16[72,512]{1,0:T(8,128)(2,1)S(1)} %get-tuple-element.100), channel_id=1, source_target_pairs={{0,16},{16,32},{32,48},{48,64},{64,80},{80,96},{96,112},{112,128},... | collective-permute-start | bytes 221192 | tf_op jit(solution)/shard_map/ppermute | solution.py:468
  32.5 8.0 %copy-start.2 = (bf16[512,512]{1,0:T(8,128)(2,1)S(1)}, bf16[512,512]{1,0:T(8,128)(2,1)}, u32[]{:S(2)}) copy-start(bf16[512,512]{1,0:T(8,128)(2,1)} %out.5) | copy-start | bytes 1572868
  33.8 14.6 %collective-permute-start.18 = (bf16[256,2048]{1,0:T(8,128)(2,1)S(1)}, bf16[256,2048]{1,0:T(8,128)(2,1)S(1)}, u32[]{:S(2)}, u32[]{:S(2)}) collective-permute-start(bf16[256,2048]{1,0:T(8,128)(2,1)S(1)} %get-tuple-element.143), channel_id=1, source_target_pairs={{0,1},{1,0},{2,3},{3,2},{4,5},{5,4},{6,7},{7,6},{8,9},{9,8},{10,11... | collective-permute-start | bytes 3145736 | tf_op jit(solution)/shard_map/ppermute | solution.py:468
  40.4 4.1 %copy-start.5 = (f32[512]{0:T(512)S(1)}, f32[512]{0:T(512)}, u32[]{:S(2)}) copy-start(f32[512]{0:T(512)} %gain.5) | copy-start | bytes 6148
  40.4 4.2 %copy-start.7 = (bf16[288,288]{1,0:T(8,128)(2,1)S(1)}, bf16[288,288]{1,0:T(8,128)(2,1)}, u32[]{:S(2)}) copy-start(bf16[288,288]{1,0:T(8,128)(2,1)} %constant.11.clone.place_t) | copy-start | bytes 497668
  44.5 7.5 %collective-permute-start.9 = (bf16[256,2048]{1,0:T(8,128)(2,1)S(1)}, bf16[256,2048]{1,0:T(8,128)(2,1)S(1)}, u32[]{:S(2)}, u32[]{:S(2)}) collective-permute-start(bf16[256,2048]{1,0:T(8,128)(2,1)S(1)} %get-tuple-element.110), channel_id=1, source_target_pairs={{0,1},{1,0},{2,3},{3,2},{4,5},{5,4},{6,7},{7,6},{8,9},{9,8},{10,11... | collective-permute-start | bytes 3145736 | tf_op jit(solution)/shard_map/ppermute | solution.py:468
  48.5 9.2 %collective-permute-start.19 = (bf16[2,64,1024]{2,1,0:T(8,128)(2,1)S(1)}, bf16[2,64,1024]{2,1,0:T(8,128)(2,1)S(1)}, u32[]{:S(2)}, u32[]{:S(2)}) collective-permute-start(bf16[2,64,1024]{2,1,0:T(8,128)(2,1)S(1)} %get-tuple-element.145), channel_id=1, source_target_pairs={{0,4},{1,5},{2,6},{3,7},{4,0},{5,1},{6,2},{7,3},{8,12},{9,13},{10,... | collective-permute-start | bytes 786440 | tf_op jit(solution)/shard_map/ppermute | solution.py:468
  50.1 10.4 %collective-permute-start.20 = (bf16[2,64,1024]{2,1,0:T(8,128)(2,1)S(1)}, bf16[2,64,1024]{2,1,0:T(8,128)(2,1)S(1)}, u32[]{:S(2)}, u32[]{:S(2)}) collective-permute-start(bf16[2,64,1024]{2,1,0:T(8,128)(2,1)S(1)} %get-tuple-element.147), channel_id=1, source_target_pairs={{0,12},{1,13},{2,14},{3,15},{4,8},{5,9},{6,10},{7,11},{8,4},{9,5},... | collective-permute-start | bytes 786440 | tf_op jit(solution)/shard_map/ppermute | solution.py:468
  52.1 10.8 %collective-permute-start.13 = (bf16[2,64,1024]{2,1,0:T(8,128)(2,1)S(1)}, bf16[2,64,1024]{2,1,0:T(8,128)(2,1)S(1)}, u32[]{:S(2)}, u32[]{:S(2)}) collective-permute-start(bf16[2,64,1024]{2,1,0:T(8,128)(2,1)S(1)} %get-tuple-element.122), channel_id=1, source_target_pairs={{0,4},{1,5},{2,6},{3,7},{4,0},{5,1},{6,2},{7,3},{8,12},{9,13},{10,... | collective-permute-start | bytes 786440 | tf_op jit(solution)/shard_map/ppermute | solution.py:468
  53.4 12.7 %collective-permute-start.14 = (bf16[2,64,1024]{2,1,0:T(8,128)(2,1)S(1)}, bf16[2,64,1024]{2,1,0:T(8,128)(2,1)S(1)}, u32[]{:S(2)}, u32[]{:S(2)}) collective-permute-start(bf16[2,64,1024]{2,1,0:T(8,128)(2,1)S(1)} %get-tuple-element.124), channel_id=1, source_target_pairs={{0,12},{1,13},{2,14},{3,15},{4,8},{5,9},{6,10},{7,11},{8,4},{9,5},... | collective-permute-start | bytes 786440 | tf_op jit(solution)/shard_map/ppermute | solution.py:468
  60.5 7.6 %collective-permute-start.21 = (bf16[64,1024]{1,0:T(8,128)(2,1)S(1)}, bf16[64,1024]{1,0:T(8,128)(2,1)S(1)}, u32[]{:S(2)}, u32[]{:S(2)}) collective-permute-start(bf16[64,1024]{1,0:T(8,128)(2,1)S(1)} %get-tuple-element.149), channel_id=1, source_target_pairs={{0,12},{1,13},{2,14},{3,15},{4,8},{5,9},{6,10},{7,11},{8,4},{9,5},... | collective-permute-start | bytes 393224 | tf_op jit(solution)/shard_map/ppermute | solution.py:468
  62.5 5.7 %collective-permute-start.22 = (bf16[64,1024]{1,0:T(8,128)(2,1)S(1)}, bf16[64,1024]{1,0:T(8,128)(2,1)S(1)}, u32[]{:S(2)}, u32[]{:S(2)}) collective-permute-start(bf16[64,1024]{1,0:T(8,128)(2,1)S(1)} %get-tuple-element.151), channel_id=1, source_target_pairs={{0,4},{1,5},{2,6},{3,7},{4,0},{5,1},{6,2},{7,3},{8,12},{9,13},{10,... | collective-permute-start | bytes 393224 | tf_op jit(solution)/shard_map/ppermute | solution.py:468
  66.2 6.3 %collective-permute-start.15 = (bf16[64,1024]{1,0:T(8,128)(2,1)S(1)}, bf16[64,1024]{1,0:T(8,128)(2,1)S(1)}, u32[]{:S(2)}, u32[]{:S(2)}) collective-permute-start(bf16[64,1024]{1,0:T(8,128)(2,1)S(1)} %get-tuple-element.134), channel_id=1, source_target_pairs={{0,12},{1,13},{2,14},{3,15},{4,8},{5,9},{6,10},{7,11},{8,4},{9,5},... | collective-permute-start | bytes 393224 | tf_op jit(solution)/shard_map/ppermute | solution.py:468
  68.1 5.0 %collective-permute-start.16 = (bf16[64,1024]{1,0:T(8,128)(2,1)S(1)}, bf16[64,1024]{1,0:T(8,128)(2,1)S(1)}, u32[]{:S(2)}, u32[]{:S(2)}) collective-permute-start(bf16[64,1024]{1,0:T(8,128)(2,1)S(1)} %get-tuple-element.136), channel_id=1, source_target_pairs={{0,4},{1,5},{2,6},{3,7},{4,0},{5,1},{6,2},{7,3},{8,12},{9,13},{10,... | collective-permute-start | bytes 393224 | tf_op jit(solution)/shard_map/ppermute | solution.py:468
  68.2 5.1 %collective-permute-start.23 = (bf16[32,2048]{1,0:T(8,128)(2,1)S(1)}, bf16[32,2048]{1,0:T(8,128)(2,1)S(1)}, u32[]{:S(2)}, u32[]{:S(2)}) collective-permute-start(bf16[32,2048]{1,0:T(8,128)(2,1)S(1)} %get-tuple-element.153), channel_id=1, source_target_pairs={{0,2},{1,3},{2,0},{3,1},{4,6},{5,7},{6,4},{7,5},{8,10},{9,11},{10,... | collective-permute-start | bytes 393224 | tf_op jit(solution)/shard_map/ppermute | solution.py:468
  73.1 5.1 %collective-permute-start.17 = (bf16[32,2048]{1,0:T(8,128)(2,1)S(1)}, bf16[32,2048]{1,0:T(8,128)(2,1)S(1)}, u32[]{:S(2)}, u32[]{:S(2)}) collective-permute-start(bf16[32,2048]{1,0:T(8,128)(2,1)S(1)} %get-tuple-element.138), channel_id=1, source_target_pairs={{0,2},{1,3},{2,0},{3,1},{4,6},{5,7},{6,4},{7,5},{8,10},{9,11},{10,... | collective-permute-start | bytes 393224 | tf_op jit(solution)/shard_map/ppermute | solution.py:468
  79.1 17.6 %all-to-all-start = ((bf16[16,2,32,128]{3,2,1,0:T(8,128)(2,1)}), bf16[16,2,32,128]{3,2,1,0:T(8,128)(2,1)S(1)}, u32[]{:S(2)}, u32[]{:S(2)}) async-start(bf16[16,2,32,128]{3,2,1,0:T(8,128)(2,1)} %shard_map.213), calls=%async_computation | async-start | bytes 524288 | tf_op jit(solution)/shard_map/all_to_all | solution.py:629
  85.0 8.5 %collective-permute-start.10 = (bf16[72,512]{1,0:T(8,128)(2,1)S(1)}, bf16[72,512]{1,0:T(8,128)(2,1)S(1)}, u32[]{:S(2)}, u32[]{:S(2)}) collective-permute-start(bf16[72,512]{1,0:T(8,128)(2,1)S(1)} %get-tuple-element.118), channel_id=1, source_target_pairs={{0,17},{1,18},{2,19},{3,20},{4,21},{5,22},{6,23},{7,24},{8,25},{9,... | collective-permute-start | bytes 221192 | tf_op jit(solution)/shard_map/ppermute | solution.py:478
  85.0 8.5 %collective-permute-start.11 = (bf16[72,512]{1,0:T(8,128)(2,1)S(1)}, bf16[72,512]{1,0:T(8,128)(2,1)S(1)}, u32[]{:S(2)}, u32[]{:S(2)}) collective-permute-start(bf16[72,512]{1,0:T(8,128)(2,1)S(1)} %get-tuple-element.119), channel_id=1, source_target_pairs={{0,1},{1,2},{2,3},{3,4},{4,5},{5,6},{6,7},{7,8},{8,9},{9,10},{10,1... | collective-permute-start | bytes 221192 | tf_op jit(solution)/shard_map/ppermute | solution.py:468
  85.6 9.7 %collective-permute-start.12 = (bf16[72,512]{1,0:T(8,128)(2,1)S(1)}, bf16[72,512]{1,0:T(8,128)(2,1)S(1)}, u32[]{:S(2)}, u32[]{:S(2)}) collective-permute-start(bf16[72,512]{1,0:T(8,128)(2,1)S(1)} %get-tuple-element.120), channel_id=1, source_target_pairs={{0,16},{16,32},{32,48},{48,64},{64,80},{80,96},{96,112},{112,128},... | collective-permute-start | bytes 221192 | tf_op jit(solution)/shard_map/ppermute | solution.py:468

commit v2 on v1

--- a/solution.py
+++ b/solution.py
@@ -363,14 +363,15 @@
     grads_half(1 - core, normed_t, mixed_t, grad_middle, d_packed, send)
 
 
-def kernel_finish_a(
-    inputs, grad_middle, gain, qkv_hbm, d_packed, normed_t, mixed_t, place_t,
-    keep, grad_fields,
-    qkv, sems,
-):
-    (qkv_in,) = fetch(((qkv_hbm, qkv),), sems)
+def kernel_keep_a(normed_t, mixed_t, grad_middle, d_packed, keep):
     core = lax.axis_index("lat") % 2
     grads_half(core, normed_t, mixed_t, grad_middle[...], d_packed, keep)
+
+
+def kernel_finish_a(
+    inputs, grad_middle, gain, qkv_hbm, d_packed, place_t, grad_fields, qkv, sems
+):
+    (qkv_in,) = fetch(((qkv_hbm, qkv),), sems)
     qkv_in.wait()
     d_inputs = norm_backward(
         inputs[...].astype(F32), gain[...].reshape(1, WIDTH), d_packed[...], qkv
@@ -586,6 +587,7 @@
         flops=2 * 10**9,
     )
     sums_b = first_sum(*first_round(send_b, keep_b))
+    sums_b, d0 = lax.optimization_barrier((sums_b, d0))
     rounds_b = second_round(*sums_b)
     grad_middle, d_packed_a, send_a = call(
         kernel_backward_a,
@@ -597,34 +599,42 @@
         ),
         flops=5 * 10**9,
     )
+    rounds_b, send_a = lax.optimization_barrier((rounds_b, send_a))
     sums_b = second_sum(*rounds_b)
     rounds_b = third_round(*sums_b)
-    keep_a, grad_fields = call(
+    keep_a = call(
+        kernel_keep_a, [half_grads], [], (normed_a_t, mixed_a, grad_middle, d_packed_a),
+        flops=10**9,
+    )[0]
+    sums_a = first_sum(*first_round(send_a, keep_a))
+    sums_a, b1, b2, b3, d_packed_a = lax.optimization_barrier((sums_a, b1, b2, b3, d_packed_a))
+    rounds_a = second_round(*sums_a)
+    grad_fields = call(
         kernel_finish_a,
-        [half_grads, grid],
+        [grid],
         [qkv_shape],
-        (inputs_a, grad_middle, gain_a, qkv_weight_a, d_packed_a, normed_a_t, mixed_a, place_t),
-        hbm=(3,), copies=1, flops=4 * 10**9, final=(1,),
-    )
-    sums_a = first_sum(*first_round(send_a, keep_a))
-    sums_a, b1, b2, b3 = lax.optimization_barrier((sums_a, b1, b2, b3))
-    rounds_a = second_round(*sums_a)
+        (inputs_a, grad_middle, gain_a, qkv_weight_a, d_packed_a, place_t),
+        hbm=(3,), copies=1, flops=4 * 10**9, final=(0,),
+    )[0]
     delta_diagonal = permute_both(b3, 1)
     delta_above = permute(b2, "lat", lambda i: i + 1)
     delta_western = permute(b1, "lon", lambda i: i + 1)
+    sums_a = second_sum(*rounds_a)
+    sums_a, grad_fields = lax.optimization_barrier((sums_a, grad_fields))
     rounds_b = fourth_round(*rounds_b)
-    sums_a = second_sum(*rounds_a)
-    sums_a, b0 = lax.optimization_barrier((sums_a, b0))
+    rounds_a = fourth_round(*third_round(*sums_a))
+    blocks = call(
+        kernel_columns, [((16, 2, 32, GROUP), BF16)], [], rounds_a + rounds_b, final=(0,)
+    )[0]
+    blocks, delta_diagonal, delta_above, delta_western = lax.optimization_barrier(
+        (blocks, delta_diagonal, delta_above, delta_western)
+    )
     advanced = call(
         kernel_advanced,
         [grid],
         [],
         (delta_diagonal, delta_above, delta_western, b0, middle_a, place_t, sort_t),
         flops=10**9, final=(0,),
-    )[0]
-    rounds_a = fourth_round(*third_round(*sums_a))
-    blocks = call(
-        kernel_columns, [((16, 2, 32, GROUP), BF16)], [], rounds_a + rounds_b, final=(0,)
     )[0]
     blocks = lax.all_to_all(blocks, "lon", 0, 0, tiled=True)
     grads = call(

time: 99.2 us -> 97.1 us (0.979)
  the two profiles are of different devices: /device:TPU:6 before, /device:TPU:32 now
where the time goes in v2:
time: 97.1 us; the launch traced here: 96.7 us
  starting transfers between devices  40.3 us (42%)
  Pallas kernels  30.6 us (32%)
  waiting for transfers between devices  24.9 us (26%)
    pallas_call x17, Pallas kernels, call(): pl.pallas_call(kernel, out_shape=tuple((jax.ShapeDtypeStruct(shape, kind)...  30.6 us
    ppermute x20, starting transfers between devices, permute(): lax.ppermute(array, axis, [(i, target(i) % length) for i in range(length)])  22.4 us
    ppermute x20, waiting for transfers between devices, permute(): lax.ppermute(array, axis, [(i, target(i) % length) for i in range(length)])  11 us
    all_to_all x1, waiting for transfers between devices, body(): blocks = lax.all_to_all(blocks, 'lon', 0, 0, tiled=True)  9.9 us
    ppermute x4, starting transfers between devices, permute_both(): return lax.ppermute(array, ('lon', 'lat'), pairs)  9.52 us
    all_to_all x1, starting transfers between devices, body(): blocks = lax.all_to_all(blocks, 'lon', 0, 0, tiled=True)  8.36 us
    ppermute x4, waiting for transfers between devices, permute_both(): return lax.ppermute(array, ('lon', 'lat'), pairs)  4.07 us
  transfers between devices with their start and end apart: 25, of which 11 were waited for; matrix products, arithmetic and copies ran while one was open for 0% of the time, Pallas kernels for 18%

profile of v2, /device:TPU:32, one launch (start us, length us, event | category | flops | bytes accessed | tf_op | source)
XLA Modules:
  0.0 96.7 jit_solution(11075423083850819276)
XLA Ops:
  0.6 0.0 copy-start.8
  0.7 0.0 copy-start.9
  0.7 0.0 copy-start.10
  0.7 6.5 %shard_map.199 = (bf16[72,512]{1,0:T(8,128)(2,1)S(1)}, bf16[72,512]{1,0:T(8,128)(2,1)S(1)}, bf16[72,512]{1,0:T(8,128)(2,1)S(1)}, bf16[72,512]{1,0:T(8,128)(2,1)S...) custom-call(bf16[12,6,4,512]{3,2,1,0:T(4,128)(2,1)} %bitcast.6, ...), custom_call_target="tpu_custom_call" | custom-call | flops 7000000000 | bytes 1048576 | tf_op jit(solution)/shard_map/pallas_call | solution.py:453
  7.2 1.9 %collective-permute-start.3 = (bf16[72,512]{1,0:T(8,128)(2,1)S(1)}, bf16[72,512]{1,0:T(8,128)(2,1)S(1)}, u32[]{:S(2)}, u32[]{:S(2)}) collective-permute-start(bf16[72,512]{1,0:T(8,128)(2,1)S(1)} %get-tuple-element.103), channel_id=1, source_target_pairs={{0,240},{16,0},{32,16},{48,32},{64,48},{80,64},{96,80},{112,96},{1... | collective-permute-start | bytes 221192 | tf_op jit(solution)/shard_map/ppermute | solution.py:469
  9.1 1.6 %collective-permute-start.4 = (bf16[72,512]{1,0:T(8,128)(2,1)S(1)}, bf16[72,512]{1,0:T(8,128)(2,1)S(1)}, u32[]{:S(2)}, u32[]{:S(2)}) collective-permute-start(bf16[72,512]{1,0:T(8,128)(2,1)S(1)} %get-tuple-element.104), channel_id=1, source_target_pairs={{0,15},{1,0},{2,1},{3,2},{4,3},{5,4},{6,5},{7,6},{8,7},{9,8},{10,9... | collective-permute-start | bytes 221192 | tf_op jit(solution)/shard_map/ppermute | solution.py:469
  10.7 7.5 %collective-permute-start.5 = (bf16[72,512]{1,0:T(8,128)(2,1)S(1)}, bf16[72,512]{1,0:T(8,128)(2,1)S(1)}, u32[]{:S(2)}, u32[]{:S(2)}) collective-permute-start(bf16[72,512]{1,0:T(8,128)(2,1)S(1)} %get-tuple-element.105), channel_id=1, source_target_pairs={{0,255},{1,240},{2,241},{3,242},{4,243},{5,244},{6,245},{7,246},{8... | collective-permute-start | bytes 221192 | tf_op jit(solution)/shard_map/ppermute | solution.py:479
  18.3 0.0 copy-start
  18.3 0.0 copy-start.1
  18.3 0.0 copy-start.4
  18.3 0.0 copy-start.6
  18.3 2.9 %shard_map.200 = (bf16[72,512]{1,0:T(8,128)(2,1)S(1)}, bf16[72,512]{1,0:T(8,128)(2,1)S(1)}, bf16[72,512]{1,0:T(8,128)(2,1)S(1)}, bf16[72,512]{1,0:T(8,128)(2,1)S...) custom-call(bf16[12,6,4,512]{3,2,1,0:T(4,128)(2,1)} %bitcast.7, ...), custom_call_target="tpu_custom_call" | custom-call | flops 2000000000 | bytes 1048576 | tf_op jit(solution)/shard_map/pallas_call | solution.py:453
  21.3 0.8 collective-permute-start
  22.1 0.2 collective-permute-start.1
  22.3 1.5 %collective-permute-start.2 = (bf16[72,512]{1,0:T(8,128)(2,1)S(1)}, bf16[72,512]{1,0:T(8,128)(2,1)S(1)}, u32[]{:S(2)}, u32[]{:S(2)}) collective-permute-start(bf16[72,512]{1,0:T(8,128)(2,1)S(1)} %get-tuple-element.101), channel_id=1, source_target_pairs={{0,255},{1,240},{2,241},{3,242},{4,243},{5,244},{6,245},{7,246},{8... | collective-permute-start | bytes 221192 | tf_op jit(solution)/shard_map/ppermute | solution.py:479
  23.8 0.0 collective-permute-done.5.piece3
  23.8 3.8 %shard_map.201 = (bf16[72,512]{1,0:T(8,128)(2,1)S(1)}, bf16[72,512]{1,0:T(8,128)(2,1)S(1)}, bf16[72,512]{1,0:T(8,128)(2,1)S(1)}, bf16[72,512]{1,0:T(8,128)(2,1)S...) custom-call(bf16[72,512]{1,0:T(8,128)(2,1)S(1)} %get-tuple-element.1, ...), custom_call_target="tpu_custom_call" | custom-call | flops 5000000000 | bytes 1048576 | tf_op jit(solution)/shard_map/pallas_call | solution.py:453
  27.6 0.0 collective-permute-done.piece1
  27.6 0.0 collective-permute-done.1.piece2
  27.6 4.5 %shard_map.202 = (bf16[72,512]{1,0:T(8,128)(2,1)S(1)}, bf16[72,512]{1,0:T(8,128)(2,1)S(1)}, bf16[72,512]{1,0:T(8,128)(2,1)S(1)}, bf16[72,512]{1,0:T(8,128)(2,1)S...) custom-call(bf16[72,512]{1,0:T(8,128)(2,1)S(1)} %get-tuple-element.98.piece0, ...), custom_call_target="tpu_custom_call" | custom-call | flops 5000000000 | bytes 1048576 | tf_op jit(solution)/shard_map/pallas_call | solution.py:453
  32.1 0.0 copy-start.2
  32.1 1.3 %shard_map.203 = (bf16[256,2048]{1,0:T(8,128)(2,1)S(1)}, bf16[256,2048]{1,0:T(8,128)(2,1)S(1)}) custom-call(bf16[288,512]{1,0:T(8,128)(2,1)S(1)} %get-tuple-element.115.normed, bf16[2,512,144]{2,1,0:T(8,128)(2,1)S(1)} %get-tuple-element.111.mixed_t, bf16[288,512]{1,0:T(8,128)(2,1)S(1)} %get-tuple-element.116.upstream, ...), custom_call_target="tpu_custom_call" | custom-call | flops 2000000000 | bytes 1048576 | tf_op jit(solution)/shard_map/pallas_call | solution.py:453
  33.5 0.4 collective-permute-start.9
  33.9 0.5 collective-permute-start.6
  34.4 1.2 %collective-permute-start.7 = (bf16[72,512]{1,0:T(8,128)(2,1)S(1)}, bf16[72,512]{1,0:T(8,128)(2,1)S(1)}, u32[]{:S(2)}, u32[]{:S(2)}) collective-permute-start(bf16[72,512]{1,0:T(8,128)(2,1)S(1)} %get-tuple-element.113), channel_id=1, source_target_pairs={{0,1},{1,2},{2,3},{3,4},{4,5},{5,6},{6,7},{7,8},{8,9},{9,10},{10,1... | collective-permute-start | bytes 221192 | tf_op jit(solution)/shard_map/ppermute | solution.py:469
  35.6 0.9 collective-permute-start.8
  36.5 0.0 collective-permute-done.9.got
  36.5 0.1 shard_map.204
  36.6 0.1 collective-permute-start.10
  36.7 2.0 %collective-permute-start.11 = (bf16[2,64,1024]{2,1,0:T(8,128)(2,1)S(1)}, bf16[2,64,1024]{2,1,0:T(8,128)(2,1)S(1)}, u32[]{:S(2)}, u32[]{:S(2)}) collective-permute-start(bf16[2,64,1024]{2,1,0:T(8,128)(2,1)S(1)} %get-tuple-element.134), channel_id=1, source_target_pairs={{0,12},{1,13},{2,14},{3,15},{4,8},{5,9},{6,10},{7,11},{8,4},{9,5},... | collective-permute-start | bytes 786440 | tf_op jit(solution)/shard_map/ppermute | solution.py:469
  38.7 2.2 %collective-permute-done.6.back0 = bf16[72,512]{1,0:T(8,128)(2,1)S(1)} collective-permute-done((bf16[72,512]{1,0:T(8,128)(2,1)S(1)}, bf16[72,512]{1,0:T(8,128)(2,1)S(1)}, u32[]{:S(2)}, u32[]{:S(2)}) %collective-permute-start.6) | collective-permute-done | bytes 73760 | tf_op jit(solution)/shard_map/ppermute | solution.py:479
  40.9 0.2 collective-permute-done.7.back1
  41.1 0.0 collective-permute-done.8.back2
  41.1 4.2 %shard_map.205 = (bf16[288,512]{1,0:T(8,128)(2,1)S(1)}, bf16[288,1536]{1,0:T(8,128)(2,1)S(1)}, bf16[256,2048]{1,0:T(8,128)(2,1)S(1)}) custom-call(bf16[72,512]{1,0:T(8,128)(2,1)S(1)} %collective-permute-done.6.back0, bf16[72,512]{1,0:T(8,128)(2,1)S(1)} %collective-permute-done.7.back1, bf16[72,512]{1,0:T(8,128)(2,1)S(1)} %collective-permute-done.8.back2, ...), custom_call_target="tpu_custom_call" | custom-call | flops 5000000000 | bytes 1048576 | tf_op jit(solution)/shard_map/pallas_call | solution.py:453
  45.3 0.0 collective-permute-done.10.got_one
  45.3 1.4 %collective-permute-done.11.got_two = bf16[2,64,1024]{2,1,0:T(8,128)(2,1)S(1)} collective-permute-done((bf16[2,64,1024]{2,1,0:T(8,128)(2,1)S(1)}, bf16[2,64,1024]{2,1,0:T(8,128)(2,1)S(1)}, u32[]{:S(2)}, u32[]{:S(2)}) %collective-permute-start.11) | collective-permute-done | bytes 262176 | tf_op jit(solution)/shard_map/ppermute | solution.py:469
  46.7 0.7 shard_map.206.keep
  47.4 0.0 copy-start.5
  47.5 0.0 copy-start.7
  47.5 0.1 shard_map.211
  47.5 1.8 %collective-permute-start.18 = (bf16[64,1024]{1,0:T(8,128)(2,1)S(1)}, bf16[64,1024]{1,0:T(8,128)(2,1)S(1)}, u32[]{:S(2)}, u32[]{:S(2)}) collective-permute-start(bf16[64,1024]{1,0:T(8,128)(2,1)S(1)} %get-tuple-element.165), channel_id=1, source_target_pairs={{0,12},{1,13},{2,14},{3,15},{4,8},{5,9},{6,10},{7,11},{8,4},{9,5},... | collective-permute-start | bytes 393224 | tf_op jit(solution)/shard_map/ppermute | solution.py:469
  49.3 0.1 collective-permute-done.12.got
  49.4 0.1 shard_map.207
  49.5 2.0 %collective-permute-start.13 = (bf16[2,64,1024]{2,1,0:T(8,128)(2,1)S(1)}, bf16[2,64,1024]{2,1,0:T(8,128)(2,1)S(1)}, u32[]{:S(2)}, u32[]{:S(2)}) collective-permute-start(bf16[2,64,1024]{2,1,0:T(8,128)(2,1)S(1)} %get-tuple-element.145), channel_id=1, source_target_pairs={{0,4},{1,5},{2,6},{3,7},{4,0},{5,1},{6,2},{7,3},{8,12},{9,13},{10,... | collective-permute-start | bytes 786440 | tf_op jit(solution)/shard_map/ppermute | solution.py:469
  51.5 1.6 %collective-permute-start.14 = (bf16[2,64,1024]{2,1,0:T(8,128)(2,1)S(1)}, bf16[2,64,1024]{2,1,0:T(8,128)(2,1)S(1)}, u32[]{:S(2)}, u32[]{:S(2)}) collective-permute-start(bf16[2,64,1024]{2,1,0:T(8,128)(2,1)S(1)} %get-tuple-element.147), channel_id=1, source_target_pairs={{0,12},{1,13},{2,14},{3,15},{4,8},{5,9},{6,10},{7,11},{8,4},{9,5},... | collective-permute-start | bytes 786440 | tf_op jit(solution)/shard_map/ppermute | solution.py:469
  53.1 3.3 %shard_map.209 = bf16[12,6,4,512]{3,2,1,0:T(4,128)(2,1)} custom-call(bf16[288,512]{1,0:T(8,128)(2,1)S(1)} %get-tuple-element.152.inputs, bf16[288,512]{1,0:T(8,128)(2,1)S(1)} %get-tuple-element.129.grad_middle, f32[512]{0:T(512)S(1)} %copy-done.5, bf16[512,1536]{1,0:T(8,128)(2,1)} %qkv_hbm.3, bf16[288,1536]{1,0:T(8,128)(2,1)S(1)} %get-tuple-element.153.d_packed, ...), custom_call_target="tpu_custom_call" | custom-call | flops 4000000000 | bytes 1048576 | tf_op jit(solution)/shard_map/pallas_call | solution.py:453
  56.3 4.2 %collective-permute-done.13.got_one = bf16[2,64,1024]{2,1,0:T(8,128)(2,1)S(1)} collective-permute-done((bf16[2,64,1024]{2,1,0:T(8,128)(2,1)S(1)}, bf16[2,64,1024]{2,1,0:T(8,128)(2,1)S(1)}, u32[]{:S(2)}, u32[]{:S(2)}) %collective-permute-start.13) | collective-permute-done | bytes 262176 | tf_op jit(solution)/shard_map/ppermute | solution.py:469
  60.5 0.1 collective-permute-done.14.got_two
  60.6 0.1 shard_map.208
  60.7 1.7 %collective-permute-start.15 = (bf16[64,1024]{1,0:T(8,128)(2,1)S(1)}, bf16[64,1024]{1,0:T(8,128)(2,1)S(1)}, u32[]{:S(2)}, u32[]{:S(2)}) collective-permute-start(bf16[64,1024]{1,0:T(8,128)(2,1)S(1)} %get-tuple-element.155), channel_id=1, source_target_pairs={{0,12},{1,13},{2,14},{3,15},{4,8},{5,9},{6,10},{7,11},{8,4},{9,5},... | collective-permute-start | bytes 393224 | tf_op jit(solution)/shard_map/ppermute | solution.py:469
  62.3 0.1 shard_map.212
  62.4 2.4 %collective-permute-start.20 = (bf16[32,2048]{1,0:T(8,128)(2,1)S(1)}, bf16[32,2048]{1,0:T(8,128)(2,1)S(1)}, u32[]{:S(2)}, u32[]{:S(2)}) collective-permute-start(bf16[32,2048]{1,0:T(8,128)(2,1)S(1)} %get-tuple-element.169), channel_id=1, source_target_pairs={{0,2},{1,3},{2,0},{3,1},{4,6},{5,7},{6,4},{7,5},{8,10},{9,11},{10,... | collective-permute-start | bytes 393224 | tf_op jit(solution)/shard_map/ppermute | solution.py:469
  64.7 2.2 %collective-permute-done.15.got_one = bf16[64,1024]{1,0:T(8,128)(2,1)S(1)} collective-permute-done((bf16[64,1024]{1,0:T(8,128)(2,1)S(1)}, bf16[64,1024]{1,0:T(8,128)(2,1)S(1)}, u32[]{:S(2)}, u32[]{:S(2)}) %collective-permute-start.15) | collective-permute-done | bytes 131104 | tf_op jit(solution)/shard_map/ppermute | solution.py:469
  66.9 0.4 collective-permute-done.16.got_two
  67.3 2.4 %collective-permute-start.17 = (bf16[32,2048]{1,0:T(8,128)(2,1)S(1)}, bf16[32,2048]{1,0:T(8,128)(2,1)S(1)}, u32[]{:S(2)}, u32[]{:S(2)}) collective-permute-start(bf16[32,2048]{1,0:T(8,128)(2,1)S(1)} %get-tuple-element.159), channel_id=1, source_target_pairs={{0,2},{1,3},{2,0},{3,1},{4,6},{5,7},{6,4},{7,5},{8,10},{9,11},{10,... | collective-permute-start | bytes 393224 | tf_op jit(solution)/shard_map/ppermute | solution.py:469
  69.7 0.6 collective-permute-start.22
  70.3 0.9 collective-permute-start.23
  71.2 2.5 %collective-permute-done.17.got_a = bf16[32,2048]{1,0:T(8,128)(2,1)S(1)} collective-permute-done((bf16[32,2048]{1,0:T(8,128)(2,1)S(1)}, bf16[32,2048]{1,0:T(8,128)(2,1)S(1)}, u32[]{:S(2)}, u32[]{:S(2)}) %collective-permute-start.17) | collective-permute-done | bytes 131104 | tf_op jit(solution)/shard_map/ppermute | solution.py:469
  73.7 0.9 shard_map.213
  74.6 1.9 %collective-permute-done.21.back0 = bf16[72,512]{1,0:T(8,128)(2,1)S(1)} collective-permute-done((bf16[72,512]{1,0:T(8,128)(2,1)S(1)}, bf16[72,512]{1,0:T(8,128)(2,1)S(1)}, u32[]{:S(2)}, u32[]{:S(2)}) %collective-permute-start.21) | collective-permute-done | bytes 73760 | tf_op jit(solution)/shard_map/ppermute | solution.py:479
  76.5 8.4 %all-to-all-start = ((bf16[16,2,32,128]{3,2,1,0:T(8,128)(2,1)}), bf16[16,2,32,128]{3,2,1,0:T(8,128)(2,1)S(1)}, u32[]{:S(2)}, u32[]{:S(2)}) async-start(bf16[16,2,32,128]{3,2,1,0:T(8,128)(2,1)} %shard_map.213), calls=%async_computation | async-start | bytes 524288 | tf_op jit(solution)/shard_map/all_to_all | solution.py:639
  84.8 1.3 %shard_map.214 = bf16[12,6,4,512]{3,2,1,0:T(4,128)(2,1)} custom-call(bf16[72,512]{1,0:T(8,128)(2,1)S(1)} %collective-permute-done.21.back0, bf16[72,512]{1,0:T(8,128)(2,1)S(1)} %collective-permute-done.22.back1, bf16[72,512]{1,0:T(8,128)(2,1)S(1)} %collective-permute-done.23.back2, bf16[72,512]{1,0:T(8,128)(2,1)S(1)} %get-tuple-element.176.back3, ...), custom_call_target="tpu_custom_call" | custom-call | flops 1000000000 | bytes 1048576 | tf_op jit(solution)/shard_map/pallas_call | solution.py:453
  86.1 9.9 %all-to-all-done.parts = bf16[16,2,32,128]{3,2,1,0:T(8,128)(2,1)S(1)} async-done(((bf16[16,2,32,128]{3,2,1,0:T(8,128)(2,1)}), bf16[16,2,32,128]{3,2,1,0:T(8,128)(2,1)S(1)}, u32[]{:S(2)}, u32[]{:S(2)}) %all-to-all-start) | async-done | bytes 262176 | tf_op jit(solution)/shard_map/all_to_all | solution.py:639
  96.0 0.7 shard_map.215
  (25 shorter events, 0.1 us)
Async XLA Ops:
  0.6 17.7 %copy-start.3 = (s32[192,96]{1,0:T(8,128)S(1)}, s32[192,96]{1,0:T(8,128)}, u32[]{:S(2)}) copy-start(s32[192,96]{1,0:T(8,128)} %ids.1) | copy-start | bytes 221188
  0.6 17.6 %copy-start.8 = (bf16[288,288]{1,0:T(8,128)(2,1)S(1)}, bf16[288,288]{1,0:T(8,128)(2,1)}, u32[]{:S(2)}) copy-start(bf16[288,288]{1,0:T(8,128)(2,1)} %constant.12.clone.sort_hbm.sort) | copy-start | bytes 497668
  0.7 17.6 %copy-start.9 = (bf16[288,288]{1,0:T(8,128)(2,1)S(1)}, bf16[288,288]{1,0:T(8,128)(2,1)}, u32[]{:S(2)}) copy-start(bf16[288,288]{1,0:T(8,128)(2,1)} %constant.10.clone.place_hbm.place) | copy-start | bytes 497668
  0.7 17.6 %copy-start.10 = (s32[144,8]{1,0:T(8,128)S(1)}, s32[144,8]{1,0:T(8,128)}, u32[]{:S(2)}) copy-start(s32[144,8]{1,0:T(8,128)} %constant.14.clone.where_hbm.where) | copy-start | bytes 13828
  7.2 15.1 %collective-permute-start.3 = (bf16[72,512]{1,0:T(8,128)(2,1)S(1)}, bf16[72,512]{1,0:T(8,128)(2,1)S(1)}, u32[]{:S(2)}, u32[]{:S(2)}) collective-permute-start(bf16[72,512]{1,0:T(8,128)(2,1)S(1)} %get-tuple-element.103), channel_id=1, source_target_pairs={{0,240},{16,0},{32,16},{48,32},{64,48},{80,64},{96,80},{112,96},{1... | collective-permute-start | bytes 221192 | tf_op jit(solution)/shard_map/ppermute | solution.py:469
  9.1 14.6 %collective-permute-start.4 = (bf16[72,512]{1,0:T(8,128)(2,1)S(1)}, bf16[72,512]{1,0:T(8,128)(2,1)S(1)}, u32[]{:S(2)}, u32[]{:S(2)}) collective-permute-start(bf16[72,512]{1,0:T(8,128)(2,1)S(1)} %get-tuple-element.104), channel_id=1, source_target_pairs={{0,15},{1,0},{2,1},{3,2},{4,3},{5,4},{6,5},{7,6},{8,7},{9,8},{10,9... | collective-permute-start | bytes 221192 | tf_op jit(solution)/shard_map/ppermute | solution.py:469
  10.7 13.0 %collective-permute-start.5 = (bf16[72,512]{1,0:T(8,128)(2,1)S(1)}, bf16[72,512]{1,0:T(8,128)(2,1)S(1)}, u32[]{:S(2)}, u32[]{:S(2)}) collective-permute-start(bf16[72,512]{1,0:T(8,128)(2,1)S(1)} %get-tuple-element.105), channel_id=1, source_target_pairs={{0,255},{1,240},{2,241},{3,242},{4,243},{5,244},{6,245},{7,246},{8... | collective-permute-start | bytes 221192 | tf_op jit(solution)/shard_map/ppermute | solution.py:479
  18.3 5.5 %copy-start = (bf16[512,1536]{1,0:T(8,128)(2,1)S(1)}, bf16[512,1536]{1,0:T(8,128)(2,1)}, u32[]{:S(2)}) copy-start(bf16[512,1536]{1,0:T(8,128)(2,1)} %qkv.3) | copy-start | bytes 4718596
  18.3 5.5 %copy-start.1 = (bf16[512,512]{1,0:T(8,128)(2,1)S(1)}, bf16[512,512]{1,0:T(8,128)(2,1)}, u32[]{:S(2)}) copy-start(bf16[512,512]{1,0:T(8,128)(2,1)} %out.4) | copy-start | bytes 1572868
  18.3 5.5 %copy-start.4 = (f32[512]{0:T(512)S(1)}, f32[512]{0:T(512)}, u32[]{:S(2)}) copy-start(f32[512]{0:T(512)} %gain.4) | copy-start | bytes 6148
  18.3 5.5 %copy-start.6 = (bf16[288,288]{1,0:T(8,128)(2,1)S(1)}, bf16[288,288]{1,0:T(8,128)(2,1)}, u32[]{:S(2)}) copy-start(bf16[288,288]{1,0:T(8,128)(2,1)} %constant.13.clone.sort_t) | copy-start | bytes 497668
  21.3 6.3 %collective-permute-start = (bf16[72,512]{1,0:T(8,128)(2,1)S(1)}, bf16[72,512]{1,0:T(8,128)(2,1)S(1)}, u32[]{:S(2)}, u32[]{:S(2)}) collective-permute-start(bf16[72,512]{1,0:T(8,128)(2,1)S(1)} %get-tuple-element.99), channel_id=1, source_target_pairs={{0,240},{16,0},{32,16},{48,32},{64,48},{80,64},{96,80},{112,96},{1... | collective-permute-start | bytes 221192 | tf_op jit(solution)/shard_map/ppermute | solution.py:469
  22.1 5.6 %collective-permute-start.1 = (bf16[72,512]{1,0:T(8,128)(2,1)S(1)}, bf16[72,512]{1,0:T(8,128)(2,1)S(1)}, u32[]{:S(2)}, u32[]{:S(2)}) collective-permute-start(bf16[72,512]{1,0:T(8,128)(2,1)S(1)} %get-tuple-element.100), channel_id=1, source_target_pairs={{0,15},{1,0},{2,1},{3,2},{4,3},{5,4},{6,5},{7,6},{8,7},{9,8},{10,9... | collective-permute-start | bytes 221192 | tf_op jit(solution)/shard_map/ppermute | solution.py:469
  22.3 5.4 %collective-permute-start.2 = (bf16[72,512]{1,0:T(8,128)(2,1)S(1)}, bf16[72,512]{1,0:T(8,128)(2,1)S(1)}, u32[]{:S(2)}, u32[]{:S(2)}) collective-permute-start(bf16[72,512]{1,0:T(8,128)(2,1)S(1)} %get-tuple-element.101), channel_id=1, source_target_pairs={{0,255},{1,240},{2,241},{3,242},{4,243},{5,244},{6,245},{7,246},{8... | collective-permute-start | bytes 221192 | tf_op jit(solution)/shard_map/ppermute | solution.py:479
  32.1 8.9 %copy-start.2 = (bf16[512,512]{1,0:T(8,128)(2,1)S(1)}, bf16[512,512]{1,0:T(8,128)(2,1)}, u32[]{:S(2)}) copy-start(bf16[512,512]{1,0:T(8,128)(2,1)} %out.5) | copy-start | bytes 1572868
  33.5 3.0 %collective-permute-start.9 = (bf16[256,2048]{1,0:T(8,128)(2,1)S(1)}, bf16[256,2048]{1,0:T(8,128)(2,1)S(1)}, u32[]{:S(2)}, u32[]{:S(2)}) collective-permute-start(bf16[256,2048]{1,0:T(8,128)(2,1)S(1)} %get-tuple-element.119), channel_id=1, source_target_pairs={{0,1},{1,0},{2,3},{3,2},{4,5},{5,4},{6,7},{7,6},{8,9},{9,8},{10,11... | collective-permute-start | bytes 3145736 | tf_op jit(solution)/shard_map/ppermute | solution.py:469
  33.9 7.0 %collective-permute-start.6 = (bf16[72,512]{1,0:T(8,128)(2,1)S(1)}, bf16[72,512]{1,0:T(8,128)(2,1)S(1)}, u32[]{:S(2)}, u32[]{:S(2)}) collective-permute-start(bf16[72,512]{1,0:T(8,128)(2,1)S(1)} %get-tuple-element.112), channel_id=1, source_target_pairs={{0,17},{1,18},{2,19},{3,20},{4,21},{5,22},{6,23},{7,24},{8,25},{9,... | collective-permute-start | bytes 221192 | tf_op jit(solution)/shard_map/ppermute | solution.py:479
  34.4 6.7 %collective-permute-start.7 = (bf16[72,512]{1,0:T(8,128)(2,1)S(1)}, bf16[72,512]{1,0:T(8,128)(2,1)S(1)}, u32[]{:S(2)}, u32[]{:S(2)}) collective-permute-start(bf16[72,512]{1,0:T(8,128)(2,1)S(1)} %get-tuple-element.113), channel_id=1, source_target_pairs={{0,1},{1,2},{2,3},{3,4},{4,5},{5,6},{6,7},{7,8},{8,9},{9,10},{10,1... | collective-permute-start | bytes 221192 | tf_op jit(solution)/shard_map/ppermute | solution.py:469
  35.6 5.5 %collective-permute-start.8 = (bf16[72,512]{1,0:T(8,128)(2,1)S(1)}, bf16[72,512]{1,0:T(8,128)(2,1)S(1)}, u32[]{:S(2)}, u32[]{:S(2)}) collective-permute-start(bf16[72,512]{1,0:T(8,128)(2,1)S(1)} %get-tuple-element.114), channel_id=1, source_target_pairs={{0,16},{16,32},{32,48},{48,64},{64,80},{80,96},{96,112},{112,128},... | collective-permute-start | bytes 221192 | tf_op jit(solution)/shard_map/ppermute | solution.py:469
  36.6 8.7 %collective-permute-start.10 = (bf16[2,64,1024]{2,1,0:T(8,128)(2,1)S(1)}, bf16[2,64,1024]{2,1,0:T(8,128)(2,1)S(1)}, u32[]{:S(2)}, u32[]{:S(2)}) collective-permute-start(bf16[2,64,1024]{2,1,0:T(8,128)(2,1)S(1)} %get-tuple-element.132), channel_id=1, source_target_pairs={{0,4},{1,5},{2,6},{3,7},{4,0},{5,1},{6,2},{7,3},{8,12},{9,13},{10,... | collective-permute-start | bytes 786440 | tf_op jit(solution)/shard_map/ppermute | solution.py:469
  36.7 10.0 %collective-permute-start.11 = (bf16[2,64,1024]{2,1,0:T(8,128)(2,1)S(1)}, bf16[2,64,1024]{2,1,0:T(8,128)(2,1)S(1)}, u32[]{:S(2)}, u32[]{:S(2)}) collective-permute-start(bf16[2,64,1024]{2,1,0:T(8,128)(2,1)S(1)} %get-tuple-element.134), channel_id=1, source_target_pairs={{0,12},{1,13},{2,14},{3,15},{4,8},{5,9},{6,10},{7,11},{8,4},{9,5},... | collective-permute-start | bytes 786440 | tf_op jit(solution)/shard_map/ppermute | solution.py:469
  46.7 2.7 %collective-permute-start.12 = (bf16[256,2048]{1,0:T(8,128)(2,1)S(1)}, bf16[256,2048]{1,0:T(8,128)(2,1)S(1)}, u32[]{:S(2)}, u32[]{:S(2)}) collective-permute-start(bf16[256,2048]{1,0:T(8,128)(2,1)S(1)} %get-tuple-element.136), channel_id=1, source_target_pairs={{0,1},{1,0},{2,3},{3,2},{4,5},{5,4},{6,7},{7,6},{8,9},{9,8},{10,11... | collective-permute-start | bytes 3145736 | tf_op jit(solution)/shard_map/ppermute | solution.py:469
  47.4 5.6 %copy-start.5 = (f32[512]{0:T(512)S(1)}, f32[512]{0:T(512)}, u32[]{:S(2)}) copy-start(f32[512]{0:T(512)} %gain.5) | copy-start | bytes 6148
  47.5 5.6 %copy-start.7 = (bf16[288,288]{1,0:T(8,128)(2,1)S(1)}, bf16[288,288]{1,0:T(8,128)(2,1)}, u32[]{:S(2)}) copy-start(bf16[288,288]{1,0:T(8,128)(2,1)} %constant.11.clone.place_t) | copy-start | bytes 497668
  47.5 14.8 %collective-permute-start.18 = (bf16[64,1024]{1,0:T(8,128)(2,1)S(1)}, bf16[64,1024]{1,0:T(8,128)(2,1)S(1)}, u32[]{:S(2)}, u32[]{:S(2)}) collective-permute-start(bf16[64,1024]{1,0:T(8,128)(2,1)S(1)} %get-tuple-element.165), channel_id=1, source_target_pairs={{0,12},{1,13},{2,14},{3,15},{4,8},{5,9},{6,10},{7,11},{8,4},{9,5},... | collective-permute-start | bytes 393224 | tf_op jit(solution)/shard_map/ppermute | solution.py:469
  49.3 13.0 %collective-permute-start.19 = (bf16[64,1024]{1,0:T(8,128)(2,1)S(1)}, bf16[64,1024]{1,0:T(8,128)(2,1)S(1)}, u32[]{:S(2)}, u32[]{:S(2)}) collective-permute-start(bf16[64,1024]{1,0:T(8,128)(2,1)S(1)} %get-tuple-element.167), channel_id=1, source_target_pairs={{0,4},{1,5},{2,6},{3,7},{4,0},{5,1},{6,2},{7,3},{8,12},{9,13},{10,... | collective-permute-start | bytes 393224 | tf_op jit(solution)/shard_map/ppermute | solution.py:469
  49.5 11.0 %collective-permute-start.13 = (bf16[2,64,1024]{2,1,0:T(8,128)(2,1)S(1)}, bf16[2,64,1024]{2,1,0:T(8,128)(2,1)S(1)}, u32[]{:S(2)}, u32[]{:S(2)}) collective-permute-start(bf16[2,64,1024]{2,1,0:T(8,128)(2,1)S(1)} %get-tuple-element.145), channel_id=1, source_target_pairs={{0,4},{1,5},{2,6},{3,7},{4,0},{5,1},{6,2},{7,3},{8,12},{9,13},{10,... | collective-permute-start | bytes 786440 | tf_op jit(solution)/shard_map/ppermute | solution.py:469
  51.5 9.1 %collective-permute-start.14 = (bf16[2,64,1024]{2,1,0:T(8,128)(2,1)S(1)}, bf16[2,64,1024]{2,1,0:T(8,128)(2,1)S(1)}, u32[]{:S(2)}, u32[]{:S(2)}) collective-permute-start(bf16[2,64,1024]{2,1,0:T(8,128)(2,1)S(1)} %get-tuple-element.147), channel_id=1, source_target_pairs={{0,12},{1,13},{2,14},{3,15},{4,8},{5,9},{6,10},{7,11},{8,4},{9,5},... | collective-permute-start | bytes 786440 | tf_op jit(solution)/shard_map/ppermute | solution.py:469
  60.7 6.3 %collective-permute-start.15 = (bf16[64,1024]{1,0:T(8,128)(2,1)S(1)}, bf16[64,1024]{1,0:T(8,128)(2,1)S(1)}, u32[]{:S(2)}, u32[]{:S(2)}) collective-permute-start(bf16[64,1024]{1,0:T(8,128)(2,1)S(1)} %get-tuple-element.155), channel_id=1, source_target_pairs={{0,12},{1,13},{2,14},{3,15},{4,8},{5,9},{6,10},{7,11},{8,4},{9,5},... | collective-permute-start | bytes 393224 | tf_op jit(solution)/shard_map/ppermute | solution.py:469
  62.3 5.0 %collective-permute-start.16 = (bf16[64,1024]{1,0:T(8,128)(2,1)S(1)}, bf16[64,1024]{1,0:T(8,128)(2,1)S(1)}, u32[]{:S(2)}, u32[]{:S(2)}) collective-permute-start(bf16[64,1024]{1,0:T(8,128)(2,1)S(1)} %get-tuple-element.157), channel_id=1, source_target_pairs={{0,4},{1,5},{2,6},{3,7},{4,0},{5,1},{6,2},{7,3},{8,12},{9,13},{10,... | collective-permute-start | bytes 393224 | tf_op jit(solution)/shard_map/ppermute | solution.py:469
  62.4 8.8 %collective-permute-start.20 = (bf16[32,2048]{1,0:T(8,128)(2,1)S(1)}, bf16[32,2048]{1,0:T(8,128)(2,1)S(1)}, u32[]{:S(2)}, u32[]{:S(2)}) collective-permute-start(bf16[32,2048]{1,0:T(8,128)(2,1)S(1)} %get-tuple-element.169), channel_id=1, source_target_pairs={{0,2},{1,3},{2,0},{3,1},{4,6},{5,7},{6,4},{7,5},{8,10},{9,11},{10,... | collective-permute-start | bytes 393224 | tf_op jit(solution)/shard_map/ppermute | solution.py:469
  67.3 6.4 %collective-permute-start.17 = (bf16[32,2048]{1,0:T(8,128)(2,1)S(1)}, bf16[32,2048]{1,0:T(8,128)(2,1)S(1)}, u32[]{:S(2)}, u32[]{:S(2)}) collective-permute-start(bf16[32,2048]{1,0:T(8,128)(2,1)S(1)} %get-tuple-element.159), channel_id=1, source_target_pairs={{0,2},{1,3},{2,0},{3,1},{4,6},{5,7},{6,4},{7,5},{8,10},{9,11},{10,... | collective-permute-start | bytes 393224 | tf_op jit(solution)/shard_map/ppermute | solution.py:469
  69.7 6.8 %collective-permute-start.21 = (bf16[72,512]{1,0:T(8,128)(2,1)S(1)}, bf16[72,512]{1,0:T(8,128)(2,1)S(1)}, u32[]{:S(2)}, u32[]{:S(2)}) collective-permute-start(bf16[72,512]{1,0:T(8,128)(2,1)S(1)} %get-tuple-element.170), channel_id=1, source_target_pairs={{0,17},{1,18},{2,19},{3,20},{4,21},{5,22},{6,23},{7,24},{8,25},{9,... | collective-permute-start | bytes 221192 | tf_op jit(solution)/shard_map/ppermute | solution.py:479
  69.7 6.8 %collective-permute-start.22 = (bf16[72,512]{1,0:T(8,128)(2,1)S(1)}, bf16[72,512]{1,0:T(8,128)(2,1)S(1)}, u32[]{:S(2)}, u32[]{:S(2)}) collective-permute-start(bf16[72,512]{1,0:T(8,128)(2,1)S(1)} %get-tuple-element.171), channel_id=1, source_target_pairs={{0,1},{1,2},{2,3},{3,4},{4,5},{5,6},{6,7},{7,8},{8,9},{9,10},{10,1... | collective-permute-start | bytes 221192 | tf_op jit(solution)/shard_map/ppermute | solution.py:469
  70.3 6.2 %collective-permute-start.23 = (bf16[72,512]{1,0:T(8,128)(2,1)S(1)}, bf16[72,512]{1,0:T(8,128)(2,1)S(1)}, u32[]{:S(2)}, u32[]{:S(2)}) collective-permute-start(bf16[72,512]{1,0:T(8,128)(2,1)S(1)} %get-tuple-element.172), channel_id=1, source_target_pairs={{0,16},{16,32},{32,48},{48,64},{64,80},{80,96},{96,112},{112,128},... | collective-permute-start | bytes 221192 | tf_op jit(solution)/shard_map/ppermute | solution.py:469
  76.5 19.5 %all-to-all-start = ((bf16[16,2,32,128]{3,2,1,0:T(8,128)(2,1)}), bf16[16,2,32,128]{3,2,1,0:T(8,128)(2,1)S(1)}, u32[]{:S(2)}, u32[]{:S(2)}) async-start(bf16[16,2,32,128]{3,2,1,0:T(8,128)(2,1)} %shard_map.213), calls=%async_computation | async-start | bytes 524288 | tf_op jit(solution)/shard_map/all_to_all | solution.py:639

commit v3 on v2

--- a/solution.py
+++ b/solution.py
@@ -18,6 +18,7 @@
 GROUPS = WIDTH // GROUP
 PER_GROUP = GROUP // HEAD
 ROOT = HEAD**0.5
+SIDE = 2 * WIDTH
 EPS = 1e-05
 NEG = -1000000000.0
 VMEM_LIMIT = 24 * 1024 * 1024
@@ -218,13 +219,17 @@
         ]
 
     left = jnp.concatenate(blocks(normed_t_ref), axis=0)
-    result_ref[:, : 3 * WIDTH] = mm(left, d_packed_ref[...]).astype(BF16)
+    qkv = mm(left, d_packed_ref[...]).astype(BF16)
     total = None
     for window in range(WINDOWS):
         left = jnp.concatenate(blocks(mixed_t_ref, window), axis=0)
         part = mm(left, upstream[window * LENGTH : (window + 1) * LENGTH])
         total = part if total is None else total + part
-    result_ref[:, 3 * WIDTH :] = total.astype(BF16)
+    total = total.astype(BF16)
+    result_ref[:, :768] = qkv[:, :768]
+    result_ref[:, 768:SIDE] = total[:, :256]
+    result_ref[:, SIDE : SIDE + 768] = qkv[:, 768:]
+    result_ref[:, SIDE + 768 :] = total[:, 256:]
 
 
 def load_grid(ref, place, spare_ref):
@@ -385,23 +390,39 @@
     store_grid(advanced, place_t[...], (middle[...].astype(F32) + delta).astype(BF16))
 
 
-def kernel_first_sum(keep, got, send_one, send_two, keep_one, keep_two):
-    y = lax.axis_index("lat") // 4
-    half = 2 * WIDTH
-
-    def put(target, place, block, columns):
-        rows = pl.ds(pl.multiple_of(block * 64, 64), 64)
-        target[place] = keep[rows, columns] + got[rows, columns]
-
-    one, two = slice(0, half), slice(half, 2 * half)
-    put(send_one, 0, y ^ 1, one)
-    put(send_one, 1, y ^ 2, one)
-    put(send_two, 0, y ^ 3, two)
-    put(send_two, 1, y ^ 2, two)
-    put(keep_one, 0, y, one)
-    put(keep_one, 1, y ^ 3, one)
-    put(keep_two, 0, y, two)
-    put(keep_two, 1, y ^ 1, two)
+def rows_of(block, count):
+    return pl.ds(pl.multiple_of(block * count, count), count)
+
+
+def place_x():
+    return lax.axis_index("lon") // 8 * 2 + lax.axis_index("lat") // 2 % 2
+
+
+def place_y():
+    return lax.axis_index("lat") // 4
+
+
+def kernel_first_sum_a(keep, got, send_one, send_two, keep_one, keep_two):
+    y = place_y()
+    for side, first, send, kept in ((0, 1, send_one, keep_one), (1, 3, send_two, keep_two)):
+        columns = slice(side * SIDE, (side + 1) * SIDE)
+        for target, place, block in (
+            (send, 0, y ^ first), (send, 1, y ^ 2), (kept, 0, y), (kept, 1, y ^ 2 ^ first)
+        ):
+            rows = rows_of(block, 64)
+            target[place] = keep[rows, columns] + got[rows, columns]
+
+
+def kernel_first_sum_b(keep, got, send_one, send_two, keep_one, keep_two):
+    x = place_x()
+    for part, first, send, kept in ((0, 1, send_one, keep_one), (1, 3, send_two, keep_two)):
+        for target, place, block in (
+            (send, 0, x ^ first), (send, 1, x ^ 2), (kept, 0, x), (kept, 1, x ^ 2 ^ first)
+        ):
+            columns = rows_of(block // 2, SIDE)
+            for inner in range(2):
+                rows = rows_of((part * 2 + inner) * 2 + block % 2, 32)
+                target[place, inner * 32 : (inner + 1) * 32] = keep[rows, columns] + got[rows, columns]
 
 
 def kernel_second_sum(keep_one, got_one, keep_two, got_two, send_one, send_two, held_one, held_two):
@@ -411,28 +432,58 @@
     held_two[...] = keep_two[0] + got_two[0]
 
 
-def kernel_third_sum(held_one, got_one, held_two, got_two, send, keep):
-    near = lax.axis_index("lat") // 2 % 2
-    half = 2 * WIDTH
-    for target, place in ((send, 1 - near), (keep, near)):
-        rows = pl.ds(pl.multiple_of(place * 32, 32), 32)
-        target[:, :half] = held_one[rows] + got_one[rows]
-        target[:, half:] = held_two[rows] + got_two[rows]
-
-
-def kernel_columns(keep_a, got_a, keep_b, got_b, result):
-    for at, (keep, got) in enumerate(((keep_a, got_a), (keep_b, got_b))):
-        total = keep[...].astype(F32) + got[...].astype(F32)
-        for block in range(16):
+def third_sum(at, halves, send, keep):
+    for target, place, block in ((send, 0, at ^ 1), (send, 1, at ^ 2), (keep, 0, at), (keep, 1, at ^ 3)):
+        rows = rows_of(block % 2, 32)
+        for half, (held, got) in enumerate(halves):
+
+            @pl.when(block // 2 == half)
+            def _(target=target, place=place, rows=rows, held=held, got=got):
+                target[place] = held[rows, :] + got[rows, :]
+
+
+def kernel_third_sum_a(held_one, got_one, held_two, got_two, send, keep):
+    third_sum(place_x(), ((held_one, got_one), (held_two, got_two)), send, keep)
+
+
+def kernel_third_sum_b(held_one, got_one, held_two, got_two, send, keep):
+    third_sum(place_y(), ((held_one, got_one), (held_two, got_two)), send, keep)
+
+
+def kernel_halve(keep, got, send, held):
+    half = keep.shape[0] // 2
+    held[...] = keep[:half] + got[:half]
+    send[...] = keep[half:] + got[half:]
+
+
+def z_partner(z, step):
+    if step == 0:
+        return z ^ 1
+    if step == 1:
+        return (z + 2 * (z & 1) + 7) & 7
+    return z ^ (3 + 4 * (((z + 1) >> 1) & 1))
+
+
+def z_blocks(z):
+    other = z_partner(z, 1)
+    return z, z_partner(z, 2), other, z_partner(other, 2)
+
+
+def kernel_columns(keep_a, got_a, keep_b, got_b, send, keep, blocks):
+    for at, (held, got) in enumerate(((keep_a, got_a), (keep_b, got_b))):
+        total = held[0].astype(F32) + got[0].astype(F32)
+        for block in range(8):
             qkv = total[:, block * 96 : (block + 1) * 96]
-            out = total[:, 3 * WIDTH + block * 32 : 3 * WIDTH + (block + 1) * 32]
-            result[block, at] = jnp.concatenate([qkv, out], axis=1).astype(BF16)
-
-
-def kernel_total(parts, qkv_a, out_a, qkv_b, out_b):
-    total = parts[0].astype(F32)
-    for at in range(1, 16):
-        total = total + parts[at].astype(F32)
+            out = total[:, 768 + block * 32 : 768 + (block + 1) * 32]
+            blocks[block, at] = jnp.concatenate([qkv, out], axis=1).astype(BF16)
+    z = lax.axis_index("lon") % 8
+    for target, owner in ((send, z_partner(z, 0)), (keep, z)):
+        for at, block in enumerate(z_blocks(owner)):
+            target[at] = blocks[block]
+
+
+def kernel_total(keep, got, qkv_a, out_a, qkv_b, out_b):
+    total = keep[0].astype(F32) + got[0].astype(F32)
     for at, (qkv, out) in enumerate(((qkv_a, out_a), (qkv_b, out_b))):
         qkv[...] = total[at, :, :96]
         out[...] = total[at, :, 96:]
@@ -479,34 +530,39 @@
     return lax.ppermute(array, ("lon", "lat"), pairs)
 
 
-def first_round(send, keep):
-    return keep, permute(send, "lat", lambda i: i ^ 1)
-
-
-def first_sum(keep, got):
-    return call(kernel_first_sum, [((2, 64, 2 * WIDTH), BF16)] * 4, [], (keep, got))
-
-
-def second_round(send_one, send_two, keep_one, keep_two):
-    got_one = permute(send_one, "lat", lambda i: i ^ 4)
-    got_two = permute(send_two, "lat", lambda i: i ^ 12)
-    return keep_one, got_one, keep_two, got_two
-
-
-def second_sum(*parts):
-    return call(kernel_second_sum, [((64, 2 * WIDTH), BF16)] * 4, [], parts)
-
-
-def third_round(send_one, send_two, held_one, held_two):
-    got_one = permute(send_one, "lat", lambda i: i ^ 12)
-    got_two = permute(send_two, "lat", lambda i: i ^ 4)
-    return held_one, got_one, held_two, got_two
-
-
-def fourth_round(*parts):
-    rows = ((32, 4 * WIDTH), BF16)
-    send, keep = call(kernel_third_sum, [rows] * 2, [], parts)
-    return keep, permute(send, "lat", lambda i: i ^ 2)
+def to_core(array):
+    return permute(array, "lat", lambda i: i ^ 1)
+
+
+def to_y(array, by):
+    return permute(array, "lat", lambda i: i ^ (4 * by))
+
+
+def to_x(array, by):
+    if by == 1:
+        return permute(array, "lat", lambda i: i ^ 2)
+    lons, lats = lax.axis_size("lon"), lax.axis_size("lat")
+    pairs = [
+        (lon * lats + lat, (lon ^ 8) * lats + (lat ^ 2)) for lon in range(lons) for lat in range(lats)
+    ]
+    return lax.ppermute(array, ("lon", "lat"), pairs)
+
+
+def to_z(array, step):
+    return permute(array, "lon", lambda i: i & 8 | z_partner(i & 7, step))
+
+
+def quarters(kernel, keep, got):
+    return call(kernel, [((2, 64, SIDE), BF16)] * 4, [], (keep, got))
+
+
+def second_sum(parts):
+    return call(kernel_second_sum, [((64, SIDE), BF16)] * 4, [], parts)
+
+
+def halve(keep, got):
+    shape = (keep.shape[0] // 2,) + keep.shape[1:]
+    return call(kernel_halve, [(shape, BF16)] * 2, [], (keep, got))
 
 
 def body(
@@ -586,9 +642,11 @@
         kernel_grads_b, [half_grads] * 2, [normed_t], (normed_b, mixed_b, upstream_b, d_packed_b),
         flops=2 * 10**9,
     )
-    sums_b = first_sum(*first_round(send_b, keep_b))
-    sums_b, d0 = lax.optimization_barrier((sums_b, d0))
-    rounds_b = second_round(*sums_b)
+    send_one_b, send_two_b, keep_one_b, keep_two_b = quarters(
+        kernel_first_sum_b, keep_b, to_core(send_b)
+    )
+    send_one_b, send_two_b, d0 = lax.optimization_barrier((send_one_b, send_two_b, d0))
+    parts_b = (keep_one_b, to_x(send_one_b, 1), keep_two_b, to_x(send_two_b, 3))
     grad_middle, d_packed_a, send_a = call(
         kernel_backward_a,
         [token, packed, half_grads],
@@ -599,16 +657,18 @@
         ),
         flops=5 * 10**9,
     )
-    rounds_b, send_a = lax.optimization_barrier((rounds_b, send_a))
-    sums_b = second_sum(*rounds_b)
-    rounds_b = third_round(*sums_b)
+    parts_b, send_a = lax.optimization_barrier((parts_b, send_a))
+    send_one_b, send_two_b, held_one_b, held_two_b = second_sum(parts_b)
+    parts_b = (held_one_b, to_x(send_one_b, 3), held_two_b, to_x(send_two_b, 1))
     keep_a = call(
         kernel_keep_a, [half_grads], [], (normed_a_t, mixed_a, grad_middle, d_packed_a),
         flops=10**9,
     )[0]
-    sums_a = first_sum(*first_round(send_a, keep_a))
-    sums_a, b1, b2, b3, d_packed_a = lax.optimization_barrier((sums_a, b1, b2, b3, d_packed_a))
-    rounds_a = second_round(*sums_a)
+    send_one_a, send_two_a, keep_one_a, keep_two_a = quarters(
+        kernel_first_sum_a, keep_a, to_core(send_a)
+    )
+    send_one_a, send_two_a, d_packed_a = lax.optimization_barrier((send_one_a, send_two_a, d_packed_a))
+    parts_a = (keep_one_a, to_y(send_one_a, 1), keep_two_a, to_y(send_two_a, 3))
     grad_fields = call(
         kernel_finish_a,
         [grid],
@@ -616,18 +676,29 @@
         (inputs_a, grad_middle, gain_a, qkv_weight_a, d_packed_a, place_t),
         hbm=(3,), copies=1, flops=4 * 10**9, final=(0,),
     )[0]
+    pair = ((2, 32, SIDE), BF16)
+    send_b, keep_b = call(kernel_third_sum_b, [pair] * 2, [], parts_b)
+    got_b = to_y(send_b, 1)
+    send_one_a, send_two_a, held_one_a, held_two_a = second_sum(parts_a)
+    send_one_a, send_two_a, grad_fields, b1, b2, b3 = lax.optimization_barrier(
+        (send_one_a, send_two_a, grad_fields, b1, b2, b3)
+    )
+    parts_a = (held_one_a, to_y(send_one_a, 3), held_two_a, to_y(send_two_a, 1))
     delta_diagonal = permute_both(b3, 1)
     delta_above = permute(b2, "lat", lambda i: i + 1)
     delta_western = permute(b1, "lon", lambda i: i + 1)
-    sums_a = second_sum(*rounds_a)
-    sums_a, grad_fields = lax.optimization_barrier((sums_a, grad_fields))
-    rounds_b = fourth_round(*rounds_b)
-    rounds_a = fourth_round(*third_round(*sums_a))
-    blocks = call(
-        kernel_columns, [((16, 2, 32, GROUP), BF16)], [], rounds_a + rounds_b, final=(0,)
-    )[0]
-    blocks, delta_diagonal, delta_above, delta_western = lax.optimization_barrier(
-        (blocks, delta_diagonal, delta_above, delta_western)
+    send_a, keep_a = call(kernel_third_sum_a, [pair] * 2, [], parts_a)
+    got_a = to_x(send_a, 1)
+    send_b, keep_b = halve(keep_b, got_b)
+    got_b = to_y(send_b, 3)
+    send_a, keep_a = halve(keep_a, got_a)
+    got_a = to_x(send_a, 3)
+    four = ((4, 2, 32, GROUP), BF16)
+    got_b, delta_diagonal, delta_above, delta_western = lax.optimization_barrier(
+        (got_b, delta_diagonal, delta_above, delta_western)
+    )
+    send, keep = call(
+        kernel_columns, [four] * 2, [((8, 2, 32, GROUP), BF16)], (keep_a, got_a, keep_b, got_b)
     )
     advanced = call(
         kernel_advanced,
@@ -636,12 +707,13 @@
         (delta_diagonal, delta_above, delta_western, b0, middle_a, place_t, sort_t),
         flops=10**9, final=(0,),
     )[0]
-    blocks = lax.all_to_all(blocks, "lon", 0, 0, tiled=True)
+    send, keep = halve(keep, to_z(send, 0))
+    send, keep = halve(keep, to_z(send, 1))
     grads = call(
         kernel_total,
         [((32, 96), F32), ((32, 32), F32)] * 2,
         [],
-        (blocks,),
+        (keep, to_z(send, 2)),
         final=(0, 1, 2, 3),
     )
     return (advanced.transpose(2, 0, 1, 3), grad_fields.transpose(2, 0, 1, 3), *grads)

time: 97.1 us -> 98.6 us (1.015)
  the two profiles are of different devices: /device:TPU:32 before, /device:TPU:6 now
where the time goes in v3:
time: 98.6 us; the launch traced here: 98.4 us
  starting transfers between devices  37.8 us (38%)
  Pallas kernels  29.9 us (30%)
  waiting for transfers between devices  29.7 us (30%)
    pallas_call x21, Pallas kernels, call(): pl.pallas_call(kernel, out_shape=tuple((jax.ShapeDtypeStruct(shape, kind)...  29.9 us
    ppermute x22, starting transfers between devices, permute(): lax.ppermute(array, axis, [(i, target(i) % length) for i in range(length)])  29 us
    ppermute x22, waiting for transfers between devices, permute(): lax.ppermute(array, axis, [(i, target(i) % length) for i in range(length)])  23.3 us
    ppermute x3, starting transfers between devices, to_x(): return lax.ppermute(array, ('lon', 'lat'), pairs)  6.4 us
    ppermute x4, waiting for transfers between devices, permute_both(): return lax.ppermute(array, ('lon', 'lat'), pairs)  3.21 us
    ppermute x3, waiting for transfers between devices, to_x(): return lax.ppermute(array, ('lon', 'lat'), pairs)  3.16 us
    ppermute x4, starting transfers between devices, permute_both(): return lax.ppermute(array, ('lon', 'lat'), pairs)  2.35 us
  transfers between devices with their start and end apart: 29, of which 15 were waited for; matrix products, arithmetic and copies ran while one was open for 0% of the time, Pallas kernels for 17%

profile of v3, /device:TPU:6, one launch (start us, length us, event | category | flops | bytes accessed | tf_op | source)
XLA Modules:
  0.0 98.4 jit_solution(3105537548368252890)
XLA Ops:
  0.6 0.0 copy-start.8
  0.7 0.0 copy-start.9
  0.7 0.0 copy-start.10
  0.7 6.5 %shard_map.199 = (bf16[72,512]{1,0:T(8,128)(2,1)S(1)}, bf16[72,512]{1,0:T(8,128)(2,1)S(1)}, bf16[72,512]{1,0:T(8,128)(2,1)S(1)}, bf16[72,512]{1,0:T(8,128)(2,1)S...) custom-call(bf16[12,6,4,512]{3,2,1,0:T(4,128)(2,1)} %bitcast.6, ...), custom_call_target="tpu_custom_call" | custom-call | flops 7000000000 | bytes 1048576 | tf_op jit(solution)/shard_map/pallas_call | solution.py:504
  7.2 6.8 %collective-permute-start = (bf16[72,512]{1,0:T(8,128)(2,1)S(1)}, bf16[72,512]{1,0:T(8,128)(2,1)S(1)}, u32[]{:S(2)}, u32[]{:S(2)}) collective-permute-start(bf16[72,512]{1,0:T(8,128)(2,1)S(1)} %get-tuple-element.100), channel_id=1, source_target_pairs={{0,240},{16,0},{32,16},{48,32},{64,48},{80,64},{96,80},{112,96},{1... | collective-permute-start | bytes 221192 | tf_op jit(solution)/shard_map/ppermute | solution.py:520
  14.0 0.2 collective-permute-start.2
  14.2 0.0 copy-start
  14.2 0.0 copy-start.1
  14.2 0.0 copy-start.4
  14.2 0.0 copy-start.6
  14.2 2.9 %shard_map.200 = (bf16[72,512]{1,0:T(8,128)(2,1)S(1)}, bf16[72,512]{1,0:T(8,128)(2,1)S(1)}, bf16[72,512]{1,0:T(8,128)(2,1)S(1)}, bf16[72,512]{1,0:T(8,128)(2,1)S...) custom-call(bf16[12,6,4,512]{3,2,1,0:T(4,128)(2,1)} %bitcast.7, ...), custom_call_target="tpu_custom_call" | custom-call | flops 2000000000 | bytes 1048576 | tf_op jit(solution)/shard_map/pallas_call | solution.py:504
  17.2 2.0 %collective-permute-start.3 = (bf16[72,512]{1,0:T(8,128)(2,1)S(1)}, bf16[72,512]{1,0:T(8,128)(2,1)S(1)}, u32[]{:S(2)}, u32[]{:S(2)}) collective-permute-start(bf16[72,512]{1,0:T(8,128)(2,1)S(1)} %get-tuple-element.109), channel_id=1, source_target_pairs={{0,240},{16,0},{32,16},{48,32},{64,48},{80,64},{96,80},{112,96},{1... | collective-permute-start | bytes 221192 | tf_op jit(solution)/shard_map/ppermute | solution.py:520
  19.1 2.4 %collective-permute-start.4 = (bf16[72,512]{1,0:T(8,128)(2,1)S(1)}, bf16[72,512]{1,0:T(8,128)(2,1)S(1)}, u32[]{:S(2)}, u32[]{:S(2)}) collective-permute-start(bf16[72,512]{1,0:T(8,128)(2,1)S(1)} %get-tuple-element.110), channel_id=1, source_target_pairs={{0,15},{1,0},{2,1},{3,2},{4,3},{5,4},{6,5},{7,6},{8,7},{9,8},{10,9... | collective-permute-start | bytes 221192 | tf_op jit(solution)/shard_map/ppermute | solution.py:520
  21.5 1.2 %collective-permute-start.5 = (bf16[72,512]{1,0:T(8,128)(2,1)S(1)}, bf16[72,512]{1,0:T(8,128)(2,1)S(1)}, u32[]{:S(2)}, u32[]{:S(2)}) collective-permute-start(bf16[72,512]{1,0:T(8,128)(2,1)S(1)} %get-tuple-element.111), channel_id=1, source_target_pairs={{0,255},{1,240},{2,241},{3,242},{4,243},{5,244},{6,245},{7,246},{8... | collective-permute-start | bytes 221192 | tf_op jit(solution)/shard_map/ppermute | solution.py:530
  22.8 3.8 %shard_map.201 = (bf16[72,512]{1,0:T(8,128)(2,1)S(1)}, bf16[72,512]{1,0:T(8,128)(2,1)S(1)}, bf16[72,512]{1,0:T(8,128)(2,1)S(1)}, bf16[72,512]{1,0:T(8,128)(2,1)S...) custom-call(bf16[72,512]{1,0:T(8,128)(2,1)S(1)} %get-tuple-element.9, ...), custom_call_target="tpu_custom_call" | custom-call | flops 5000000000 | bytes 1048576 | tf_op jit(solution)/shard_map/pallas_call | solution.py:504
  26.6 4.5 %shard_map.202 = (bf16[72,512]{1,0:T(8,128)(2,1)S(1)}, bf16[72,512]{1,0:T(8,128)(2,1)S(1)}, bf16[72,512]{1,0:T(8,128)(2,1)S(1)}, bf16[72,512]{1,0:T(8,128)(2,1)S...) custom-call(bf16[72,512]{1,0:T(8,128)(2,1)S(1)} %get-tuple-element.108.piece0, ...), custom_call_target="tpu_custom_call" | custom-call | flops 5000000000 | bytes 1048576 | tf_op jit(solution)/shard_map/pallas_call | solution.py:504
  31.1 0.0 copy-start.2
  31.1 1.3 %shard_map.203 = (bf16[256,2048]{1,0:T(8,128)(2,1)S(1)}, bf16[256,2048]{1,0:T(8,128)(2,1)S(1)}) custom-call(bf16[288,512]{1,0:T(8,128)(2,1)S(1)} %get-tuple-element.106.normed, bf16[2,512,144]{2,1,0:T(8,128)(2,1)S(1)} %get-tuple-element.107.mixed_t, bf16[288,512]{1,0:T(8,128)(2,1)S(1)} %get-tuple-element.115.upstream, ...), custom_call_target="tpu_custom_call" | custom-call | flops 2000000000 | bytes 1048576 | tf_op jit(solution)/shard_map/pallas_call | solution.py:504
  32.5 0.6 collective-permute-start.6
  33.1 0.9 collective-permute-start.9
  34.0 0.7 collective-permute-start.11
  34.7 0.6 collective-permute-done.6.got
  35.3 0.1 shard_map.204
  35.4 1.0 %collective-permute-start.7 = (bf16[2,64,1024]{2,1,0:T(8,128)(2,1)S(1)}, bf16[2,64,1024]{2,1,0:T(8,128)(2,1)S(1)}, u32[]{:S(2)}, u32[]{:S(2)}) collective-permute-start(bf16[2,64,1024]{2,1,0:T(8,128)(2,1)S(1)} %get-tuple-element.123), channel_id=1, source_target_pairs={{0,2},{1,3},{2,0},{3,1},{4,6},{5,7},{6,4},{7,5},{8,10},{9,11},{10,... | collective-permute-start | bytes 786440 | tf_op jit(solution)/shard_map/ppermute | solution.py:520
  36.4 2.0 %collective-permute-start.8 = (bf16[2,64,1024]{2,1,0:T(8,128)(2,1)S(1)}, bf16[2,64,1024]{2,1,0:T(8,128)(2,1)S(1)}, u32[]{:S(2)}, u32[]{:S(2)}) collective-permute-start(bf16[2,64,1024]{2,1,0:T(8,128)(2,1)S(1)} %get-tuple-element.125), channel_id=1, source_target_pairs={{0,130},{1,131},{2,128},{3,129},{4,134},{5,135},{6,132},{7,133},{8... | collective-permute-start | bytes 786440 | tf_op jit(solution)/shard_map/ppermute | solution.py:548
  38.5 2.7 %collective-permute-done.9.back0 = bf16[72,512]{1,0:T(8,128)(2,1)S(1)} collective-permute-done((bf16[72,512]{1,0:T(8,128)(2,1)S(1)}, bf16[72,512]{1,0:T(8,128)(2,1)S(1)}, u32[]{:S(2)}, u32[]{:S(2)}) %collective-permute-start.9) | collective-permute-done | bytes 73760 | tf_op jit(solution)/shard_map/ppermute | solution.py:530
  41.2 1.6 %collective-permute-done.11.back2 = bf16[72,512]{1,0:T(8,128)(2,1)S(1)} collective-permute-done((bf16[72,512]{1,0:T(8,128)(2,1)S(1)}, bf16[72,512]{1,0:T(8,128)(2,1)S(1)}, u32[]{:S(2)}, u32[]{:S(2)}) %collective-permute-start.11) | collective-permute-done | bytes 73760 | tf_op jit(solution)/shard_map/ppermute | solution.py:520
  42.8 4.2 %shard_map.205 = (bf16[288,512]{1,0:T(8,128)(2,1)S(1)}, bf16[288,1536]{1,0:T(8,128)(2,1)S(1)}, bf16[256,2048]{1,0:T(8,128)(2,1)S(1)}) custom-call(bf16[72,512]{1,0:T(8,128)(2,1)S(1)} %collective-permute-done.9.back0, bf16[72,512]{1,0:T(8,128)(2,1)S(1)} %collective-permute-done.10.back1, bf16[72,512]{1,0:T(8,128)(2,1)S(1)} %collective-permute-done.11.back2, ...), custom_call_target="tpu_custom_call" | custom-call | flops 5000000000 | bytes 1048576 | tf_op jit(solution)/shard_map/pallas_call | solution.py:504
  47.0 1.3 %collective-permute-done.8.got_two = bf16[2,64,1024]{2,1,0:T(8,128)(2,1)S(1)} collective-permute-done((bf16[2,64,1024]{2,1,0:T(8,128)(2,1)S(1)}, bf16[2,64,1024]{2,1,0:T(8,128)(2,1)S(1)}, u32[]{:S(2)}, u32[]{:S(2)}) %collective-permute-start.8) | collective-permute-done | bytes 262176 | tf_op jit(solution)/shard_map/ppermute | solution.py:548
  48.3 0.0 collective-permute-start.16
  48.3 0.7 shard_map.209.keep
  49.0 0.0 copy-start.5
  49.0 0.0 copy-start.7
  49.1 0.1 shard_map.206
  49.1 2.6 %collective-permute-start.12 = (bf16[64,1024]{1,0:T(8,128)(2,1)S(1)}, bf16[64,1024]{1,0:T(8,128)(2,1)S(1)}, u32[]{:S(2)}, u32[]{:S(2)}) collective-permute-start(bf16[64,1024]{1,0:T(8,128)(2,1)S(1)} %get-tuple-element.141), channel_id=1, source_target_pairs={{0,130},{1,131},{2,128},{3,129},{4,134},{5,135},{6,132},{7,133},{8... | collective-permute-start | bytes 393224 | tf_op jit(solution)/shard_map/ppermute | solution.py:548
  51.7 0.1 shard_map.210
  51.9 1.0 %collective-permute-start.17 = (bf16[2,64,1024]{2,1,0:T(8,128)(2,1)S(1)}, bf16[2,64,1024]{2,1,0:T(8,128)(2,1)S(1)}, u32[]{:S(2)}, u32[]{:S(2)}) collective-permute-start(bf16[2,64,1024]{2,1,0:T(8,128)(2,1)S(1)} %get-tuple-element.153), channel_id=1, source_target_pairs={{0,4},{1,5},{2,6},{3,7},{4,0},{5,1},{6,2},{7,3},{8,12},{9,13},{10,... | collective-permute-start | bytes 786440 | tf_op jit(solution)/shard_map/ppermute | solution.py:520
  52.9 2.1 %collective-permute-start.18 = (bf16[2,64,1024]{2,1,0:T(8,128)(2,1)S(1)}, bf16[2,64,1024]{2,1,0:T(8,128)(2,1)S(1)}, u32[]{:S(2)}, u32[]{:S(2)}) collective-permute-start(bf16[2,64,1024]{2,1,0:T(8,128)(2,1)S(1)} %get-tuple-element.155), channel_id=1, source_target_pairs={{0,12},{1,13},{2,14},{3,15},{4,8},{5,9},{6,10},{7,11},{8,4},{9,5},... | collective-permute-start | bytes 786440 | tf_op jit(solution)/shard_map/ppermute | solution.py:520
  54.9 3.3 %shard_map.212 = bf16[12,6,4,512]{3,2,1,0:T(4,128)(2,1)} custom-call(bf16[288,512]{1,0:T(8,128)(2,1)S(1)} %get-tuple-element.158.inputs, bf16[288,512]{1,0:T(8,128)(2,1)S(1)} %get-tuple-element.147.grad_middle, f32[512]{0:T(512)S(1)} %copy-done.5, bf16[512,1536]{1,0:T(8,128)(2,1)} %qkv_hbm.3, bf16[288,1536]{1,0:T(8,128)(2,1)S(1)} %get-tuple-element.159.d_packed, ...), custom_call_target="tpu_custom_call" | custom-call | flops 4000000000 | bytes 1048576 | tf_op jit(solution)/shard_map/pallas_call | solution.py:504
  58.2 2.1 %collective-permute-done.17.got_one = bf16[2,64,1024]{2,1,0:T(8,128)(2,1)S(1)} collective-permute-done((bf16[2,64,1024]{2,1,0:T(8,128)(2,1)S(1)}, bf16[2,64,1024]{2,1,0:T(8,128)(2,1)S(1)}, u32[]{:S(2)}, u32[]{:S(2)}) %collective-permute-start.17) | collective-permute-done | bytes 262176 | tf_op jit(solution)/shard_map/ppermute | solution.py:520
  60.3 1.8 %collective-permute-done.18.got_two = bf16[2,64,1024]{2,1,0:T(8,128)(2,1)S(1)} collective-permute-done((bf16[2,64,1024]{2,1,0:T(8,128)(2,1)S(1)}, bf16[2,64,1024]{2,1,0:T(8,128)(2,1)S(1)}, u32[]{:S(2)}, u32[]{:S(2)}) %collective-permute-start.18) | collective-permute-done | bytes 262176 | tf_op jit(solution)/shard_map/ppermute | solution.py:520
  62.2 0.1 shard_map.211
  62.3 2.2 %collective-permute-start.22 = (bf16[64,1024]{1,0:T(8,128)(2,1)S(1)}, bf16[64,1024]{1,0:T(8,128)(2,1)S(1)}, u32[]{:S(2)}, u32[]{:S(2)}) collective-permute-start(bf16[64,1024]{1,0:T(8,128)(2,1)S(1)} %get-tuple-element.173), channel_id=1, source_target_pairs={{0,12},{1,13},{2,14},{3,15},{4,8},{5,9},{6,10},{7,11},{8,4},{9,5},... | collective-permute-start | bytes 393224 | tf_op jit(solution)/shard_map/ppermute | solution.py:520
  64.4 0.1 shard_map.207
  64.6 2.1 %collective-permute-start.14 = (bf16[2,32,1024]{2,1,0:T(8,128)(2,1)S(1)}, bf16[2,32,1024]{2,1,0:T(8,128)(2,1)S(1)}, u32[]{:S(2)}, u32[]{:S(2)}) collective-permute-start(bf16[2,32,1024]{2,1,0:T(8,128)(2,1)S(1)} %get-tuple-element.145), channel_id=1, source_target_pairs={{0,4},{1,5},{2,6},{3,7},{4,0},{5,1},{6,2},{7,3},{8,12},{9,13},{10,... | collective-permute-start | bytes 393224 | tf_op jit(solution)/shard_map/ppermute | solution.py:520
  66.6 1.9 %collective-permute-done.22.got_one = bf16[64,1024]{1,0:T(8,128)(2,1)S(1)} collective-permute-done((bf16[64,1024]{1,0:T(8,128)(2,1)S(1)}, bf16[64,1024]{1,0:T(8,128)(2,1)S(1)}, u32[]{:S(2)}, u32[]{:S(2)}) %collective-permute-start.22) | collective-permute-done | bytes 131104 | tf_op jit(solution)/shard_map/ppermute | solution.py:520
  68.5 1.5 %collective-permute-done.23.got_two = bf16[64,1024]{1,0:T(8,128)(2,1)S(1)} collective-permute-done((bf16[64,1024]{1,0:T(8,128)(2,1)S(1)}, bf16[64,1024]{1,0:T(8,128)(2,1)S(1)}, u32[]{:S(2)}, u32[]{:S(2)}) %collective-permute-start.23) | collective-permute-done | bytes 131104 | tf_op jit(solution)/shard_map/ppermute | solution.py:520
  70.0 0.1 shard_map.214
  70.1 1.5 %collective-permute-start.24 = (bf16[2,32,1024]{2,1,0:T(8,128)(2,1)S(1)}, bf16[2,32,1024]{2,1,0:T(8,128)(2,1)S(1)}, u32[]{:S(2)}, u32[]{:S(2)}) collective-permute-start(bf16[2,32,1024]{2,1,0:T(8,128)(2,1)S(1)} %get-tuple-element.177), channel_id=1, source_target_pairs={{0,2},{1,3},{2,0},{3,1},{4,6},{5,7},{6,4},{7,5},{8,10},{9,11},{10,... | collective-permute-start | bytes 393224 | tf_op jit(solution)/shard_map/ppermute | solution.py:520
  71.7 2.8 %collective-permute-start.15 = (bf16[1,32,1024]{2,1,0:T(8,128)(2,1)S(1)}, bf16[1,32,1024]{2,1,0:T(8,128)(2,1)S(1)}, u32[]{:S(2)}, u32[]{:S(2)}) collective-permute-start(bf16[1,32,1024]{2,1,0:T(8,128)(2,1)S(1)} %get-tuple-element.146), channel_id=1, source_target_pairs={{0,12},{1,13},{2,14},{3,15},{4,8},{5,9},{6,10},{7,11},{8,4},{9,5},... | collective-permute-start | bytes 196616 | tf_op jit(solution)/shard_map/ppermute | solution.py:520
  74.4 2.2 %collective-permute-done.24.got = bf16[2,32,1024]{2,1,0:T(8,128)(2,1)S(1)} collective-permute-done((bf16[2,32,1024]{2,1,0:T(8,128)(2,1)S(1)}, bf16[2,32,1024]{2,1,0:T(8,128)(2,1)S(1)}, u32[]{:S(2)}, u32[]{:S(2)}) %collective-permute-start.24) | collective-permute-done | bytes 131104 | tf_op jit(solution)/shard_map/ppermute | solution.py:520
  76.7 1.8 %collective-permute-start.25 = (bf16[1,32,1024]{2,1,0:T(8,128)(2,1)S(1)}, bf16[1,32,1024]{2,1,0:T(8,128)(2,1)S(1)}, u32[]{:S(2)}, u32[]{:S(2)}) collective-permute-start(bf16[1,32,1024]{2,1,0:T(8,128)(2,1)S(1)} %get-tuple-element.179), channel_id=1, source_target_pairs={{0,130},{1,131},{2,128},{3,129},{4,134},{5,135},{6,132},{7,133},{8... | collective-permute-start | bytes 196616 | tf_op jit(solution)/shard_map/ppermute | solution.py:548
  78.4 0.5 collective-permute-done.19.back0
  78.9 1.5 %collective-permute-done.21.back2 = bf16[72,512]{1,0:T(8,128)(2,1)S(1)} collective-permute-done((bf16[72,512]{1,0:T(8,128)(2,1)S(1)}, bf16[72,512]{1,0:T(8,128)(2,1)S(1)}, u32[]{:S(2)}, u32[]{:S(2)}) %collective-permute-start.21) | collective-permute-done | bytes 73760 | tf_op jit(solution)/shard_map/ppermute | solution.py:520
  80.4 1.9 %collective-permute-done.25.got_a = bf16[1,32,1024]{2,1,0:T(8,128)(2,1)S(1)} collective-permute-done((bf16[1,32,1024]{2,1,0:T(8,128)(2,1)S(1)}, bf16[1,32,1024]{2,1,0:T(8,128)(2,1)S(1)}, u32[]{:S(2)}, u32[]{:S(2)}) %collective-permute-start.25) | collective-permute-done | bytes 65568 | tf_op jit(solution)/shard_map/ppermute | solution.py:548
  82.2 0.1 shard_map.216
  82.4 0.1 collective-permute-start.26
  82.5 4.3 %collective-permute-done.26.got = bf16[4,2,32,128]{3,2,1,0:T(8,128)(2,1)S(1)} collective-permute-done((bf16[4,2,32,128]{3,2,1,0:T(8,128)(2,1)S(1)}, bf16[4,2,32,128]{3,2,1,0:T(8,128)(2,1)S(1)}, u32[]{:S(2)}, u32[]{:S(2)}) %collective-permute-start.26) | collective-permute-done | bytes 65568 | tf_op jit(solution)/shard_map/ppermute | solution.py:520
  86.8 2.4 %collective-permute-start.27 = (bf16[2,2,32,128]{3,2,1,0:T(8,128)(2,1)S(1)}, bf16[2,2,32,128]{3,2,1,0:T(8,128)(2,1)S(1)}, u32[]{:S(2)}, u32[]{:S(2)}) collective-permute-start(bf16[2,2,32,128]{3,2,1,0:T(8,128)(2,1)S(1)} %get-tuple-element.185), channel_id=1, source_target_pairs={{0,112},{16,32},{32,16},{48,64},{64,48},{80,96},{96,80},{112,0},{1... | collective-permute-start | bytes 98312 | tf_op jit(solution)/shard_map/ppermute | solution.py:520
  89.1 3.0 %collective-permute-done.27.got = bf16[2,2,32,128]{3,2,1,0:T(8,128)(2,1)S(1)} collective-permute-done((bf16[2,2,32,128]{3,2,1,0:T(8,128)(2,1)S(1)}, bf16[2,2,32,128]{3,2,1,0:T(8,128)(2,1)S(1)}, u32[]{:S(2)}, u32[]{:S(2)}) %collective-permute-start.27) | collective-permute-done | bytes 32800 | tf_op jit(solution)/shard_map/ppermute | solution.py:520
  92.1 1.5 %collective-permute-start.28 = (bf16[1,2,32,128]{3,2,1,0:T(8,128)(2,1)S(1)}, bf16[1,2,32,128]{3,2,1,0:T(8,128)(2,1)S(1)}, u32[]{:S(2)}, u32[]{:S(2)}) collective-permute-start(bf16[1,2,32,128]{3,2,1,0:T(8,128)(2,1)S(1)} %get-tuple-element.187), channel_id=1, source_target_pairs={{0,48},{16,96},{32,80},{48,0},{64,112},{80,32},{96,16},{112,64},{1... | collective-permute-start | bytes 49160 | tf_op jit(solution)/shard_map/ppermute | solution.py:520
  93.6 1.3 %shard_map.213 = bf16[12,6,4,512]{3,2,1,0:T(4,128)(2,1)} custom-call(bf16[72,512]{1,0:T(8,128)(2,1)S(1)} %collective-permute-done.19.back0, bf16[72,512]{1,0:T(8,128)(2,1)S(1)} %collective-permute-done.20.back1, bf16[72,512]{1,0:T(8,128)(2,1)S(1)} %collective-permute-done.21.back2, bf16[72,512]{1,0:T(8,128)(2,1)S(1)} %get-tuple-element.169.back3, ...), custom_call_target="tpu_custom_call" | custom-call | flops 1000000000 | bytes 1048576 | tf_op jit(solution)/shard_map/pallas_call | solution.py:504
  94.9 2.8 %collective-permute-done.28.got = bf16[1,2,32,128]{3,2,1,0:T(8,128)(2,1)S(1)} collective-permute-done((bf16[1,2,32,128]{3,2,1,0:T(8,128)(2,1)S(1)}, bf16[1,2,32,128]{3,2,1,0:T(8,128)(2,1)S(1)}, u32[]{:S(2)}, u32[]{:S(2)}) %collective-permute-start.28) | collective-permute-done | bytes 16416 | tf_op jit(solution)/shard_map/ppermute | solution.py:520
  97.7 0.7 shard_map.219
  (37 shorter events, 0.1 us)
Async XLA Ops:
  0.6 13.5 %copy-start.3 = (s32[192,96]{1,0:T(8,128)S(1)}, s32[192,96]{1,0:T(8,128)}, u32[]{:S(2)}) copy-start(s32[192,96]{1,0:T(8,128)} %ids.1) | copy-start | bytes 221188
  0.6 13.5 %copy-start.8 = (bf16[288,288]{1,0:T(8,128)(2,1)S(1)}, bf16[288,288]{1,0:T(8,128)(2,1)}, u32[]{:S(2)}) copy-start(bf16[288,288]{1,0:T(8,128)(2,1)} %constant.12.clone.sort_hbm.sort) | copy-start | bytes 497668
  0.7 13.5 %copy-start.9 = (bf16[288,288]{1,0:T(8,128)(2,1)S(1)}, bf16[288,288]{1,0:T(8,128)(2,1)}, u32[]{:S(2)}) copy-start(bf16[288,288]{1,0:T(8,128)(2,1)} %constant.10.clone.place_hbm.place) | copy-start | bytes 497668
  0.7 13.5 %copy-start.10 = (s32[144,8]{1,0:T(8,128)S(1)}, s32[144,8]{1,0:T(8,128)}, u32[]{:S(2)}) copy-start(s32[144,8]{1,0:T(8,128)} %constant.14.clone.where_hbm.where) | copy-start | bytes 13828
  7.2 14.3 %collective-permute-start = (bf16[72,512]{1,0:T(8,128)(2,1)S(1)}, bf16[72,512]{1,0:T(8,128)(2,1)S(1)}, u32[]{:S(2)}, u32[]{:S(2)}) collective-permute-start(bf16[72,512]{1,0:T(8,128)(2,1)S(1)} %get-tuple-element.100), channel_id=1, source_target_pairs={{0,240},{16,0},{32,16},{48,32},{64,48},{80,64},{96,80},{112,96},{1... | collective-permute-start | bytes 221192 | tf_op jit(solution)/shard_map/ppermute | solution.py:520
  14.0 8.8 %collective-permute-start.1 = (bf16[72,512]{1,0:T(8,128)(2,1)S(1)}, bf16[72,512]{1,0:T(8,128)(2,1)S(1)}, u32[]{:S(2)}, u32[]{:S(2)}) collective-permute-start(bf16[72,512]{1,0:T(8,128)(2,1)S(1)} %get-tuple-element.101), channel_id=1, source_target_pairs={{0,15},{1,0},{2,1},{3,2},{4,3},{5,4},{6,5},{7,6},{8,7},{9,8},{10,9... | collective-permute-start | bytes 221192 | tf_op jit(solution)/shard_map/ppermute | solution.py:520
  14.0 8.8 %collective-permute-start.2 = (bf16[72,512]{1,0:T(8,128)(2,1)S(1)}, bf16[72,512]{1,0:T(8,128)(2,1)S(1)}, u32[]{:S(2)}, u32[]{:S(2)}) collective-permute-start(bf16[72,512]{1,0:T(8,128)(2,1)S(1)} %get-tuple-element.102), channel_id=1, source_target_pairs={{0,255},{1,240},{2,241},{3,242},{4,243},{5,244},{6,245},{7,246},{8... | collective-permute-start | bytes 221192 | tf_op jit(solution)/shard_map/ppermute | solution.py:530
  14.2 8.6 %copy-start = (bf16[512,1536]{1,0:T(8,128)(2,1)S(1)}, bf16[512,1536]{1,0:T(8,128)(2,1)}, u32[]{:S(2)}) copy-start(bf16[512,1536]{1,0:T(8,128)(2,1)} %qkv.3) | copy-start | bytes 4718596
  14.2 8.6 %copy-start.1 = (bf16[512,512]{1,0:T(8,128)(2,1)S(1)}, bf16[512,512]{1,0:T(8,128)(2,1)}, u32[]{:S(2)}) copy-start(bf16[512,512]{1,0:T(8,128)(2,1)} %out.4) | copy-start | bytes 1572868
  14.2 8.6 %copy-start.4 = (f32[512]{0:T(512)S(1)}, f32[512]{0:T(512)}, u32[]{:S(2)}) copy-start(f32[512]{0:T(512)} %gain.4) | copy-start | bytes 6148
  14.2 8.6 %copy-start.6 = (bf16[288,288]{1,0:T(8,128)(2,1)S(1)}, bf16[288,288]{1,0:T(8,128)(2,1)}, u32[]{:S(2)}) copy-start(bf16[288,288]{1,0:T(8,128)(2,1)} %constant.13.clone.sort_t) | copy-start | bytes 497668
  17.2 9.5 %collective-permute-start.3 = (bf16[72,512]{1,0:T(8,128)(2,1)S(1)}, bf16[72,512]{1,0:T(8,128)(2,1)S(1)}, u32[]{:S(2)}, u32[]{:S(2)}) collective-permute-start(bf16[72,512]{1,0:T(8,128)(2,1)S(1)} %get-tuple-element.109), channel_id=1, source_target_pairs={{0,240},{16,0},{32,16},{48,32},{64,48},{80,64},{96,80},{112,96},{1... | collective-permute-start | bytes 221192 | tf_op jit(solution)/shard_map/ppermute | solution.py:520
  19.1 7.5 %collective-permute-start.4 = (bf16[72,512]{1,0:T(8,128)(2,1)S(1)}, bf16[72,512]{1,0:T(8,128)(2,1)S(1)}, u32[]{:S(2)}, u32[]{:S(2)}) collective-permute-start(bf16[72,512]{1,0:T(8,128)(2,1)S(1)} %get-tuple-element.110), channel_id=1, source_target_pairs={{0,15},{1,0},{2,1},{3,2},{4,3},{5,4},{6,5},{7,6},{8,7},{9,8},{10,9... | collective-permute-start | bytes 221192 | tf_op jit(solution)/shard_map/ppermute | solution.py:520
  21.5 5.1 %collective-permute-start.5 = (bf16[72,512]{1,0:T(8,128)(2,1)S(1)}, bf16[72,512]{1,0:T(8,128)(2,1)S(1)}, u32[]{:S(2)}, u32[]{:S(2)}) collective-permute-start(bf16[72,512]{1,0:T(8,128)(2,1)S(1)} %get-tuple-element.111), channel_id=1, source_target_pairs={{0,255},{1,240},{2,241},{3,242},{4,243},{5,244},{6,245},{7,246},{8... | collective-permute-start | bytes 221192 | tf_op jit(solution)/shard_map/ppermute | solution.py:530
  31.1 11.7 %copy-start.2 = (bf16[512,512]{1,0:T(8,128)(2,1)S(1)}, bf16[512,512]{1,0:T(8,128)(2,1)}, u32[]{:S(2)}) copy-start(bf16[512,512]{1,0:T(8,128)(2,1)} %out.5) | copy-start | bytes 1572868
  32.5 2.9 %collective-permute-start.6 = (bf16[256,2048]{1,0:T(8,128)(2,1)S(1)}, bf16[256,2048]{1,0:T(8,128)(2,1)S(1)}, u32[]{:S(2)}, u32[]{:S(2)}) collective-permute-start(bf16[256,2048]{1,0:T(8,128)(2,1)S(1)} %get-tuple-element.118), channel_id=1, source_target_pairs={{0,1},{1,0},{2,3},{3,2},{4,5},{5,4},{6,7},{7,6},{8,9},{9,8},{10,11... | collective-permute-start | bytes 3145736 | tf_op jit(solution)/shard_map/ppermute | solution.py:520
  33.1 8.1 %collective-permute-start.9 = (bf16[72,512]{1,0:T(8,128)(2,1)S(1)}, bf16[72,512]{1,0:T(8,128)(2,1)S(1)}, u32[]{:S(2)}, u32[]{:S(2)}) collective-permute-start(bf16[72,512]{1,0:T(8,128)(2,1)S(1)} %get-tuple-element.126), channel_id=1, source_target_pairs={{0,17},{1,18},{2,19},{3,20},{4,21},{5,22},{6,23},{7,24},{8,25},{9,... | collective-permute-start | bytes 221192 | tf_op jit(solution)/shard_map/ppermute | solution.py:530
  34.0 7.2 %collective-permute-start.10 = (bf16[72,512]{1,0:T(8,128)(2,1)S(1)}, bf16[72,512]{1,0:T(8,128)(2,1)S(1)}, u32[]{:S(2)}, u32[]{:S(2)}) collective-permute-start(bf16[72,512]{1,0:T(8,128)(2,1)S(1)} %get-tuple-element.127), channel_id=1, source_target_pairs={{0,1},{1,2},{2,3},{3,4},{4,5},{5,6},{6,7},{7,8},{8,9},{9,10},{10,1... | collective-permute-start | bytes 221192 | tf_op jit(solution)/shard_map/ppermute | solution.py:520
  34.0 8.8 %collective-permute-start.11 = (bf16[72,512]{1,0:T(8,128)(2,1)S(1)}, bf16[72,512]{1,0:T(8,128)(2,1)S(1)}, u32[]{:S(2)}, u32[]{:S(2)}) collective-permute-start(bf16[72,512]{1,0:T(8,128)(2,1)S(1)} %get-tuple-element.128), channel_id=1, source_target_pairs={{0,16},{16,32},{32,48},{48,64},{64,80},{80,96},{96,112},{112,128},... | collective-permute-start | bytes 221192 | tf_op jit(solution)/shard_map/ppermute | solution.py:520
  35.4 11.5 %collective-permute-start.7 = (bf16[2,64,1024]{2,1,0:T(8,128)(2,1)S(1)}, bf16[2,64,1024]{2,1,0:T(8,128)(2,1)S(1)}, u32[]{:S(2)}, u32[]{:S(2)}) collective-permute-start(bf16[2,64,1024]{2,1,0:T(8,128)(2,1)S(1)} %get-tuple-element.123), channel_id=1, source_target_pairs={{0,2},{1,3},{2,0},{3,1},{4,6},{5,7},{6,4},{7,5},{8,10},{9,11},{10,... | collective-permute-start | bytes 786440 | tf_op jit(solution)/shard_map/ppermute | solution.py:520
  36.4 11.9 %collective-permute-start.8 = (bf16[2,64,1024]{2,1,0:T(8,128)(2,1)S(1)}, bf16[2,64,1024]{2,1,0:T(8,128)(2,1)S(1)}, u32[]{:S(2)}, u32[]{:S(2)}) collective-permute-start(bf16[2,64,1024]{2,1,0:T(8,128)(2,1)S(1)} %get-tuple-element.125), channel_id=1, source_target_pairs={{0,130},{1,131},{2,128},{3,129},{4,134},{5,135},{6,132},{7,133},{8... | collective-permute-start | bytes 786440 | tf_op jit(solution)/shard_map/ppermute | solution.py:548
  48.3 3.4 %collective-permute-start.16 = (bf16[256,2048]{1,0:T(8,128)(2,1)S(1)}, bf16[256,2048]{1,0:T(8,128)(2,1)S(1)}, u32[]{:S(2)}, u32[]{:S(2)}) collective-permute-start(bf16[256,2048]{1,0:T(8,128)(2,1)S(1)} %get-tuple-element.149), channel_id=1, source_target_pairs={{0,1},{1,0},{2,3},{3,2},{4,5},{5,4},{6,7},{7,6},{8,9},{9,8},{10,11... | collective-permute-start | bytes 3145736 | tf_op jit(solution)/shard_map/ppermute | solution.py:520
  49.0 5.9 %copy-start.5 = (f32[512]{0:T(512)S(1)}, f32[512]{0:T(512)}, u32[]{:S(2)}) copy-start(f32[512]{0:T(512)} %gain.5) | copy-start | bytes 6148
  49.0 5.9 %copy-start.7 = (bf16[288,288]{1,0:T(8,128)(2,1)S(1)}, bf16[288,288]{1,0:T(8,128)(2,1)}, u32[]{:S(2)}) copy-start(bf16[288,288]{1,0:T(8,128)(2,1)} %constant.11.clone.place_t) | copy-start | bytes 497668
  49.1 15.3 %collective-permute-start.12 = (bf16[64,1024]{1,0:T(8,128)(2,1)S(1)}, bf16[64,1024]{1,0:T(8,128)(2,1)S(1)}, u32[]{:S(2)}, u32[]{:S(2)}) collective-permute-start(bf16[64,1024]{1,0:T(8,128)(2,1)S(1)} %get-tuple-element.141), channel_id=1, source_target_pairs={{0,130},{1,131},{2,128},{3,129},{4,134},{5,135},{6,132},{7,133},{8... | collective-permute-start | bytes 393224 | tf_op jit(solution)/shard_map/ppermute | solution.py:548
  51.7 12.7 %collective-permute-start.13 = (bf16[64,1024]{1,0:T(8,128)(2,1)S(1)}, bf16[64,1024]{1,0:T(8,128)(2,1)S(1)}, u32[]{:S(2)}, u32[]{:S(2)}) collective-permute-start(bf16[64,1024]{1,0:T(8,128)(2,1)S(1)} %get-tuple-element.143), channel_id=1, source_target_pairs={{0,2},{1,3},{2,0},{3,1},{4,6},{5,7},{6,4},{7,5},{8,10},{9,11},{10,... | collective-permute-start | bytes 393224 | tf_op jit(solution)/shard_map/ppermute | solution.py:520
  51.9 8.5 %collective-permute-start.17 = (bf16[2,64,1024]{2,1,0:T(8,128)(2,1)S(1)}, bf16[2,64,1024]{2,1,0:T(8,128)(2,1)S(1)}, u32[]{:S(2)}, u32[]{:S(2)}) collective-permute-start(bf16[2,64,1024]{2,1,0:T(8,128)(2,1)S(1)} %get-tuple-element.153), channel_id=1, source_target_pairs={{0,4},{1,5},{2,6},{3,7},{4,0},{5,1},{6,2},{7,3},{8,12},{9,13},{10,... | collective-permute-start | bytes 786440 | tf_op jit(solution)/shard_map/ppermute | solution.py:520
  52.9 9.3 %collective-permute-start.18 = (bf16[2,64,1024]{2,1,0:T(8,128)(2,1)S(1)}, bf16[2,64,1024]{2,1,0:T(8,128)(2,1)S(1)}, u32[]{:S(2)}, u32[]{:S(2)}) collective-permute-start(bf16[2,64,1024]{2,1,0:T(8,128)(2,1)S(1)} %get-tuple-element.155), channel_id=1, source_target_pairs={{0,12},{1,13},{2,14},{3,15},{4,8},{5,9},{6,10},{7,11},{8,4},{9,5},... | collective-permute-start | bytes 786440 | tf_op jit(solution)/shard_map/ppermute | solution.py:520
  62.3 6.3 %collective-permute-start.22 = (bf16[64,1024]{1,0:T(8,128)(2,1)S(1)}, bf16[64,1024]{1,0:T(8,128)(2,1)S(1)}, u32[]{:S(2)}, u32[]{:S(2)}) collective-permute-start(bf16[64,1024]{1,0:T(8,128)(2,1)S(1)} %get-tuple-element.173), channel_id=1, source_target_pairs={{0,12},{1,13},{2,14},{3,15},{4,8},{5,9},{6,10},{7,11},{8,4},{9,5},... | collective-permute-start | bytes 393224 | tf_op jit(solution)/shard_map/ppermute | solution.py:520
  64.4 5.6 %collective-permute-start.23 = (bf16[64,1024]{1,0:T(8,128)(2,1)S(1)}, bf16[64,1024]{1,0:T(8,128)(2,1)S(1)}, u32[]{:S(2)}, u32[]{:S(2)}) collective-permute-start(bf16[64,1024]{1,0:T(8,128)(2,1)S(1)} %get-tuple-element.175), channel_id=1, source_target_pairs={{0,4},{1,5},{2,6},{3,7},{4,0},{5,1},{6,2},{7,3},{8,12},{9,13},{10,... | collective-permute-start | bytes 393224 | tf_op jit(solution)/shard_map/ppermute | solution.py:520
  64.6 7.1 %collective-permute-start.14 = (bf16[2,32,1024]{2,1,0:T(8,128)(2,1)S(1)}, bf16[2,32,1024]{2,1,0:T(8,128)(2,1)S(1)}, u32[]{:S(2)}, u32[]{:S(2)}) collective-permute-start(bf16[2,32,1024]{2,1,0:T(8,128)(2,1)S(1)} %get-tuple-element.145), channel_id=1, source_target_pairs={{0,4},{1,5},{2,6},{3,7},{4,0},{5,1},{6,2},{7,3},{8,12},{9,13},{10,... | collective-permute-start | bytes 393224 | tf_op jit(solution)/shard_map/ppermute | solution.py:520
  70.1 6.6 %collective-permute-start.24 = (bf16[2,32,1024]{2,1,0:T(8,128)(2,1)S(1)}, bf16[2,32,1024]{2,1,0:T(8,128)(2,1)S(1)}, u32[]{:S(2)}, u32[]{:S(2)}) collective-permute-start(bf16[2,32,1024]{2,1,0:T(8,128)(2,1)S(1)} %get-tuple-element.177), channel_id=1, source_target_pairs={{0,2},{1,3},{2,0},{3,1},{4,6},{5,7},{6,4},{7,5},{8,10},{9,11},{10,... | collective-permute-start | bytes 393224 | tf_op jit(solution)/shard_map/ppermute | solution.py:520
  71.6 7.3 %collective-permute-start.19 = (bf16[72,512]{1,0:T(8,128)(2,1)S(1)}, bf16[72,512]{1,0:T(8,128)(2,1)S(1)}, u32[]{:S(2)}, u32[]{:S(2)}) collective-permute-start(bf16[72,512]{1,0:T(8,128)(2,1)S(1)} %get-tuple-element.163), channel_id=1, source_target_pairs={{0,17},{1,18},{2,19},{3,20},{4,21},{5,22},{6,23},{7,24},{8,25},{9,... | collective-permute-start | bytes 221192 | tf_op jit(solution)/shard_map/ppermute | solution.py:530
  71.6 7.3 %collective-permute-start.20 = (bf16[72,512]{1,0:T(8,128)(2,1)S(1)}, bf16[72,512]{1,0:T(8,128)(2,1)S(1)}, u32[]{:S(2)}, u32[]{:S(2)}) collective-permute-start(bf16[72,512]{1,0:T(8,128)(2,1)S(1)} %get-tuple-element.164), channel_id=1, source_target_pairs={{0,1},{1,2},{2,3},{3,4},{4,5},{5,6},{6,7},{7,8},{8,9},{9,10},{10,1... | collective-permute-start | bytes 221192 | tf_op jit(solution)/shard_map/ppermute | solution.py:520
  71.6 8.8 %collective-permute-start.21 = (bf16[72,512]{1,0:T(8,128)(2,1)S(1)}, bf16[72,512]{1,0:T(8,128)(2,1)S(1)}, u32[]{:S(2)}, u32[]{:S(2)}) collective-permute-start(bf16[72,512]{1,0:T(8,128)(2,1)S(1)} %get-tuple-element.165), channel_id=1, source_target_pairs={{0,16},{16,32},{32,48},{48,64},{64,80},{80,96},{96,112},{112,128},... | collective-permute-start | bytes 221192 | tf_op jit(solution)/shard_map/ppermute | solution.py:520
  71.7 6.8 %collective-permute-start.15 = (bf16[1,32,1024]{2,1,0:T(8,128)(2,1)S(1)}, bf16[1,32,1024]{2,1,0:T(8,128)(2,1)S(1)}, u32[]{:S(2)}, u32[]{:S(2)}) collective-permute-start(bf16[1,32,1024]{2,1,0:T(8,128)(2,1)S(1)} %get-tuple-element.146), channel_id=1, source_target_pairs={{0,12},{1,13},{2,14},{3,15},{4,8},{5,9},{6,10},{7,11},{8,4},{9,5},... | collective-permute-start | bytes 196616 | tf_op jit(solution)/shard_map/ppermute | solution.py:520
  76.7 5.6 %collective-permute-start.25 = (bf16[1,32,1024]{2,1,0:T(8,128)(2,1)S(1)}, bf16[1,32,1024]{2,1,0:T(8,128)(2,1)S(1)}, u32[]{:S(2)}, u32[]{:S(2)}) collective-permute-start(bf16[1,32,1024]{2,1,0:T(8,128)(2,1)S(1)} %get-tuple-element.179), channel_id=1, source_target_pairs={{0,130},{1,131},{2,128},{3,129},{4,134},{5,135},{6,132},{7,133},{8... | collective-permute-start | bytes 196616 | tf_op jit(solution)/shard_map/ppermute | solution.py:548
  82.4 4.4 %collective-permute-start.26 = (bf16[4,2,32,128]{3,2,1,0:T(8,128)(2,1)S(1)}, bf16[4,2,32,128]{3,2,1,0:T(8,128)(2,1)S(1)}, u32[]{:S(2)}, u32[]{:S(2)}) collective-permute-start(bf16[4,2,32,128]{3,2,1,0:T(8,128)(2,1)S(1)} %get-tuple-element.183), channel_id=1, source_target_pairs={{0,16},{16,0},{32,48},{48,32},{64,80},{80,64},{96,112},{112,96},{1... | collective-permute-start | bytes 196616 | tf_op jit(solution)/shard_map/ppermute | solution.py:520
  86.8 5.3 %collective-permute-start.27 = (bf16[2,2,32,128]{3,2,1,0:T(8,128)(2,1)S(1)}, bf16[2,2,32,128]{3,2,1,0:T(8,128)(2,1)S(1)}, u32[]{:S(2)}, u32[]{:S(2)}) collective-permute-start(bf16[2,2,32,128]{3,2,1,0:T(8,128)(2,1)S(1)} %get-tuple-element.185), channel_id=1, source_target_pairs={{0,112},{16,32},{32,16},{48,64},{64,48},{80,96},{96,80},{112,0},{1... | collective-permute-start | bytes 98312 | tf_op jit(solution)/shard_map/ppermute | solution.py:520
  92.1 5.6 %collective-permute-start.28 = (bf16[1,2,32,128]{3,2,1,0:T(8,128)(2,1)S(1)}, bf16[1,2,32,128]{3,2,1,0:T(8,128)(2,1)S(1)}, u32[]{:S(2)}, u32[]{:S(2)}) collective-permute-start(bf16[1,2,32,128]{3,2,1,0:T(8,128)(2,1)S(1)} %get-tuple-element.187), channel_id=1, source_target_pairs={{0,48},{16,96},{32,80},{48,0},{64,112},{80,32},{96,16},{112,64},{1... | collective-permute-start | bytes 49160 | tf_op jit(solution)/shard_map/ppermute | solution.py:520

commit v4 on v3

--- a/solution.py
+++ b/solution.py
@@ -254,8 +254,8 @@
         ref[...] = tokens[at * PIECE : (at + 1) * PIECE].astype(BF16)
 
 
-def join_pieces(sort_t, refs):
-    tokens = jnp.concatenate([ref[...].astype(F32) for ref in refs], axis=0)
+def join_pieces(sort_t, pieces):
+    tokens = jnp.concatenate([piece.astype(F32) for piece in pieces], axis=0)
     return mm(sort_t, tokens.astype(BF16))
 
 
@@ -324,7 +324,7 @@
     back0, back1, back2, back3, inputs_out, normed_out, packed, probs, mixed_t,
     scores,
 ):
-    inputs = join_pieces(sort_t[...], (piece0, piece1, piece2, piece3))
+    inputs = join_pieces(sort_t[...], [ref[...] for ref in (piece0, piece1, piece2, piece3)])
     inputs_out[...] = inputs.astype(BF16)
     normed, delta = forward_core(
         inputs, gain[...].reshape(1, WIDTH), qkv, out, query_features[...], key_features,
@@ -335,17 +335,22 @@
 
 
 def kernel_backward_b(
-    piece0, piece1, piece2, piece3, inputs, gain, qkv, out, packed, probs, mixed_t, sort, sort_t,
+    piece0, piece1, piece2, piece3, delta0, delta1, delta2, delta3,
+    inputs, gain, qkv, out, packed, probs, mixed_t, sort, sort_t,
     back0, back1, back2, back3, upstream_out, d_packed,
     d_probs, d_scores,
 ):
-    upstream = join_pieces(sort_t[...], (piece0, piece1, piece2, piece3)).astype(BF16)
+    pieces = [ref[...] for ref in (piece0, piece1, piece2, piece3)]
+    upstream = join_pieces(sort_t[...], pieces).astype(BF16)
     upstream_out[...] = upstream
     backward_core(upstream, out, packed, probs, mixed_t, d_packed, d_probs, d_scores)
     d_inputs = norm_backward(
         inputs[...].astype(F32), gain[...].reshape(1, WIDTH), d_packed[...], qkv
     )
-    split_pieces(sort[...], d_inputs.astype(BF16), (back0, back1, back2, back3))
+    backs = (back0, back1, back2, back3)
+    split_pieces(sort[...], d_inputs.astype(BF16), [back.at[0] for back in backs])
+    for back, delta in zip(backs, (delta0, delta1, delta2, delta3), strict=True):
+        back[1] = delta[...]
 
 
 def kernel_grads_b(normed, mixed_t, upstream, d_packed, send, keep, normed_t):
@@ -360,7 +365,7 @@
     grad_middle_out, d_packed, send,
     d_probs, d_scores,
 ):
-    d_inputs = join_pieces(sort_t[...], (back0, back1, back2, back3))
+    d_inputs = join_pieces(sort_t[...], [back[0] for back in (back0, back1, back2, back3)])
     grad_middle = (upstream[...].astype(F32) + d_inputs).astype(BF16)
     grad_middle_out[...] = grad_middle
     backward_core(grad_middle, out, packed, probs, mixed_t, d_packed, d_probs, d_scores)
@@ -368,9 +373,14 @@
     grads_half(1 - core, normed_t, mixed_t, grad_middle, d_packed, send)
 
 
-def kernel_keep_a(normed_t, mixed_t, grad_middle, d_packed, keep):
+def kernel_keep_a(
+    back0, back1, back2, back3, middle, normed_t, mixed_t, grad_middle, d_packed, place_t, sort_t,
+    keep, advanced,
+):
     core = lax.axis_index("lat") % 2
     grads_half(core, normed_t, mixed_t, grad_middle[...], d_packed, keep)
+    delta = join_pieces(sort_t[...], [back[1] for back in (back0, back1, back2, back3)])
+    store_grid(advanced, place_t[...], (middle[...].astype(F32) + delta).astype(BF16))
 
 
 def kernel_finish_a(
@@ -383,11 +393,6 @@
     )
     total = (grad_middle[...].astype(F32) + d_inputs).astype(BF16)
     store_grid(grad_fields, place_t[...], total)
-
-
-def kernel_advanced(back0, back1, back2, back3, middle, place_t, sort_t, advanced):
-    delta = join_pieces(sort_t[...], (back0, back1, back2, back3))
-    store_grid(advanced, place_t[...], (middle[...].astype(F32) + delta).astype(BF16))
 
 
 def rows_of(block, count):
@@ -456,37 +461,22 @@
     send[...] = keep[half:] + got[half:]
 
 
-def z_partner(z, step):
-    if step == 0:
-        return z ^ 1
-    if step == 1:
-        return (z + 2 * (z & 1) + 7) & 7
-    return z ^ (3 + 4 * (((z + 1) >> 1) & 1))
-
-
-def z_blocks(z):
-    other = z_partner(z, 1)
-    return z, z_partner(z, 2), other, z_partner(other, 2)
-
-
-def kernel_columns(keep_a, got_a, keep_b, got_b, send, keep, blocks):
-    for at, (held, got) in enumerate(((keep_a, got_a), (keep_b, got_b))):
+def kernel_columns(keep_a, got_a, keep_b, got_b, blocks):
+    for rows, held, got in ((slice(0, 32), keep_a, got_a), (slice(32, 64), keep_b, got_b)):
         total = held[0].astype(F32) + got[0].astype(F32)
         for block in range(8):
             qkv = total[:, block * 96 : (block + 1) * 96]
             out = total[:, 768 + block * 32 : 768 + (block + 1) * 32]
-            blocks[block, at] = jnp.concatenate([qkv, out], axis=1).astype(BF16)
-    z = lax.axis_index("lon") % 8
-    for target, owner in ((send, z_partner(z, 0)), (keep, z)):
-        for at, block in enumerate(z_blocks(owner)):
-            target[at] = blocks[block]
-
-
-def kernel_total(keep, got, qkv_a, out_a, qkv_b, out_b):
-    total = keep[0].astype(F32) + got[0].astype(F32)
-    for at, (qkv, out) in enumerate(((qkv_a, out_a), (qkv_b, out_b))):
-        qkv[...] = total[at, :, :96]
-        out[...] = total[at, :, 96:]
+            blocks[block, rows] = jnp.concatenate([qkv, out], axis=1).astype(BF16)
+
+
+def kernel_total(parts, qkv_a, out_a, qkv_b, out_b):
+    total = parts[0].astype(F32)
+    for at in range(1, 8):
+        total = total + parts[at].astype(F32)
+    for rows, qkv, out in ((slice(0, 32), qkv_a, out_a), (slice(32, 64), qkv_b, out_b)):
+        qkv[...] = total[rows, :96]
+        out[...] = total[rows, 96:]
 
 
 def call(kernel, outs, scratch, args, smem=(), hbm=(), copies=0, flops=0, final=()):
@@ -548,10 +538,6 @@
     return lax.ppermute(array, ("lon", "lat"), pairs)
 
 
-def to_z(array, step):
-    return permute(array, "lon", lambda i: i & 8 | z_partner(i & 7, step))
-
-
 def quarters(kernel, keep, got):
     return call(kernel, [((2, 64, SIDE), BF16)] * 4, [], (keep, got))
 
@@ -563,6 +549,11 @@
 def halve(keep, got):
     shape = (keep.shape[0] // 2,) + keep.shape[1:]
     return call(kernel_halve, [(shape, BF16)] * 2, [], (keep, got))
+
+
+def exchange_z(messages):
+    groups = [[x_hi * 8 + z for z in range(8)] for x_hi in range(2)]
+    return lax.all_to_all(messages, "lon", 0, 0, axis_index_groups=groups, tiled=True)
 
 
 def body(
@@ -625,19 +616,20 @@
         (p3, eastern, below, diagonal, query_b, keys_b, gain_b, qkv_weight_b, out_weight_b, sort, sort_t),
         flops=5 * 10**9,
     )
+    twin = ((2, PIECE, WIDTH), BF16)
     d0, d1, d2, d3, upstream_b, d_packed_b = call(
         kernel_backward_b,
-        [piece] * 4 + [token, packed],
+        [twin] * 4 + [token, packed],
         [scores, probs],
         (
-            c3, c_eastern, c_below, c_diagonal, inputs_b, gain_b, qkv_weight_b, out_weight_b,
-            packed_b, probs_b, mixed_b, sort, sort_t,
+            c3, c_eastern, c_below, c_diagonal, b0, b1, b2, b3, inputs_b, gain_b, qkv_weight_b,
+            out_weight_b, packed_b, probs_b, mixed_b, sort, sort_t,
         ),
         flops=5 * 10**9,
     )
-    d_diagonal = permute_both(d3, 1)
-    d_above = permute(d2, "lat", lambda i: i + 1)
-    d_western = permute(d1, "lon", lambda i: i + 1)
+    d3 = permute_both(d3, 1)
+    d2 = permute(d2, "lat", lambda i: i + 1)
+    d1 = permute(d1, "lon", lambda i: i + 1)
     send_b, keep_b = call(
         kernel_grads_b, [half_grads] * 2, [normed_t], (normed_b, mixed_b, upstream_b, d_packed_b),
         flops=2 * 10**9,
@@ -645,28 +637,31 @@
     send_one_b, send_two_b, keep_one_b, keep_two_b = quarters(
         kernel_first_sum_b, keep_b, to_core(send_b)
     )
-    send_one_b, send_two_b, d0 = lax.optimization_barrier((send_one_b, send_two_b, d0))
     parts_b = (keep_one_b, to_x(send_one_b, 1), keep_two_b, to_x(send_two_b, 3))
+    send_one_b, send_two_b, held_one_b, held_two_b = second_sum(parts_b)
+    parts_b = (held_one_b, to_x(send_one_b, 3), held_two_b, to_x(send_two_b, 1))
     grad_middle, d_packed_a, send_a = call(
         kernel_backward_a,
         [token, packed, half_grads],
         [scores, probs],
         (
-            d_diagonal, d_above, d_western, d0, upstream_a, out_weight_a, packed_a, probs_a,
-            mixed_a, normed_a_t, sort_t,
+            d3, d2, d1, d0, upstream_a, out_weight_a, packed_a, probs_a, mixed_a, normed_a_t,
+            sort_t,
         ),
         flops=5 * 10**9,
     )
-    parts_b, send_a = lax.optimization_barrier((parts_b, send_a))
-    send_one_b, send_two_b, held_one_b, held_two_b = second_sum(parts_b)
-    parts_b = (held_one_b, to_x(send_one_b, 3), held_two_b, to_x(send_two_b, 1))
-    keep_a = call(
-        kernel_keep_a, [half_grads], [], (normed_a_t, mixed_a, grad_middle, d_packed_a),
-        flops=10**9,
-    )[0]
-    send_one_a, send_two_a, keep_one_a, keep_two_a = quarters(
-        kernel_first_sum_a, keep_a, to_core(send_a)
-    )
+    got_a = to_core(send_a)
+    keep_a, advanced = call(
+        kernel_keep_a,
+        [half_grads, grid],
+        [],
+        (
+            d3, d2, d1, d0, middle_a, normed_a_t, mixed_a, grad_middle, d_packed_a, place_t,
+            sort_t,
+        ),
+        flops=2 * 10**9, final=(1,),
+    )
+    send_one_a, send_two_a, keep_one_a, keep_two_a = quarters(kernel_first_sum_a, keep_a, got_a)
     send_one_a, send_two_a, d_packed_a = lax.optimization_barrier((send_one_a, send_two_a, d_packed_a))
     parts_a = (keep_one_a, to_y(send_one_a, 1), keep_two_a, to_y(send_two_a, 3))
     grad_fields = call(
@@ -680,40 +675,25 @@
     send_b, keep_b = call(kernel_third_sum_b, [pair] * 2, [], parts_b)
     got_b = to_y(send_b, 1)
     send_one_a, send_two_a, held_one_a, held_two_a = second_sum(parts_a)
-    send_one_a, send_two_a, grad_fields, b1, b2, b3 = lax.optimization_barrier(
-        (send_one_a, send_two_a, grad_fields, b1, b2, b3)
+    send_one_a, send_two_a, grad_fields = lax.optimization_barrier(
+        (send_one_a, send_two_a, grad_fields)
     )
     parts_a = (held_one_a, to_y(send_one_a, 3), held_two_a, to_y(send_two_a, 1))
-    delta_diagonal = permute_both(b3, 1)
-    delta_above = permute(b2, "lat", lambda i: i + 1)
-    delta_western = permute(b1, "lon", lambda i: i + 1)
     send_a, keep_a = call(kernel_third_sum_a, [pair] * 2, [], parts_a)
     got_a = to_x(send_a, 1)
     send_b, keep_b = halve(keep_b, got_b)
     got_b = to_y(send_b, 3)
     send_a, keep_a = halve(keep_a, got_a)
     got_a = to_x(send_a, 3)
-    four = ((4, 2, 32, GROUP), BF16)
-    got_b, delta_diagonal, delta_above, delta_western = lax.optimization_barrier(
-        (got_b, delta_diagonal, delta_above, delta_western)
-    )
-    send, keep = call(
-        kernel_columns, [four] * 2, [((8, 2, 32, GROUP), BF16)], (keep_a, got_a, keep_b, got_b)
-    )
-    advanced = call(
-        kernel_advanced,
-        [grid],
-        [],
-        (delta_diagonal, delta_above, delta_western, b0, middle_a, place_t, sort_t),
-        flops=10**9, final=(0,),
+    blocks = call(
+        kernel_columns, [((8, 64, GROUP), BF16)], [], (keep_a, got_a, keep_b, got_b)
     )[0]
-    send, keep = halve(keep, to_z(send, 0))
-    send, keep = halve(keep, to_z(send, 1))
+    parts = exchange_z(blocks)
     grads = call(
         kernel_total,
         [((32, 96), F32), ((32, 32), F32)] * 2,
         [],
-        (keep, to_z(send, 2)),
+        (parts,),
         final=(0, 1, 2, 3),
     )
     return (advanced.transpose(2, 0, 1, 3), grad_fields.transpose(2, 0, 1, 3), *grads)

time: 98.6 us -> 94.7 us (0.960)
  blocking collectives: 0 us -> 11.5 us
  waiting for transfers between devices: 29.7 us -> 21.2 us
  starting transfers between devices: 37.8 us -> 31.1 us
    ppermute x22 -> x17, waiting for transfers between devices: 23.3 us -> 8.93 us  [permute(): lax.ppermute(array, axis, [(i, target(i) % length) for i in range(length)])]
    all_to_all x0 -> x1, blocking collectives: none -> 11.5 us  [exchange_z(): lax.all_to_all(messages, 'lon', 0, 0, axis_index_groups=groups, tiled=True)]
    ppermute x22 -> x17, starting transfers between devices: 29 us -> 25.6 us  [permute(): lax.ppermute(array, axis, [(i, target(i) % length) for i in range(length)])]
    ppermute x4 -> x3, waiting for transfers between devices: 3.21 us -> 6.51 us  [permute_both(): return lax.ppermute(array, ('lon', 'lat'), pairs)]
    ppermute x3, starting transfers between devices: 6.4 us -> 3.46 us  [to_x(): return lax.ppermute(array, ('lon', 'lat'), pairs)]
    ppermute x3, waiting for transfers between devices: 3.16 us -> 5.72 us  [to_x(): return lax.ppermute(array, ('lon', 'lat'), pairs)]
    ppermute x4 -> x3, starting transfers between devices: 2.35 us -> 2 us  [permute_both(): return lax.ppermute(array, ('lon', 'lat'), pairs)]
    pallas_call x21 -> x18, Pallas kernels: 29.9 us -> 29.8 us  [call(): pl.pallas_call(kernel, out_shape=tuple((jax.ShapeDtypeStruct(shape, kind)...]
  transfers between devices with their start and end apart: 29 -> 23, of which waited for: 15 -> 11; matrix products, arithmetic and copies ran while one was open for 0% -> 0% of each run, Pallas kernels for 17% -> 19%
where the time goes in v4:
time: 94.7 us; the launch traced here: 94.5 us
  starting transfers between devices  31.1 us (33%)
  Pallas kernels  29.8 us (31%)
  waiting for transfers between devices  21.2 us (22%)
  blocking collectives  11.5 us (12%)
    pallas_call x18, Pallas kernels, call(): pl.pallas_call(kernel, out_shape=tuple((jax.ShapeDtypeStruct(shape, kind)...  29.8 us
    ppermute x17, starting transfers between devices, permute(): lax.ppermute(array, axis, [(i, target(i) % length) for i in range(length)])  25.6 us
    all_to_all x1, blocking collectives, exchange_z(): lax.all_to_all(messages, 'lon', 0, 0, axis_index_groups=groups, tiled=True)  11.5 us
    ppermute x17, waiting for transfers between devices, permute(): lax.ppermute(array, axis, [(i, target(i) % length) for i in range(length)])  8.93 us
    ppermute x3, waiting for transfers between devices, permute_both(): return lax.ppermute(array, ('lon', 'lat'), pairs)  6.51 us
    ppermute x3, waiting for transfers between devices, to_x(): return lax.ppermute(array, ('lon', 'lat'), pairs)  5.72 us
    ppermute x3, starting transfers between devices, to_x(): return lax.ppermute(array, ('lon', 'lat'), pairs)  3.46 us
    ppermute x3, starting transfers between devices, permute_both(): return lax.ppermute(array, ('lon', 'lat'), pairs)  2 us
  transfers between devices with their start and end apart: 23, of which 11 were waited for; matrix products, arithmetic and copies ran while one was open for 0% of the time, Pallas kernels for 19%

profile of v4, /device:TPU:6, one launch (start us, length us, event | category | flops | bytes accessed | tf_op | source)
XLA Modules:
  0.0 94.5 jit_solution(2843322166431447601)
XLA Ops:
  0.6 0.0 copy-start.8
  0.7 0.0 copy-start.9
  0.7 0.0 copy-start.10
  0.7 6.5 %shard_map.199 = (bf16[72,512]{1,0:T(8,128)(2,1)S(1)}, bf16[72,512]{1,0:T(8,128)(2,1)S(1)}, bf16[72,512]{1,0:T(8,128)(2,1)S(1)}, bf16[72,512]{1,0:T(8,128)(2,1)S...) custom-call(bf16[12,6,4,512]{3,2,1,0:T(4,128)(2,1)} %bitcast.6, ...), custom_call_target="tpu_custom_call" | custom-call | flops 7000000000 | bytes 1048576 | tf_op jit(solution)/shard_map/pallas_call | solution.py:494
  7.2 6.8 %collective-permute-start.3 = (bf16[72,512]{1,0:T(8,128)(2,1)S(1)}, bf16[72,512]{1,0:T(8,128)(2,1)S(1)}, u32[]{:S(2)}, u32[]{:S(2)}) collective-permute-start(bf16[72,512]{1,0:T(8,128)(2,1)S(1)} %get-tuple-element.86), channel_id=1, source_target_pairs={{0,240},{16,0},{32,16},{48,32},{64,48},{80,64},{96,80},{112,96},{1... | collective-permute-start | bytes 221192 | tf_op jit(solution)/shard_map/ppermute | solution.py:510
  14.0 0.0 collective-permute-start.4
  14.0 0.2 collective-permute-start.5
  14.2 0.0 copy-start
  14.2 0.0 copy-start.1
  14.2 0.0 copy-start.4
  14.2 0.0 copy-start.7
  14.2 2.9 %shard_map.200 = (bf16[72,512]{1,0:T(8,128)(2,1)S(1)}, bf16[72,512]{1,0:T(8,128)(2,1)S(1)}, bf16[72,512]{1,0:T(8,128)(2,1)S(1)}, bf16[72,512]{1,0:T(8,128)(2,1)S...) custom-call(bf16[12,6,4,512]{3,2,1,0:T(4,128)(2,1)} %bitcast.7, ...), custom_call_target="tpu_custom_call" | custom-call | flops 2000000000 | bytes 1048576 | tf_op jit(solution)/shard_map/pallas_call | solution.py:494
  17.2 2.0 %collective-permute-start = (bf16[72,512]{1,0:T(8,128)(2,1)S(1)}, bf16[72,512]{1,0:T(8,128)(2,1)S(1)}, u32[]{:S(2)}, u32[]{:S(2)}) collective-permute-start(bf16[72,512]{1,0:T(8,128)(2,1)S(1)} %get-tuple-element.82), channel_id=1, source_target_pairs={{0,240},{16,0},{32,16},{48,32},{64,48},{80,64},{96,80},{112,96},{1... | collective-permute-start | bytes 221192 | tf_op jit(solution)/shard_map/ppermute | solution.py:510
  19.1 2.4 %collective-permute-start.1 = (bf16[72,512]{1,0:T(8,128)(2,1)S(1)}, bf16[72,512]{1,0:T(8,128)(2,1)S(1)}, u32[]{:S(2)}, u32[]{:S(2)}) collective-permute-start(bf16[72,512]{1,0:T(8,128)(2,1)S(1)} %get-tuple-element.83), channel_id=1, source_target_pairs={{0,15},{1,0},{2,1},{3,2},{4,3},{5,4},{6,5},{7,6},{8,7},{9,8},{10,9... | collective-permute-start | bytes 221192 | tf_op jit(solution)/shard_map/ppermute | solution.py:510
  21.5 0.0 collective-permute-done.3.piece1
  21.5 1.2 %collective-permute-start.2 = (bf16[72,512]{1,0:T(8,128)(2,1)S(1)}, bf16[72,512]{1,0:T(8,128)(2,1)S(1)}, u32[]{:S(2)}, u32[]{:S(2)}) collective-permute-start(bf16[72,512]{1,0:T(8,128)(2,1)S(1)} %get-tuple-element.84), channel_id=1, source_target_pairs={{0,255},{1,240},{2,241},{3,242},{4,243},{5,244},{6,245},{7,246},{8... | collective-permute-start | bytes 221192 | tf_op jit(solution)/shard_map/ppermute | solution.py:520
  22.7 0.0 collective-permute-done.4.piece2
  22.7 0.0 collective-permute-done.5.piece3
  22.8 3.9 %shard_map.201 = (bf16[72,512]{1,0:T(8,128)(2,1)S(1)}, bf16[72,512]{1,0:T(8,128)(2,1)S(1)}, bf16[72,512]{1,0:T(8,128)(2,1)S(1)}, bf16[72,512]{1,0:T(8,128)(2,1)S...) custom-call(bf16[72,512]{1,0:T(8,128)(2,1)S(1)} %get-tuple-element.8, ...), custom_call_target="tpu_custom_call" | custom-call | flops 5000000000 | bytes 1048576 | tf_op jit(solution)/shard_map/pallas_call | solution.py:494
  26.6 0.0 collective-permute-done.piece1
  26.7 0.0 collective-permute-done.2.piece3
  26.7 4.5 %shard_map.202 = (bf16[2,72,512]{2,1,0:T(8,128)(2,1)S(1)}, bf16[2,72,512]{2,1,0:T(8,128)(2,1)S(1)}, bf16[2,72,512]{2,1,0:T(8,128)(2,1)S(1)}, bf16[2,72,512]{2,1,...) custom-call(bf16[72,512]{1,0:T(8,128)(2,1)S(1)} %get-tuple-element.81.piece0, ...), custom_call_target="tpu_custom_call" | custom-call | flops 5000000000 | bytes 1048576 | tf_op jit(solution)/shard_map/pallas_call | solution.py:494
  31.2 0.6 collective-permute-start.6
  31.7 0.1 collective-permute-start.7
  31.8 1.0 %collective-permute-start.8 = (bf16[2,72,512]{2,1,0:T(8,128)(2,1)S(1)}, bf16[2,72,512]{2,1,0:T(8,128)(2,1)S(1)}, u32[]{:S(2)}, u32[]{:S(2)}) collective-permute-start(bf16[2,72,512]{2,1,0:T(8,128)(2,1)S(1)} %get-tuple-element.101), channel_id=1, source_target_pairs={{0,16},{16,32},{32,48},{48,64},{64,80},{80,96},{96,112},{112,128},... | collective-permute-start | bytes 442376 | tf_op jit(solution)/shard_map/ppermute | solution.py:510
  32.8 1.3 %shard_map.210 = (bf16[256,2048]{1,0:T(8,128)(2,1)S(1)}, bf16[256,2048]{1,0:T(8,128)(2,1)S(1)}) custom-call(bf16[288,512]{1,0:T(8,128)(2,1)S(1)} %get-tuple-element.133.normed, bf16[2,512,144]{2,1,0:T(8,128)(2,1)S(1)} %get-tuple-element.98.mixed_t, bf16[288,512]{1,0:T(8,128)(2,1)S(1)} %get-tuple-element.134.upstream, ...), custom_call_target="tpu_custom_call" | custom-call | flops 2000000000 | bytes 1048576 | tf_op jit(solution)/shard_map/pallas_call | solution.py:494
  34.1 0.3 collective-permute-start.16
  34.4 6.5 %collective-permute-done.6.back0 = bf16[2,72,512]{2,1,0:T(8,128)(2,1)S(1)} collective-permute-done((bf16[2,72,512]{2,1,0:T(8,128)(2,1)S(1)}, bf16[2,72,512]{2,1,0:T(8,128)(2,1)S(1)}, u32[]{:S(2)}, u32[]{:S(2)}) %collective-permute-start.6) | collective-permute-done | bytes 147488 | tf_op jit(solution)/shard_map/ppermute | solution.py:520
  41.0 3.0 %collective-permute-done.8.back2 = bf16[2,72,512]{2,1,0:T(8,128)(2,1)S(1)} collective-permute-done((bf16[2,72,512]{2,1,0:T(8,128)(2,1)S(1)}, bf16[2,72,512]{2,1,0:T(8,128)(2,1)S(1)}, u32[]{:S(2)}, u32[]{:S(2)}) %collective-permute-start.8) | collective-permute-done | bytes 147488 | tf_op jit(solution)/shard_map/ppermute | solution.py:510
  44.0 4.2 %shard_map.203 = (bf16[288,512]{1,0:T(8,128)(2,1)S(1)}, bf16[288,1536]{1,0:T(8,128)(2,1)S(1)}, bf16[256,2048]{1,0:T(8,128)(2,1)S(1)}) custom-call(bf16[2,72,512]{2,1,0:T(8,128)(2,1)S(1)} %collective-permute-done.6.back0, bf16[2,72,512]{2,1,0:T(8,128)(2,1)S(1)} %collective-permute-done.7.back1, bf16[2,72,512]{2,1,0:T(8,128)(2,1)S(1)} %collective-permute-done.8.back2, ...), custom_call_target="tpu_custom_call" | custom-call | flops 5000000000 | bytes 1048576 | tf_op jit(solution)/shard_map/pallas_call | solution.py:494
  48.2 0.1 collective-permute-start.9
  48.3 1.9 %shard_map.204 = (bf16[256,2048]{1,0:T(8,128)(2,1)S(1)}, bf16[12,6,4,512]{3,2,1,0:T(4,128)(2,1)}) custom-call(bf16[2,72,512]{2,1,0:T(8,128)(2,1)S(1)} %collective-permute-done.6.back0, bf16[2,72,512]{2,1,0:T(8,128)(2,1)S(1)} %collective-permute-done.7.back1, bf16[2,72,512]{2,1,0:T(8,128)(2,1)S(1)} %collective-permute-done.8.back2, ...), custom_call_target="tpu_custom_call" | custom-call | flops 2000000000 | bytes 1048576 | tf_op jit(solution)/shard_map/pallas_call | solution.py:494
  50.2 0.1 shard_map.211
  50.3 0.8 collective-permute-start.17
  51.1 1.2 %collective-permute-start.18 = (bf16[2,64,1024]{2,1,0:T(8,128)(2,1)S(1)}, bf16[2,64,1024]{2,1,0:T(8,128)(2,1)S(1)}, u32[]{:S(2)}, u32[]{:S(2)}) collective-permute-start(bf16[2,64,1024]{2,1,0:T(8,128)(2,1)S(1)} %get-tuple-element.141), channel_id=1, source_target_pairs={{0,130},{1,131},{2,128},{3,129},{4,134},{5,135},{6,132},{7,133},{8... | collective-permute-start | bytes 786440 | tf_op jit(solution)/shard_map/ppermute | solution.py:538
  52.4 0.0 collective-permute-done.9.got
  52.4 0.1 shard_map.205
  52.5 1.0 %collective-permute-start.10 = (bf16[2,64,1024]{2,1,0:T(8,128)(2,1)S(1)}, bf16[2,64,1024]{2,1,0:T(8,128)(2,1)S(1)}, u32[]{:S(2)}, u32[]{:S(2)}) collective-permute-start(bf16[2,64,1024]{2,1,0:T(8,128)(2,1)S(1)} %get-tuple-element.117), channel_id=1, source_target_pairs={{0,4},{1,5},{2,6},{3,7},{4,0},{5,1},{6,2},{7,3},{8,12},{9,13},{10,... | collective-permute-start | bytes 786440 | tf_op jit(solution)/shard_map/ppermute | solution.py:510
  53.5 2.7 %collective-permute-start.11 = (bf16[2,64,1024]{2,1,0:T(8,128)(2,1)S(1)}, bf16[2,64,1024]{2,1,0:T(8,128)(2,1)S(1)}, u32[]{:S(2)}, u32[]{:S(2)}) collective-permute-start(bf16[2,64,1024]{2,1,0:T(8,128)(2,1)S(1)} %get-tuple-element.119), channel_id=1, source_target_pairs={{0,12},{1,13},{2,14},{3,15},{4,8},{5,9},{6,10},{7,11},{8,4},{9,5},... | collective-permute-start | bytes 786440 | tf_op jit(solution)/shard_map/ppermute | solution.py:510
  56.2 3.3 %shard_map.207 = bf16[12,6,4,512]{3,2,1,0:T(4,128)(2,1)} custom-call(bf16[288,512]{1,0:T(8,128)(2,1)S(1)} %get-tuple-element.122.inputs, bf16[288,512]{1,0:T(8,128)(2,1)S(1)} %get-tuple-element.109.grad_middle, f32[512]{0:T(512)S(1)} %copy-done.5, bf16[512,1536]{1,0:T(8,128)(2,1)} %qkv_hbm.3, bf16[288,1536]{1,0:T(8,128)(2,1)S(1)} %get-tuple-element.123.d_packed, ...), custom_call_target="tpu_custom_call" | custom-call | flops 4000000000 | bytes 1048576 | tf_op jit(solution)/shard_map/pallas_call | solution.py:494
  59.5 0.0 collective-permute-done.17.got_one
  59.5 1.3 %collective-permute-done.18.got_two = bf16[2,64,1024]{2,1,0:T(8,128)(2,1)S(1)} collective-permute-done((bf16[2,64,1024]{2,1,0:T(8,128)(2,1)S(1)}, bf16[2,64,1024]{2,1,0:T(8,128)(2,1)S(1)}, u32[]{:S(2)}, u32[]{:S(2)}) %collective-permute-start.18) | collective-permute-done | bytes 262176 | tf_op jit(solution)/shard_map/ppermute | solution.py:538
  60.7 0.1 shard_map.212
  60.8 1.4 %collective-permute-start.19 = (bf16[64,1024]{1,0:T(8,128)(2,1)S(1)}, bf16[64,1024]{1,0:T(8,128)(2,1)S(1)}, u32[]{:S(2)}, u32[]{:S(2)}) collective-permute-start(bf16[64,1024]{1,0:T(8,128)(2,1)S(1)} %get-tuple-element.143), channel_id=1, source_target_pairs={{0,130},{1,131},{2,128},{3,129},{4,134},{5,135},{6,132},{7,133},{8... | collective-permute-start | bytes 393224 | tf_op jit(solution)/shard_map/ppermute | solution.py:538
  62.2 0.4 collective-permute-done.11.got_two
  62.6 0.1 shard_map.206
  62.6 3.2 %collective-permute-start.12 = (bf16[64,1024]{1,0:T(8,128)(2,1)S(1)}, bf16[64,1024]{1,0:T(8,128)(2,1)S(1)}, u32[]{:S(2)}, u32[]{:S(2)}) collective-permute-start(bf16[64,1024]{1,0:T(8,128)(2,1)S(1)} %get-tuple-element.126), channel_id=1, source_target_pairs={{0,12},{1,13},{2,14},{3,15},{4,8},{5,9},{6,10},{7,11},{8,4},{9,5},... | collective-permute-start | bytes 393224 | tf_op jit(solution)/shard_map/ppermute | solution.py:510
  65.8 1.2 %collective-permute-done.19.got_one = bf16[64,1024]{1,0:T(8,128)(2,1)S(1)} collective-permute-done((bf16[64,1024]{1,0:T(8,128)(2,1)S(1)}, bf16[64,1024]{1,0:T(8,128)(2,1)S(1)}, u32[]{:S(2)}, u32[]{:S(2)}) %collective-permute-start.19) | collective-permute-done | bytes 131104 | tf_op jit(solution)/shard_map/ppermute | solution.py:538
  67.1 0.1 collective-permute-done.20.got_two
  67.1 0.1 shard_map.213
  67.2 1.0 %collective-permute-start.21 = (bf16[2,32,1024]{2,1,0:T(8,128)(2,1)S(1)}, bf16[2,32,1024]{2,1,0:T(8,128)(2,1)S(1)}, u32[]{:S(2)}, u32[]{:S(2)}) collective-permute-start(bf16[2,32,1024]{2,1,0:T(8,128)(2,1)S(1)} %get-tuple-element.147), channel_id=1, source_target_pairs={{0,4},{1,5},{2,6},{3,7},{4,0},{5,1},{6,2},{7,3},{8,12},{9,13},{10,... | collective-permute-start | bytes 393224 | tf_op jit(solution)/shard_map/ppermute | solution.py:510
  68.2 0.7 collective-permute-done.12.got_one
  68.9 2.5 %collective-permute-done.13.got_two = bf16[64,1024]{1,0:T(8,128)(2,1)S(1)} collective-permute-done((bf16[64,1024]{1,0:T(8,128)(2,1)S(1)}, bf16[64,1024]{1,0:T(8,128)(2,1)S(1)}, u32[]{:S(2)}, u32[]{:S(2)}) %collective-permute-start.13) | collective-permute-done | bytes 131104 | tf_op jit(solution)/shard_map/ppermute | solution.py:510
  71.4 0.1 shard_map.208
  71.5 1.8 %collective-permute-start.14 = (bf16[2,32,1024]{2,1,0:T(8,128)(2,1)S(1)}, bf16[2,32,1024]{2,1,0:T(8,128)(2,1)S(1)}, u32[]{:S(2)}, u32[]{:S(2)}) collective-permute-start(bf16[2,32,1024]{2,1,0:T(8,128)(2,1)S(1)} %get-tuple-element.130), channel_id=1, source_target_pairs={{0,2},{1,3},{2,0},{3,1},{4,6},{5,7},{6,4},{7,5},{8,10},{9,11},{10,... | collective-permute-start | bytes 393224 | tf_op jit(solution)/shard_map/ppermute | solution.py:510
  73.3 0.0 collective-permute-done.21.got
  73.4 2.5 %collective-permute-start.22 = (bf16[1,32,1024]{2,1,0:T(8,128)(2,1)S(1)}, bf16[1,32,1024]{2,1,0:T(8,128)(2,1)S(1)}, u32[]{:S(2)}, u32[]{:S(2)}) collective-permute-start(bf16[1,32,1024]{2,1,0:T(8,128)(2,1)S(1)} %get-tuple-element.149), channel_id=1, source_target_pairs={{0,12},{1,13},{2,14},{3,15},{4,8},{5,9},{6,10},{7,11},{8,4},{9,5},... | collective-permute-start | bytes 196616 | tf_op jit(solution)/shard_map/ppermute | solution.py:510
  75.9 0.7 collective-permute-done.14.got
  76.6 0.9 collective-permute-start.15
  77.5 1.5 %collective-permute-done.22.got_b = bf16[1,32,1024]{2,1,0:T(8,128)(2,1)S(1)} collective-permute-done((bf16[1,32,1024]{2,1,0:T(8,128)(2,1)S(1)}, bf16[1,32,1024]{2,1,0:T(8,128)(2,1)S(1)}, u32[]{:S(2)}, u32[]{:S(2)}) %collective-permute-start.22) | collective-permute-done | bytes 65568 | tf_op jit(solution)/shard_map/ppermute | solution.py:510
  78.9 3.2 %collective-permute-done.15.got_a = bf16[1,32,1024]{2,1,0:T(8,128)(2,1)S(1)} collective-permute-done((bf16[1,32,1024]{2,1,0:T(8,128)(2,1)S(1)}, bf16[1,32,1024]{2,1,0:T(8,128)(2,1)S(1)}, u32[]{:S(2)}, u32[]{:S(2)}) %collective-permute-start.15) | collective-permute-done | bytes 65568 | tf_op jit(solution)/shard_map/ppermute | solution.py:538
  82.2 0.1 shard_map.215
  82.3 11.5 %all_to_all.5.parts = bf16[8,64,128]{2,1,0:T(8,128)(2,1)S(1)} all-to-all(bf16[8,64,128]{2,1,0:T(8,128)(2,1)S(1)} %shard_map.215), channel_id=1, replica_groups={{0,16,32,48,64,80,96,112},{128,144,160,176,192,208,224,240},{1,17,33,49..., dimensions={0} | all-to-all | bytes 262144 | tf_op jit(solution)/shard_map/all_to_all | solution.py:556
  93.8 0.7 shard_map.216
  (23 shorter events, 0.1 us)
Async XLA Ops:
  0.6 13.5 %copy-start.3 = (s32[192,96]{1,0:T(8,128)S(1)}, s32[192,96]{1,0:T(8,128)}, u32[]{:S(2)}) copy-start(s32[192,96]{1,0:T(8,128)} %ids.1) | copy-start | bytes 221188
  0.6 13.5 %copy-start.8 = (bf16[288,288]{1,0:T(8,128)(2,1)S(1)}, bf16[288,288]{1,0:T(8,128)(2,1)}, u32[]{:S(2)}) copy-start(bf16[288,288]{1,0:T(8,128)(2,1)} %constant.12.clone.sort_hbm.sort) | copy-start | bytes 497668
  0.7 13.5 %copy-start.9 = (bf16[288,288]{1,0:T(8,128)(2,1)S(1)}, bf16[288,288]{1,0:T(8,128)(2,1)}, u32[]{:S(2)}) copy-start(bf16[288,288]{1,0:T(8,128)(2,1)} %constant.10.clone.place_hbm.place) | copy-start | bytes 497668
  0.7 13.5 %copy-start.10 = (s32[144,8]{1,0:T(8,128)S(1)}, s32[144,8]{1,0:T(8,128)}, u32[]{:S(2)}) copy-start(s32[144,8]{1,0:T(8,128)} %constant.14.clone.where_hbm.where) | copy-start | bytes 13828
  7.2 14.3 %collective-permute-start.3 = (bf16[72,512]{1,0:T(8,128)(2,1)S(1)}, bf16[72,512]{1,0:T(8,128)(2,1)S(1)}, u32[]{:S(2)}, u32[]{:S(2)}) collective-permute-start(bf16[72,512]{1,0:T(8,128)(2,1)S(1)} %get-tuple-element.86), channel_id=1, source_target_pairs={{0,240},{16,0},{32,16},{48,32},{64,48},{80,64},{96,80},{112,96},{1... | collective-permute-start | bytes 221192 | tf_op jit(solution)/shard_map/ppermute | solution.py:510
  14.0 8.8 %collective-permute-start.4 = (bf16[72,512]{1,0:T(8,128)(2,1)S(1)}, bf16[72,512]{1,0:T(8,128)(2,1)S(1)}, u32[]{:S(2)}, u32[]{:S(2)}) collective-permute-start(bf16[72,512]{1,0:T(8,128)(2,1)S(1)} %get-tuple-element.87), channel_id=1, source_target_pairs={{0,15},{1,0},{2,1},{3,2},{4,3},{5,4},{6,5},{7,6},{8,7},{9,8},{10,9... | collective-permute-start | bytes 221192 | tf_op jit(solution)/shard_map/ppermute | solution.py:510
  14.0 8.8 %collective-permute-start.5 = (bf16[72,512]{1,0:T(8,128)(2,1)S(1)}, bf16[72,512]{1,0:T(8,128)(2,1)S(1)}, u32[]{:S(2)}, u32[]{:S(2)}) collective-permute-start(bf16[72,512]{1,0:T(8,128)(2,1)S(1)} %get-tuple-element.88), channel_id=1, source_target_pairs={{0,255},{1,240},{2,241},{3,242},{4,243},{5,244},{6,245},{7,246},{8... | collective-permute-start | bytes 221192 | tf_op jit(solution)/shard_map/ppermute | solution.py:520
  14.2 8.6 %copy-start = (bf16[512,1536]{1,0:T(8,128)(2,1)S(1)}, bf16[512,1536]{1,0:T(8,128)(2,1)}, u32[]{:S(2)}) copy-start(bf16[512,1536]{1,0:T(8,128)(2,1)} %qkv.3) | copy-start | bytes 4718596
  14.2 8.6 %copy-start.1 = (bf16[512,512]{1,0:T(8,128)(2,1)S(1)}, bf16[512,512]{1,0:T(8,128)(2,1)}, u32[]{:S(2)}) copy-start(bf16[512,512]{1,0:T(8,128)(2,1)} %out.4) | copy-start | bytes 1572868
  14.2 8.6 %copy-start.4 = (f32[512]{0:T(512)S(1)}, f32[512]{0:T(512)}, u32[]{:S(2)}) copy-start(f32[512]{0:T(512)} %gain.4) | copy-start | bytes 6148
  14.2 8.6 %copy-start.7 = (bf16[288,288]{1,0:T(8,128)(2,1)S(1)}, bf16[288,288]{1,0:T(8,128)(2,1)}, u32[]{:S(2)}) copy-start(bf16[288,288]{1,0:T(8,128)(2,1)} %constant.13.clone.sort_t) | copy-start | bytes 497668
  17.2 9.5 %collective-permute-start = (bf16[72,512]{1,0:T(8,128)(2,1)S(1)}, bf16[72,512]{1,0:T(8,128)(2,1)S(1)}, u32[]{:S(2)}, u32[]{:S(2)}) collective-permute-start(bf16[72,512]{1,0:T(8,128)(2,1)S(1)} %get-tuple-element.82), channel_id=1, source_target_pairs={{0,240},{16,0},{32,16},{48,32},{64,48},{80,64},{96,80},{112,96},{1... | collective-permute-start | bytes 221192 | tf_op jit(solution)/shard_map/ppermute | solution.py:510
  19.1 7.5 %collective-permute-start.1 = (bf16[72,512]{1,0:T(8,128)(2,1)S(1)}, bf16[72,512]{1,0:T(8,128)(2,1)S(1)}, u32[]{:S(2)}, u32[]{:S(2)}) collective-permute-start(bf16[72,512]{1,0:T(8,128)(2,1)S(1)} %get-tuple-element.83), channel_id=1, source_target_pairs={{0,15},{1,0},{2,1},{3,2},{4,3},{5,4},{6,5},{7,6},{8,7},{9,8},{10,9... | collective-permute-start | bytes 221192 | tf_op jit(solution)/shard_map/ppermute | solution.py:510
  21.5 5.1 %collective-permute-start.2 = (bf16[72,512]{1,0:T(8,128)(2,1)S(1)}, bf16[72,512]{1,0:T(8,128)(2,1)S(1)}, u32[]{:S(2)}, u32[]{:S(2)}) collective-permute-start(bf16[72,512]{1,0:T(8,128)(2,1)S(1)} %get-tuple-element.84), channel_id=1, source_target_pairs={{0,255},{1,240},{2,241},{3,242},{4,243},{5,244},{6,245},{7,246},{8... | collective-permute-start | bytes 221192 | tf_op jit(solution)/shard_map/ppermute | solution.py:520
  31.2 9.8 %collective-permute-start.6 = (bf16[2,72,512]{2,1,0:T(8,128)(2,1)S(1)}, bf16[2,72,512]{2,1,0:T(8,128)(2,1)S(1)}, u32[]{:S(2)}, u32[]{:S(2)}) collective-permute-start(bf16[2,72,512]{2,1,0:T(8,128)(2,1)S(1)} %get-tuple-element.99), channel_id=1, source_target_pairs={{0,17},{1,18},{2,19},{3,20},{4,21},{5,22},{6,23},{7,24},{8,25},{9,... | collective-permute-start | bytes 442376 | tf_op jit(solution)/shard_map/ppermute | solution.py:520
  31.7 9.2 %collective-permute-start.7 = (bf16[2,72,512]{2,1,0:T(8,128)(2,1)S(1)}, bf16[2,72,512]{2,1,0:T(8,128)(2,1)S(1)}, u32[]{:S(2)}, u32[]{:S(2)}) collective-permute-start(bf16[2,72,512]{2,1,0:T(8,128)(2,1)S(1)} %get-tuple-element.100), channel_id=1, source_target_pairs={{0,1},{1,2},{2,3},{3,4},{4,5},{5,6},{6,7},{7,8},{8,9},{9,10},{10,1... | collective-permute-start | bytes 442376 | tf_op jit(solution)/shard_map/ppermute | solution.py:510
  31.8 12.2 %collective-permute-start.8 = (bf16[2,72,512]{2,1,0:T(8,128)(2,1)S(1)}, bf16[2,72,512]{2,1,0:T(8,128)(2,1)S(1)}, u32[]{:S(2)}, u32[]{:S(2)}) collective-permute-start(bf16[2,72,512]{2,1,0:T(8,128)(2,1)S(1)} %get-tuple-element.101), channel_id=1, source_target_pairs={{0,16},{16,32},{32,48},{48,64},{64,80},{80,96},{96,112},{112,128},... | collective-permute-start | bytes 442376 | tf_op jit(solution)/shard_map/ppermute | solution.py:510
  32.8 11.2 %copy-start.2 = (bf16[512,512]{1,0:T(8,128)(2,1)S(1)}, bf16[512,512]{1,0:T(8,128)(2,1)}, u32[]{:S(2)}) copy-start(bf16[512,512]{1,0:T(8,128)(2,1)} %out.5) | copy-start | bytes 1572868
  34.1 16.1 %collective-permute-start.16 = (bf16[256,2048]{1,0:T(8,128)(2,1)S(1)}, bf16[256,2048]{1,0:T(8,128)(2,1)S(1)}, u32[]{:S(2)}, u32[]{:S(2)}) collective-permute-start(bf16[256,2048]{1,0:T(8,128)(2,1)S(1)} %get-tuple-element.137), channel_id=1, source_target_pairs={{0,1},{1,0},{2,3},{3,2},{4,5},{5,4},{6,7},{7,6},{8,9},{9,8},{10,11... | collective-permute-start | bytes 3145736 | tf_op jit(solution)/shard_map/ppermute | solution.py:510
  44.0 4.3 %copy-start.6 = (bf16[288,288]{1,0:T(8,128)(2,1)S(1)}, bf16[288,288]{1,0:T(8,128)(2,1)}, u32[]{:S(2)}) copy-start(bf16[288,288]{1,0:T(8,128)(2,1)} %constant.11.clone.place_t) | copy-start | bytes 497668
  48.2 4.2 %collective-permute-start.9 = (bf16[256,2048]{1,0:T(8,128)(2,1)S(1)}, bf16[256,2048]{1,0:T(8,128)(2,1)S(1)}, u32[]{:S(2)}, u32[]{:S(2)}) collective-permute-start(bf16[256,2048]{1,0:T(8,128)(2,1)S(1)} %get-tuple-element.113), channel_id=1, source_target_pairs={{0,1},{1,0},{2,3},{3,2},{4,5},{5,4},{6,7},{7,6},{8,9},{9,8},{10,11... | collective-permute-start | bytes 3145736 | tf_op jit(solution)/shard_map/ppermute | solution.py:510
  50.2 6.0 %copy-start.5 = (f32[512]{0:T(512)S(1)}, f32[512]{0:T(512)}, u32[]{:S(2)}) copy-start(f32[512]{0:T(512)} %gain.5) | copy-start | bytes 6148
  50.3 9.2 %collective-permute-start.17 = (bf16[2,64,1024]{2,1,0:T(8,128)(2,1)S(1)}, bf16[2,64,1024]{2,1,0:T(8,128)(2,1)S(1)}, u32[]{:S(2)}, u32[]{:S(2)}) collective-permute-start(bf16[2,64,1024]{2,1,0:T(8,128)(2,1)S(1)} %get-tuple-element.139), channel_id=1, source_target_pairs={{0,2},{1,3},{2,0},{3,1},{4,6},{5,7},{6,4},{7,5},{8,10},{9,11},{10,... | collective-permute-start | bytes 786440 | tf_op jit(solution)/shard_map/ppermute | solution.py:510
  51.1 9.6 %collective-permute-start.18 = (bf16[2,64,1024]{2,1,0:T(8,128)(2,1)S(1)}, bf16[2,64,1024]{2,1,0:T(8,128)(2,1)S(1)}, u32[]{:S(2)}, u32[]{:S(2)}) collective-permute-start(bf16[2,64,1024]{2,1,0:T(8,128)(2,1)S(1)} %get-tuple-element.141), channel_id=1, source_target_pairs={{0,130},{1,131},{2,128},{3,129},{4,134},{5,135},{6,132},{7,133},{8... | collective-permute-start | bytes 786440 | tf_op jit(solution)/shard_map/ppermute | solution.py:538
  52.5 9.7 %collective-permute-start.10 = (bf16[2,64,1024]{2,1,0:T(8,128)(2,1)S(1)}, bf16[2,64,1024]{2,1,0:T(8,128)(2,1)S(1)}, u32[]{:S(2)}, u32[]{:S(2)}) collective-permute-start(bf16[2,64,1024]{2,1,0:T(8,128)(2,1)S(1)} %get-tuple-element.117), channel_id=1, source_target_pairs={{0,4},{1,5},{2,6},{3,7},{4,0},{5,1},{6,2},{7,3},{8,12},{9,13},{10,... | collective-permute-start | bytes 786440 | tf_op jit(solution)/shard_map/ppermute | solution.py:510
  53.5 9.1 %collective-permute-start.11 = (bf16[2,64,1024]{2,1,0:T(8,128)(2,1)S(1)}, bf16[2,64,1024]{2,1,0:T(8,128)(2,1)S(1)}, u32[]{:S(2)}, u32[]{:S(2)}) collective-permute-start(bf16[2,64,1024]{2,1,0:T(8,128)(2,1)S(1)} %get-tuple-element.119), channel_id=1, source_target_pairs={{0,12},{1,13},{2,14},{3,15},{4,8},{5,9},{6,10},{7,11},{8,4},{9,5},... | collective-permute-start | bytes 786440 | tf_op jit(solution)/shard_map/ppermute | solution.py:510
  60.8 6.3 %collective-permute-start.19 = (bf16[64,1024]{1,0:T(8,128)(2,1)S(1)}, bf16[64,1024]{1,0:T(8,128)(2,1)S(1)}, u32[]{:S(2)}, u32[]{:S(2)}) collective-permute-start(bf16[64,1024]{1,0:T(8,128)(2,1)S(1)} %get-tuple-element.143), channel_id=1, source_target_pairs={{0,130},{1,131},{2,128},{3,129},{4,134},{5,135},{6,132},{7,133},{8... | collective-permute-start | bytes 393224 | tf_op jit(solution)/shard_map/ppermute | solution.py:538
  62.2 5.0 %collective-permute-start.20 = (bf16[64,1024]{1,0:T(8,128)(2,1)S(1)}, bf16[64,1024]{1,0:T(8,128)(2,1)S(1)}, u32[]{:S(2)}, u32[]{:S(2)}) collective-permute-start(bf16[64,1024]{1,0:T(8,128)(2,1)S(1)} %get-tuple-element.145), channel_id=1, source_target_pairs={{0,2},{1,3},{2,0},{3,1},{4,6},{5,7},{6,4},{7,5},{8,10},{9,11},{10,... | collective-permute-start | bytes 393224 | tf_op jit(solution)/shard_map/ppermute | solution.py:510
  62.6 6.3 %collective-permute-start.12 = (bf16[64,1024]{1,0:T(8,128)(2,1)S(1)}, bf16[64,1024]{1,0:T(8,128)(2,1)S(1)}, u32[]{:S(2)}, u32[]{:S(2)}) collective-permute-start(bf16[64,1024]{1,0:T(8,128)(2,1)S(1)} %get-tuple-element.126), channel_id=1, source_target_pairs={{0,12},{1,13},{2,14},{3,15},{4,8},{5,9},{6,10},{7,11},{8,4},{9,5},... | collective-permute-start | bytes 393224 | tf_op jit(solution)/shard_map/ppermute | solution.py:510
  65.8 5.6 %collective-permute-start.13 = (bf16[64,1024]{1,0:T(8,128)(2,1)S(1)}, bf16[64,1024]{1,0:T(8,128)(2,1)S(1)}, u32[]{:S(2)}, u32[]{:S(2)}) collective-permute-start(bf16[64,1024]{1,0:T(8,128)(2,1)S(1)} %get-tuple-element.128), channel_id=1, source_target_pairs={{0,4},{1,5},{2,6},{3,7},{4,0},{5,1},{6,2},{7,3},{8,12},{9,13},{10,... | collective-permute-start | bytes 393224 | tf_op jit(solution)/shard_map/ppermute | solution.py:510
  67.2 6.1 %collective-permute-start.21 = (bf16[2,32,1024]{2,1,0:T(8,128)(2,1)S(1)}, bf16[2,32,1024]{2,1,0:T(8,128)(2,1)S(1)}, u32[]{:S(2)}, u32[]{:S(2)}) collective-permute-start(bf16[2,32,1024]{2,1,0:T(8,128)(2,1)S(1)} %get-tuple-element.147), channel_id=1, source_target_pairs={{0,4},{1,5},{2,6},{3,7},{4,0},{5,1},{6,2},{7,3},{8,12},{9,13},{10,... | collective-permute-start | bytes 393224 | tf_op jit(solution)/shard_map/ppermute | solution.py:510
  71.5 5.1 %collective-permute-start.14 = (bf16[2,32,1024]{2,1,0:T(8,128)(2,1)S(1)}, bf16[2,32,1024]{2,1,0:T(8,128)(2,1)S(1)}, u32[]{:S(2)}, u32[]{:S(2)}) collective-permute-start(bf16[2,32,1024]{2,1,0:T(8,128)(2,1)S(1)} %get-tuple-element.130), channel_id=1, source_target_pairs={{0,2},{1,3},{2,0},{3,1},{4,6},{5,7},{6,4},{7,5},{8,10},{9,11},{10,... | collective-permute-start | bytes 393224 | tf_op jit(solution)/shard_map/ppermute | solution.py:510
  73.4 5.6 %collective-permute-start.22 = (bf16[1,32,1024]{2,1,0:T(8,128)(2,1)S(1)}, bf16[1,32,1024]{2,1,0:T(8,128)(2,1)S(1)}, u32[]{:S(2)}, u32[]{:S(2)}) collective-permute-start(bf16[1,32,1024]{2,1,0:T(8,128)(2,1)S(1)} %get-tuple-element.149), channel_id=1, source_target_pairs={{0,12},{1,13},{2,14},{3,15},{4,8},{5,9},{6,10},{7,11},{8,4},{9,5},... | collective-permute-start | bytes 196616 | tf_op jit(solution)/shard_map/ppermute | solution.py:510
  76.6 5.6 %collective-permute-start.15 = (bf16[1,32,1024]{2,1,0:T(8,128)(2,1)S(1)}, bf16[1,32,1024]{2,1,0:T(8,128)(2,1)S(1)}, u32[]{:S(2)}, u32[]{:S(2)}) collective-permute-start(bf16[1,32,1024]{2,1,0:T(8,128)(2,1)S(1)} %get-tuple-element.132), channel_id=1, source_target_pairs={{0,130},{1,131},{2,128},{3,129},{4,134},{5,135},{6,132},{7,133},{8... | collective-permute-start | bytes 196616 | tf_op jit(solution)/shard_map/ppermute | solution.py:538

commit v5 on v4

--- a/solution.py
+++ b/solution.py
@@ -270,26 +270,23 @@
 
 
 def kernel_forward_a(
-    fields_hbm, ids_hbm, gain_hbm, table, qkv_hbm, out_hbm, place_hbm, sort_hbm, where_hbm,
+    fields_hbm, ids_hbm, gain_hbm, table_hbm, qkv_hbm, out_hbm, place_hbm, sort_hbm, where_hbm,
     piece0, piece1, piece2, piece3, inputs_out, middle_out, normed_out, packed, probs, mixed_t,
-    fields, ids, gain, qkv, out, place, sort, where, grid, spare, key_features, scores, sems,
-):
-    ids_in, where_in, fields_in, place_in, gain_in, qkv_in, out_in, sort_in = fetch(
+    fields, ids, gain, table, qkv, out, place, sort, where, grid, spare, key_features, scores, sems,
+):
+    *early, qkv_in, out_in, sort_in = fetch(
         (
-            (ids_hbm, ids), (where_hbm, where), (fields_hbm, fields), (place_hbm, place),
-            (gain_hbm, gain), (qkv_hbm, qkv), (out_hbm, out), (sort_hbm, sort),
+            (ids_hbm, ids), (where_hbm, where), (table_hbm, table), (fields_hbm, fields),
+            (place_hbm, place), (gain_hbm, gain), (qkv_hbm, qkv), (out_hbm, out), (sort_hbm, sort),
         ),
         sems,
     )
-    ids_in.wait()
-    where_in.wait()
+    for copy in early:
+        copy.wait()
     query_features, features = bias_features(ids, where, table, spare, 0, False)
     key_features[...] = features
-    fields_in.wait()
-    place_in.wait()
     inputs = load_grid(fields, place[...], grid)
     inputs_out[...] = inputs.astype(BF16)
-    gain_in.wait()
     qkv_in.wait()
     out_in.wait()
     normed, delta = forward_core(
@@ -335,8 +332,7 @@
 
 
 def kernel_backward_b(
-    piece0, piece1, piece2, piece3, delta0, delta1, delta2, delta3,
-    inputs, gain, qkv, out, packed, probs, mixed_t, sort, sort_t,
+    piece0, piece1, piece2, piece3, inputs, gain, qkv, out, packed, probs, mixed_t, sort, sort_t,
     back0, back1, back2, back3, upstream_out, d_packed,
     d_probs, d_scores,
 ):
@@ -347,10 +343,7 @@
     d_inputs = norm_backward(
         inputs[...].astype(F32), gain[...].reshape(1, WIDTH), d_packed[...], qkv
     )
-    backs = (back0, back1, back2, back3)
-    split_pieces(sort[...], d_inputs.astype(BF16), [back.at[0] for back in backs])
-    for back, delta in zip(backs, (delta0, delta1, delta2, delta3), strict=True):
-        back[1] = delta[...]
+    split_pieces(sort[...], d_inputs.astype(BF16), (back0, back1, back2, back3))
 
 
 def kernel_grads_b(normed, mixed_t, upstream, d_packed, send, keep, normed_t):
@@ -365,7 +358,7 @@
     grad_middle_out, d_packed, send,
     d_probs, d_scores,
 ):
-    d_inputs = join_pieces(sort_t[...], [back[0] for back in (back0, back1, back2, back3)])
+    d_inputs = join_pieces(sort_t[...], [ref[...] for ref in (back0, back1, back2, back3)])
     grad_middle = (upstream[...].astype(F32) + d_inputs).astype(BF16)
     grad_middle_out[...] = grad_middle
     backward_core(grad_middle, out, packed, probs, mixed_t, d_packed, d_probs, d_scores)
@@ -373,13 +366,13 @@
     grads_half(1 - core, normed_t, mixed_t, grad_middle, d_packed, send)
 
 
-def kernel_keep_a(
-    back0, back1, back2, back3, middle, normed_t, mixed_t, grad_middle, d_packed, place_t, sort_t,
-    keep, advanced,
-):
+def kernel_keep_a(normed_t, mixed_t, grad_middle, d_packed, keep):
     core = lax.axis_index("lat") % 2
     grads_half(core, normed_t, mixed_t, grad_middle[...], d_packed, keep)
-    delta = join_pieces(sort_t[...], [back[1] for back in (back0, back1, back2, back3)])
+
+
+def kernel_advanced(back0, back1, back2, back3, middle, place_t, sort_t, advanced):
+    delta = join_pieces(sort_t[...], [ref[...] for ref in (back0, back1, back2, back3)])
     store_grid(advanced, place_t[...], (middle[...].astype(F32) + delta).astype(BF16))
 
 
@@ -418,16 +411,13 @@
             target[place] = keep[rows, columns] + got[rows, columns]
 
 
-def kernel_first_sum_b(keep, got, send_one, send_two, keep_one, keep_two):
+def kernel_first_sum_b(keep, got, send, kept):
     x = place_x()
-    for part, first, send, kept in ((0, 1, send_one, keep_one), (1, 3, send_two, keep_two)):
-        for target, place, block in (
-            (send, 0, x ^ first), (send, 1, x ^ 2), (kept, 0, x), (kept, 1, x ^ 2 ^ first)
-        ):
-            columns = rows_of(block // 2, SIDE)
-            for inner in range(2):
-                rows = rows_of((part * 2 + inner) * 2 + block % 2, 32)
-                target[place, inner * 32 : (inner + 1) * 32] = keep[rows, columns] + got[rows, columns]
+    for target, place, block in ((send, 0, x ^ 1), (send, 1, x ^ 2), (kept, 0, x), (kept, 1, x ^ 3)):
+        columns = rows_of(block // 2, SIDE)
+        for y in range(4):
+            rows = rows_of(y * 2 + block % 2, 32)
+            target[place, y * 32 : (y + 1) * 32] = keep[rows, columns] + got[rows, columns]
 
 
 def kernel_second_sum(keep_one, got_one, keep_two, got_two, send_one, send_two, held_one, held_two):
@@ -451,8 +441,11 @@
     third_sum(place_x(), ((held_one, got_one), (held_two, got_two)), send, keep)
 
 
-def kernel_third_sum_b(held_one, got_one, held_two, got_two, send, keep):
-    third_sum(place_y(), ((held_one, got_one), (held_two, got_two)), send, keep)
+def kernel_third_sum_b(held, got, send, keep):
+    y = place_y()
+    for target, place, block in ((send, 0, y ^ 1), (send, 1, y ^ 2), (keep, 0, y), (keep, 1, y ^ 3)):
+        rows = rows_of(block, 32)
+        target[place] = held[0, rows] + got[0, rows]
 
 
 def kernel_halve(keep, got, send, held):
@@ -488,7 +481,7 @@
         pltpu.with_memory_space_constraint(arg, pltpu.HBM) if at in hbm or at in smem else arg
         for at, arg in enumerate(args)
     ]
-    shapes = [pltpu.VMEM(shape, kind) for shape, kind in scratch]
+    shapes = [pltpu.VMEM(*item) if isinstance(item, tuple) else item for item in scratch]
     if copies:
         shapes.append(pltpu.SemaphoreType.DMA((copies,)))
     return pl.pallas_call(
@@ -592,9 +585,12 @@
     p0, p1, p2, p3, inputs_a, middle_a, normed_a, packed_a, probs_a, mixed_a = call(
         kernel_forward_a,
         [piece] * 4 + [token] * 3 + [packed, probs, mixed_t],
-        [grid, ids, vector, qkv_shape, out_shape, square, square, place_of, token_wide, spare, keys, scores],
+        [
+            grid, ids, vector, pltpu.SMEM(table_a.shape, F32), qkv_shape, out_shape, square, square,
+            place_of, token_wide, spare, keys, scores,
+        ],
         (fields, land_ids, gain_a, table_a, qkv_weight_a, out_weight_a, place, sort, where),
-        smem=(3,), hbm=(0, 1, 2, 4, 5, 6, 7, 8), copies=8, flops=7 * 10**9,
+        hbm=(0, 1, 2, 3, 4, 5, 6, 7, 8), copies=9, flops=7 * 10**9,
     )
     diagonal = permute_both(p0, -1)
     below = permute(p1, "lat", lambda i: i - 1)
@@ -616,14 +612,13 @@
         (p3, eastern, below, diagonal, query_b, keys_b, gain_b, qkv_weight_b, out_weight_b, sort, sort_t),
         flops=5 * 10**9,
     )
-    twin = ((2, PIECE, WIDTH), BF16)
     d0, d1, d2, d3, upstream_b, d_packed_b = call(
         kernel_backward_b,
-        [twin] * 4 + [token, packed],
+        [piece] * 4 + [token, packed],
         [scores, probs],
         (
-            c3, c_eastern, c_below, c_diagonal, b0, b1, b2, b3, inputs_b, gain_b, qkv_weight_b,
-            out_weight_b, packed_b, probs_b, mixed_b, sort, sort_t,
+            c3, c_eastern, c_below, c_diagonal, inputs_b, gain_b, qkv_weight_b, out_weight_b,
+            packed_b, probs_b, mixed_b, sort, sort_t,
         ),
         flops=5 * 10**9,
     )
@@ -634,12 +629,10 @@
         kernel_grads_b, [half_grads] * 2, [normed_t], (normed_b, mixed_b, upstream_b, d_packed_b),
         flops=2 * 10**9,
     )
-    send_one_b, send_two_b, keep_one_b, keep_two_b = quarters(
-        kernel_first_sum_b, keep_b, to_core(send_b)
-    )
-    parts_b = (keep_one_b, to_x(send_one_b, 1), keep_two_b, to_x(send_two_b, 3))
-    send_one_b, send_two_b, held_one_b, held_two_b = second_sum(parts_b)
-    parts_b = (held_one_b, to_x(send_one_b, 3), held_two_b, to_x(send_two_b, 1))
+    send_b, keep_b = call(
+        kernel_first_sum_b, [((2, 128, SIDE), BF16)] * 2, [], (keep_b, to_core(send_b))
+    )
+    got_b = to_x(send_b, 1)
     grad_middle, d_packed_a, send_a = call(
         kernel_backward_a,
         [token, packed, half_grads],
@@ -651,16 +644,10 @@
         flops=5 * 10**9,
     )
     got_a = to_core(send_a)
-    keep_a, advanced = call(
-        kernel_keep_a,
-        [half_grads, grid],
-        [],
-        (
-            d3, d2, d1, d0, middle_a, normed_a_t, mixed_a, grad_middle, d_packed_a, place_t,
-            sort_t,
-        ),
-        flops=2 * 10**9, final=(1,),
-    )
+    keep_a = call(
+        kernel_keep_a, [half_grads], [], (normed_a_t, mixed_a, grad_middle, d_packed_a),
+        flops=10**9,
+    )[0]
     send_one_a, send_two_a, keep_one_a, keep_two_a = quarters(kernel_first_sum_a, keep_a, got_a)
     send_one_a, send_two_a, d_packed_a = lax.optimization_barrier((send_one_a, send_two_a, d_packed_a))
     parts_a = (keep_one_a, to_y(send_one_a, 1), keep_two_a, to_y(send_two_a, 3))
@@ -671,8 +658,11 @@
         (inputs_a, grad_middle, gain_a, qkv_weight_a, d_packed_a, place_t),
         hbm=(3,), copies=1, flops=4 * 10**9, final=(0,),
     )[0]
+    got_b, grad_fields = lax.optimization_barrier((got_b, grad_fields))
+    send_b, keep_b = halve(keep_b, got_b)
+    got_b = to_x(send_b, 3)
     pair = ((2, 32, SIDE), BF16)
-    send_b, keep_b = call(kernel_third_sum_b, [pair] * 2, [], parts_b)
+    send_b, keep_b = call(kernel_third_sum_b, [pair] * 2, [], (keep_b, got_b))
     got_b = to_y(send_b, 1)
     send_one_a, send_two_a, held_one_a, held_two_a = second_sum(parts_a)
     send_one_a, send_two_a, grad_fields = lax.optimization_barrier(
@@ -688,7 +678,18 @@
     blocks = call(
         kernel_columns, [((8, 64, GROUP), BF16)], [], (keep_a, got_a, keep_b, got_b)
     )[0]
+    blocks, b1, b2, b3 = lax.optimization_barrier((blocks, b1, b2, b3))
     parts = exchange_z(blocks)
+    advanced = call(
+        kernel_advanced,
+        [grid],
+        [],
+        (
+            permute_both(b3, 1), permute(b2, "lat", lambda i: i + 1),
+            permute(b1, "lon", lambda i: i + 1), b0, middle_a, place_t, sort_t,
+        ),
+        flops=10**9, final=(0,),
+    )[0]
     grads = call(
         kernel_total,
         [((32, 96), F32), ((32, 32), F32)] * 2,

time: 94.7 us -> 98.8 us (1.043)
  the two profiles are of different devices: /device:TPU:6 before, /device:TPU:1 now
where the time goes in v5:
time: 98.8 us; the launch traced here: 98.6 us
  starting transfers between devices  39 us (39%)
  waiting for transfers between devices  29.4 us (30%)
  Pallas kernels  29.1 us (29%)
    pallas_call x19, Pallas kernels, call(): pl.pallas_call(kernel, out_shape=tuple((jax.ShapeDtypeStruct(shape, kind)...  29.1 us
    ppermute x18, starting transfers between devices, permute(): lax.ppermute(array, axis, [(i, target(i) % length) for i in range(length)])  21.9 us
    ppermute x18, waiting for transfers between devices, permute(): lax.ppermute(array, axis, [(i, target(i) % length) for i in range(length)])  18 us
    ppermute x4, starting transfers between devices, permute_both(): return lax.ppermute(array, ('lon', 'lat'), pairs)  12.1 us
    ppermute x4, waiting for transfers between devices, permute_both(): return lax.ppermute(array, ('lon', 'lat'), pairs)  9.25 us
    all_to_all x1, starting transfers between devices, exchange_z(): lax.all_to_all(messages, 'lon', 0, 0, axis_index_groups=groups, tiled=True)  3.37 us
    ppermute x2, waiting for transfers between devices, to_x(): return lax.ppermute(array, ('lon', 'lat'), pairs)  2.2 us
  transfers between devices with their start and end apart: 25, of which 13 were waited for; matrix products, arithmetic and copies ran while one was open for 0% of the time, Pallas kernels for 18%

profile of v5, /device:TPU:1, one launch (start us, length us, event | category | flops | bytes accessed | tf_op | source)
XLA Modules:
  0.0 98.6 jit_solution(2955582936509222363)
XLA Ops:
  0.6 0.0 copy-start.8
  0.7 0.0 copy-start.9
  0.7 0.0 copy-start.10
  0.7 5.5 %shard_map.199 = (bf16[72,512]{1,0:T(8,128)(2,1)S(1)}, bf16[72,512]{1,0:T(8,128)(2,1)S(1)}, bf16[72,512]{1,0:T(8,128)(2,1)S(1)}, bf16[72,512]{1,0:T(8,128)(2,1)S...) custom-call(bf16[12,6,4,512]{3,2,1,0:T(4,128)(2,1)} %bitcast.6, ...), custom_call_target="tpu_custom_call" | custom-call | flops 7000000000 | bytes 1048576 | tf_op jit(solution)/shard_map/pallas_call | solution.py:487
  6.2 8.9 %collective-permute-start.3 = (bf16[72,512]{1,0:T(8,128)(2,1)S(1)}, bf16[72,512]{1,0:T(8,128)(2,1)S(1)}, u32[]{:S(2)}, u32[]{:S(2)}) collective-permute-start(bf16[72,512]{1,0:T(8,128)(2,1)S(1)} %get-tuple-element.88), channel_id=1, source_target_pairs={{0,240},{16,0},{32,16},{48,32},{64,48},{80,64},{96,80},{112,96},{1... | collective-permute-start | bytes 221192 | tf_op jit(solution)/shard_map/ppermute | solution.py:503
  15.1 1.0 collective-permute-start.4
  16.1 3.4 %collective-permute-start.5 = (bf16[72,512]{1,0:T(8,128)(2,1)S(1)}, bf16[72,512]{1,0:T(8,128)(2,1)S(1)}, u32[]{:S(2)}, u32[]{:S(2)}) collective-permute-start(bf16[72,512]{1,0:T(8,128)(2,1)S(1)} %get-tuple-element.90), channel_id=1, source_target_pairs={{0,255},{1,240},{2,241},{3,242},{4,243},{5,244},{6,245},{7,246},{8... | collective-permute-start | bytes 221192 | tf_op jit(solution)/shard_map/ppermute | solution.py:513
  19.5 0.0 copy-start
  19.5 0.0 copy-start.1
  19.6 0.0 copy-start.4
  19.6 0.0 copy-start.6
  19.6 2.9 %shard_map.200 = (bf16[72,512]{1,0:T(8,128)(2,1)S(1)}, bf16[72,512]{1,0:T(8,128)(2,1)S(1)}, bf16[72,512]{1,0:T(8,128)(2,1)S(1)}, bf16[72,512]{1,0:T(8,128)(2,1)S...) custom-call(bf16[12,6,4,512]{3,2,1,0:T(4,128)(2,1)} %bitcast.7, ...), custom_call_target="tpu_custom_call" | custom-call | flops 2000000000 | bytes 1048576 | tf_op jit(solution)/shard_map/pallas_call | solution.py:487
  22.5 0.8 collective-permute-start
  23.3 1.1 %collective-permute-start.1 = (bf16[72,512]{1,0:T(8,128)(2,1)S(1)}, bf16[72,512]{1,0:T(8,128)(2,1)S(1)}, u32[]{:S(2)}, u32[]{:S(2)}) collective-permute-start(bf16[72,512]{1,0:T(8,128)(2,1)S(1)} %get-tuple-element.85), channel_id=1, source_target_pairs={{0,15},{1,0},{2,1},{3,2},{4,3},{5,4},{6,5},{7,6},{8,7},{9,8},{10,9... | collective-permute-start | bytes 221192 | tf_op jit(solution)/shard_map/ppermute | solution.py:503
  24.4 0.0 collective-permute-done.3.piece1
  24.4 0.6 collective-permute-start.2
  25.0 0.0 collective-permute-done.5.piece3
  25.0 3.8 %shard_map.201 = (bf16[72,512]{1,0:T(8,128)(2,1)S(1)}, bf16[72,512]{1,0:T(8,128)(2,1)S(1)}, bf16[72,512]{1,0:T(8,128)(2,1)S(1)}, bf16[72,512]{1,0:T(8,128)(2,1)S...) custom-call(bf16[72,512]{1,0:T(8,128)(2,1)S(1)} %get-tuple-element.8, ...), custom_call_target="tpu_custom_call" | custom-call | flops 5000000000 | bytes 1048576 | tf_op jit(solution)/shard_map/pallas_call | solution.py:487
  28.8 0.0 collective-permute-done.piece1
  28.8 0.0 collective-permute-done.1.piece2
  28.8 0.2 collective-permute-done.2.piece3
  29.1 4.4 %shard_map.202 = (bf16[72,512]{1,0:T(8,128)(2,1)S(1)}, bf16[72,512]{1,0:T(8,128)(2,1)S(1)}, bf16[72,512]{1,0:T(8,128)(2,1)S(1)}, bf16[72,512]{1,0:T(8,128)(2,1)S...) custom-call(bf16[72,512]{1,0:T(8,128)(2,1)S(1)} %get-tuple-element.83.piece0, ...), custom_call_target="tpu_custom_call" | custom-call | flops 5000000000 | bytes 1048576 | tf_op jit(solution)/shard_map/pallas_call | solution.py:487
  33.4 1.9 %collective-permute-start.6 = (bf16[72,512]{1,0:T(8,128)(2,1)S(1)}, bf16[72,512]{1,0:T(8,128)(2,1)S(1)}, u32[]{:S(2)}, u32[]{:S(2)}) collective-permute-start(bf16[72,512]{1,0:T(8,128)(2,1)S(1)} %get-tuple-element.97), channel_id=1, source_target_pairs={{0,17},{1,18},{2,19},{3,20},{4,21},{5,22},{6,23},{7,24},{8,25},{9,... | collective-permute-start | bytes 221192 | tf_op jit(solution)/shard_map/ppermute | solution.py:513
  35.3 0.5 collective-permute-start.8
  35.9 1.3 %shard_map.207 = (bf16[256,2048]{1,0:T(8,128)(2,1)S(1)}, bf16[256,2048]{1,0:T(8,128)(2,1)S(1)}) custom-call(bf16[288,512]{1,0:T(8,128)(2,1)S(1)} %get-tuple-element.116.normed, bf16[2,512,144]{2,1,0:T(8,128)(2,1)S(1)} %get-tuple-element.96.mixed_t, bf16[288,512]{1,0:T(8,128)(2,1)S(1)} %get-tuple-element.117.upstream, ...), custom_call_target="tpu_custom_call" | custom-call | flops 2000000000 | bytes 1048576 | tf_op jit(solution)/shard_map/pallas_call | solution.py:487
  37.2 0.4 collective-permute-start.12
  37.6 3.3 %collective-permute-done.6.back0 = bf16[72,512]{1,0:T(8,128)(2,1)S(1)} collective-permute-done((bf16[72,512]{1,0:T(8,128)(2,1)S(1)}, bf16[72,512]{1,0:T(8,128)(2,1)S(1)}, u32[]{:S(2)}, u32[]{:S(2)}) %collective-permute-start.6) | collective-permute-done | bytes 73760 | tf_op jit(solution)/shard_map/ppermute | solution.py:513
  40.9 1.2 %collective-permute-done.8.back2 = bf16[72,512]{1,0:T(8,128)(2,1)S(1)} collective-permute-done((bf16[72,512]{1,0:T(8,128)(2,1)S(1)}, bf16[72,512]{1,0:T(8,128)(2,1)S(1)}, u32[]{:S(2)}, u32[]{:S(2)}) %collective-permute-start.8) | collective-permute-done | bytes 73760 | tf_op jit(solution)/shard_map/ppermute | solution.py:503
  42.1 4.0 %shard_map.203 = (bf16[288,512]{1,0:T(8,128)(2,1)S(1)}, bf16[288,1536]{1,0:T(8,128)(2,1)S(1)}, bf16[256,2048]{1,0:T(8,128)(2,1)S(1)}) custom-call(bf16[72,512]{1,0:T(8,128)(2,1)S(1)} %collective-permute-done.6.back0, bf16[72,512]{1,0:T(8,128)(2,1)S(1)} %collective-permute-done.7.back1, bf16[72,512]{1,0:T(8,128)(2,1)S(1)} %collective-permute-done.8.back2, ...), custom_call_target="tpu_custom_call" | custom-call | flops 5000000000 | bytes 1048576 | tf_op jit(solution)/shard_map/pallas_call | solution.py:487
  46.2 1.8 %collective-permute-start.9 = (bf16[256,2048]{1,0:T(8,128)(2,1)S(1)}, bf16[256,2048]{1,0:T(8,128)(2,1)S(1)}, u32[]{:S(2)}, u32[]{:S(2)}) collective-permute-start(bf16[256,2048]{1,0:T(8,128)(2,1)S(1)} %get-tuple-element.106), channel_id=1, source_target_pairs={{0,1},{1,0},{2,3},{3,2},{4,5},{5,4},{6,7},{7,6},{8,9},{9,8},{10,11... | collective-permute-start | bytes 3145736 | tf_op jit(solution)/shard_map/ppermute | solution.py:503
  47.9 0.1 shard_map.208
  48.0 0.1 collective-permute-start.13
  48.1 0.0 copy-start.5
  48.2 0.0 copy-start.7
  48.2 0.7 shard_map.204.keep
  48.9 1.3 %collective-permute-done.9.got = bf16[256,2048]{1,0:T(8,128)(2,1)S(1)} collective-permute-done((bf16[256,2048]{1,0:T(8,128)(2,1)S(1)}, bf16[256,2048]{1,0:T(8,128)(2,1)S(1)}, u32[]{:S(2)}, u32[]{:S(2)}) %collective-permute-start.9) | collective-permute-done | bytes 1048608 | tf_op jit(solution)/shard_map/ppermute | solution.py:503
  50.2 0.1 shard_map.205
  50.3 0.1 collective-permute-start.10
  50.4 1.5 %collective-permute-start.11 = (bf16[2,64,1024]{2,1,0:T(8,128)(2,1)S(1)}, bf16[2,64,1024]{2,1,0:T(8,128)(2,1)S(1)}, u32[]{:S(2)}, u32[]{:S(2)}) collective-permute-start(bf16[2,64,1024]{2,1,0:T(8,128)(2,1)S(1)} %get-tuple-element.112), channel_id=1, source_target_pairs={{0,12},{1,13},{2,14},{3,15},{4,8},{5,9},{6,10},{7,11},{8,4},{9,5},... | collective-permute-start | bytes 786440 | tf_op jit(solution)/shard_map/ppermute | solution.py:503
  51.9 3.2 %shard_map.209 = bf16[12,6,4,512]{3,2,1,0:T(4,128)(2,1)} custom-call(bf16[288,512]{1,0:T(8,128)(2,1)S(1)} %get-tuple-element.122.inputs, bf16[288,512]{1,0:T(8,128)(2,1)S(1)} %get-tuple-element.104.grad_middle, f32[512]{0:T(512)S(1)} %copy-done.5, bf16[512,1536]{1,0:T(8,128)(2,1)} %qkv_hbm.3, bf16[288,1536]{1,0:T(8,128)(2,1)S(1)} %get-tuple-element.123.d_packed, ...), custom_call_target="tpu_custom_call" | custom-call | flops 4000000000 | bytes 1048576 | tf_op jit(solution)/shard_map/pallas_call | solution.py:487
  55.1 6.5 %collective-permute-done.13.got = bf16[2,128,1024]{2,1,0:T(8,128)(2,1)S(1)} collective-permute-done((bf16[2,128,1024]{2,1,0:T(8,128)(2,1)S(1)}, bf16[2,128,1024]{2,1,0:T(8,128)(2,1)S(1)}, u32[]{:S(2)}, u32[]{:S(2)}) %collective-permute-start.13) | collective-permute-done | bytes 524320 | tf_op jit(solution)/shard_map/ppermute | solution.py:503
  61.6 0.1 shard_map.212
  61.7 0.1 collective-permute-start.18
  61.8 0.1 shard_map.206
  61.9 2.6 %collective-permute-start.14 = (bf16[64,1024]{1,0:T(8,128)(2,1)S(1)}, bf16[64,1024]{1,0:T(8,128)(2,1)S(1)}, u32[]{:S(2)}, u32[]{:S(2)}) collective-permute-start(bf16[64,1024]{1,0:T(8,128)(2,1)S(1)} %get-tuple-element.125), channel_id=1, source_target_pairs={{0,12},{1,13},{2,14},{3,15},{4,8},{5,9},{6,10},{7,11},{8,4},{9,5},... | collective-permute-start | bytes 393224 | tf_op jit(solution)/shard_map/ppermute | solution.py:503
  64.5 2.8 %collective-permute-done.14.got_one = bf16[64,1024]{1,0:T(8,128)(2,1)S(1)} collective-permute-done((bf16[64,1024]{1,0:T(8,128)(2,1)S(1)}, bf16[64,1024]{1,0:T(8,128)(2,1)S(1)}, u32[]{:S(2)}, u32[]{:S(2)}) %collective-permute-start.14) | collective-permute-done | bytes 131104 | tf_op jit(solution)/shard_map/ppermute | solution.py:503
  67.3 1.3 %collective-permute-done.15.got_two = bf16[64,1024]{1,0:T(8,128)(2,1)S(1)} collective-permute-done((bf16[64,1024]{1,0:T(8,128)(2,1)S(1)}, bf16[64,1024]{1,0:T(8,128)(2,1)S(1)}, u32[]{:S(2)}, u32[]{:S(2)}) %collective-permute-start.15) | collective-permute-done | bytes 131104 | tf_op jit(solution)/shard_map/ppermute | solution.py:503
  68.6 0.1 shard_map.210
  68.7 0.2 collective-permute-start.16
  68.9 1.1 %collective-permute-done.18.got = bf16[1,128,1024]{2,1,0:T(8,128)(2,1)S(1)} collective-permute-done((bf16[1,128,1024]{2,1,0:T(8,128)(2,1)S(1)}, bf16[1,128,1024]{2,1,0:T(8,128)(2,1)S(1)}, u32[]{:S(2)}, u32[]{:S(2)}) %collective-permute-start.18) | collective-permute-done | bytes 262176 | tf_op jit(solution)/shard_map/ppermute | solution.py:531
  70.0 0.1 collective-permute-start.19
  70.1 2.5 %collective-permute-done.16.got = bf16[2,32,1024]{2,1,0:T(8,128)(2,1)S(1)} collective-permute-done((bf16[2,32,1024]{2,1,0:T(8,128)(2,1)S(1)}, bf16[2,32,1024]{2,1,0:T(8,128)(2,1)S(1)}, u32[]{:S(2)}, u32[]{:S(2)}) %collective-permute-start.16) | collective-permute-done | bytes 131104 | tf_op jit(solution)/shard_map/ppermute | solution.py:503
  72.6 1.6 %collective-permute-start.17 = (bf16[1,32,1024]{2,1,0:T(8,128)(2,1)S(1)}, bf16[1,32,1024]{2,1,0:T(8,128)(2,1)S(1)}, u32[]{:S(2)}, u32[]{:S(2)}) collective-permute-start(bf16[1,32,1024]{2,1,0:T(8,128)(2,1)S(1)} %get-tuple-element.131), channel_id=1, source_target_pairs={{0,130},{1,131},{2,128},{3,129},{4,134},{5,135},{6,132},{7,133},{8... | collective-permute-start | bytes 196616 | tf_op jit(solution)/shard_map/ppermute | solution.py:531
  74.2 1.7 %collective-permute-start.20 = (bf16[1,32,1024]{2,1,0:T(8,128)(2,1)S(1)}, bf16[1,32,1024]{2,1,0:T(8,128)(2,1)S(1)}, u32[]{:S(2)}, u32[]{:S(2)}) collective-permute-start(bf16[1,32,1024]{2,1,0:T(8,128)(2,1)S(1)} %get-tuple-element.139), channel_id=1, source_target_pairs={{0,12},{1,13},{2,14},{3,15},{4,8},{5,9},{6,10},{7,11},{8,4},{9,5},... | collective-permute-start | bytes 196616 | tf_op jit(solution)/shard_map/ppermute | solution.py:503
  75.9 1.1 %collective-permute-done.17.got_a = bf16[1,32,1024]{2,1,0:T(8,128)(2,1)S(1)} collective-permute-done((bf16[1,32,1024]{2,1,0:T(8,128)(2,1)S(1)}, bf16[1,32,1024]{2,1,0:T(8,128)(2,1)S(1)}, u32[]{:S(2)}, u32[]{:S(2)}) %collective-permute-start.17) | collective-permute-done | bytes 65568 | tf_op jit(solution)/shard_map/ppermute | solution.py:531
  77.0 1.6 %collective-permute-done.20.got_b = bf16[1,32,1024]{2,1,0:T(8,128)(2,1)S(1)} collective-permute-done((bf16[1,32,1024]{2,1,0:T(8,128)(2,1)S(1)}, bf16[1,32,1024]{2,1,0:T(8,128)(2,1)S(1)}, u32[]{:S(2)}, u32[]{:S(2)}) %collective-permute-start.20) | collective-permute-done | bytes 65568 | tf_op jit(solution)/shard_map/ppermute | solution.py:503
  78.6 0.8 shard_map.215
  79.4 3.4 %all-to-all-start = ((bf16[8,64,128]{2,1,0:T(8,128)(2,1)}), bf16[8,64,128]{2,1,0:T(8,128)(2,1)S(1)}, u32[]{:S(2)}, u32[]{:S(2)}) async-start(bf16[8,64,128]{2,1,0:T(8,128)(2,1)} %shard_map.215), calls=%async_computation | async-start | bytes 262144 | tf_op jit(solution)/shard_map/all_to_all | solution.py:549
  82.8 6.1 %collective-permute-start.21 = (bf16[72,512]{1,0:T(8,128)(2,1)S(1)}, bf16[72,512]{1,0:T(8,128)(2,1)S(1)}, u32[]{:S(2)}, u32[]{:S(2)}) collective-permute-start(bf16[72,512]{1,0:T(8,128)(2,1)S(1)} %get-tuple-element.143), channel_id=1, source_target_pairs={{0,17},{1,18},{2,19},{3,20},{4,21},{5,22},{6,23},{7,24},{8,25},{9,... | collective-permute-start | bytes 221192 | tf_op jit(solution)/shard_map/ppermute | solution.py:513
  88.9 1.2 %collective-permute-start.23 = (bf16[72,512]{1,0:T(8,128)(2,1)S(1)}, bf16[72,512]{1,0:T(8,128)(2,1)S(1)}, u32[]{:S(2)}, u32[]{:S(2)}) collective-permute-start(bf16[72,512]{1,0:T(8,128)(2,1)S(1)} %get-tuple-element.145), channel_id=1, source_target_pairs={{0,16},{16,32},{32,48},{48,64},{64,80},{80,96},{96,112},{112,128},... | collective-permute-start | bytes 221192 | tf_op jit(solution)/shard_map/ppermute | solution.py:503
  90.1 5.8 %collective-permute-done.21.back0 = bf16[72,512]{1,0:T(8,128)(2,1)S(1)} collective-permute-done((bf16[72,512]{1,0:T(8,128)(2,1)S(1)}, bf16[72,512]{1,0:T(8,128)(2,1)S(1)}, u32[]{:S(2)}, u32[]{:S(2)}) %collective-permute-start.21) | collective-permute-done | bytes 73760 | tf_op jit(solution)/shard_map/ppermute | solution.py:513
  95.9 0.7 collective-permute-done.23.back2
  96.6 1.3 %shard_map.216 = bf16[12,6,4,512]{3,2,1,0:T(4,128)(2,1)} custom-call(bf16[72,512]{1,0:T(8,128)(2,1)S(1)} %collective-permute-done.21.back0, bf16[72,512]{1,0:T(8,128)(2,1)S(1)} %collective-permute-done.22.back1, bf16[72,512]{1,0:T(8,128)(2,1)S(1)} %collective-permute-done.23.back2, bf16[72,512]{1,0:T(8,128)(2,1)S(1)} %get-tuple-element.146.back3, ...), custom_call_target="tpu_custom_call" | custom-call | flops 1000000000 | bytes 1048576 | tf_op jit(solution)/shard_map/pallas_call | solution.py:487
  97.9 0.7 shard_map.217
  (27 shorter events, 0.1 us)
Async XLA Ops:
  0.6 18.9 %copy-start.3 = (s32[192,96]{1,0:T(8,128)S(1)}, s32[192,96]{1,0:T(8,128)}, u32[]{:S(2)}) copy-start(s32[192,96]{1,0:T(8,128)} %ids.1) | copy-start | bytes 221188
  0.6 18.9 %copy-start.8 = (bf16[288,288]{1,0:T(8,128)(2,1)S(1)}, bf16[288,288]{1,0:T(8,128)(2,1)}, u32[]{:S(2)}) copy-start(bf16[288,288]{1,0:T(8,128)(2,1)} %constant.12.clone.sort_hbm.sort) | copy-start | bytes 497668
  0.7 18.9 %copy-start.9 = (bf16[288,288]{1,0:T(8,128)(2,1)S(1)}, bf16[288,288]{1,0:T(8,128)(2,1)}, u32[]{:S(2)}) copy-start(bf16[288,288]{1,0:T(8,128)(2,1)} %constant.10.clone.place_hbm.place) | copy-start | bytes 497668
  0.7 18.9 %copy-start.10 = (s32[144,8]{1,0:T(8,128)S(1)}, s32[144,8]{1,0:T(8,128)}, u32[]{:S(2)}) copy-start(s32[144,8]{1,0:T(8,128)} %constant.14.clone.where_hbm.where) | copy-start | bytes 13828
  6.2 18.2 %collective-permute-start.3 = (bf16[72,512]{1,0:T(8,128)(2,1)S(1)}, bf16[72,512]{1,0:T(8,128)(2,1)S(1)}, u32[]{:S(2)}, u32[]{:S(2)}) collective-permute-start(bf16[72,512]{1,0:T(8,128)(2,1)S(1)} %get-tuple-element.88), channel_id=1, source_target_pairs={{0,240},{16,0},{32,16},{48,32},{64,48},{80,64},{96,80},{112,96},{1... | collective-permute-start | bytes 221192 | tf_op jit(solution)/shard_map/ppermute | solution.py:503
  15.1 9.9 %collective-permute-start.4 = (bf16[72,512]{1,0:T(8,128)(2,1)S(1)}, bf16[72,512]{1,0:T(8,128)(2,1)S(1)}, u32[]{:S(2)}, u32[]{:S(2)}) collective-permute-start(bf16[72,512]{1,0:T(8,128)(2,1)S(1)} %get-tuple-element.89), channel_id=1, source_target_pairs={{0,15},{1,0},{2,1},{3,2},{4,3},{5,4},{6,5},{7,6},{8,7},{9,8},{10,9... | collective-permute-start | bytes 221192 | tf_op jit(solution)/shard_map/ppermute | solution.py:503
  16.1 8.9 %collective-permute-start.5 = (bf16[72,512]{1,0:T(8,128)(2,1)S(1)}, bf16[72,512]{1,0:T(8,128)(2,1)S(1)}, u32[]{:S(2)}, u32[]{:S(2)}) collective-permute-start(bf16[72,512]{1,0:T(8,128)(2,1)S(1)} %get-tuple-element.90), channel_id=1, source_target_pairs={{0,255},{1,240},{2,241},{3,242},{4,243},{5,244},{6,245},{7,246},{8... | collective-permute-start | bytes 221192 | tf_op jit(solution)/shard_map/ppermute | solution.py:513
  19.5 5.5 %copy-start = (bf16[512,1536]{1,0:T(8,128)(2,1)S(1)}, bf16[512,1536]{1,0:T(8,128)(2,1)}, u32[]{:S(2)}) copy-start(bf16[512,1536]{1,0:T(8,128)(2,1)} %qkv.3) | copy-start | bytes 4718596
  19.5 5.5 %copy-start.1 = (bf16[512,512]{1,0:T(8,128)(2,1)S(1)}, bf16[512,512]{1,0:T(8,128)(2,1)}, u32[]{:S(2)}) copy-start(bf16[512,512]{1,0:T(8,128)(2,1)} %out.4) | copy-start | bytes 1572868
  19.6 5.5 %copy-start.4 = (f32[512]{0:T(512)S(1)}, f32[512]{0:T(512)}, u32[]{:S(2)}) copy-start(f32[512]{0:T(512)} %gain.4) | copy-start | bytes 6148
  19.6 5.5 %copy-start.6 = (bf16[288,288]{1,0:T(8,128)(2,1)S(1)}, bf16[288,288]{1,0:T(8,128)(2,1)}, u32[]{:S(2)}) copy-start(bf16[288,288]{1,0:T(8,128)(2,1)} %constant.13.clone.sort_t) | copy-start | bytes 497668
  22.5 6.3 %collective-permute-start = (bf16[72,512]{1,0:T(8,128)(2,1)S(1)}, bf16[72,512]{1,0:T(8,128)(2,1)S(1)}, u32[]{:S(2)}, u32[]{:S(2)}) collective-permute-start(bf16[72,512]{1,0:T(8,128)(2,1)S(1)} %get-tuple-element.84), channel_id=1, source_target_pairs={{0,240},{16,0},{32,16},{48,32},{64,48},{80,64},{96,80},{112,96},{1... | collective-permute-start | bytes 221192 | tf_op jit(solution)/shard_map/ppermute | solution.py:503
  23.3 5.5 %collective-permute-start.1 = (bf16[72,512]{1,0:T(8,128)(2,1)S(1)}, bf16[72,512]{1,0:T(8,128)(2,1)S(1)}, u32[]{:S(2)}, u32[]{:S(2)}) collective-permute-start(bf16[72,512]{1,0:T(8,128)(2,1)S(1)} %get-tuple-element.85), channel_id=1, source_target_pairs={{0,15},{1,0},{2,1},{3,2},{4,3},{5,4},{6,5},{7,6},{8,7},{9,8},{10,9... | collective-permute-start | bytes 221192 | tf_op jit(solution)/shard_map/ppermute | solution.py:503
  24.4 4.7 %collective-permute-start.2 = (bf16[72,512]{1,0:T(8,128)(2,1)S(1)}, bf16[72,512]{1,0:T(8,128)(2,1)S(1)}, u32[]{:S(2)}, u32[]{:S(2)}) collective-permute-start(bf16[72,512]{1,0:T(8,128)(2,1)S(1)} %get-tuple-element.86), channel_id=1, source_target_pairs={{0,255},{1,240},{2,241},{3,242},{4,243},{5,244},{6,245},{7,246},{8... | collective-permute-start | bytes 221192 | tf_op jit(solution)/shard_map/ppermute | solution.py:513
  33.4 7.5 %collective-permute-start.6 = (bf16[72,512]{1,0:T(8,128)(2,1)S(1)}, bf16[72,512]{1,0:T(8,128)(2,1)S(1)}, u32[]{:S(2)}, u32[]{:S(2)}) collective-permute-start(bf16[72,512]{1,0:T(8,128)(2,1)S(1)} %get-tuple-element.97), channel_id=1, source_target_pairs={{0,17},{1,18},{2,19},{3,20},{4,21},{5,22},{6,23},{7,24},{8,25},{9,... | collective-permute-start | bytes 221192 | tf_op jit(solution)/shard_map/ppermute | solution.py:513
  35.3 5.6 %collective-permute-start.7 = (bf16[72,512]{1,0:T(8,128)(2,1)S(1)}, bf16[72,512]{1,0:T(8,128)(2,1)S(1)}, u32[]{:S(2)}, u32[]{:S(2)}) collective-permute-start(bf16[72,512]{1,0:T(8,128)(2,1)S(1)} %get-tuple-element.98), channel_id=1, source_target_pairs={{0,1},{1,2},{2,3},{3,4},{4,5},{5,6},{6,7},{7,8},{8,9},{9,10},{10,1... | collective-permute-start | bytes 221192 | tf_op jit(solution)/shard_map/ppermute | solution.py:503
  35.3 6.8 %collective-permute-start.8 = (bf16[72,512]{1,0:T(8,128)(2,1)S(1)}, bf16[72,512]{1,0:T(8,128)(2,1)S(1)}, u32[]{:S(2)}, u32[]{:S(2)}) collective-permute-start(bf16[72,512]{1,0:T(8,128)(2,1)S(1)} %get-tuple-element.99), channel_id=1, source_target_pairs={{0,16},{16,32},{32,48},{48,64},{64,80},{80,96},{96,112},{112,128},... | collective-permute-start | bytes 221192 | tf_op jit(solution)/shard_map/ppermute | solution.py:503
  35.8 6.3 %copy-start.2 = (bf16[512,512]{1,0:T(8,128)(2,1)S(1)}, bf16[512,512]{1,0:T(8,128)(2,1)}, u32[]{:S(2)}) copy-start(bf16[512,512]{1,0:T(8,128)(2,1)} %out.5) | copy-start | bytes 1572868
  37.2 10.7 %collective-permute-start.12 = (bf16[256,2048]{1,0:T(8,128)(2,1)S(1)}, bf16[256,2048]{1,0:T(8,128)(2,1)S(1)}, u32[]{:S(2)}, u32[]{:S(2)}) collective-permute-start(bf16[256,2048]{1,0:T(8,128)(2,1)S(1)} %get-tuple-element.120), channel_id=1, source_target_pairs={{0,1},{1,0},{2,3},{3,2},{4,5},{5,4},{6,7},{7,6},{8,9},{9,8},{10,11... | collective-permute-start | bytes 3145736 | tf_op jit(solution)/shard_map/ppermute | solution.py:503
  46.2 4.0 %collective-permute-start.9 = (bf16[256,2048]{1,0:T(8,128)(2,1)S(1)}, bf16[256,2048]{1,0:T(8,128)(2,1)S(1)}, u32[]{:S(2)}, u32[]{:S(2)}) collective-permute-start(bf16[256,2048]{1,0:T(8,128)(2,1)S(1)} %get-tuple-element.106), channel_id=1, source_target_pairs={{0,1},{1,0},{2,3},{3,2},{4,5},{5,4},{6,7},{7,6},{8,9},{9,8},{10,11... | collective-permute-start | bytes 3145736 | tf_op jit(solution)/shard_map/ppermute | solution.py:503
  48.0 13.6 %collective-permute-start.13 = (bf16[2,128,1024]{2,1,0:T(8,128)(2,1)S(1)}, bf16[2,128,1024]{2,1,0:T(8,128)(2,1)S(1)}, u32[]{:S(2)}, u32[]{:S(2)}) collective-permute-start(bf16[2,128,1024]{2,1,0:T(8,128)(2,1)S(1)} %get-tuple-element.121), channel_id=1, source_target_pairs={{0,2},{1,3},{2,0},{3,1},{4,6},{5,7},{6,4},{7,5},{8,10},{9,11},{10,... | collective-permute-start | bytes 1572872 | tf_op jit(solution)/shard_map/ppermute | solution.py:503
  48.1 3.7 %copy-start.5 = (f32[512]{0:T(512)S(1)}, f32[512]{0:T(512)}, u32[]{:S(2)}) copy-start(f32[512]{0:T(512)} %gain.5) | copy-start | bytes 6148
  48.2 3.7 %copy-start.7 = (bf16[288,288]{1,0:T(8,128)(2,1)S(1)}, bf16[288,288]{1,0:T(8,128)(2,1)}, u32[]{:S(2)}) copy-start(bf16[288,288]{1,0:T(8,128)(2,1)} %constant.11.clone.place_t) | copy-start | bytes 497668
  50.3 11.5 %collective-permute-start.10 = (bf16[2,64,1024]{2,1,0:T(8,128)(2,1)S(1)}, bf16[2,64,1024]{2,1,0:T(8,128)(2,1)S(1)}, u32[]{:S(2)}, u32[]{:S(2)}) collective-permute-start(bf16[2,64,1024]{2,1,0:T(8,128)(2,1)S(1)} %get-tuple-element.110), channel_id=1, source_target_pairs={{0,4},{1,5},{2,6},{3,7},{4,0},{5,1},{6,2},{7,3},{8,12},{9,13},{10,... | collective-permute-start | bytes 786440 | tf_op jit(solution)/shard_map/ppermute | solution.py:503
  50.4 11.4 %collective-permute-start.11 = (bf16[2,64,1024]{2,1,0:T(8,128)(2,1)S(1)}, bf16[2,64,1024]{2,1,0:T(8,128)(2,1)S(1)}, u32[]{:S(2)}, u32[]{:S(2)}) collective-permute-start(bf16[2,64,1024]{2,1,0:T(8,128)(2,1)S(1)} %get-tuple-element.112), channel_id=1, source_target_pairs={{0,12},{1,13},{2,14},{3,15},{4,8},{5,9},{6,10},{7,11},{8,4},{9,5},... | collective-permute-start | bytes 786440 | tf_op jit(solution)/shard_map/ppermute | solution.py:503
  61.7 8.3 %collective-permute-start.18 = (bf16[1,128,1024]{2,1,0:T(8,128)(2,1)S(1)}, bf16[1,128,1024]{2,1,0:T(8,128)(2,1)S(1)}, u32[]{:S(2)}, u32[]{:S(2)}) collective-permute-start(bf16[1,128,1024]{2,1,0:T(8,128)(2,1)S(1)} %get-tuple-element.135), channel_id=1, source_target_pairs={{0,130},{1,131},{2,128},{3,129},{4,134},{5,135},{6,132},{7,133},{8... | collective-permute-start | bytes 786440 | tf_op jit(solution)/shard_map/ppermute | solution.py:531
  61.9 5.5 %collective-permute-start.14 = (bf16[64,1024]{1,0:T(8,128)(2,1)S(1)}, bf16[64,1024]{1,0:T(8,128)(2,1)S(1)}, u32[]{:S(2)}, u32[]{:S(2)}) collective-permute-start(bf16[64,1024]{1,0:T(8,128)(2,1)S(1)} %get-tuple-element.125), channel_id=1, source_target_pairs={{0,12},{1,13},{2,14},{3,15},{4,8},{5,9},{6,10},{7,11},{8,4},{9,5},... | collective-permute-start | bytes 393224 | tf_op jit(solution)/shard_map/ppermute | solution.py:503
  64.5 4.1 %collective-permute-start.15 = (bf16[64,1024]{1,0:T(8,128)(2,1)S(1)}, bf16[64,1024]{1,0:T(8,128)(2,1)S(1)}, u32[]{:S(2)}, u32[]{:S(2)}) collective-permute-start(bf16[64,1024]{1,0:T(8,128)(2,1)S(1)} %get-tuple-element.127), channel_id=1, source_target_pairs={{0,4},{1,5},{2,6},{3,7},{4,0},{5,1},{6,2},{7,3},{8,12},{9,13},{10,... | collective-permute-start | bytes 393224 | tf_op jit(solution)/shard_map/ppermute | solution.py:503
  68.7 3.9 %collective-permute-start.16 = (bf16[2,32,1024]{2,1,0:T(8,128)(2,1)S(1)}, bf16[2,32,1024]{2,1,0:T(8,128)(2,1)S(1)}, u32[]{:S(2)}, u32[]{:S(2)}) collective-permute-start(bf16[2,32,1024]{2,1,0:T(8,128)(2,1)S(1)} %get-tuple-element.129), channel_id=1, source_target_pairs={{0,2},{1,3},{2,0},{3,1},{4,6},{5,7},{6,4},{7,5},{8,10},{9,11},{10,... | collective-permute-start | bytes 393224 | tf_op jit(solution)/shard_map/ppermute | solution.py:503
  70.0 4.2 %collective-permute-start.19 = (bf16[2,32,1024]{2,1,0:T(8,128)(2,1)S(1)}, bf16[2,32,1024]{2,1,0:T(8,128)(2,1)S(1)}, u32[]{:S(2)}, u32[]{:S(2)}) collective-permute-start(bf16[2,32,1024]{2,1,0:T(8,128)(2,1)S(1)} %get-tuple-element.137), channel_id=1, source_target_pairs={{0,4},{1,5},{2,6},{3,7},{4,0},{5,1},{6,2},{7,3},{8,12},{9,13},{10,... | collective-permute-start | bytes 393224 | tf_op jit(solution)/shard_map/ppermute | solution.py:503
  72.6 4.4 %collective-permute-start.17 = (bf16[1,32,1024]{2,1,0:T(8,128)(2,1)S(1)}, bf16[1,32,1024]{2,1,0:T(8,128)(2,1)S(1)}, u32[]{:S(2)}, u32[]{:S(2)}) collective-permute-start(bf16[1,32,1024]{2,1,0:T(8,128)(2,1)S(1)} %get-tuple-element.131), channel_id=1, source_target_pairs={{0,130},{1,131},{2,128},{3,129},{4,134},{5,135},{6,132},{7,133},{8... | collective-permute-start | bytes 196616 | tf_op jit(solution)/shard_map/ppermute | solution.py:531
  74.2 4.4 %collective-permute-start.20 = (bf16[1,32,1024]{2,1,0:T(8,128)(2,1)S(1)}, bf16[1,32,1024]{2,1,0:T(8,128)(2,1)S(1)}, u32[]{:S(2)}, u32[]{:S(2)}) collective-permute-start(bf16[1,32,1024]{2,1,0:T(8,128)(2,1)S(1)} %get-tuple-element.139), channel_id=1, source_target_pairs={{0,12},{1,13},{2,14},{3,15},{4,8},{5,9},{6,10},{7,11},{8,4},{9,5},... | collective-permute-start | bytes 196616 | tf_op jit(solution)/shard_map/ppermute | solution.py:503
  79.4 18.4 %all-to-all-start = ((bf16[8,64,128]{2,1,0:T(8,128)(2,1)}), bf16[8,64,128]{2,1,0:T(8,128)(2,1)S(1)}, u32[]{:S(2)}, u32[]{:S(2)}) async-start(bf16[8,64,128]{2,1,0:T(8,128)(2,1)} %shard_map.215), calls=%async_computation | async-start | bytes 262144 | tf_op jit(solution)/shard_map/all_to_all | solution.py:549
  82.8 13.1 %collective-permute-start.21 = (bf16[72,512]{1,0:T(8,128)(2,1)S(1)}, bf16[72,512]{1,0:T(8,128)(2,1)S(1)}, u32[]{:S(2)}, u32[]{:S(2)}) collective-permute-start(bf16[72,512]{1,0:T(8,128)(2,1)S(1)} %get-tuple-element.143), channel_id=1, source_target_pairs={{0,17},{1,18},{2,19},{3,20},{4,21},{5,22},{6,23},{7,24},{8,25},{9,... | collective-permute-start | bytes 221192 | tf_op jit(solution)/shard_map/ppermute | solution.py:513
  88.9 6.9 %collective-permute-start.22 = (bf16[72,512]{1,0:T(8,128)(2,1)S(1)}, bf16[72,512]{1,0:T(8,128)(2,1)S(1)}, u32[]{:S(2)}, u32[]{:S(2)}) collective-permute-start(bf16[72,512]{1,0:T(8,128)(2,1)S(1)} %get-tuple-element.144), channel_id=1, source_target_pairs={{0,1},{1,2},{2,3},{3,4},{4,5},{5,6},{6,7},{7,8},{8,9},{9,10},{10,1... | collective-permute-start | bytes 221192 | tf_op jit(solution)/shard_map/ppermute | solution.py:503
  88.9 7.6 %collective-permute-start.23 = (bf16[72,512]{1,0:T(8,128)(2,1)S(1)}, bf16[72,512]{1,0:T(8,128)(2,1)S(1)}, u32[]{:S(2)}, u32[]{:S(2)}) collective-permute-start(bf16[72,512]{1,0:T(8,128)(2,1)S(1)} %get-tuple-element.145), channel_id=1, source_target_pairs={{0,16},{16,32},{32,48},{48,64},{64,80},{80,96},{96,112},{112,128},... | collective-permute-start | bytes 221192 | tf_op jit(solution)/shard_map/ppermute | solution.py:503

commit v6 on v4

--- a/solution.py
+++ b/solution.py
@@ -18,6 +18,7 @@
 GROUPS = WIDTH // GROUP
 PER_GROUP = GROUP // HEAD
 ROOT = HEAD**0.5
+Z_GROUPS = ((0, 3, 4, 7), (1, 2, 5, 6))
 SIDE = 2 * WIDTH
 EPS = 1e-05
 NEG = -1000000000.0
@@ -270,26 +271,23 @@
 
 
 def kernel_forward_a(
-    fields_hbm, ids_hbm, gain_hbm, table, qkv_hbm, out_hbm, place_hbm, sort_hbm, where_hbm,
+    fields_hbm, ids_hbm, gain_hbm, table_hbm, qkv_hbm, out_hbm, place_hbm, sort_hbm, where_hbm,
     piece0, piece1, piece2, piece3, inputs_out, middle_out, normed_out, packed, probs, mixed_t,
-    fields, ids, gain, qkv, out, place, sort, where, grid, spare, key_features, scores, sems,
-):
-    ids_in, where_in, fields_in, place_in, gain_in, qkv_in, out_in, sort_in = fetch(
+    fields, ids, gain, table, qkv, out, place, sort, where, grid, spare, key_features, scores, sems,
+):
+    *early, qkv_in, out_in, sort_in = fetch(
         (
-            (ids_hbm, ids), (where_hbm, where), (fields_hbm, fields), (place_hbm, place),
-            (gain_hbm, gain), (qkv_hbm, qkv), (out_hbm, out), (sort_hbm, sort),
+            (ids_hbm, ids), (where_hbm, where), (table_hbm, table), (fields_hbm, fields),
+            (place_hbm, place), (gain_hbm, gain), (qkv_hbm, qkv), (out_hbm, out), (sort_hbm, sort),
         ),
         sems,
     )
-    ids_in.wait()
-    where_in.wait()
+    for copy in early:
+        copy.wait()
     query_features, features = bias_features(ids, where, table, spare, 0, False)
     key_features[...] = features
-    fields_in.wait()
-    place_in.wait()
     inputs = load_grid(fields, place[...], grid)
     inputs_out[...] = inputs.astype(BF16)
-    gain_in.wait()
     qkv_in.wait()
     out_in.wait()
     normed, delta = forward_core(
@@ -373,12 +371,12 @@
     grads_half(1 - core, normed_t, mixed_t, grad_middle, d_packed, send)
 
 
-def kernel_keep_a(
-    back0, back1, back2, back3, middle, normed_t, mixed_t, grad_middle, d_packed, place_t, sort_t,
-    keep, advanced,
-):
+def kernel_keep_a(normed_t, mixed_t, grad_middle, d_packed, keep):
     core = lax.axis_index("lat") % 2
     grads_half(core, normed_t, mixed_t, grad_middle[...], d_packed, keep)
+
+
+def kernel_advanced(back0, back1, back2, back3, middle, place_t, sort_t, advanced):
     delta = join_pieces(sort_t[...], [back[1] for back in (back0, back1, back2, back3)])
     store_grid(advanced, place_t[...], (middle[...].astype(F32) + delta).astype(BF16))
 
@@ -461,18 +459,26 @@
     send[...] = keep[half:] + got[half:]
 
 
-def kernel_columns(keep_a, got_a, keep_b, got_b, blocks):
+def kernel_columns(keep_a, got_a, keep_b, got_b, send, keep, blocks):
     for rows, held, got in ((slice(0, 32), keep_a, got_a), (slice(32, 64), keep_b, got_b)):
         total = held[0].astype(F32) + got[0].astype(F32)
         for block in range(8):
             qkv = total[:, block * 96 : (block + 1) * 96]
             out = total[:, 768 + block * 32 : 768 + (block + 1) * 32]
             blocks[block, rows] = jnp.concatenate([qkv, out], axis=1).astype(BF16)
+    group = (lax.axis_index("lon") % 8 + 1) // 2 % 2
+    for at, (outer, inner) in enumerate(zip(*Z_GROUPS, strict=True)):
+        keep[at] = blocks[outer + group * (inner - outer)]
+        send[at] = blocks[inner + group * (outer - inner)]
+
+
+def kernel_sum(keep, got, total):
+    total[...] = keep[...] + got[...]
 
 
 def kernel_total(parts, qkv_a, out_a, qkv_b, out_b):
     total = parts[0].astype(F32)
-    for at in range(1, 8):
+    for at in range(1, 4):
         total = total + parts[at].astype(F32)
     for rows, qkv, out in ((slice(0, 32), qkv_a, out_a), (slice(32, 64), qkv_b, out_b)):
         qkv[...] = total[rows, :96]
@@ -488,7 +494,7 @@
         pltpu.with_memory_space_constraint(arg, pltpu.HBM) if at in hbm or at in smem else arg
         for at, arg in enumerate(args)
     ]
-    shapes = [pltpu.VMEM(shape, kind) for shape, kind in scratch]
+    shapes = [pltpu.VMEM(*item) if isinstance(item, tuple) else item for item in scratch]
     if copies:
         shapes.append(pltpu.SemaphoreType.DMA((copies,)))
     return pl.pallas_call(
@@ -551,8 +557,12 @@
     return call(kernel_halve, [(shape, BF16)] * 2, [], (keep, got))
 
 
+def to_z(array):
+    return permute(array, "lon", lambda i: i ^ 1)
+
+
 def exchange_z(messages):
-    groups = [[x_hi * 8 + z for z in range(8)] for x_hi in range(2)]
+    groups = [[x_hi * 8 + z for z in group] for x_hi in range(2) for group in Z_GROUPS]
     return lax.all_to_all(messages, "lon", 0, 0, axis_index_groups=groups, tiled=True)
 
 
@@ -592,9 +602,12 @@
     p0, p1, p2, p3, inputs_a, middle_a, normed_a, packed_a, probs_a, mixed_a = call(
         kernel_forward_a,
         [piece] * 4 + [token] * 3 + [packed, probs, mixed_t],
-        [grid, ids, vector, qkv_shape, out_shape, square, square, place_of, token_wide, spare, keys, scores],
+        [
+            grid, ids, vector, pltpu.SMEM(table_a.shape, F32), qkv_shape, out_shape, square, square,
+            place_of, token_wide, spare, keys, scores,
+        ],
         (fields, land_ids, gain_a, table_a, qkv_weight_a, out_weight_a, place, sort, where),
-        smem=(3,), hbm=(0, 1, 2, 4, 5, 6, 7, 8), copies=8, flops=7 * 10**9,
+        hbm=(0, 1, 2, 3, 4, 5, 6, 7, 8), copies=9, flops=7 * 10**9,
     )
     diagonal = permute_both(p0, -1)
     below = permute(p1, "lat", lambda i: i - 1)
@@ -651,16 +664,10 @@
         flops=5 * 10**9,
     )
     got_a = to_core(send_a)
-    keep_a, advanced = call(
-        kernel_keep_a,
-        [half_grads, grid],
-        [],
-        (
-            d3, d2, d1, d0, middle_a, normed_a_t, mixed_a, grad_middle, d_packed_a, place_t,
-            sort_t,
-        ),
-        flops=2 * 10**9, final=(1,),
-    )
+    keep_a = call(
+        kernel_keep_a, [half_grads], [], (normed_a_t, mixed_a, grad_middle, d_packed_a),
+        flops=10**9,
+    )[0]
     send_one_a, send_two_a, keep_one_a, keep_two_a = quarters(kernel_first_sum_a, keep_a, got_a)
     send_one_a, send_two_a, d_packed_a = lax.optimization_barrier((send_one_a, send_two_a, d_packed_a))
     parts_a = (keep_one_a, to_y(send_one_a, 1), keep_two_a, to_y(send_two_a, 3))
@@ -684,11 +691,18 @@
     send_b, keep_b = halve(keep_b, got_b)
     got_b = to_y(send_b, 3)
     send_a, keep_a = halve(keep_a, got_a)
+    send_a, middle_a = lax.optimization_barrier((send_a, middle_a))
     got_a = to_x(send_a, 3)
-    blocks = call(
-        kernel_columns, [((8, 64, GROUP), BF16)], [], (keep_a, got_a, keep_b, got_b)
+    advanced = call(
+        kernel_advanced, [grid], [], (d3, d2, d1, d0, middle_a, place_t, sort_t),
+        flops=2 * 10**9, final=(0,),
     )[0]
-    parts = exchange_z(blocks)
+    got_a, got_b, advanced = lax.optimization_barrier((got_a, got_b, advanced))
+    four = ((4, 64, GROUP), BF16)
+    send, keep = call(
+        kernel_columns, [four] * 2, [((8, 64, GROUP), BF16)], (keep_a, got_a, keep_b, got_b)
+    )
+    parts = exchange_z(call(kernel_sum, [four], [], (keep, to_z(send)))[0])
     grads = call(
         kernel_total,
         [((32, 96), F32), ((32, 32), F32)] * 2,

time: 94.7 us -> 95.5 us (level)
  waiting for transfers between devices: 21.2 us -> 23.4 us
  Pallas kernels: 29.8 us -> 28.6 us
  blocking collectives: 11.5 us -> 10.4 us
    ppermute x17 -> x18, waiting for transfers between devices: 8.93 us -> 11.8 us  [permute(): lax.ppermute(array, axis, [(i, target(i) % length) for i in range(length)])]
    pallas_call x18 -> x20, Pallas kernels: 29.8 us -> 28.6 us  [call(): pl.pallas_call(kernel, out_shape=tuple((jax.ShapeDtypeStruct(shape, kind)...]
    all_to_all x1, blocking collectives: 11.5 us -> 10.4 us  [exchange_z(): lax.all_to_all(messages, 'lon', 0, 0, axis_index_groups=groups, tiled=True)]
    ppermute x17 -> x18, starting transfers between devices: 25.6 us -> 25.8 us  [permute(): lax.ppermute(array, axis, [(i, target(i) % length) for i in range(length)])]
  transfers between devices with their start and end apart: 23 -> 24, of which waited for: 11 -> 11; matrix products, arithmetic and copies ran while one was open for 0% -> 0% of each run, Pallas kernels for 19% -> 19%
where the time goes in v6:
time: 95.5 us; the launch traced here: 95.4 us
  starting transfers between devices  31.9 us (33%)
  Pallas kernels  28.6 us (30%)
  waiting for transfers between devices  23.4 us (25%)
  blocking collectives  10.4 us (11%)
    pallas_call x20, Pallas kernels, call(): pl.pallas_call(kernel, out_shape=tuple((jax.ShapeDtypeStruct(shape, kind)...  28.6 us
    ppermute x18, starting transfers between devices, permute(): lax.ppermute(array, axis, [(i, target(i) % length) for i in range(length)])  25.8 us
    ppermute x18, waiting for transfers between devices, permute(): lax.ppermute(array, axis, [(i, target(i) % length) for i in range(length)])  11.8 us
    all_to_all x1, blocking collectives, exchange_z(): lax.all_to_all(messages, 'lon', 0, 0, axis_index_groups=groups, tiled=True)  10.4 us
    ppermute x3, waiting for transfers between devices, permute_both(): return lax.ppermute(array, ('lon', 'lat'), pairs)  6.35 us
    ppermute x3, waiting for transfers between devices, to_x(): return lax.ppermute(array, ('lon', 'lat'), pairs)  5.34 us
    ppermute x3, starting transfers between devices, to_x(): return lax.ppermute(array, ('lon', 'lat'), pairs)  4.14 us
    ppermute x3, starting transfers between devices, permute_both(): return lax.ppermute(array, ('lon', 'lat'), pairs)  2 us
  transfers between devices with their start and end apart: 24, of which 11 were waited for; matrix products, arithmetic and copies ran while one was open for 0% of the time, Pallas kernels for 19%

profile of v6, /device:TPU:6, one launch (start us, length us, event | category | flops | bytes accessed | tf_op | source)
XLA Modules:
  0.0 95.4 jit_solution(10411942274065037681)
XLA Ops:
  0.6 0.0 copy-start.8
  0.7 0.0 copy-start.9
  0.7 0.0 copy-start.10
  0.7 5.5 %shard_map.199 = (bf16[72,512]{1,0:T(8,128)(2,1)S(1)}, bf16[72,512]{1,0:T(8,128)(2,1)S(1)}, bf16[72,512]{1,0:T(8,128)(2,1)S(1)}, bf16[72,512]{1,0:T(8,128)(2,1)S...) custom-call(bf16[12,6,4,512]{3,2,1,0:T(4,128)(2,1)} %bitcast.6, ...), custom_call_target="tpu_custom_call" | custom-call | flops 7000000000 | bytes 1048576 | tf_op jit(solution)/shard_map/pallas_call | solution.py:500
  6.2 6.8 %collective-permute-start.3 = (bf16[72,512]{1,0:T(8,128)(2,1)S(1)}, bf16[72,512]{1,0:T(8,128)(2,1)S(1)}, u32[]{:S(2)}, u32[]{:S(2)}) collective-permute-start(bf16[72,512]{1,0:T(8,128)(2,1)S(1)} %get-tuple-element.93), channel_id=1, source_target_pairs={{0,240},{16,0},{32,16},{48,32},{64,48},{80,64},{96,80},{112,96},{1... | collective-permute-start | bytes 221192 | tf_op jit(solution)/shard_map/ppermute | solution.py:516
  13.0 0.0 collective-permute-start.4
  13.0 0.2 collective-permute-start.5
  13.2 0.0 copy-start
  13.2 0.0 copy-start.1
  13.2 0.0 copy-start.4
  13.2 0.0 copy-start.6
  13.2 2.9 %shard_map.200 = (bf16[72,512]{1,0:T(8,128)(2,1)S(1)}, bf16[72,512]{1,0:T(8,128)(2,1)S(1)}, bf16[72,512]{1,0:T(8,128)(2,1)S(1)}, bf16[72,512]{1,0:T(8,128)(2,1)S...) custom-call(bf16[12,6,4,512]{3,2,1,0:T(4,128)(2,1)} %bitcast.7, ...), custom_call_target="tpu_custom_call" | custom-call | flops 2000000000 | bytes 1048576 | tf_op jit(solution)/shard_map/pallas_call | solution.py:500
  16.2 2.0 %collective-permute-start = (bf16[72,512]{1,0:T(8,128)(2,1)S(1)}, bf16[72,512]{1,0:T(8,128)(2,1)S(1)}, u32[]{:S(2)}, u32[]{:S(2)}) collective-permute-start(bf16[72,512]{1,0:T(8,128)(2,1)S(1)} %get-tuple-element.89), channel_id=1, source_target_pairs={{0,240},{16,0},{32,16},{48,32},{64,48},{80,64},{96,80},{112,96},{1... | collective-permute-start | bytes 221192 | tf_op jit(solution)/shard_map/ppermute | solution.py:516
  18.2 2.4 %collective-permute-start.1 = (bf16[72,512]{1,0:T(8,128)(2,1)S(1)}, bf16[72,512]{1,0:T(8,128)(2,1)S(1)}, u32[]{:S(2)}, u32[]{:S(2)}) collective-permute-start(bf16[72,512]{1,0:T(8,128)(2,1)S(1)} %get-tuple-element.90), channel_id=1, source_target_pairs={{0,15},{1,0},{2,1},{3,2},{4,3},{5,4},{6,5},{7,6},{8,7},{9,8},{10,9... | collective-permute-start | bytes 221192 | tf_op jit(solution)/shard_map/ppermute | solution.py:516
  20.5 1.2 %collective-permute-start.2 = (bf16[72,512]{1,0:T(8,128)(2,1)S(1)}, bf16[72,512]{1,0:T(8,128)(2,1)S(1)}, u32[]{:S(2)}, u32[]{:S(2)}) collective-permute-start(bf16[72,512]{1,0:T(8,128)(2,1)S(1)} %get-tuple-element.91), channel_id=1, source_target_pairs={{0,255},{1,240},{2,241},{3,242},{4,243},{5,244},{6,245},{7,246},{8... | collective-permute-start | bytes 221192 | tf_op jit(solution)/shard_map/ppermute | solution.py:526
  21.8 3.8 %shard_map.201 = (bf16[72,512]{1,0:T(8,128)(2,1)S(1)}, bf16[72,512]{1,0:T(8,128)(2,1)S(1)}, bf16[72,512]{1,0:T(8,128)(2,1)S(1)}, bf16[72,512]{1,0:T(8,128)(2,1)S...) custom-call(bf16[72,512]{1,0:T(8,128)(2,1)S(1)} %get-tuple-element.9, ...), custom_call_target="tpu_custom_call" | custom-call | flops 5000000000 | bytes 1048576 | tf_op jit(solution)/shard_map/pallas_call | solution.py:500
  25.6 0.0 collective-permute-done.piece1
  25.6 4.4 %shard_map.202 = (bf16[2,72,512]{2,1,0:T(8,128)(2,1)S(1)}, bf16[2,72,512]{2,1,0:T(8,128)(2,1)S(1)}, bf16[2,72,512]{2,1,0:T(8,128)(2,1)S(1)}, bf16[2,72,512]{2,1,...) custom-call(bf16[72,512]{1,0:T(8,128)(2,1)S(1)} %get-tuple-element.88.piece0, ...), custom_call_target="tpu_custom_call" | custom-call | flops 5000000000 | bytes 1048576 | tf_op jit(solution)/shard_map/pallas_call | solution.py:500
  30.0 0.6 collective-permute-start.6
  30.6 0.1 collective-permute-start.7
  30.7 1.0 %collective-permute-start.8 = (bf16[2,72,512]{2,1,0:T(8,128)(2,1)S(1)}, bf16[2,72,512]{2,1,0:T(8,128)(2,1)S(1)}, u32[]{:S(2)}, u32[]{:S(2)}) collective-permute-start(bf16[2,72,512]{2,1,0:T(8,128)(2,1)S(1)} %get-tuple-element.108), channel_id=1, source_target_pairs={{0,16},{16,32},{32,48},{48,64},{64,80},{80,96},{96,112},{112,128},... | collective-permute-start | bytes 442376 | tf_op jit(solution)/shard_map/ppermute | solution.py:516
  31.6 1.3 %shard_map.210 = (bf16[256,2048]{1,0:T(8,128)(2,1)S(1)}, bf16[256,2048]{1,0:T(8,128)(2,1)S(1)}) custom-call(bf16[288,512]{1,0:T(8,128)(2,1)S(1)} %get-tuple-element.135.normed, bf16[2,512,144]{2,1,0:T(8,128)(2,1)S(1)} %get-tuple-element.105.mixed_t, bf16[288,512]{1,0:T(8,128)(2,1)S(1)} %get-tuple-element.136.upstream, ...), custom_call_target="tpu_custom_call" | custom-call | flops 2000000000 | bytes 1048576 | tf_op jit(solution)/shard_map/pallas_call | solution.py:500
  33.0 0.4 collective-permute-start.16
  33.3 6.3 %collective-permute-done.6.back0 = bf16[2,72,512]{2,1,0:T(8,128)(2,1)S(1)} collective-permute-done((bf16[2,72,512]{2,1,0:T(8,128)(2,1)S(1)}, bf16[2,72,512]{2,1,0:T(8,128)(2,1)S(1)}, u32[]{:S(2)}, u32[]{:S(2)}) %collective-permute-start.6) | collective-permute-done | bytes 147488 | tf_op jit(solution)/shard_map/ppermute | solution.py:526
  39.7 0.0 collective-permute-done.7.back1
  39.7 3.1 %collective-permute-done.8.back2 = bf16[2,72,512]{2,1,0:T(8,128)(2,1)S(1)} collective-permute-done((bf16[2,72,512]{2,1,0:T(8,128)(2,1)S(1)}, bf16[2,72,512]{2,1,0:T(8,128)(2,1)S(1)}, u32[]{:S(2)}, u32[]{:S(2)}) %collective-permute-start.8) | collective-permute-done | bytes 147488 | tf_op jit(solution)/shard_map/ppermute | solution.py:516
  42.8 4.1 %shard_map.203 = (bf16[288,512]{1,0:T(8,128)(2,1)S(1)}, bf16[288,1536]{1,0:T(8,128)(2,1)S(1)}, bf16[256,2048]{1,0:T(8,128)(2,1)S(1)}) custom-call(bf16[2,72,512]{2,1,0:T(8,128)(2,1)S(1)} %collective-permute-done.6.back0, bf16[2,72,512]{2,1,0:T(8,128)(2,1)S(1)} %collective-permute-done.7.back1, bf16[2,72,512]{2,1,0:T(8,128)(2,1)S(1)} %collective-permute-done.8.back2, ...), custom_call_target="tpu_custom_call" | custom-call | flops 5000000000 | bytes 1048576 | tf_op jit(solution)/shard_map/pallas_call | solution.py:500
  46.8 0.1 collective-permute-start.9
  46.9 0.7 shard_map.204.keep
  47.6 0.0 copy-start.5
  47.6 0.0 copy-start.7
  47.7 0.0 collective-permute-done.16.got
  47.7 0.1 shard_map.211
  47.8 0.9 collective-permute-start.17
  48.7 1.2 %collective-permute-start.18 = (bf16[2,64,1024]{2,1,0:T(8,128)(2,1)S(1)}, bf16[2,64,1024]{2,1,0:T(8,128)(2,1)S(1)}, u32[]{:S(2)}, u32[]{:S(2)}) collective-permute-start(bf16[2,64,1024]{2,1,0:T(8,128)(2,1)S(1)} %get-tuple-element.143), channel_id=1, source_target_pairs={{0,130},{1,131},{2,128},{3,129},{4,134},{5,135},{6,132},{7,133},{8... | collective-permute-start | bytes 786440 | tf_op jit(solution)/shard_map/ppermute | solution.py:544
  49.9 0.0 collective-permute-done.9.got
  49.9 0.1 shard_map.205
  50.0 1.0 %collective-permute-start.10 = (bf16[2,64,1024]{2,1,0:T(8,128)(2,1)S(1)}, bf16[2,64,1024]{2,1,0:T(8,128)(2,1)S(1)}, u32[]{:S(2)}, u32[]{:S(2)}) collective-permute-start(bf16[2,64,1024]{2,1,0:T(8,128)(2,1)S(1)} %get-tuple-element.119), channel_id=1, source_target_pairs={{0,4},{1,5},{2,6},{3,7},{4,0},{5,1},{6,2},{7,3},{8,12},{9,13},{10,... | collective-permute-start | bytes 786440 | tf_op jit(solution)/shard_map/ppermute | solution.py:516
  51.1 2.7 %collective-permute-start.11 = (bf16[2,64,1024]{2,1,0:T(8,128)(2,1)S(1)}, bf16[2,64,1024]{2,1,0:T(8,128)(2,1)S(1)}, u32[]{:S(2)}, u32[]{:S(2)}) collective-permute-start(bf16[2,64,1024]{2,1,0:T(8,128)(2,1)S(1)} %get-tuple-element.121), channel_id=1, source_target_pairs={{0,12},{1,13},{2,14},{3,15},{4,8},{5,9},{6,10},{7,11},{8,4},{9,5},... | collective-permute-start | bytes 786440 | tf_op jit(solution)/shard_map/ppermute | solution.py:516
  53.8 3.2 %shard_map.207 = bf16[12,6,4,512]{3,2,1,0:T(4,128)(2,1)} custom-call(bf16[288,512]{1,0:T(8,128)(2,1)S(1)} %get-tuple-element.125.inputs, bf16[288,512]{1,0:T(8,128)(2,1)S(1)} %get-tuple-element.113.grad_middle, f32[512]{0:T(512)S(1)} %copy-done.5, bf16[512,1536]{1,0:T(8,128)(2,1)} %qkv_hbm.3, bf16[288,1536]{1,0:T(8,128)(2,1)S(1)} %get-tuple-element.126.d_packed, ...), custom_call_target="tpu_custom_call" | custom-call | flops 4000000000 | bytes 1048576 | tf_op jit(solution)/shard_map/pallas_call | solution.py:500
  57.0 1.3 %collective-permute-done.18.got_two = bf16[2,64,1024]{2,1,0:T(8,128)(2,1)S(1)} collective-permute-done((bf16[2,64,1024]{2,1,0:T(8,128)(2,1)S(1)}, bf16[2,64,1024]{2,1,0:T(8,128)(2,1)S(1)}, u32[]{:S(2)}, u32[]{:S(2)}) %collective-permute-start.18) | collective-permute-done | bytes 262176 | tf_op jit(solution)/shard_map/ppermute | solution.py:544
  58.4 0.1 shard_map.212
  58.4 1.4 %collective-permute-start.19 = (bf16[64,1024]{1,0:T(8,128)(2,1)S(1)}, bf16[64,1024]{1,0:T(8,128)(2,1)S(1)}, u32[]{:S(2)}, u32[]{:S(2)}) collective-permute-start(bf16[64,1024]{1,0:T(8,128)(2,1)S(1)} %get-tuple-element.145), channel_id=1, source_target_pairs={{0,130},{1,131},{2,128},{3,129},{4,134},{5,135},{6,132},{7,133},{8... | collective-permute-start | bytes 393224 | tf_op jit(solution)/shard_map/ppermute | solution.py:544
  59.8 0.3 collective-permute-done.11.got_two
  60.2 0.1 shard_map.206
  60.2 3.2 %collective-permute-start.12 = (bf16[64,1024]{1,0:T(8,128)(2,1)S(1)}, bf16[64,1024]{1,0:T(8,128)(2,1)S(1)}, u32[]{:S(2)}, u32[]{:S(2)}) collective-permute-start(bf16[64,1024]{1,0:T(8,128)(2,1)S(1)} %get-tuple-element.127), channel_id=1, source_target_pairs={{0,12},{1,13},{2,14},{3,15},{4,8},{5,9},{6,10},{7,11},{8,4},{9,5},... | collective-permute-start | bytes 393224 | tf_op jit(solution)/shard_map/ppermute | solution.py:516
  63.4 1.3 %collective-permute-done.19.got_one = bf16[64,1024]{1,0:T(8,128)(2,1)S(1)} collective-permute-done((bf16[64,1024]{1,0:T(8,128)(2,1)S(1)}, bf16[64,1024]{1,0:T(8,128)(2,1)S(1)}, u32[]{:S(2)}, u32[]{:S(2)}) %collective-permute-start.19) | collective-permute-done | bytes 131104 | tf_op jit(solution)/shard_map/ppermute | solution.py:544
  64.7 0.1 collective-permute-done.20.got_two
  64.8 0.1 shard_map.213
  64.9 0.9 collective-permute-start.21
  65.8 0.7 collective-permute-done.12.got_one
  66.5 2.5 %collective-permute-done.13.got_two = bf16[64,1024]{1,0:T(8,128)(2,1)S(1)} collective-permute-done((bf16[64,1024]{1,0:T(8,128)(2,1)S(1)}, bf16[64,1024]{1,0:T(8,128)(2,1)S(1)}, u32[]{:S(2)}, u32[]{:S(2)}) %collective-permute-start.13) | collective-permute-done | bytes 131104 | tf_op jit(solution)/shard_map/ppermute | solution.py:516
  69.0 0.1 shard_map.208
  69.1 1.8 %collective-permute-start.14 = (bf16[2,32,1024]{2,1,0:T(8,128)(2,1)S(1)}, bf16[2,32,1024]{2,1,0:T(8,128)(2,1)S(1)}, u32[]{:S(2)}, u32[]{:S(2)}) collective-permute-start(bf16[2,32,1024]{2,1,0:T(8,128)(2,1)S(1)} %get-tuple-element.131), channel_id=1, source_target_pairs={{0,2},{1,3},{2,0},{3,1},{4,6},{5,7},{6,4},{7,5},{8,10},{9,11},{10,... | collective-permute-start | bytes 393224 | tf_op jit(solution)/shard_map/ppermute | solution.py:516
  71.0 2.5 %collective-permute-start.22 = (bf16[1,32,1024]{2,1,0:T(8,128)(2,1)S(1)}, bf16[1,32,1024]{2,1,0:T(8,128)(2,1)S(1)}, u32[]{:S(2)}, u32[]{:S(2)}) collective-permute-start(bf16[1,32,1024]{2,1,0:T(8,128)(2,1)S(1)} %get-tuple-element.150), channel_id=1, source_target_pairs={{0,12},{1,13},{2,14},{3,15},{4,8},{5,9},{6,10},{7,11},{8,4},{9,5},... | collective-permute-start | bytes 196616 | tf_op jit(solution)/shard_map/ppermute | solution.py:516
  73.4 0.7 collective-permute-done.14.got
  74.2 1.5 %collective-permute-start.15 = (bf16[1,32,1024]{2,1,0:T(8,128)(2,1)S(1)}, bf16[1,32,1024]{2,1,0:T(8,128)(2,1)S(1)}, u32[]{:S(2)}, u32[]{:S(2)}) collective-permute-start(bf16[1,32,1024]{2,1,0:T(8,128)(2,1)S(1)} %get-tuple-element.134), channel_id=1, source_target_pairs={{0,130},{1,131},{2,128},{3,129},{4,134},{5,135},{6,132},{7,133},{8... | collective-permute-start | bytes 196616 | tf_op jit(solution)/shard_map/ppermute | solution.py:544
  75.7 1.3 %shard_map.215 = bf16[12,6,4,512]{3,2,1,0:T(4,128)(2,1)} custom-call(bf16[2,72,512]{2,1,0:T(8,128)(2,1)S(1)} %collective-permute-done.6.back0, bf16[2,72,512]{2,1,0:T(8,128)(2,1)S(1)} %collective-permute-done.7.back1, bf16[2,72,512]{2,1,0:T(8,128)(2,1)S(1)} %collective-permute-done.8.back2, bf16[2,72,512]{2,1,0:T(8,128)(2,1)S(1)} %get-tuple-element.109.back3, ...), custom_call_target="tpu_custom_call" | custom-call | flops 2000000000 | bytes 1048576 | tf_op jit(solution)/shard_map/pallas_call | solution.py:500
  77.0 2.7 %collective-permute-done.15.got_a = bf16[1,32,1024]{2,1,0:T(8,128)(2,1)S(1)} collective-permute-done((bf16[1,32,1024]{2,1,0:T(8,128)(2,1)S(1)}, bf16[1,32,1024]{2,1,0:T(8,128)(2,1)S(1)}, u32[]{:S(2)}, u32[]{:S(2)}) %collective-permute-start.15) | collective-permute-done | bytes 65568 | tf_op jit(solution)/shard_map/ppermute | solution.py:544
  79.7 0.1 shard_map.216
  79.9 0.1 collective-permute-start.23
  80.0 4.3 %collective-permute-done.23.got = bf16[4,64,128]{2,1,0:T(8,128)(2,1)S(1)} collective-permute-done((bf16[4,64,128]{2,1,0:T(8,128)(2,1)S(1)}, bf16[4,64,128]{2,1,0:T(8,128)(2,1)S(1)}, u32[]{:S(2)}, u32[]{:S(2)}) %collective-permute-start.23) | collective-permute-done | bytes 65568 | tf_op jit(solution)/shard_map/ppermute | solution.py:516
  84.3 10.4 %all_to_all.5.parts = bf16[4,64,128]{2,1,0:T(8,128)(2,1)S(1)} all-to-all(bf16[4,64,128]{2,1,0:T(8,128)(2,1)S(1)} %shard_map.217), channel_id=1, replica_groups={{0,48,64,112},{16,32,80,96},{128,176,192,240},{144,160,208,224},{1,49,6..., dimensions={0} | all-to-all | bytes 131072 | tf_op jit(solution)/shard_map/all_to_all | solution.py:566
  94.7 0.7 shard_map.218
  (27 shorter events, 0.1 us)
Async XLA Ops:
  0.6 12.5 %copy-start.3 = (s32[192,96]{1,0:T(8,128)S(1)}, s32[192,96]{1,0:T(8,128)}, u32[]{:S(2)}) copy-start(s32[192,96]{1,0:T(8,128)} %ids.1) | copy-start | bytes 221188
  0.6 12.5 %copy-start.8 = (bf16[288,288]{1,0:T(8,128)(2,1)S(1)}, bf16[288,288]{1,0:T(8,128)(2,1)}, u32[]{:S(2)}) copy-start(bf16[288,288]{1,0:T(8,128)(2,1)} %constant.12.clone.sort_hbm.sort) | copy-start | bytes 497668
  0.7 12.5 %copy-start.9 = (bf16[288,288]{1,0:T(8,128)(2,1)S(1)}, bf16[288,288]{1,0:T(8,128)(2,1)}, u32[]{:S(2)}) copy-start(bf16[288,288]{1,0:T(8,128)(2,1)} %constant.10.clone.place_hbm.place) | copy-start | bytes 497668
  0.7 12.5 %copy-start.10 = (s32[144,8]{1,0:T(8,128)S(1)}, s32[144,8]{1,0:T(8,128)}, u32[]{:S(2)}) copy-start(s32[144,8]{1,0:T(8,128)} %constant.14.clone.where_hbm.where) | copy-start | bytes 13828
  6.2 14.3 %collective-permute-start.3 = (bf16[72,512]{1,0:T(8,128)(2,1)S(1)}, bf16[72,512]{1,0:T(8,128)(2,1)S(1)}, u32[]{:S(2)}, u32[]{:S(2)}) collective-permute-start(bf16[72,512]{1,0:T(8,128)(2,1)S(1)} %get-tuple-element.93), channel_id=1, source_target_pairs={{0,240},{16,0},{32,16},{48,32},{64,48},{80,64},{96,80},{112,96},{1... | collective-permute-start | bytes 221192 | tf_op jit(solution)/shard_map/ppermute | solution.py:516
  13.0 8.8 %collective-permute-start.4 = (bf16[72,512]{1,0:T(8,128)(2,1)S(1)}, bf16[72,512]{1,0:T(8,128)(2,1)S(1)}, u32[]{:S(2)}, u32[]{:S(2)}) collective-permute-start(bf16[72,512]{1,0:T(8,128)(2,1)S(1)} %get-tuple-element.94), channel_id=1, source_target_pairs={{0,15},{1,0},{2,1},{3,2},{4,3},{5,4},{6,5},{7,6},{8,7},{9,8},{10,9... | collective-permute-start | bytes 221192 | tf_op jit(solution)/shard_map/ppermute | solution.py:516
  13.0 8.8 %collective-permute-start.5 = (bf16[72,512]{1,0:T(8,128)(2,1)S(1)}, bf16[72,512]{1,0:T(8,128)(2,1)S(1)}, u32[]{:S(2)}, u32[]{:S(2)}) collective-permute-start(bf16[72,512]{1,0:T(8,128)(2,1)S(1)} %get-tuple-element.95), channel_id=1, source_target_pairs={{0,255},{1,240},{2,241},{3,242},{4,243},{5,244},{6,245},{7,246},{8... | collective-permute-start | bytes 221192 | tf_op jit(solution)/shard_map/ppermute | solution.py:526
  13.2 8.6 %copy-start = (bf16[512,1536]{1,0:T(8,128)(2,1)S(1)}, bf16[512,1536]{1,0:T(8,128)(2,1)}, u32[]{:S(2)}) copy-start(bf16[512,1536]{1,0:T(8,128)(2,1)} %qkv.3) | copy-start | bytes 4718596
  13.2 8.6 %copy-start.1 = (bf16[512,512]{1,0:T(8,128)(2,1)S(1)}, bf16[512,512]{1,0:T(8,128)(2,1)}, u32[]{:S(2)}) copy-start(bf16[512,512]{1,0:T(8,128)(2,1)} %out.4) | copy-start | bytes 1572868
  13.2 8.6 %copy-start.4 = (f32[512]{0:T(512)S(1)}, f32[512]{0:T(512)}, u32[]{:S(2)}) copy-start(f32[512]{0:T(512)} %gain.4) | copy-start | bytes 6148
  13.2 8.6 %copy-start.6 = (bf16[288,288]{1,0:T(8,128)(2,1)S(1)}, bf16[288,288]{1,0:T(8,128)(2,1)}, u32[]{:S(2)}) copy-start(bf16[288,288]{1,0:T(8,128)(2,1)} %constant.13.clone.sort_t) | copy-start | bytes 497668
  16.2 9.4 %collective-permute-start = (bf16[72,512]{1,0:T(8,128)(2,1)S(1)}, bf16[72,512]{1,0:T(8,128)(2,1)S(1)}, u32[]{:S(2)}, u32[]{:S(2)}) collective-permute-start(bf16[72,512]{1,0:T(8,128)(2,1)S(1)} %get-tuple-element.89), channel_id=1, source_target_pairs={{0,240},{16,0},{32,16},{48,32},{64,48},{80,64},{96,80},{112,96},{1... | collective-permute-start | bytes 221192 | tf_op jit(solution)/shard_map/ppermute | solution.py:516
  18.2 7.4 %collective-permute-start.1 = (bf16[72,512]{1,0:T(8,128)(2,1)S(1)}, bf16[72,512]{1,0:T(8,128)(2,1)S(1)}, u32[]{:S(2)}, u32[]{:S(2)}) collective-permute-start(bf16[72,512]{1,0:T(8,128)(2,1)S(1)} %get-tuple-element.90), channel_id=1, source_target_pairs={{0,15},{1,0},{2,1},{3,2},{4,3},{5,4},{6,5},{7,6},{8,7},{9,8},{10,9... | collective-permute-start | bytes 221192 | tf_op jit(solution)/shard_map/ppermute | solution.py:516
  20.5 5.1 %collective-permute-start.2 = (bf16[72,512]{1,0:T(8,128)(2,1)S(1)}, bf16[72,512]{1,0:T(8,128)(2,1)S(1)}, u32[]{:S(2)}, u32[]{:S(2)}) collective-permute-start(bf16[72,512]{1,0:T(8,128)(2,1)S(1)} %get-tuple-element.91), channel_id=1, source_target_pairs={{0,255},{1,240},{2,241},{3,242},{4,243},{5,244},{6,245},{7,246},{8... | collective-permute-start | bytes 221192 | tf_op jit(solution)/shard_map/ppermute | solution.py:526
  30.0 9.7 %collective-permute-start.6 = (bf16[2,72,512]{2,1,0:T(8,128)(2,1)S(1)}, bf16[2,72,512]{2,1,0:T(8,128)(2,1)S(1)}, u32[]{:S(2)}, u32[]{:S(2)}) collective-permute-start(bf16[2,72,512]{2,1,0:T(8,128)(2,1)S(1)} %get-tuple-element.106), channel_id=1, source_target_pairs={{0,17},{1,18},{2,19},{3,20},{4,21},{5,22},{6,23},{7,24},{8,25},{9,... | collective-permute-start | bytes 442376 | tf_op jit(solution)/shard_map/ppermute | solution.py:526
  30.6 9.1 %collective-permute-start.7 = (bf16[2,72,512]{2,1,0:T(8,128)(2,1)S(1)}, bf16[2,72,512]{2,1,0:T(8,128)(2,1)S(1)}, u32[]{:S(2)}, u32[]{:S(2)}) collective-permute-start(bf16[2,72,512]{2,1,0:T(8,128)(2,1)S(1)} %get-tuple-element.107), channel_id=1, source_target_pairs={{0,1},{1,2},{2,3},{3,4},{4,5},{5,6},{6,7},{7,8},{8,9},{9,10},{10,1... | collective-permute-start | bytes 442376 | tf_op jit(solution)/shard_map/ppermute | solution.py:516
  30.7 12.1 %collective-permute-start.8 = (bf16[2,72,512]{2,1,0:T(8,128)(2,1)S(1)}, bf16[2,72,512]{2,1,0:T(8,128)(2,1)S(1)}, u32[]{:S(2)}, u32[]{:S(2)}) collective-permute-start(bf16[2,72,512]{2,1,0:T(8,128)(2,1)S(1)} %get-tuple-element.108), channel_id=1, source_target_pairs={{0,16},{16,32},{32,48},{48,64},{64,80},{80,96},{96,112},{112,128},... | collective-permute-start | bytes 442376 | tf_op jit(solution)/shard_map/ppermute | solution.py:516
  31.6 11.1 %copy-start.2 = (bf16[512,512]{1,0:T(8,128)(2,1)S(1)}, bf16[512,512]{1,0:T(8,128)(2,1)}, u32[]{:S(2)}) copy-start(bf16[512,512]{1,0:T(8,128)(2,1)} %out.5) | copy-start | bytes 1572868
  33.0 14.7 %collective-permute-start.16 = (bf16[256,2048]{1,0:T(8,128)(2,1)S(1)}, bf16[256,2048]{1,0:T(8,128)(2,1)S(1)}, u32[]{:S(2)}, u32[]{:S(2)}) collective-permute-start(bf16[256,2048]{1,0:T(8,128)(2,1)S(1)} %get-tuple-element.139), channel_id=1, source_target_pairs={{0,1},{1,0},{2,3},{3,2},{4,5},{5,4},{6,7},{7,6},{8,9},{9,8},{10,11... | collective-permute-start | bytes 3145736 | tf_op jit(solution)/shard_map/ppermute | solution.py:516
  46.8 3.1 %collective-permute-start.9 = (bf16[256,2048]{1,0:T(8,128)(2,1)S(1)}, bf16[256,2048]{1,0:T(8,128)(2,1)S(1)}, u32[]{:S(2)}, u32[]{:S(2)}) collective-permute-start(bf16[256,2048]{1,0:T(8,128)(2,1)S(1)} %get-tuple-element.115), channel_id=1, source_target_pairs={{0,1},{1,0},{2,3},{3,2},{4,5},{5,4},{6,7},{7,6},{8,9},{9,8},{10,11... | collective-permute-start | bytes 3145736 | tf_op jit(solution)/shard_map/ppermute | solution.py:516
  47.6 6.1 %copy-start.5 = (f32[512]{0:T(512)S(1)}, f32[512]{0:T(512)}, u32[]{:S(2)}) copy-start(f32[512]{0:T(512)} %gain.5) | copy-start | bytes 6148
  47.6 6.1 %copy-start.7 = (bf16[288,288]{1,0:T(8,128)(2,1)S(1)}, bf16[288,288]{1,0:T(8,128)(2,1)}, u32[]{:S(2)}) copy-start(bf16[288,288]{1,0:T(8,128)(2,1)} %constant.11.clone.place_t) | copy-start | bytes 497668
  47.8 9.2 %collective-permute-start.17 = (bf16[2,64,1024]{2,1,0:T(8,128)(2,1)S(1)}, bf16[2,64,1024]{2,1,0:T(8,128)(2,1)S(1)}, u32[]{:S(2)}, u32[]{:S(2)}) collective-permute-start(bf16[2,64,1024]{2,1,0:T(8,128)(2,1)S(1)} %get-tuple-element.141), channel_id=1, source_target_pairs={{0,2},{1,3},{2,0},{3,1},{4,6},{5,7},{6,4},{7,5},{8,10},{9,11},{10,... | collective-permute-start | bytes 786440 | tf_op jit(solution)/shard_map/ppermute | solution.py:516
  48.7 9.6 %collective-permute-start.18 = (bf16[2,64,1024]{2,1,0:T(8,128)(2,1)S(1)}, bf16[2,64,1024]{2,1,0:T(8,128)(2,1)S(1)}, u32[]{:S(2)}, u32[]{:S(2)}) collective-permute-start(bf16[2,64,1024]{2,1,0:T(8,128)(2,1)S(1)} %get-tuple-element.143), channel_id=1, source_target_pairs={{0,130},{1,131},{2,128},{3,129},{4,134},{5,135},{6,132},{7,133},{8... | collective-permute-start | bytes 786440 | tf_op jit(solution)/shard_map/ppermute | solution.py:544
  50.0 9.8 %collective-permute-start.10 = (bf16[2,64,1024]{2,1,0:T(8,128)(2,1)S(1)}, bf16[2,64,1024]{2,1,0:T(8,128)(2,1)S(1)}, u32[]{:S(2)}, u32[]{:S(2)}) collective-permute-start(bf16[2,64,1024]{2,1,0:T(8,128)(2,1)S(1)} %get-tuple-element.119), channel_id=1, source_target_pairs={{0,4},{1,5},{2,6},{3,7},{4,0},{5,1},{6,2},{7,3},{8,12},{9,13},{10,... | collective-permute-start | bytes 786440 | tf_op jit(solution)/shard_map/ppermute | solution.py:516
  51.1 9.1 %collective-permute-start.11 = (bf16[2,64,1024]{2,1,0:T(8,128)(2,1)S(1)}, bf16[2,64,1024]{2,1,0:T(8,128)(2,1)S(1)}, u32[]{:S(2)}, u32[]{:S(2)}) collective-permute-start(bf16[2,64,1024]{2,1,0:T(8,128)(2,1)S(1)} %get-tuple-element.121), channel_id=1, source_target_pairs={{0,12},{1,13},{2,14},{3,15},{4,8},{5,9},{6,10},{7,11},{8,4},{9,5},... | collective-permute-start | bytes 786440 | tf_op jit(solution)/shard_map/ppermute | solution.py:516
  58.4 6.3 %collective-permute-start.19 = (bf16[64,1024]{1,0:T(8,128)(2,1)S(1)}, bf16[64,1024]{1,0:T(8,128)(2,1)S(1)}, u32[]{:S(2)}, u32[]{:S(2)}) collective-permute-start(bf16[64,1024]{1,0:T(8,128)(2,1)S(1)} %get-tuple-element.145), channel_id=1, source_target_pairs={{0,130},{1,131},{2,128},{3,129},{4,134},{5,135},{6,132},{7,133},{8... | collective-permute-start | bytes 393224 | tf_op jit(solution)/shard_map/ppermute | solution.py:544
  59.8 5.0 %collective-permute-start.20 = (bf16[64,1024]{1,0:T(8,128)(2,1)S(1)}, bf16[64,1024]{1,0:T(8,128)(2,1)S(1)}, u32[]{:S(2)}, u32[]{:S(2)}) collective-permute-start(bf16[64,1024]{1,0:T(8,128)(2,1)S(1)} %get-tuple-element.147), channel_id=1, source_target_pairs={{0,2},{1,3},{2,0},{3,1},{4,6},{5,7},{6,4},{7,5},{8,10},{9,11},{10,... | collective-permute-start | bytes 393224 | tf_op jit(solution)/shard_map/ppermute | solution.py:516
  60.2 6.3 %collective-permute-start.12 = (bf16[64,1024]{1,0:T(8,128)(2,1)S(1)}, bf16[64,1024]{1,0:T(8,128)(2,1)S(1)}, u32[]{:S(2)}, u32[]{:S(2)}) collective-permute-start(bf16[64,1024]{1,0:T(8,128)(2,1)S(1)} %get-tuple-element.127), channel_id=1, source_target_pairs={{0,12},{1,13},{2,14},{3,15},{4,8},{5,9},{6,10},{7,11},{8,4},{9,5},... | collective-permute-start | bytes 393224 | tf_op jit(solution)/shard_map/ppermute | solution.py:516
  63.4 5.6 %collective-permute-start.13 = (bf16[64,1024]{1,0:T(8,128)(2,1)S(1)}, bf16[64,1024]{1,0:T(8,128)(2,1)S(1)}, u32[]{:S(2)}, u32[]{:S(2)}) collective-permute-start(bf16[64,1024]{1,0:T(8,128)(2,1)S(1)} %get-tuple-element.129), channel_id=1, source_target_pairs={{0,4},{1,5},{2,6},{3,7},{4,0},{5,1},{6,2},{7,3},{8,12},{9,13},{10,... | collective-permute-start | bytes 393224 | tf_op jit(solution)/shard_map/ppermute | solution.py:516
  64.9 6.1 %collective-permute-start.21 = (bf16[2,32,1024]{2,1,0:T(8,128)(2,1)S(1)}, bf16[2,32,1024]{2,1,0:T(8,128)(2,1)S(1)}, u32[]{:S(2)}, u32[]{:S(2)}) collective-permute-start(bf16[2,32,1024]{2,1,0:T(8,128)(2,1)S(1)} %get-tuple-element.149), channel_id=1, source_target_pairs={{0,4},{1,5},{2,6},{3,7},{4,0},{5,1},{6,2},{7,3},{8,12},{9,13},{10,... | collective-permute-start | bytes 393224 | tf_op jit(solution)/shard_map/ppermute | solution.py:516
  69.1 5.1 %collective-permute-start.14 = (bf16[2,32,1024]{2,1,0:T(8,128)(2,1)S(1)}, bf16[2,32,1024]{2,1,0:T(8,128)(2,1)S(1)}, u32[]{:S(2)}, u32[]{:S(2)}) collective-permute-start(bf16[2,32,1024]{2,1,0:T(8,128)(2,1)S(1)} %get-tuple-element.131), channel_id=1, source_target_pairs={{0,2},{1,3},{2,0},{3,1},{4,6},{5,7},{6,4},{7,5},{8,10},{9,11},{10,... | collective-permute-start | bytes 393224 | tf_op jit(solution)/shard_map/ppermute | solution.py:516
  71.0 6.0 %collective-permute-start.22 = (bf16[1,32,1024]{2,1,0:T(8,128)(2,1)S(1)}, bf16[1,32,1024]{2,1,0:T(8,128)(2,1)S(1)}, u32[]{:S(2)}, u32[]{:S(2)}) collective-permute-start(bf16[1,32,1024]{2,1,0:T(8,128)(2,1)S(1)} %get-tuple-element.150), channel_id=1, source_target_pairs={{0,12},{1,13},{2,14},{3,15},{4,8},{5,9},{6,10},{7,11},{8,4},{9,5},... | collective-permute-start | bytes 196616 | tf_op jit(solution)/shard_map/ppermute | solution.py:516
  74.2 5.6 %collective-permute-start.15 = (bf16[1,32,1024]{2,1,0:T(8,128)(2,1)S(1)}, bf16[1,32,1024]{2,1,0:T(8,128)(2,1)S(1)}, u32[]{:S(2)}, u32[]{:S(2)}) collective-permute-start(bf16[1,32,1024]{2,1,0:T(8,128)(2,1)S(1)} %get-tuple-element.134), channel_id=1, source_target_pairs={{0,130},{1,131},{2,128},{3,129},{4,134},{5,135},{6,132},{7,133},{8... | collective-permute-start | bytes 196616 | tf_op jit(solution)/shard_map/ppermute | solution.py:544
  79.9 4.4 %collective-permute-start.23 = (bf16[4,64,128]{2,1,0:T(8,128)(2,1)S(1)}, bf16[4,64,128]{2,1,0:T(8,128)(2,1)S(1)}, u32[]{:S(2)}, u32[]{:S(2)}) collective-permute-start(bf16[4,64,128]{2,1,0:T(8,128)(2,1)S(1)} %get-tuple-element.159), channel_id=1, source_target_pairs={{0,16},{16,0},{32,48},{48,32},{64,80},{80,64},{96,112},{112,96},{1... | collective-permute-start | bytes 196616 | tf_op jit(solution)/shard_map/ppermute | solution.py:516

commit v7 on v6

--- a/solution.py
+++ b/solution.py
@@ -18,7 +18,6 @@
 GROUPS = WIDTH // GROUP
 PER_GROUP = GROUP // HEAD
 ROOT = HEAD**0.5
-Z_GROUPS = ((0, 3, 4, 7), (1, 2, 5, 6))
 SIDE = 2 * WIDTH
 EPS = 1e-05
 NEG = -1000000000.0
@@ -459,26 +458,18 @@
     send[...] = keep[half:] + got[half:]
 
 
-def kernel_columns(keep_a, got_a, keep_b, got_b, send, keep, blocks):
+def kernel_columns(keep_a, got_a, keep_b, got_b, blocks):
     for rows, held, got in ((slice(0, 32), keep_a, got_a), (slice(32, 64), keep_b, got_b)):
         total = held[0].astype(F32) + got[0].astype(F32)
         for block in range(8):
             qkv = total[:, block * 96 : (block + 1) * 96]
             out = total[:, 768 + block * 32 : 768 + (block + 1) * 32]
             blocks[block, rows] = jnp.concatenate([qkv, out], axis=1).astype(BF16)
-    group = (lax.axis_index("lon") % 8 + 1) // 2 % 2
-    for at, (outer, inner) in enumerate(zip(*Z_GROUPS, strict=True)):
-        keep[at] = blocks[outer + group * (inner - outer)]
-        send[at] = blocks[inner + group * (outer - inner)]
-
-
-def kernel_sum(keep, got, total):
-    total[...] = keep[...] + got[...]
 
 
 def kernel_total(parts, qkv_a, out_a, qkv_b, out_b):
     total = parts[0].astype(F32)
-    for at in range(1, 4):
+    for at in range(1, 8):
         total = total + parts[at].astype(F32)
     for rows, qkv, out in ((slice(0, 32), qkv_a, out_a), (slice(32, 64), qkv_b, out_b)):
         qkv[...] = total[rows, :96]
@@ -557,12 +548,8 @@
     return call(kernel_halve, [(shape, BF16)] * 2, [], (keep, got))
 
 
-def to_z(array):
-    return permute(array, "lon", lambda i: i ^ 1)
-
-
 def exchange_z(messages):
-    groups = [[x_hi * 8 + z for z in group] for x_hi in range(2) for group in Z_GROUPS]
+    groups = [[x_hi * 8 + z for z in range(8)] for x_hi in range(2)]
     return lax.all_to_all(messages, "lon", 0, 0, axis_index_groups=groups, tiled=True)
 
 
@@ -669,8 +656,27 @@
         flops=10**9,
     )[0]
     send_one_a, send_two_a, keep_one_a, keep_two_a = quarters(kernel_first_sum_a, keep_a, got_a)
-    send_one_a, send_two_a, d_packed_a = lax.optimization_barrier((send_one_a, send_two_a, d_packed_a))
     parts_a = (keep_one_a, to_y(send_one_a, 1), keep_two_a, to_y(send_two_a, 3))
+    pair = ((2, 32, SIDE), BF16)
+    send_b, keep_b = call(kernel_third_sum_b, [pair] * 2, [], parts_b)
+    got_b = to_y(send_b, 1)
+    send_one_a, send_two_a, held_one_a, held_two_a = second_sum(parts_a)
+    parts_a = (held_one_a, to_y(send_one_a, 3), held_two_a, to_y(send_two_a, 1))
+    send_a, keep_a = call(kernel_third_sum_a, [pair] * 2, [], parts_a)
+    got_a = to_x(send_a, 1)
+    send_b, keep_b = halve(keep_b, got_b)
+    got_b = to_y(send_b, 3)
+    send_a, keep_a = halve(keep_a, got_a)
+    got_a = to_x(send_a, 3)
+    blocks = call(
+        kernel_columns, [((8, 64, GROUP), BF16)], [], (keep_a, got_a, keep_b, got_b)
+    )[0]
+    blocks, d_packed_a, middle_a = lax.optimization_barrier((blocks, d_packed_a, middle_a))
+    parts = exchange_z(blocks)
+    advanced = call(
+        kernel_advanced, [grid], [], (d3, d2, d1, d0, middle_a, place_t, sort_t),
+        flops=2 * 10**9, final=(0,),
+    )[0]
     grad_fields = call(
         kernel_finish_a,
         [grid],
@@ -678,31 +684,6 @@
         (inputs_a, grad_middle, gain_a, qkv_weight_a, d_packed_a, place_t),
         hbm=(3,), copies=1, flops=4 * 10**9, final=(0,),
     )[0]
-    pair = ((2, 32, SIDE), BF16)
-    send_b, keep_b = call(kernel_third_sum_b, [pair] * 2, [], parts_b)
-    got_b = to_y(send_b, 1)
-    send_one_a, send_two_a, held_one_a, held_two_a = second_sum(parts_a)
-    send_one_a, send_two_a, grad_fields = lax.optimization_barrier(
-        (send_one_a, send_two_a, grad_fields)
-    )
-    parts_a = (held_one_a, to_y(send_one_a, 3), held_two_a, to_y(send_two_a, 1))
-    send_a, keep_a = call(kernel_third_sum_a, [pair] * 2, [], parts_a)
-    got_a = to_x(send_a, 1)
-    send_b, keep_b = halve(keep_b, got_b)
-    got_b = to_y(send_b, 3)
-    send_a, keep_a = halve(keep_a, got_a)
-    send_a, middle_a = lax.optimization_barrier((send_a, middle_a))
-    got_a = to_x(send_a, 3)
-    advanced = call(
-        kernel_advanced, [grid], [], (d3, d2, d1, d0, middle_a, place_t, sort_t),
-        flops=2 * 10**9, final=(0,),
-    )[0]
-    got_a, got_b, advanced = lax.optimization_barrier((got_a, got_b, advanced))
-    four = ((4, 64, GROUP), BF16)
-    send, keep = call(
-        kernel_columns, [four] * 2, [((8, 64, GROUP), BF16)], (keep_a, got_a, keep_b, got_b)
-    )
-    parts = exchange_z(call(kernel_sum, [four], [], (keep, to_z(send)))[0])
     grads = call(
         kernel_total,
         [((32, 96), F32), ((32, 32), F32)] * 2,

time: 95.5 us -> 94.1 us (0.985)
  blocking collectives: 10.4 us -> 0 us
  waiting for transfers between devices: 23.4 us -> 28.4 us
  starting transfers between devices: 31.9 us -> 34.6 us
  Pallas kernels: 28.6 us -> 29.8 us
    all_to_all x1 -> x0, blocking collectives: 10.4 us -> none  [exchange_z(): lax.all_to_all(messages, 'lon', 0, 0, axis_index_groups=groups, tiled=True)]
    all_to_all x0 -> x1, waiting for transfers between devices: none -> 4.39 us  [exchange_z(): lax.all_to_all(messages, 'lon', 0, 0, axis_index_groups=groups, tiled=True)]
    all_to_all x0 -> x1, starting transfers between devices: none -> 3.37 us  [exchange_z(): lax.all_to_all(messages, 'lon', 0, 0, axis_index_groups=groups, tiled=True)]
    pallas_call x20 -> x19, Pallas kernels: 28.6 us -> 29.8 us  [call(): pl.pallas_call(kernel, out_shape=tuple((jax.ShapeDtypeStruct(shape, kind)...]
    ppermute x18 -> x17, starting transfers between devices: 25.8 us -> 25.3 us  [permute(): lax.ppermute(array, axis, [(i, target(i) % length) for i in range(length)])]
    ppermute x18 -> x17, waiting for transfers between devices: 11.8 us -> 11.5 us  [permute(): lax.ppermute(array, axis, [(i, target(i) % length) for i in range(length)])]
  transfers between devices with their start and end apart: 24 -> 24, of which waited for: 11 -> 13; matrix products, arithmetic and copies ran while one was open for 0% -> 0% of each run, Pallas kernels for 19% -> 19%
where the time goes in v7:
time: 94.1 us; the launch traced here: 93.9 us
  starting transfers between devices  34.6 us (37%)
  Pallas kernels  29.8 us (32%)
  waiting for transfers between devices  28.4 us (30%)
  between operations  0.95 us (1%)
    pallas_call x19, Pallas kernels, call(): pl.pallas_call(kernel, out_shape=tuple((jax.ShapeDtypeStruct(shape, kind)...  29.8 us
    ppermute x17, starting transfers between devices, permute(): lax.ppermute(array, axis, [(i, target(i) % length) for i in range(length)])  25.3 us
    ppermute x17, waiting for transfers between devices, permute(): lax.ppermute(array, axis, [(i, target(i) % length) for i in range(length)])  11.5 us
    ppermute x3, waiting for transfers between devices, permute_both(): return lax.ppermute(array, ('lon', 'lat'), pairs)  6.55 us
    ppermute x3, waiting for transfers between devices, to_x(): return lax.ppermute(array, ('lon', 'lat'), pairs)  6.02 us
    all_to_all x1, waiting for transfers between devices, exchange_z(): lax.all_to_all(messages, 'lon', 0, 0, axis_index_groups=groups, tiled=True)  4.39 us
    ppermute x3, starting transfers between devices, to_x(): return lax.ppermute(array, ('lon', 'lat'), pairs)  3.91 us
    all_to_all x1, starting transfers between devices, exchange_z(): lax.all_to_all(messages, 'lon', 0, 0, axis_index_groups=groups, tiled=True)  3.37 us
  transfers between devices with their start and end apart: 24, of which 13 were waited for; matrix products, arithmetic and copies ran while one was open for 0% of the time, Pallas kernels for 19%

profile of v7, /device:TPU:6, one launch (start us, length us, event | category | flops | bytes accessed | tf_op | source)
XLA Modules:
  0.0 93.9 jit_solution(8942601659749162677)
XLA Ops:
  0.6 0.0 copy-start.8
  0.7 0.0 copy-start.9
  0.7 0.0 copy-start.10
  0.7 5.6 %shard_map.199 = (bf16[72,512]{1,0:T(8,128)(2,1)S(1)}, bf16[72,512]{1,0:T(8,128)(2,1)S(1)}, bf16[72,512]{1,0:T(8,128)(2,1)S(1)}, bf16[72,512]{1,0:T(8,128)(2,1)S...) custom-call(bf16[12,6,4,512]{3,2,1,0:T(4,128)(2,1)} %bitcast.6, ...), custom_call_target="tpu_custom_call" | custom-call | flops 7000000000 | bytes 1048576 | tf_op jit(solution)/shard_map/pallas_call | solution.py:491
  6.3 6.8 %collective-permute-start.3 = (bf16[72,512]{1,0:T(8,128)(2,1)S(1)}, bf16[72,512]{1,0:T(8,128)(2,1)S(1)}, u32[]{:S(2)}, u32[]{:S(2)}) collective-permute-start(bf16[72,512]{1,0:T(8,128)(2,1)S(1)} %get-tuple-element.81), channel_id=1, source_target_pairs={{0,240},{16,0},{32,16},{48,32},{64,48},{80,64},{96,80},{112,96},{1... | collective-permute-start | bytes 221192 | tf_op jit(solution)/shard_map/ppermute | solution.py:507
  13.1 0.0 collective-permute-start.4
  13.1 0.2 collective-permute-start.5
  13.3 0.0 copy-start
  13.3 0.0 copy-start.1
  13.3 0.0 copy-start.4
  13.3 0.0 copy-start.6
  13.3 2.9 %shard_map.200 = (bf16[72,512]{1,0:T(8,128)(2,1)S(1)}, bf16[72,512]{1,0:T(8,128)(2,1)S(1)}, bf16[72,512]{1,0:T(8,128)(2,1)S(1)}, bf16[72,512]{1,0:T(8,128)(2,1)S...) custom-call(bf16[12,6,4,512]{3,2,1,0:T(4,128)(2,1)} %bitcast.7, ...), custom_call_target="tpu_custom_call" | custom-call | flops 2000000000 | bytes 1048576 | tf_op jit(solution)/shard_map/pallas_call | solution.py:491
  16.3 2.0 %collective-permute-start = (bf16[72,512]{1,0:T(8,128)(2,1)S(1)}, bf16[72,512]{1,0:T(8,128)(2,1)S(1)}, u32[]{:S(2)}, u32[]{:S(2)}) collective-permute-start(bf16[72,512]{1,0:T(8,128)(2,1)S(1)} %get-tuple-element.77), channel_id=1, source_target_pairs={{0,240},{16,0},{32,16},{48,32},{64,48},{80,64},{96,80},{112,96},{1... | collective-permute-start | bytes 221192 | tf_op jit(solution)/shard_map/ppermute | solution.py:507
  18.3 2.4 %collective-permute-start.1 = (bf16[72,512]{1,0:T(8,128)(2,1)S(1)}, bf16[72,512]{1,0:T(8,128)(2,1)S(1)}, u32[]{:S(2)}, u32[]{:S(2)}) collective-permute-start(bf16[72,512]{1,0:T(8,128)(2,1)S(1)} %get-tuple-element.78), channel_id=1, source_target_pairs={{0,15},{1,0},{2,1},{3,2},{4,3},{5,4},{6,5},{7,6},{8,7},{9,8},{10,9... | collective-permute-start | bytes 221192 | tf_op jit(solution)/shard_map/ppermute | solution.py:507
  20.6 0.0 collective-permute-done.3.piece1
  20.6 1.2 %collective-permute-start.2 = (bf16[72,512]{1,0:T(8,128)(2,1)S(1)}, bf16[72,512]{1,0:T(8,128)(2,1)S(1)}, u32[]{:S(2)}, u32[]{:S(2)}) collective-permute-start(bf16[72,512]{1,0:T(8,128)(2,1)S(1)} %get-tuple-element.79), channel_id=1, source_target_pairs={{0,255},{1,240},{2,241},{3,242},{4,243},{5,244},{6,245},{7,246},{8... | collective-permute-start | bytes 221192 | tf_op jit(solution)/shard_map/ppermute | solution.py:517
  21.9 0.0 collective-permute-done.4.piece2
  21.9 3.9 %shard_map.201 = (bf16[72,512]{1,0:T(8,128)(2,1)S(1)}, bf16[72,512]{1,0:T(8,128)(2,1)S(1)}, bf16[72,512]{1,0:T(8,128)(2,1)S(1)}, bf16[72,512]{1,0:T(8,128)(2,1)S...) custom-call(bf16[72,512]{1,0:T(8,128)(2,1)S(1)} %get-tuple-element.8, ...), custom_call_target="tpu_custom_call" | custom-call | flops 5000000000 | bytes 1048576 | tf_op jit(solution)/shard_map/pallas_call | solution.py:491
  25.8 4.5 %shard_map.202 = (bf16[2,72,512]{2,1,0:T(8,128)(2,1)S(1)}, bf16[2,72,512]{2,1,0:T(8,128)(2,1)S(1)}, bf16[2,72,512]{2,1,0:T(8,128)(2,1)S(1)}, bf16[2,72,512]{2,1,...) custom-call(bf16[72,512]{1,0:T(8,128)(2,1)S(1)} %get-tuple-element.76.piece0, ...), custom_call_target="tpu_custom_call" | custom-call | flops 5000000000 | bytes 1048576 | tf_op jit(solution)/shard_map/pallas_call | solution.py:491
  30.3 0.6 collective-permute-start.6
  30.9 0.1 collective-permute-start.7
  31.0 1.0 %collective-permute-start.8 = (bf16[2,72,512]{2,1,0:T(8,128)(2,1)S(1)}, bf16[2,72,512]{2,1,0:T(8,128)(2,1)S(1)}, u32[]{:S(2)}, u32[]{:S(2)}) collective-permute-start(bf16[2,72,512]{2,1,0:T(8,128)(2,1)S(1)} %get-tuple-element.96), channel_id=1, source_target_pairs={{0,16},{16,32},{32,48},{48,64},{64,80},{80,96},{96,112},{112,128},... | collective-permute-start | bytes 442376 | tf_op jit(solution)/shard_map/ppermute | solution.py:507
  31.9 1.3 %shard_map.209 = (bf16[256,2048]{1,0:T(8,128)(2,1)S(1)}, bf16[256,2048]{1,0:T(8,128)(2,1)S(1)}) custom-call(bf16[288,512]{1,0:T(8,128)(2,1)S(1)} %get-tuple-element.118.normed, bf16[2,512,144]{2,1,0:T(8,128)(2,1)S(1)} %get-tuple-element.93.mixed_t, bf16[288,512]{1,0:T(8,128)(2,1)S(1)} %get-tuple-element.119.upstream, ...), custom_call_target="tpu_custom_call" | custom-call | flops 2000000000 | bytes 1048576 | tf_op jit(solution)/shard_map/pallas_call | solution.py:491
  33.3 0.3 collective-permute-start.16
  33.6 6.5 %collective-permute-done.6.back0 = bf16[2,72,512]{2,1,0:T(8,128)(2,1)S(1)} collective-permute-done((bf16[2,72,512]{2,1,0:T(8,128)(2,1)S(1)}, bf16[2,72,512]{2,1,0:T(8,128)(2,1)S(1)}, u32[]{:S(2)}, u32[]{:S(2)}) %collective-permute-start.6) | collective-permute-done | bytes 147488 | tf_op jit(solution)/shard_map/ppermute | solution.py:517
  40.2 3.0 %collective-permute-done.8.back2 = bf16[2,72,512]{2,1,0:T(8,128)(2,1)S(1)} collective-permute-done((bf16[2,72,512]{2,1,0:T(8,128)(2,1)S(1)}, bf16[2,72,512]{2,1,0:T(8,128)(2,1)S(1)}, u32[]{:S(2)}, u32[]{:S(2)}) %collective-permute-start.8) | collective-permute-done | bytes 147488 | tf_op jit(solution)/shard_map/ppermute | solution.py:507
  43.2 4.2 %shard_map.203 = (bf16[288,512]{1,0:T(8,128)(2,1)S(1)}, bf16[288,1536]{1,0:T(8,128)(2,1)S(1)}, bf16[256,2048]{1,0:T(8,128)(2,1)S(1)}) custom-call(bf16[2,72,512]{2,1,0:T(8,128)(2,1)S(1)} %collective-permute-done.6.back0, bf16[2,72,512]{2,1,0:T(8,128)(2,1)S(1)} %collective-permute-done.7.back1, bf16[2,72,512]{2,1,0:T(8,128)(2,1)S(1)} %collective-permute-done.8.back2, ...), custom_call_target="tpu_custom_call" | custom-call | flops 5000000000 | bytes 1048576 | tf_op jit(solution)/shard_map/pallas_call | solution.py:491
  47.4 0.1 collective-permute-start.9
  47.5 0.1 shard_map.210
  47.7 0.8 collective-permute-start.17
  48.5 1.2 %collective-permute-start.18 = (bf16[2,64,1024]{2,1,0:T(8,128)(2,1)S(1)}, bf16[2,64,1024]{2,1,0:T(8,128)(2,1)S(1)}, u32[]{:S(2)}, u32[]{:S(2)}) collective-permute-start(bf16[2,64,1024]{2,1,0:T(8,128)(2,1)S(1)} %get-tuple-element.126), channel_id=1, source_target_pairs={{0,130},{1,131},{2,128},{3,129},{4,134},{5,135},{6,132},{7,133},{8... | collective-permute-start | bytes 786440 | tf_op jit(solution)/shard_map/ppermute | solution.py:535
  49.7 0.7 shard_map.204.keep
  50.4 0.1 shard_map.205
  50.5 0.0 copy-start.5
  50.5 0.0 copy-start.7
  50.6 1.0 %collective-permute-start.10 = (bf16[2,64,1024]{2,1,0:T(8,128)(2,1)S(1)}, bf16[2,64,1024]{2,1,0:T(8,128)(2,1)S(1)}, u32[]{:S(2)}, u32[]{:S(2)}) collective-permute-start(bf16[2,64,1024]{2,1,0:T(8,128)(2,1)S(1)} %get-tuple-element.107), channel_id=1, source_target_pairs={{0,4},{1,5},{2,6},{3,7},{4,0},{5,1},{6,2},{7,3},{8,12},{9,13},{10,... | collective-permute-start | bytes 786440 | tf_op jit(solution)/shard_map/ppermute | solution.py:507
  51.6 2.7 %collective-permute-start.11 = (bf16[2,64,1024]{2,1,0:T(8,128)(2,1)S(1)}, bf16[2,64,1024]{2,1,0:T(8,128)(2,1)S(1)}, u32[]{:S(2)}, u32[]{:S(2)}) collective-permute-start(bf16[2,64,1024]{2,1,0:T(8,128)(2,1)S(1)} %get-tuple-element.109), channel_id=1, source_target_pairs={{0,12},{1,13},{2,14},{3,15},{4,8},{5,9},{6,10},{7,11},{8,4},{9,5},... | collective-permute-start | bytes 786440 | tf_op jit(solution)/shard_map/ppermute | solution.py:507
  54.3 2.1 %collective-permute-done.17.got_one = bf16[2,64,1024]{2,1,0:T(8,128)(2,1)S(1)} collective-permute-done((bf16[2,64,1024]{2,1,0:T(8,128)(2,1)S(1)}, bf16[2,64,1024]{2,1,0:T(8,128)(2,1)S(1)}, u32[]{:S(2)}, u32[]{:S(2)}) %collective-permute-start.17) | collective-permute-done | bytes 262176 | tf_op jit(solution)/shard_map/ppermute | solution.py:507
  56.4 1.7 %collective-permute-done.18.got_two = bf16[2,64,1024]{2,1,0:T(8,128)(2,1)S(1)} collective-permute-done((bf16[2,64,1024]{2,1,0:T(8,128)(2,1)S(1)}, bf16[2,64,1024]{2,1,0:T(8,128)(2,1)S(1)}, u32[]{:S(2)}, u32[]{:S(2)}) %collective-permute-start.18) | collective-permute-done | bytes 262176 | tf_op jit(solution)/shard_map/ppermute | solution.py:535
  58.1 0.1 shard_map.211
  58.1 1.3 %collective-permute-start.19 = (bf16[64,1024]{1,0:T(8,128)(2,1)S(1)}, bf16[64,1024]{1,0:T(8,128)(2,1)S(1)}, u32[]{:S(2)}, u32[]{:S(2)}) collective-permute-start(bf16[64,1024]{1,0:T(8,128)(2,1)S(1)} %get-tuple-element.128), channel_id=1, source_target_pairs={{0,130},{1,131},{2,128},{3,129},{4,134},{5,135},{6,132},{7,133},{8... | collective-permute-start | bytes 393224 | tf_op jit(solution)/shard_map/ppermute | solution.py:535
  59.4 1.2 %collective-permute-done.11.got_two = bf16[2,64,1024]{2,1,0:T(8,128)(2,1)S(1)} collective-permute-done((bf16[2,64,1024]{2,1,0:T(8,128)(2,1)S(1)}, bf16[2,64,1024]{2,1,0:T(8,128)(2,1)S(1)}, u32[]{:S(2)}, u32[]{:S(2)}) %collective-permute-start.11) | collective-permute-done | bytes 262176 | tf_op jit(solution)/shard_map/ppermute | solution.py:507
  60.6 0.1 shard_map.206
  60.7 3.0 %collective-permute-start.12 = (bf16[64,1024]{1,0:T(8,128)(2,1)S(1)}, bf16[64,1024]{1,0:T(8,128)(2,1)S(1)}, u32[]{:S(2)}, u32[]{:S(2)}) collective-permute-start(bf16[64,1024]{1,0:T(8,128)(2,1)S(1)} %get-tuple-element.111), channel_id=1, source_target_pairs={{0,12},{1,13},{2,14},{3,15},{4,8},{5,9},{6,10},{7,11},{8,4},{9,5},... | collective-permute-start | bytes 393224 | tf_op jit(solution)/shard_map/ppermute | solution.py:507
  63.7 0.6 collective-permute-done.19.got_one
  64.4 0.0 collective-permute-done.20.got_two
  64.4 0.1 shard_map.212
  64.5 1.5 %collective-permute-start.21 = (bf16[2,32,1024]{2,1,0:T(8,128)(2,1)S(1)}, bf16[2,32,1024]{2,1,0:T(8,128)(2,1)S(1)}, u32[]{:S(2)}, u32[]{:S(2)}) collective-permute-start(bf16[2,32,1024]{2,1,0:T(8,128)(2,1)S(1)} %get-tuple-element.132), channel_id=1, source_target_pairs={{0,4},{1,5},{2,6},{3,7},{4,0},{5,1},{6,2},{7,3},{8,12},{9,13},{10,... | collective-permute-start | bytes 393224 | tf_op jit(solution)/shard_map/ppermute | solution.py:507
  65.9 1.0 %collective-permute-done.12.got_one = bf16[64,1024]{1,0:T(8,128)(2,1)S(1)} collective-permute-done((bf16[64,1024]{1,0:T(8,128)(2,1)S(1)}, bf16[64,1024]{1,0:T(8,128)(2,1)S(1)}, u32[]{:S(2)}, u32[]{:S(2)}) %collective-permute-start.12) | collective-permute-done | bytes 131104 | tf_op jit(solution)/shard_map/ppermute | solution.py:507
  67.0 2.3 %collective-permute-done.13.got_two = bf16[64,1024]{1,0:T(8,128)(2,1)S(1)} collective-permute-done((bf16[64,1024]{1,0:T(8,128)(2,1)S(1)}, bf16[64,1024]{1,0:T(8,128)(2,1)S(1)}, u32[]{:S(2)}, u32[]{:S(2)}) %collective-permute-start.13) | collective-permute-done | bytes 131104 | tf_op jit(solution)/shard_map/ppermute | solution.py:507
  69.3 0.1 shard_map.207
  69.4 1.3 %collective-permute-start.14 = (bf16[2,32,1024]{2,1,0:T(8,128)(2,1)S(1)}, bf16[2,32,1024]{2,1,0:T(8,128)(2,1)S(1)}, u32[]{:S(2)}, u32[]{:S(2)}) collective-permute-start(bf16[2,32,1024]{2,1,0:T(8,128)(2,1)S(1)} %get-tuple-element.115), channel_id=1, source_target_pairs={{0,2},{1,3},{2,0},{3,1},{4,6},{5,7},{6,4},{7,5},{8,10},{9,11},{10,... | collective-permute-start | bytes 393224 | tf_op jit(solution)/shard_map/ppermute | solution.py:507
  70.6 0.1 collective-permute-done.21.got
  70.7 2.5 %collective-permute-start.22 = (bf16[1,32,1024]{2,1,0:T(8,128)(2,1)S(1)}, bf16[1,32,1024]{2,1,0:T(8,128)(2,1)S(1)}, u32[]{:S(2)}, u32[]{:S(2)}) collective-permute-start(bf16[1,32,1024]{2,1,0:T(8,128)(2,1)S(1)} %get-tuple-element.134), channel_id=1, source_target_pairs={{0,12},{1,13},{2,14},{3,15},{4,8},{5,9},{6,10},{7,11},{8,4},{9,5},... | collective-permute-start | bytes 196616 | tf_op jit(solution)/shard_map/ppermute | solution.py:507
  73.2 1.3 %collective-permute-done.14.got = bf16[2,32,1024]{2,1,0:T(8,128)(2,1)S(1)} collective-permute-done((bf16[2,32,1024]{2,1,0:T(8,128)(2,1)S(1)}, bf16[2,32,1024]{2,1,0:T(8,128)(2,1)S(1)}, u32[]{:S(2)}, u32[]{:S(2)}) %collective-permute-start.14) | collective-permute-done | bytes 131104 | tf_op jit(solution)/shard_map/ppermute | solution.py:507
  74.4 1.4 %collective-permute-start.15 = (bf16[1,32,1024]{2,1,0:T(8,128)(2,1)S(1)}, bf16[1,32,1024]{2,1,0:T(8,128)(2,1)S(1)}, u32[]{:S(2)}, u32[]{:S(2)}) collective-permute-start(bf16[1,32,1024]{2,1,0:T(8,128)(2,1)S(1)} %get-tuple-element.117), channel_id=1, source_target_pairs={{0,130},{1,131},{2,128},{3,129},{4,134},{5,135},{6,132},{7,133},{8... | collective-permute-start | bytes 196616 | tf_op jit(solution)/shard_map/ppermute | solution.py:535
  75.8 0.5 collective-permute-done.22.got_b
  76.3 3.7 %collective-permute-done.15.got_a = bf16[1,32,1024]{2,1,0:T(8,128)(2,1)S(1)} collective-permute-done((bf16[1,32,1024]{2,1,0:T(8,128)(2,1)S(1)}, bf16[1,32,1024]{2,1,0:T(8,128)(2,1)S(1)}, u32[]{:S(2)}, u32[]{:S(2)}) %collective-permute-start.15) | collective-permute-done | bytes 65568 | tf_op jit(solution)/shard_map/ppermute | solution.py:535
  80.0 0.8 shard_map.214
  80.8 3.4 %all-to-all-start = ((bf16[8,64,128]{2,1,0:T(8,128)(2,1)}), bf16[8,64,128]{2,1,0:T(8,128)(2,1)S(1)}, u32[]{:S(2)}, u32[]{:S(2)}) async-start(bf16[8,64,128]{2,1,0:T(8,128)(2,1)} %shard_map.214), calls=%async_computation | async-start | bytes 262144 | tf_op jit(solution)/shard_map/all_to_all | solution.py:553
  84.2 3.3 %shard_map.216 = bf16[12,6,4,512]{3,2,1,0:T(4,128)(2,1)} custom-call(bf16[288,512]{1,0:T(8,128)(2,1)S(1)} %get-tuple-element.137.inputs, bf16[288,512]{1,0:T(8,128)(2,1)S(1)} %get-tuple-element.103.grad_middle, f32[512]{0:T(512)S(1)} %copy-done.5, bf16[512,1536]{1,0:T(8,128)(2,1)} %qkv_hbm.3, bf16[288,1536]{1,0:T(8,128)(2,1)S(1)} %get-tuple-element.138.d_packed, ...), custom_call_target="tpu_custom_call" | custom-call | flops 4000000000 | bytes 1048576 | tf_op jit(solution)/shard_map/pallas_call | solution.py:491
  87.5 1.3 %shard_map.215 = bf16[12,6,4,512]{3,2,1,0:T(4,128)(2,1)} custom-call(bf16[2,72,512]{2,1,0:T(8,128)(2,1)S(1)} %collective-permute-done.6.back0, bf16[2,72,512]{2,1,0:T(8,128)(2,1)S(1)} %collective-permute-done.7.back1, bf16[2,72,512]{2,1,0:T(8,128)(2,1)S(1)} %collective-permute-done.8.back2, bf16[2,72,512]{2,1,0:T(8,128)(2,1)S(1)} %get-tuple-element.97.back3, ...), custom_call_target="tpu_custom_call" | custom-call | flops 2000000000 | bytes 1048576 | tf_op jit(solution)/shard_map/pallas_call | solution.py:491
  88.8 4.4 %all-to-all-done.parts = bf16[8,64,128]{2,1,0:T(8,128)(2,1)S(1)} async-done(((bf16[8,64,128]{2,1,0:T(8,128)(2,1)}), bf16[8,64,128]{2,1,0:T(8,128)(2,1)S(1)}, u32[]{:S(2)}, u32[]{:S(2)}) %all-to-all-start) | async-done | bytes 131104 | tf_op jit(solution)/shard_map/all_to_all | solution.py:553
  93.2 0.7 shard_map.217
  (25 shorter events, 0.1 us)
Async XLA Ops:
  0.6 12.6 %copy-start.3 = (s32[192,96]{1,0:T(8,128)S(1)}, s32[192,96]{1,0:T(8,128)}, u32[]{:S(2)}) copy-start(s32[192,96]{1,0:T(8,128)} %ids.1) | copy-start | bytes 221188
  0.6 12.6 %copy-start.8 = (bf16[288,288]{1,0:T(8,128)(2,1)S(1)}, bf16[288,288]{1,0:T(8,128)(2,1)}, u32[]{:S(2)}) copy-start(bf16[288,288]{1,0:T(8,128)(2,1)} %constant.12.clone.sort_hbm.sort) | copy-start | bytes 497668
  0.7 12.6 %copy-start.9 = (bf16[288,288]{1,0:T(8,128)(2,1)S(1)}, bf16[288,288]{1,0:T(8,128)(2,1)}, u32[]{:S(2)}) copy-start(bf16[288,288]{1,0:T(8,128)(2,1)} %constant.10.clone.place_hbm.place) | copy-start | bytes 497668
  0.7 12.6 %copy-start.10 = (s32[144,8]{1,0:T(8,128)S(1)}, s32[144,8]{1,0:T(8,128)}, u32[]{:S(2)}) copy-start(s32[144,8]{1,0:T(8,128)} %constant.14.clone.where_hbm.where) | copy-start | bytes 13828
  6.3 14.3 %collective-permute-start.3 = (bf16[72,512]{1,0:T(8,128)(2,1)S(1)}, bf16[72,512]{1,0:T(8,128)(2,1)S(1)}, u32[]{:S(2)}, u32[]{:S(2)}) collective-permute-start(bf16[72,512]{1,0:T(8,128)(2,1)S(1)} %get-tuple-element.81), channel_id=1, source_target_pairs={{0,240},{16,0},{32,16},{48,32},{64,48},{80,64},{96,80},{112,96},{1... | collective-permute-start | bytes 221192 | tf_op jit(solution)/shard_map/ppermute | solution.py:507
  13.1 8.8 %collective-permute-start.4 = (bf16[72,512]{1,0:T(8,128)(2,1)S(1)}, bf16[72,512]{1,0:T(8,128)(2,1)S(1)}, u32[]{:S(2)}, u32[]{:S(2)}) collective-permute-start(bf16[72,512]{1,0:T(8,128)(2,1)S(1)} %get-tuple-element.82), channel_id=1, source_target_pairs={{0,15},{1,0},{2,1},{3,2},{4,3},{5,4},{6,5},{7,6},{8,7},{9,8},{10,9... | collective-permute-start | bytes 221192 | tf_op jit(solution)/shard_map/ppermute | solution.py:507
  13.1 8.8 %collective-permute-start.5 = (bf16[72,512]{1,0:T(8,128)(2,1)S(1)}, bf16[72,512]{1,0:T(8,128)(2,1)S(1)}, u32[]{:S(2)}, u32[]{:S(2)}) collective-permute-start(bf16[72,512]{1,0:T(8,128)(2,1)S(1)} %get-tuple-element.83), channel_id=1, source_target_pairs={{0,255},{1,240},{2,241},{3,242},{4,243},{5,244},{6,245},{7,246},{8... | collective-permute-start | bytes 221192 | tf_op jit(solution)/shard_map/ppermute | solution.py:517
  13.3 8.6 %copy-start = (bf16[512,1536]{1,0:T(8,128)(2,1)S(1)}, bf16[512,1536]{1,0:T(8,128)(2,1)}, u32[]{:S(2)}) copy-start(bf16[512,1536]{1,0:T(8,128)(2,1)} %qkv.3) | copy-start | bytes 4718596
  13.3 8.6 %copy-start.1 = (bf16[512,512]{1,0:T(8,128)(2,1)S(1)}, bf16[512,512]{1,0:T(8,128)(2,1)}, u32[]{:S(2)}) copy-start(bf16[512,512]{1,0:T(8,128)(2,1)} %out.4) | copy-start | bytes 1572868
  13.3 8.6 %copy-start.4 = (f32[512]{0:T(512)S(1)}, f32[512]{0:T(512)}, u32[]{:S(2)}) copy-start(f32[512]{0:T(512)} %gain.4) | copy-start | bytes 6148
  13.3 8.6 %copy-start.6 = (bf16[288,288]{1,0:T(8,128)(2,1)S(1)}, bf16[288,288]{1,0:T(8,128)(2,1)}, u32[]{:S(2)}) copy-start(bf16[288,288]{1,0:T(8,128)(2,1)} %constant.13.clone.sort_t) | copy-start | bytes 497668
  16.3 9.5 %collective-permute-start = (bf16[72,512]{1,0:T(8,128)(2,1)S(1)}, bf16[72,512]{1,0:T(8,128)(2,1)S(1)}, u32[]{:S(2)}, u32[]{:S(2)}) collective-permute-start(bf16[72,512]{1,0:T(8,128)(2,1)S(1)} %get-tuple-element.77), channel_id=1, source_target_pairs={{0,240},{16,0},{32,16},{48,32},{64,48},{80,64},{96,80},{112,96},{1... | collective-permute-start | bytes 221192 | tf_op jit(solution)/shard_map/ppermute | solution.py:507
  18.3 7.5 %collective-permute-start.1 = (bf16[72,512]{1,0:T(8,128)(2,1)S(1)}, bf16[72,512]{1,0:T(8,128)(2,1)S(1)}, u32[]{:S(2)}, u32[]{:S(2)}) collective-permute-start(bf16[72,512]{1,0:T(8,128)(2,1)S(1)} %get-tuple-element.78), channel_id=1, source_target_pairs={{0,15},{1,0},{2,1},{3,2},{4,3},{5,4},{6,5},{7,6},{8,7},{9,8},{10,9... | collective-permute-start | bytes 221192 | tf_op jit(solution)/shard_map/ppermute | solution.py:507
  20.6 5.2 %collective-permute-start.2 = (bf16[72,512]{1,0:T(8,128)(2,1)S(1)}, bf16[72,512]{1,0:T(8,128)(2,1)S(1)}, u32[]{:S(2)}, u32[]{:S(2)}) collective-permute-start(bf16[72,512]{1,0:T(8,128)(2,1)S(1)} %get-tuple-element.79), channel_id=1, source_target_pairs={{0,255},{1,240},{2,241},{3,242},{4,243},{5,244},{6,245},{7,246},{8... | collective-permute-start | bytes 221192 | tf_op jit(solution)/shard_map/ppermute | solution.py:517
  30.3 9.8 %collective-permute-start.6 = (bf16[2,72,512]{2,1,0:T(8,128)(2,1)S(1)}, bf16[2,72,512]{2,1,0:T(8,128)(2,1)S(1)}, u32[]{:S(2)}, u32[]{:S(2)}) collective-permute-start(bf16[2,72,512]{2,1,0:T(8,128)(2,1)S(1)} %get-tuple-element.94), channel_id=1, source_target_pairs={{0,17},{1,18},{2,19},{3,20},{4,21},{5,22},{6,23},{7,24},{8,25},{9,... | collective-permute-start | bytes 442376 | tf_op jit(solution)/shard_map/ppermute | solution.py:517
  30.9 9.3 %collective-permute-start.7 = (bf16[2,72,512]{2,1,0:T(8,128)(2,1)S(1)}, bf16[2,72,512]{2,1,0:T(8,128)(2,1)S(1)}, u32[]{:S(2)}, u32[]{:S(2)}) collective-permute-start(bf16[2,72,512]{2,1,0:T(8,128)(2,1)S(1)} %get-tuple-element.95), channel_id=1, source_target_pairs={{0,1},{1,2},{2,3},{3,4},{4,5},{5,6},{6,7},{7,8},{8,9},{9,10},{10,1... | collective-permute-start | bytes 442376 | tf_op jit(solution)/shard_map/ppermute | solution.py:507
  31.0 12.2 %collective-permute-start.8 = (bf16[2,72,512]{2,1,0:T(8,128)(2,1)S(1)}, bf16[2,72,512]{2,1,0:T(8,128)(2,1)S(1)}, u32[]{:S(2)}, u32[]{:S(2)}) collective-permute-start(bf16[2,72,512]{2,1,0:T(8,128)(2,1)S(1)} %get-tuple-element.96), channel_id=1, source_target_pairs={{0,16},{16,32},{32,48},{48,64},{64,80},{80,96},{96,112},{112,128},... | collective-permute-start | bytes 442376 | tf_op jit(solution)/shard_map/ppermute | solution.py:507
  31.9 11.2 %copy-start.2 = (bf16[512,512]{1,0:T(8,128)(2,1)S(1)}, bf16[512,512]{1,0:T(8,128)(2,1)}, u32[]{:S(2)}) copy-start(bf16[512,512]{1,0:T(8,128)(2,1)} %out.5) | copy-start | bytes 1572868
  33.3 14.2 %collective-permute-start.16 = (bf16[256,2048]{1,0:T(8,128)(2,1)S(1)}, bf16[256,2048]{1,0:T(8,128)(2,1)S(1)}, u32[]{:S(2)}, u32[]{:S(2)}) collective-permute-start(bf16[256,2048]{1,0:T(8,128)(2,1)S(1)} %get-tuple-element.122), channel_id=1, source_target_pairs={{0,1},{1,0},{2,3},{3,2},{4,5},{5,4},{6,7},{7,6},{8,9},{9,8},{10,11... | collective-permute-start | bytes 3145736 | tf_op jit(solution)/shard_map/ppermute | solution.py:507
  47.4 3.0 %collective-permute-start.9 = (bf16[256,2048]{1,0:T(8,128)(2,1)S(1)}, bf16[256,2048]{1,0:T(8,128)(2,1)S(1)}, u32[]{:S(2)}, u32[]{:S(2)}) collective-permute-start(bf16[256,2048]{1,0:T(8,128)(2,1)S(1)} %get-tuple-element.105), channel_id=1, source_target_pairs={{0,1},{1,0},{2,3},{3,2},{4,5},{5,4},{6,7},{7,6},{8,9},{9,8},{10,11... | collective-permute-start | bytes 3145736 | tf_op jit(solution)/shard_map/ppermute | solution.py:507
  47.7 8.8 %collective-permute-start.17 = (bf16[2,64,1024]{2,1,0:T(8,128)(2,1)S(1)}, bf16[2,64,1024]{2,1,0:T(8,128)(2,1)S(1)}, u32[]{:S(2)}, u32[]{:S(2)}) collective-permute-start(bf16[2,64,1024]{2,1,0:T(8,128)(2,1)S(1)} %get-tuple-element.124), channel_id=1, source_target_pairs={{0,2},{1,3},{2,0},{3,1},{4,6},{5,7},{6,4},{7,5},{8,10},{9,11},{10,... | collective-permute-start | bytes 786440 | tf_op jit(solution)/shard_map/ppermute | solution.py:507
  48.5 9.6 %collective-permute-start.18 = (bf16[2,64,1024]{2,1,0:T(8,128)(2,1)S(1)}, bf16[2,64,1024]{2,1,0:T(8,128)(2,1)S(1)}, u32[]{:S(2)}, u32[]{:S(2)}) collective-permute-start(bf16[2,64,1024]{2,1,0:T(8,128)(2,1)S(1)} %get-tuple-element.126), channel_id=1, source_target_pairs={{0,130},{1,131},{2,128},{3,129},{4,134},{5,135},{6,132},{7,133},{8... | collective-permute-start | bytes 786440 | tf_op jit(solution)/shard_map/ppermute | solution.py:535
  50.5 33.6 %copy-start.5 = (f32[512]{0:T(512)S(1)}, f32[512]{0:T(512)}, u32[]{:S(2)}) copy-start(f32[512]{0:T(512)} %gain.5) | copy-start | bytes 6148
  50.5 33.6 %copy-start.7 = (bf16[288,288]{1,0:T(8,128)(2,1)S(1)}, bf16[288,288]{1,0:T(8,128)(2,1)}, u32[]{:S(2)}) copy-start(bf16[288,288]{1,0:T(8,128)(2,1)} %constant.11.clone.place_t) | copy-start | bytes 497668
  50.6 8.9 %collective-permute-start.10 = (bf16[2,64,1024]{2,1,0:T(8,128)(2,1)S(1)}, bf16[2,64,1024]{2,1,0:T(8,128)(2,1)S(1)}, u32[]{:S(2)}, u32[]{:S(2)}) collective-permute-start(bf16[2,64,1024]{2,1,0:T(8,128)(2,1)S(1)} %get-tuple-element.107), channel_id=1, source_target_pairs={{0,4},{1,5},{2,6},{3,7},{4,0},{5,1},{6,2},{7,3},{8,12},{9,13},{10,... | collective-permute-start | bytes 786440 | tf_op jit(solution)/shard_map/ppermute | solution.py:507
  51.6 9.0 %collective-permute-start.11 = (bf16[2,64,1024]{2,1,0:T(8,128)(2,1)S(1)}, bf16[2,64,1024]{2,1,0:T(8,128)(2,1)S(1)}, u32[]{:S(2)}, u32[]{:S(2)}) collective-permute-start(bf16[2,64,1024]{2,1,0:T(8,128)(2,1)S(1)} %get-tuple-element.109), channel_id=1, source_target_pairs={{0,12},{1,13},{2,14},{3,15},{4,8},{5,9},{6,10},{7,11},{8,4},{9,5},... | collective-permute-start | bytes 786440 | tf_op jit(solution)/shard_map/ppermute | solution.py:507
  58.1 6.3 %collective-permute-start.19 = (bf16[64,1024]{1,0:T(8,128)(2,1)S(1)}, bf16[64,1024]{1,0:T(8,128)(2,1)S(1)}, u32[]{:S(2)}, u32[]{:S(2)}) collective-permute-start(bf16[64,1024]{1,0:T(8,128)(2,1)S(1)} %get-tuple-element.128), channel_id=1, source_target_pairs={{0,130},{1,131},{2,128},{3,129},{4,134},{5,135},{6,132},{7,133},{8... | collective-permute-start | bytes 393224 | tf_op jit(solution)/shard_map/ppermute | solution.py:535
  59.4 5.0 %collective-permute-start.20 = (bf16[64,1024]{1,0:T(8,128)(2,1)S(1)}, bf16[64,1024]{1,0:T(8,128)(2,1)S(1)}, u32[]{:S(2)}, u32[]{:S(2)}) collective-permute-start(bf16[64,1024]{1,0:T(8,128)(2,1)S(1)} %get-tuple-element.130), channel_id=1, source_target_pairs={{0,2},{1,3},{2,0},{3,1},{4,6},{5,7},{6,4},{7,5},{8,10},{9,11},{10,... | collective-permute-start | bytes 393224 | tf_op jit(solution)/shard_map/ppermute | solution.py:507
  60.7 6.3 %collective-permute-start.12 = (bf16[64,1024]{1,0:T(8,128)(2,1)S(1)}, bf16[64,1024]{1,0:T(8,128)(2,1)S(1)}, u32[]{:S(2)}, u32[]{:S(2)}) collective-permute-start(bf16[64,1024]{1,0:T(8,128)(2,1)S(1)} %get-tuple-element.111), channel_id=1, source_target_pairs={{0,12},{1,13},{2,14},{3,15},{4,8},{5,9},{6,10},{7,11},{8,4},{9,5},... | collective-permute-start | bytes 393224 | tf_op jit(solution)/shard_map/ppermute | solution.py:507
  63.7 5.5 %collective-permute-start.13 = (bf16[64,1024]{1,0:T(8,128)(2,1)S(1)}, bf16[64,1024]{1,0:T(8,128)(2,1)S(1)}, u32[]{:S(2)}, u32[]{:S(2)}) collective-permute-start(bf16[64,1024]{1,0:T(8,128)(2,1)S(1)} %get-tuple-element.113), channel_id=1, source_target_pairs={{0,4},{1,5},{2,6},{3,7},{4,0},{5,1},{6,2},{7,3},{8,12},{9,13},{10,... | collective-permute-start | bytes 393224 | tf_op jit(solution)/shard_map/ppermute | solution.py:507
  64.5 6.2 %collective-permute-start.21 = (bf16[2,32,1024]{2,1,0:T(8,128)(2,1)S(1)}, bf16[2,32,1024]{2,1,0:T(8,128)(2,1)S(1)}, u32[]{:S(2)}, u32[]{:S(2)}) collective-permute-start(bf16[2,32,1024]{2,1,0:T(8,128)(2,1)S(1)} %get-tuple-element.132), channel_id=1, source_target_pairs={{0,4},{1,5},{2,6},{3,7},{4,0},{5,1},{6,2},{7,3},{8,12},{9,13},{10,... | collective-permute-start | bytes 393224 | tf_op jit(solution)/shard_map/ppermute | solution.py:507
  69.4 5.1 %collective-permute-start.14 = (bf16[2,32,1024]{2,1,0:T(8,128)(2,1)S(1)}, bf16[2,32,1024]{2,1,0:T(8,128)(2,1)S(1)}, u32[]{:S(2)}, u32[]{:S(2)}) collective-permute-start(bf16[2,32,1024]{2,1,0:T(8,128)(2,1)S(1)} %get-tuple-element.115), channel_id=1, source_target_pairs={{0,2},{1,3},{2,0},{3,1},{4,6},{5,7},{6,4},{7,5},{8,10},{9,11},{10,... | collective-permute-start | bytes 393224 | tf_op jit(solution)/shard_map/ppermute | solution.py:507
  70.7 5.6 %collective-permute-start.22 = (bf16[1,32,1024]{2,1,0:T(8,128)(2,1)S(1)}, bf16[1,32,1024]{2,1,0:T(8,128)(2,1)S(1)}, u32[]{:S(2)}, u32[]{:S(2)}) collective-permute-start(bf16[1,32,1024]{2,1,0:T(8,128)(2,1)S(1)} %get-tuple-element.134), channel_id=1, source_target_pairs={{0,12},{1,13},{2,14},{3,15},{4,8},{5,9},{6,10},{7,11},{8,4},{9,5},... | collective-permute-start | bytes 196616 | tf_op jit(solution)/shard_map/ppermute | solution.py:507
  74.4 5.6 %collective-permute-start.15 = (bf16[1,32,1024]{2,1,0:T(8,128)(2,1)S(1)}, bf16[1,32,1024]{2,1,0:T(8,128)(2,1)S(1)}, u32[]{:S(2)}, u32[]{:S(2)}) collective-permute-start(bf16[1,32,1024]{2,1,0:T(8,128)(2,1)S(1)} %get-tuple-element.117), channel_id=1, source_target_pairs={{0,130},{1,131},{2,128},{3,129},{4,134},{5,135},{6,132},{7,133},{8... | collective-permute-start | bytes 196616 | tf_op jit(solution)/shard_map/ppermute | solution.py:535
  80.8 12.4 %all-to-all-start = ((bf16[8,64,128]{2,1,0:T(8,128)(2,1)}), bf16[8,64,128]{2,1,0:T(8,128)(2,1)S(1)}, u32[]{:S(2)}, u32[]{:S(2)}) async-start(bf16[8,64,128]{2,1,0:T(8,128)(2,1)} %shard_map.214), calls=%async_computation | async-start | bytes 262144 | tf_op jit(solution)/shard_map/all_to_all | solution.py:553

commit v8 on v7

--- a/solution.py
+++ b/solution.py
@@ -332,8 +332,7 @@
 
 
 def kernel_backward_b(
-    piece0, piece1, piece2, piece3, delta0, delta1, delta2, delta3,
-    inputs, gain, qkv, out, packed, probs, mixed_t, sort, sort_t,
+    piece0, piece1, piece2, piece3, inputs, gain, qkv, out, packed, probs, mixed_t, sort, sort_t,
     back0, back1, back2, back3, upstream_out, d_packed,
     d_probs, d_scores,
 ):
@@ -344,10 +343,7 @@
     d_inputs = norm_backward(
         inputs[...].astype(F32), gain[...].reshape(1, WIDTH), d_packed[...], qkv
     )
-    backs = (back0, back1, back2, back3)
-    split_pieces(sort[...], d_inputs.astype(BF16), [back.at[0] for back in backs])
-    for back, delta in zip(backs, (delta0, delta1, delta2, delta3), strict=True):
-        back[1] = delta[...]
+    split_pieces(sort[...], d_inputs.astype(BF16), (back0, back1, back2, back3))
 
 
 def kernel_grads_b(normed, mixed_t, upstream, d_packed, send, keep, normed_t):
@@ -362,7 +358,7 @@
     grad_middle_out, d_packed, send,
     d_probs, d_scores,
 ):
-    d_inputs = join_pieces(sort_t[...], [back[0] for back in (back0, back1, back2, back3)])
+    d_inputs = join_pieces(sort_t[...], [ref[...] for ref in (back0, back1, back2, back3)])
     grad_middle = (upstream[...].astype(F32) + d_inputs).astype(BF16)
     grad_middle_out[...] = grad_middle
     backward_core(grad_middle, out, packed, probs, mixed_t, d_packed, d_probs, d_scores)
@@ -376,7 +372,7 @@
 
 
 def kernel_advanced(back0, back1, back2, back3, middle, place_t, sort_t, advanced):
-    delta = join_pieces(sort_t[...], [back[1] for back in (back0, back1, back2, back3)])
+    delta = join_pieces(sort_t[...], [ref[...] for ref in (back0, back1, back2, back3)])
     store_grid(advanced, place_t[...], (middle[...].astype(F32) + delta).astype(BF16))
 
 
@@ -616,14 +612,13 @@
         (p3, eastern, below, diagonal, query_b, keys_b, gain_b, qkv_weight_b, out_weight_b, sort, sort_t),
         flops=5 * 10**9,
     )
-    twin = ((2, PIECE, WIDTH), BF16)
     d0, d1, d2, d3, upstream_b, d_packed_b = call(
         kernel_backward_b,
-        [twin] * 4 + [token, packed],
+        [piece] * 4 + [token, packed],
         [scores, probs],
         (
-            c3, c_eastern, c_below, c_diagonal, b0, b1, b2, b3, inputs_b, gain_b, qkv_weight_b,
-            out_weight_b, packed_b, probs_b, mixed_b, sort, sort_t,
+            c3, c_eastern, c_below, c_diagonal, inputs_b, gain_b, qkv_weight_b, out_weight_b,
+            packed_b, probs_b, mixed_b, sort, sort_t,
         ),
         flops=5 * 10**9,
     )
@@ -656,10 +651,17 @@
         flops=10**9,
     )[0]
     send_one_a, send_two_a, keep_one_a, keep_two_a = quarters(kernel_first_sum_a, keep_a, got_a)
+    send_one_a, send_two_a, b1, b2, b3 = lax.optimization_barrier(
+        (send_one_a, send_two_a, b1, b2, b3)
+    )
+    b3 = permute_both(b3, 1)
+    b2 = permute(b2, "lat", lambda i: i + 1)
+    b1 = permute(b1, "lon", lambda i: i + 1)
     parts_a = (keep_one_a, to_y(send_one_a, 1), keep_two_a, to_y(send_two_a, 3))
     pair = ((2, 32, SIDE), BF16)
     send_b, keep_b = call(kernel_third_sum_b, [pair] * 2, [], parts_b)
     got_b = to_y(send_b, 1)
+    parts_a, b1, b2, b3 = lax.optimization_barrier((parts_a, b1, b2, b3))
     send_one_a, send_two_a, held_one_a, held_two_a = second_sum(parts_a)
     parts_a = (held_one_a, to_y(send_one_a, 3), held_two_a, to_y(send_two_a, 1))
     send_a, keep_a = call(kernel_third_sum_a, [pair] * 2, [], parts_a)
@@ -674,7 +676,7 @@
     blocks, d_packed_a, middle_a = lax.optimization_barrier((blocks, d_packed_a, middle_a))
     parts = exchange_z(blocks)
     advanced = call(
-        kernel_advanced, [grid], [], (d3, d2, d1, d0, middle_a, place_t, sort_t),
+        kernel_advanced, [grid], [], (b3, b2, b1, b0, middle_a, place_t, sort_t),
         flops=2 * 10**9, final=(0,),
     )[0]
     grad_fields = call(

time: 94.1 us -> 98.4 us (1.046); the launches traced: 93.9 us -> 96.8 us
  waiting for transfers between devices: 28.4 us -> 31.1 us
    ppermute x17 -> x19, waiting for transfers between devices: 11.5 us -> 15.6 us  [permute(): lax.ppermute(array, axis, [(i, target(i) % length) for i in range(length)])]
    ppermute x3, starting transfers between devices: 3.91 us -> 5.71 us  [to_x(): return lax.ppermute(array, ('lon', 'lat'), pairs)]
    ppermute x17 -> x19, starting transfers between devices: 25.3 us -> 23.6 us  [permute(): lax.ppermute(array, axis, [(i, target(i) % length) for i in range(length)])]
    ppermute x3, waiting for transfers between devices: 6.02 us -> 4.53 us  [to_x(): return lax.ppermute(array, ('lon', 'lat'), pairs)]
    ppermute x3 -> x4, waiting for transfers between devices: 6.55 us -> 6.59 us  [permute_both(): return lax.ppermute(array, ('lon', 'lat'), pairs)]
    ppermute x3 -> x4, starting transfers between devices: 2 us -> 2 us  [permute_both(): return lax.ppermute(array, ('lon', 'lat'), pairs)]
  transfers between devices with their start and end apart: 24 -> 27, of which waited for: 13 -> 13; matrix products, arithmetic and copies ran while one was open for 0% -> 0% of each run, Pallas kernels for 19% -> 19%
where the time goes in v8:
time: 98.4 us; the launch traced here: 96.8 us
  starting transfers between devices  34.7 us (35%)
  waiting for transfers between devices  31.1 us (32%)
  Pallas kernels  30 us (30%)
    pallas_call x19, Pallas kernels, call(): pl.pallas_call(kernel, out_shape=tuple((jax.ShapeDtypeStruct(shape, kind)...  30 us
    ppermute x19, starting transfers between devices, permute(): lax.ppermute(array, axis, [(i, target(i) % length) for i in range(length)])  23.6 us
    ppermute x19, waiting for transfers between devices, permute(): lax.ppermute(array, axis, [(i, target(i) % length) for i in range(length)])  15.6 us
    ppermute x4, waiting for transfers between devices, permute_both(): return lax.ppermute(array, ('lon', 'lat'), pairs)  6.59 us
    ppermute x3, starting transfers between devices, to_x(): return lax.ppermute(array, ('lon', 'lat'), pairs)  5.71 us
    ppermute x3, waiting for transfers between devices, to_x(): return lax.ppermute(array, ('lon', 'lat'), pairs)  4.53 us
    all_to_all x1, waiting for transfers between devices, exchange_z(): lax.all_to_all(messages, 'lon', 0, 0, axis_index_groups=groups, tiled=True)  4.39 us
    all_to_all x1, starting transfers between devices, exchange_z(): lax.all_to_all(messages, 'lon', 0, 0, axis_index_groups=groups, tiled=True)  3.37 us
  transfers between devices with their start and end apart: 27, of which 13 were waited for; matrix products, arithmetic and copies ran while one was open for 0% of the time, Pallas kernels for 19%

profile of v8, /device:TPU:6, one launch (start us, length us, event | category | flops | bytes accessed | tf_op | source)
XLA Modules:
  0.0 96.8 jit_solution(9298803561074439363)
XLA Ops:
  0.6 0.0 copy-start.8
  0.7 0.0 copy-start.9
  0.7 0.0 copy-start.10
  0.7 5.6 %shard_map.199 = (bf16[72,512]{1,0:T(8,128)(2,1)S(1)}, bf16[72,512]{1,0:T(8,128)(2,1)S(1)}, bf16[72,512]{1,0:T(8,128)(2,1)S(1)}, bf16[72,512]{1,0:T(8,128)(2,1)S...) custom-call(bf16[12,6,4,512]{3,2,1,0:T(4,128)(2,1)} %bitcast.6, ...), custom_call_target="tpu_custom_call" | custom-call | flops 7000000000 | bytes 1048576 | tf_op jit(solution)/shard_map/pallas_call | solution.py:487
  6.3 6.8 %collective-permute-start.3 = (bf16[72,512]{1,0:T(8,128)(2,1)S(1)}, bf16[72,512]{1,0:T(8,128)(2,1)S(1)}, u32[]{:S(2)}, u32[]{:S(2)}) collective-permute-start(bf16[72,512]{1,0:T(8,128)(2,1)S(1)} %get-tuple-element.95), channel_id=1, source_target_pairs={{0,240},{16,0},{32,16},{48,32},{64,48},{80,64},{96,80},{112,96},{1... | collective-permute-start | bytes 221192 | tf_op jit(solution)/shard_map/ppermute | solution.py:503
  13.1 0.2 collective-permute-start.5
  13.3 0.0 copy-start
  13.3 0.0 copy-start.1
  13.3 0.0 copy-start.4
  13.3 0.0 copy-start.6
  13.3 2.9 %shard_map.200 = (bf16[72,512]{1,0:T(8,128)(2,1)S(1)}, bf16[72,512]{1,0:T(8,128)(2,1)S(1)}, bf16[72,512]{1,0:T(8,128)(2,1)S(1)}, bf16[72,512]{1,0:T(8,128)(2,1)S...) custom-call(bf16[12,6,4,512]{3,2,1,0:T(4,128)(2,1)} %bitcast.7, ...), custom_call_target="tpu_custom_call" | custom-call | flops 2000000000 | bytes 1048576 | tf_op jit(solution)/shard_map/pallas_call | solution.py:487
  16.2 2.0 %collective-permute-start = (bf16[72,512]{1,0:T(8,128)(2,1)S(1)}, bf16[72,512]{1,0:T(8,128)(2,1)S(1)}, u32[]{:S(2)}, u32[]{:S(2)}) collective-permute-start(bf16[72,512]{1,0:T(8,128)(2,1)S(1)} %get-tuple-element.91), channel_id=1, source_target_pairs={{0,240},{16,0},{32,16},{48,32},{64,48},{80,64},{96,80},{112,96},{1... | collective-permute-start | bytes 221192 | tf_op jit(solution)/shard_map/ppermute | solution.py:503
  18.2 2.4 %collective-permute-start.1 = (bf16[72,512]{1,0:T(8,128)(2,1)S(1)}, bf16[72,512]{1,0:T(8,128)(2,1)S(1)}, u32[]{:S(2)}, u32[]{:S(2)}) collective-permute-start(bf16[72,512]{1,0:T(8,128)(2,1)S(1)} %get-tuple-element.92), channel_id=1, source_target_pairs={{0,15},{1,0},{2,1},{3,2},{4,3},{5,4},{6,5},{7,6},{8,7},{9,8},{10,9... | collective-permute-start | bytes 221192 | tf_op jit(solution)/shard_map/ppermute | solution.py:503
  20.6 0.0 collective-permute-done.3.piece1
  20.6 1.2 %collective-permute-start.2 = (bf16[72,512]{1,0:T(8,128)(2,1)S(1)}, bf16[72,512]{1,0:T(8,128)(2,1)S(1)}, u32[]{:S(2)}, u32[]{:S(2)}) collective-permute-start(bf16[72,512]{1,0:T(8,128)(2,1)S(1)} %get-tuple-element.93), channel_id=1, source_target_pairs={{0,255},{1,240},{2,241},{3,242},{4,243},{5,244},{6,245},{7,246},{8... | collective-permute-start | bytes 221192 | tf_op jit(solution)/shard_map/ppermute | solution.py:513
  21.9 3.8 %shard_map.201 = (bf16[72,512]{1,0:T(8,128)(2,1)S(1)}, bf16[72,512]{1,0:T(8,128)(2,1)S(1)}, bf16[72,512]{1,0:T(8,128)(2,1)S(1)}, bf16[72,512]{1,0:T(8,128)(2,1)S...) custom-call(bf16[72,512]{1,0:T(8,128)(2,1)S(1)} %get-tuple-element.9, ...), custom_call_target="tpu_custom_call" | custom-call | flops 5000000000 | bytes 1048576 | tf_op jit(solution)/shard_map/pallas_call | solution.py:487
  25.8 0.0 collective-permute-done.1.piece2
  25.8 0.0 collective-permute-done.2.piece3
  25.8 4.5 %shard_map.202 = (bf16[72,512]{1,0:T(8,128)(2,1)S(1)}, bf16[72,512]{1,0:T(8,128)(2,1)S(1)}, bf16[72,512]{1,0:T(8,128)(2,1)S(1)}, bf16[72,512]{1,0:T(8,128)(2,1)S...) custom-call(bf16[72,512]{1,0:T(8,128)(2,1)S(1)} %get-tuple-element.90.piece0, ...), custom_call_target="tpu_custom_call" | custom-call | flops 5000000000 | bytes 1048576 | tf_op jit(solution)/shard_map/pallas_call | solution.py:487
  30.3 0.6 collective-permute-start.6
  30.9 0.1 collective-permute-start.7
  30.9 1.0 collective-permute-start.8
  31.9 1.3 %shard_map.209 = (bf16[256,2048]{1,0:T(8,128)(2,1)S(1)}, bf16[256,2048]{1,0:T(8,128)(2,1)S(1)}) custom-call(bf16[288,512]{1,0:T(8,128)(2,1)S(1)} %get-tuple-element.142.normed, bf16[2,512,144]{2,1,0:T(8,128)(2,1)S(1)} %get-tuple-element.103.mixed_t, bf16[288,512]{1,0:T(8,128)(2,1)S(1)} %get-tuple-element.143.upstream, ...), custom_call_target="tpu_custom_call" | custom-call | flops 2000000000 | bytes 1048576 | tf_op jit(solution)/shard_map/pallas_call | solution.py:487
  33.2 0.3 collective-permute-start.19
  33.6 4.3 %collective-permute-done.6.back0 = bf16[72,512]{1,0:T(8,128)(2,1)S(1)} collective-permute-done((bf16[72,512]{1,0:T(8,128)(2,1)S(1)}, bf16[72,512]{1,0:T(8,128)(2,1)S(1)}, u32[]{:S(2)}, u32[]{:S(2)}) %collective-permute-start.6) | collective-permute-done | bytes 73760 | tf_op jit(solution)/shard_map/ppermute | solution.py:513
  37.9 2.1 %collective-permute-done.8.back2 = bf16[72,512]{1,0:T(8,128)(2,1)S(1)} collective-permute-done((bf16[72,512]{1,0:T(8,128)(2,1)S(1)}, bf16[72,512]{1,0:T(8,128)(2,1)S(1)}, u32[]{:S(2)}, u32[]{:S(2)}) %collective-permute-start.8) | collective-permute-done | bytes 73760 | tf_op jit(solution)/shard_map/ppermute | solution.py:503
  39.9 4.2 %shard_map.203 = (bf16[288,512]{1,0:T(8,128)(2,1)S(1)}, bf16[288,1536]{1,0:T(8,128)(2,1)S(1)}, bf16[256,2048]{1,0:T(8,128)(2,1)S(1)}) custom-call(bf16[72,512]{1,0:T(8,128)(2,1)S(1)} %collective-permute-done.6.back0, bf16[72,512]{1,0:T(8,128)(2,1)S(1)} %collective-permute-done.7.back1, bf16[72,512]{1,0:T(8,128)(2,1)S(1)} %collective-permute-done.8.back2, ...), custom_call_target="tpu_custom_call" | custom-call | flops 5000000000 | bytes 1048576 | tf_op jit(solution)/shard_map/pallas_call | solution.py:487
  44.1 0.1 collective-permute-start.9
  44.3 0.1 shard_map.210
  44.4 1.4 %collective-permute-start.20 = (bf16[2,64,1024]{2,1,0:T(8,128)(2,1)S(1)}, bf16[2,64,1024]{2,1,0:T(8,128)(2,1)S(1)}, u32[]{:S(2)}, u32[]{:S(2)}) collective-permute-start(bf16[2,64,1024]{2,1,0:T(8,128)(2,1)S(1)} %get-tuple-element.148), channel_id=1, source_target_pairs={{0,2},{1,3},{2,0},{3,1},{4,6},{5,7},{6,4},{7,5},{8,10},{9,11},{10,... | collective-permute-start | bytes 786440 | tf_op jit(solution)/shard_map/ppermute | solution.py:503
  45.8 2.0 %collective-permute-start.21 = (bf16[2,64,1024]{2,1,0:T(8,128)(2,1)S(1)}, bf16[2,64,1024]{2,1,0:T(8,128)(2,1)S(1)}, u32[]{:S(2)}, u32[]{:S(2)}) collective-permute-start(bf16[2,64,1024]{2,1,0:T(8,128)(2,1)S(1)} %get-tuple-element.150), channel_id=1, source_target_pairs={{0,130},{1,131},{2,128},{3,129},{4,134},{5,135},{6,132},{7,133},{8... | collective-permute-start | bytes 786440 | tf_op jit(solution)/shard_map/ppermute | solution.py:531
  47.7 0.7 shard_map.204.keep
  48.4 0.1 shard_map.205
  48.6 0.0 copy-start.5
  48.6 0.0 copy-start.7
  48.6 0.9 collective-permute-start.10
  49.5 2.4 %collective-permute-start.11 = (bf16[2,64,1024]{2,1,0:T(8,128)(2,1)S(1)}, bf16[2,64,1024]{2,1,0:T(8,128)(2,1)S(1)}, u32[]{:S(2)}, u32[]{:S(2)}) collective-permute-start(bf16[2,64,1024]{2,1,0:T(8,128)(2,1)S(1)} %get-tuple-element.122), channel_id=1, source_target_pairs={{0,12},{1,13},{2,14},{3,15},{4,8},{5,9},{6,10},{7,11},{8,4},{9,5},... | collective-permute-start | bytes 786440 | tf_op jit(solution)/shard_map/ppermute | solution.py:503
  51.9 1.2 %collective-permute-done.20.got_one = bf16[2,64,1024]{2,1,0:T(8,128)(2,1)S(1)} collective-permute-done((bf16[2,64,1024]{2,1,0:T(8,128)(2,1)S(1)}, bf16[2,64,1024]{2,1,0:T(8,128)(2,1)S(1)}, u32[]{:S(2)}, u32[]{:S(2)}) %collective-permute-start.20) | collective-permute-done | bytes 262176 | tf_op jit(solution)/shard_map/ppermute | solution.py:503
  53.2 2.2 %collective-permute-done.21.got_two = bf16[2,64,1024]{2,1,0:T(8,128)(2,1)S(1)} collective-permute-done((bf16[2,64,1024]{2,1,0:T(8,128)(2,1)S(1)}, bf16[2,64,1024]{2,1,0:T(8,128)(2,1)S(1)}, u32[]{:S(2)}, u32[]{:S(2)}) %collective-permute-start.21) | collective-permute-done | bytes 262176 | tf_op jit(solution)/shard_map/ppermute | solution.py:531
  55.4 0.1 shard_map.211
  55.4 4.6 %collective-permute-done.12.back2 = bf16[72,512]{1,0:T(8,128)(2,1)S(1)} collective-permute-done((bf16[72,512]{1,0:T(8,128)(2,1)S(1)}, bf16[72,512]{1,0:T(8,128)(2,1)S(1)}, u32[]{:S(2)}, u32[]{:S(2)}) %collective-permute-start.12) | collective-permute-done | bytes 73760 | tf_op jit(solution)/shard_map/ppermute | solution.py:503
  60.0 0.3 collective-permute-start.22
  60.3 0.6 collective-permute-start.23
  60.9 2.3 %collective-permute-done.14.back0 = bf16[72,512]{1,0:T(8,128)(2,1)S(1)} collective-permute-done((bf16[72,512]{1,0:T(8,128)(2,1)S(1)}, bf16[72,512]{1,0:T(8,128)(2,1)S(1)}, u32[]{:S(2)}, u32[]{:S(2)}) %collective-permute-start.14) | collective-permute-done | bytes 73760 | tf_op jit(solution)/shard_map/ppermute | solution.py:513
  63.2 0.1 shard_map.206
  63.3 2.8 %collective-permute-start.15 = (bf16[64,1024]{1,0:T(8,128)(2,1)S(1)}, bf16[64,1024]{1,0:T(8,128)(2,1)S(1)}, u32[]{:S(2)}, u32[]{:S(2)}) collective-permute-start(bf16[64,1024]{1,0:T(8,128)(2,1)S(1)} %get-tuple-element.135), channel_id=1, source_target_pairs={{0,12},{1,13},{2,14},{3,15},{4,8},{5,9},{6,10},{7,11},{8,4},{9,5},... | collective-permute-start | bytes 393224 | tf_op jit(solution)/shard_map/ppermute | solution.py:503
  66.1 0.1 collective-permute-done.22.got_one
  66.2 0.1 shard_map.212
  66.3 2.0 %collective-permute-start.24 = (bf16[2,32,1024]{2,1,0:T(8,128)(2,1)S(1)}, bf16[2,32,1024]{2,1,0:T(8,128)(2,1)S(1)}, u32[]{:S(2)}, u32[]{:S(2)}) collective-permute-start(bf16[2,32,1024]{2,1,0:T(8,128)(2,1)S(1)} %get-tuple-element.156), channel_id=1, source_target_pairs={{0,4},{1,5},{2,6},{3,7},{4,0},{5,1},{6,2},{7,3},{8,12},{9,13},{10,... | collective-permute-start | bytes 393224 | tf_op jit(solution)/shard_map/ppermute | solution.py:503
  68.3 1.3 %collective-permute-done.15.got_one = bf16[64,1024]{1,0:T(8,128)(2,1)S(1)} collective-permute-done((bf16[64,1024]{1,0:T(8,128)(2,1)S(1)}, bf16[64,1024]{1,0:T(8,128)(2,1)S(1)}, u32[]{:S(2)}, u32[]{:S(2)}) %collective-permute-start.15) | collective-permute-done | bytes 131104 | tf_op jit(solution)/shard_map/ppermute | solution.py:503
  69.6 2.3 %collective-permute-done.16.got_two = bf16[64,1024]{1,0:T(8,128)(2,1)S(1)} collective-permute-done((bf16[64,1024]{1,0:T(8,128)(2,1)S(1)}, bf16[64,1024]{1,0:T(8,128)(2,1)S(1)}, u32[]{:S(2)}, u32[]{:S(2)}) %collective-permute-start.16) | collective-permute-done | bytes 131104 | tf_op jit(solution)/shard_map/ppermute | solution.py:503
  71.8 0.3 shard_map.207
  72.2 0.1 collective-permute-start.17
  72.3 1.0 collective-permute-done.24.got
  73.3 0.8 collective-permute-start.25
  74.1 3.1 %collective-permute-done.17.got = bf16[2,32,1024]{2,1,0:T(8,128)(2,1)S(1)} collective-permute-done((bf16[2,32,1024]{2,1,0:T(8,128)(2,1)S(1)}, bf16[2,32,1024]{2,1,0:T(8,128)(2,1)S(1)}, u32[]{:S(2)}, u32[]{:S(2)}) %collective-permute-start.17) | collective-permute-done | bytes 131104 | tf_op jit(solution)/shard_map/ppermute | solution.py:503
  77.2 3.4 %collective-permute-start.18 = (bf16[1,32,1024]{2,1,0:T(8,128)(2,1)S(1)}, bf16[1,32,1024]{2,1,0:T(8,128)(2,1)S(1)}, u32[]{:S(2)}, u32[]{:S(2)}) collective-permute-start(bf16[1,32,1024]{2,1,0:T(8,128)(2,1)S(1)} %get-tuple-element.141), channel_id=1, source_target_pairs={{0,130},{1,131},{2,128},{3,129},{4,134},{5,135},{6,132},{7,133},{8... | collective-permute-start | bytes 196616 | tf_op jit(solution)/shard_map/ppermute | solution.py:531
  80.7 2.2 %collective-permute-done.18.got_a = bf16[1,32,1024]{2,1,0:T(8,128)(2,1)S(1)} collective-permute-done((bf16[1,32,1024]{2,1,0:T(8,128)(2,1)S(1)}, bf16[1,32,1024]{2,1,0:T(8,128)(2,1)S(1)}, u32[]{:S(2)}, u32[]{:S(2)}) %collective-permute-start.18) | collective-permute-done | bytes 65568 | tf_op jit(solution)/shard_map/ppermute | solution.py:531
  82.9 0.8 shard_map.214
  83.7 3.4 %all-to-all-start = ((bf16[8,64,128]{2,1,0:T(8,128)(2,1)}), bf16[8,64,128]{2,1,0:T(8,128)(2,1)S(1)}, u32[]{:S(2)}, u32[]{:S(2)}) async-start(bf16[8,64,128]{2,1,0:T(8,128)(2,1)} %shard_map.214), calls=%async_computation | async-start | bytes 262144 | tf_op jit(solution)/shard_map/all_to_all | solution.py:549
  87.1 3.3 %shard_map.216 = bf16[12,6,4,512]{3,2,1,0:T(4,128)(2,1)} custom-call(bf16[288,512]{1,0:T(8,128)(2,1)S(1)} %get-tuple-element.161.inputs, bf16[288,512]{1,0:T(8,128)(2,1)S(1)} %get-tuple-element.111.grad_middle, f32[512]{0:T(512)S(1)} %copy-done.5, bf16[512,1536]{1,0:T(8,128)(2,1)} %qkv_hbm.3, bf16[288,1536]{1,0:T(8,128)(2,1)S(1)} %get-tuple-element.162.d_packed, ...), custom_call_target="tpu_custom_call" | custom-call | flops 4000000000 | bytes 1048576 | tf_op jit(solution)/shard_map/pallas_call | solution.py:487
  90.4 1.3 %shard_map.215 = bf16[12,6,4,512]{3,2,1,0:T(4,128)(2,1)} custom-call(bf16[72,512]{1,0:T(8,128)(2,1)S(1)} %collective-permute-done.14.back0, bf16[72,512]{1,0:T(8,128)(2,1)S(1)} %collective-permute-done.13.back1, bf16[72,512]{1,0:T(8,128)(2,1)S(1)} %collective-permute-done.12.back2, bf16[72,512]{1,0:T(8,128)(2,1)S(1)} %get-tuple-element.129.back3, ...), custom_call_target="tpu_custom_call" | custom-call | flops 2000000000 | bytes 1048576 | tf_op jit(solution)/shard_map/pallas_call | solution.py:487
  91.7 4.4 %all-to-all-done.parts = bf16[8,64,128]{2,1,0:T(8,128)(2,1)S(1)} async-done(((bf16[8,64,128]{2,1,0:T(8,128)(2,1)}), bf16[8,64,128]{2,1,0:T(8,128)(2,1)S(1)}, u32[]{:S(2)}, u32[]{:S(2)}) %all-to-all-start) | async-done | bytes 131104 | tf_op jit(solution)/shard_map/all_to_all | solution.py:549
  96.1 0.7 shard_map.217
  (31 shorter events, 0.1 us)
Async XLA Ops:
  0.6 12.6 %copy-start.3 = (s32[192,96]{1,0:T(8,128)S(1)}, s32[192,96]{1,0:T(8,128)}, u32[]{:S(2)}) copy-start(s32[192,96]{1,0:T(8,128)} %ids.1) | copy-start | bytes 221188
  0.6 12.6 %copy-start.8 = (bf16[288,288]{1,0:T(8,128)(2,1)S(1)}, bf16[288,288]{1,0:T(8,128)(2,1)}, u32[]{:S(2)}) copy-start(bf16[288,288]{1,0:T(8,128)(2,1)} %constant.12.clone.sort_hbm.sort) | copy-start | bytes 497668
  0.7 12.6 %copy-start.9 = (bf16[288,288]{1,0:T(8,128)(2,1)S(1)}, bf16[288,288]{1,0:T(8,128)(2,1)}, u32[]{:S(2)}) copy-start(bf16[288,288]{1,0:T(8,128)(2,1)} %constant.10.clone.place_hbm.place) | copy-start | bytes 497668
  0.7 12.6 %copy-start.10 = (s32[144,8]{1,0:T(8,128)S(1)}, s32[144,8]{1,0:T(8,128)}, u32[]{:S(2)}) copy-start(s32[144,8]{1,0:T(8,128)} %constant.14.clone.where_hbm.where) | copy-start | bytes 13828
  6.3 14.3 %collective-permute-start.3 = (bf16[72,512]{1,0:T(8,128)(2,1)S(1)}, bf16[72,512]{1,0:T(8,128)(2,1)S(1)}, u32[]{:S(2)}, u32[]{:S(2)}) collective-permute-start(bf16[72,512]{1,0:T(8,128)(2,1)S(1)} %get-tuple-element.95), channel_id=1, source_target_pairs={{0,240},{16,0},{32,16},{48,32},{64,48},{80,64},{96,80},{112,96},{1... | collective-permute-start | bytes 221192 | tf_op jit(solution)/shard_map/ppermute | solution.py:503
  13.1 8.8 %collective-permute-start.4 = (bf16[72,512]{1,0:T(8,128)(2,1)S(1)}, bf16[72,512]{1,0:T(8,128)(2,1)S(1)}, u32[]{:S(2)}, u32[]{:S(2)}) collective-permute-start(bf16[72,512]{1,0:T(8,128)(2,1)S(1)} %get-tuple-element.96), channel_id=1, source_target_pairs={{0,15},{1,0},{2,1},{3,2},{4,3},{5,4},{6,5},{7,6},{8,7},{9,8},{10,9... | collective-permute-start | bytes 221192 | tf_op jit(solution)/shard_map/ppermute | solution.py:503
  13.1 8.8 %collective-permute-start.5 = (bf16[72,512]{1,0:T(8,128)(2,1)S(1)}, bf16[72,512]{1,0:T(8,128)(2,1)S(1)}, u32[]{:S(2)}, u32[]{:S(2)}) collective-permute-start(bf16[72,512]{1,0:T(8,128)(2,1)S(1)} %get-tuple-element.97), channel_id=1, source_target_pairs={{0,255},{1,240},{2,241},{3,242},{4,243},{5,244},{6,245},{7,246},{8... | collective-permute-start | bytes 221192 | tf_op jit(solution)/shard_map/ppermute | solution.py:513
  13.3 8.6 %copy-start = (bf16[512,1536]{1,0:T(8,128)(2,1)S(1)}, bf16[512,1536]{1,0:T(8,128)(2,1)}, u32[]{:S(2)}) copy-start(bf16[512,1536]{1,0:T(8,128)(2,1)} %qkv.3) | copy-start | bytes 4718596
  13.3 8.6 %copy-start.1 = (bf16[512,512]{1,0:T(8,128)(2,1)S(1)}, bf16[512,512]{1,0:T(8,128)(2,1)}, u32[]{:S(2)}) copy-start(bf16[512,512]{1,0:T(8,128)(2,1)} %out.4) | copy-start | bytes 1572868
  13.3 8.6 %copy-start.4 = (f32[512]{0:T(512)S(1)}, f32[512]{0:T(512)}, u32[]{:S(2)}) copy-start(f32[512]{0:T(512)} %gain.4) | copy-start | bytes 6148
  13.3 8.6 %copy-start.6 = (bf16[288,288]{1,0:T(8,128)(2,1)S(1)}, bf16[288,288]{1,0:T(8,128)(2,1)}, u32[]{:S(2)}) copy-start(bf16[288,288]{1,0:T(8,128)(2,1)} %constant.13.clone.sort_t) | copy-start | bytes 497668
  16.2 9.5 %collective-permute-start = (bf16[72,512]{1,0:T(8,128)(2,1)S(1)}, bf16[72,512]{1,0:T(8,128)(2,1)S(1)}, u32[]{:S(2)}, u32[]{:S(2)}) collective-permute-start(bf16[72,512]{1,0:T(8,128)(2,1)S(1)} %get-tuple-element.91), channel_id=1, source_target_pairs={{0,240},{16,0},{32,16},{48,32},{64,48},{80,64},{96,80},{112,96},{1... | collective-permute-start | bytes 221192 | tf_op jit(solution)/shard_map/ppermute | solution.py:503
  18.2 7.5 %collective-permute-start.1 = (bf16[72,512]{1,0:T(8,128)(2,1)S(1)}, bf16[72,512]{1,0:T(8,128)(2,1)S(1)}, u32[]{:S(2)}, u32[]{:S(2)}) collective-permute-start(bf16[72,512]{1,0:T(8,128)(2,1)S(1)} %get-tuple-element.92), channel_id=1, source_target_pairs={{0,15},{1,0},{2,1},{3,2},{4,3},{5,4},{6,5},{7,6},{8,7},{9,8},{10,9... | collective-permute-start | bytes 221192 | tf_op jit(solution)/shard_map/ppermute | solution.py:503
  20.6 5.1 %collective-permute-start.2 = (bf16[72,512]{1,0:T(8,128)(2,1)S(1)}, bf16[72,512]{1,0:T(8,128)(2,1)S(1)}, u32[]{:S(2)}, u32[]{:S(2)}) collective-permute-start(bf16[72,512]{1,0:T(8,128)(2,1)S(1)} %get-tuple-element.93), channel_id=1, source_target_pairs={{0,255},{1,240},{2,241},{3,242},{4,243},{5,244},{6,245},{7,246},{8... | collective-permute-start | bytes 221192 | tf_op jit(solution)/shard_map/ppermute | solution.py:513
  30.3 7.6 %collective-permute-start.6 = (bf16[72,512]{1,0:T(8,128)(2,1)S(1)}, bf16[72,512]{1,0:T(8,128)(2,1)S(1)}, u32[]{:S(2)}, u32[]{:S(2)}) collective-permute-start(bf16[72,512]{1,0:T(8,128)(2,1)S(1)} %get-tuple-element.104), channel_id=1, source_target_pairs={{0,17},{1,18},{2,19},{3,20},{4,21},{5,22},{6,23},{7,24},{8,25},{9,... | collective-permute-start | bytes 221192 | tf_op jit(solution)/shard_map/ppermute | solution.py:513
  30.9 7.0 %collective-permute-start.7 = (bf16[72,512]{1,0:T(8,128)(2,1)S(1)}, bf16[72,512]{1,0:T(8,128)(2,1)S(1)}, u32[]{:S(2)}, u32[]{:S(2)}) collective-permute-start(bf16[72,512]{1,0:T(8,128)(2,1)S(1)} %get-tuple-element.105), channel_id=1, source_target_pairs={{0,1},{1,2},{2,3},{3,4},{4,5},{5,6},{6,7},{7,8},{8,9},{9,10},{10,1... | collective-permute-start | bytes 221192 | tf_op jit(solution)/shard_map/ppermute | solution.py:503
  30.9 9.0 %collective-permute-start.8 = (bf16[72,512]{1,0:T(8,128)(2,1)S(1)}, bf16[72,512]{1,0:T(8,128)(2,1)S(1)}, u32[]{:S(2)}, u32[]{:S(2)}) collective-permute-start(bf16[72,512]{1,0:T(8,128)(2,1)S(1)} %get-tuple-element.106), channel_id=1, source_target_pairs={{0,16},{16,32},{32,48},{48,64},{64,80},{80,96},{96,112},{112,128},... | collective-permute-start | bytes 221192 | tf_op jit(solution)/shard_map/ppermute | solution.py:503
  31.9 8.0 %copy-start.2 = (bf16[512,512]{1,0:T(8,128)(2,1)S(1)}, bf16[512,512]{1,0:T(8,128)(2,1)}, u32[]{:S(2)}) copy-start(bf16[512,512]{1,0:T(8,128)(2,1)} %out.5) | copy-start | bytes 1572868
  33.2 11.0 %collective-permute-start.19 = (bf16[256,2048]{1,0:T(8,128)(2,1)S(1)}, bf16[256,2048]{1,0:T(8,128)(2,1)S(1)}, u32[]{:S(2)}, u32[]{:S(2)}) collective-permute-start(bf16[256,2048]{1,0:T(8,128)(2,1)S(1)} %get-tuple-element.146), channel_id=1, source_target_pairs={{0,1},{1,0},{2,3},{3,2},{4,5},{5,4},{6,7},{7,6},{8,9},{9,8},{10,11... | collective-permute-start | bytes 3145736 | tf_op jit(solution)/shard_map/ppermute | solution.py:503
  44.1 4.3 %collective-permute-start.9 = (bf16[256,2048]{1,0:T(8,128)(2,1)S(1)}, bf16[256,2048]{1,0:T(8,128)(2,1)S(1)}, u32[]{:S(2)}, u32[]{:S(2)}) collective-permute-start(bf16[256,2048]{1,0:T(8,128)(2,1)S(1)} %get-tuple-element.113), channel_id=1, source_target_pairs={{0,1},{1,0},{2,3},{3,2},{4,5},{5,4},{6,7},{7,6},{8,9},{9,8},{10,11... | collective-permute-start | bytes 3145736 | tf_op jit(solution)/shard_map/ppermute | solution.py:503
  44.4 8.8 %collective-permute-start.20 = (bf16[2,64,1024]{2,1,0:T(8,128)(2,1)S(1)}, bf16[2,64,1024]{2,1,0:T(8,128)(2,1)S(1)}, u32[]{:S(2)}, u32[]{:S(2)}) collective-permute-start(bf16[2,64,1024]{2,1,0:T(8,128)(2,1)S(1)} %get-tuple-element.148), channel_id=1, source_target_pairs={{0,2},{1,3},{2,0},{3,1},{4,6},{5,7},{6,4},{7,5},{8,10},{9,11},{10,... | collective-permute-start | bytes 786440 | tf_op jit(solution)/shard_map/ppermute | solution.py:503
  45.8 9.6 %collective-permute-start.21 = (bf16[2,64,1024]{2,1,0:T(8,128)(2,1)S(1)}, bf16[2,64,1024]{2,1,0:T(8,128)(2,1)S(1)}, u32[]{:S(2)}, u32[]{:S(2)}) collective-permute-start(bf16[2,64,1024]{2,1,0:T(8,128)(2,1)S(1)} %get-tuple-element.150), channel_id=1, source_target_pairs={{0,130},{1,131},{2,128},{3,129},{4,134},{5,135},{6,132},{7,133},{8... | collective-permute-start | bytes 786440 | tf_op jit(solution)/shard_map/ppermute | solution.py:531
  48.6 38.5 %copy-start.5 = (f32[512]{0:T(512)S(1)}, f32[512]{0:T(512)}, u32[]{:S(2)}) copy-start(f32[512]{0:T(512)} %gain.5) | copy-start | bytes 6148
  48.6 38.5 %copy-start.7 = (bf16[288,288]{1,0:T(8,128)(2,1)S(1)}, bf16[288,288]{1,0:T(8,128)(2,1)}, u32[]{:S(2)}) copy-start(bf16[288,288]{1,0:T(8,128)(2,1)} %constant.11.clone.place_t) | copy-start | bytes 497668
  48.6 14.6 %collective-permute-start.10 = (bf16[2,64,1024]{2,1,0:T(8,128)(2,1)S(1)}, bf16[2,64,1024]{2,1,0:T(8,128)(2,1)S(1)}, u32[]{:S(2)}, u32[]{:S(2)}) collective-permute-start(bf16[2,64,1024]{2,1,0:T(8,128)(2,1)S(1)} %get-tuple-element.120), channel_id=1, source_target_pairs={{0,4},{1,5},{2,6},{3,7},{4,0},{5,1},{6,2},{7,3},{8,12},{9,13},{10,... | collective-permute-start | bytes 786440 | tf_op jit(solution)/shard_map/ppermute | solution.py:503
  49.5 13.7 %collective-permute-start.11 = (bf16[2,64,1024]{2,1,0:T(8,128)(2,1)S(1)}, bf16[2,64,1024]{2,1,0:T(8,128)(2,1)S(1)}, u32[]{:S(2)}, u32[]{:S(2)}) collective-permute-start(bf16[2,64,1024]{2,1,0:T(8,128)(2,1)S(1)} %get-tuple-element.122), channel_id=1, source_target_pairs={{0,12},{1,13},{2,14},{3,15},{4,8},{5,9},{6,10},{7,11},{8,4},{9,5},... | collective-permute-start | bytes 786440 | tf_op jit(solution)/shard_map/ppermute | solution.py:503
  51.9 8.1 %collective-permute-start.12 = (bf16[72,512]{1,0:T(8,128)(2,1)S(1)}, bf16[72,512]{1,0:T(8,128)(2,1)S(1)}, u32[]{:S(2)}, u32[]{:S(2)}) collective-permute-start(bf16[72,512]{1,0:T(8,128)(2,1)S(1)} %get-tuple-element.123), channel_id=1, source_target_pairs={{0,16},{16,32},{32,48},{48,64},{64,80},{80,96},{96,112},{112,128},... | collective-permute-start | bytes 221192 | tf_op jit(solution)/shard_map/ppermute | solution.py:503
  53.2 7.2 %collective-permute-start.13 = (bf16[72,512]{1,0:T(8,128)(2,1)S(1)}, bf16[72,512]{1,0:T(8,128)(2,1)S(1)}, u32[]{:S(2)}, u32[]{:S(2)}) collective-permute-start(bf16[72,512]{1,0:T(8,128)(2,1)S(1)} %get-tuple-element.124), channel_id=1, source_target_pairs={{0,1},{1,2},{2,3},{3,4},{4,5},{5,6},{6,7},{7,8},{8,9},{9,10},{10,1... | collective-permute-start | bytes 221192 | tf_op jit(solution)/shard_map/ppermute | solution.py:503
  55.4 7.9 %collective-permute-start.14 = (bf16[72,512]{1,0:T(8,128)(2,1)S(1)}, bf16[72,512]{1,0:T(8,128)(2,1)S(1)}, u32[]{:S(2)}, u32[]{:S(2)}) collective-permute-start(bf16[72,512]{1,0:T(8,128)(2,1)S(1)} %get-tuple-element.125), channel_id=1, source_target_pairs={{0,17},{1,18},{2,19},{3,20},{4,21},{5,22},{6,23},{7,24},{8,25},{9,... | collective-permute-start | bytes 221192 | tf_op jit(solution)/shard_map/ppermute | solution.py:513
  60.0 6.2 %collective-permute-start.22 = (bf16[64,1024]{1,0:T(8,128)(2,1)S(1)}, bf16[64,1024]{1,0:T(8,128)(2,1)S(1)}, u32[]{:S(2)}, u32[]{:S(2)}) collective-permute-start(bf16[64,1024]{1,0:T(8,128)(2,1)S(1)} %get-tuple-element.152), channel_id=1, source_target_pairs={{0,130},{1,131},{2,128},{3,129},{4,134},{5,135},{6,132},{7,133},{8... | collective-permute-start | bytes 393224 | tf_op jit(solution)/shard_map/ppermute | solution.py:531
  60.3 5.8 %collective-permute-start.23 = (bf16[64,1024]{1,0:T(8,128)(2,1)S(1)}, bf16[64,1024]{1,0:T(8,128)(2,1)S(1)}, u32[]{:S(2)}, u32[]{:S(2)}) collective-permute-start(bf16[64,1024]{1,0:T(8,128)(2,1)S(1)} %get-tuple-element.154), channel_id=1, source_target_pairs={{0,2},{1,3},{2,0},{3,1},{4,6},{5,7},{6,4},{7,5},{8,10},{9,11},{10,... | collective-permute-start | bytes 393224 | tf_op jit(solution)/shard_map/ppermute | solution.py:503
  63.3 6.3 %collective-permute-start.15 = (bf16[64,1024]{1,0:T(8,128)(2,1)S(1)}, bf16[64,1024]{1,0:T(8,128)(2,1)S(1)}, u32[]{:S(2)}, u32[]{:S(2)}) collective-permute-start(bf16[64,1024]{1,0:T(8,128)(2,1)S(1)} %get-tuple-element.135), channel_id=1, source_target_pairs={{0,12},{1,13},{2,14},{3,15},{4,8},{5,9},{6,10},{7,11},{8,4},{9,5},... | collective-permute-start | bytes 393224 | tf_op jit(solution)/shard_map/ppermute | solution.py:503
  66.1 5.8 %collective-permute-start.16 = (bf16[64,1024]{1,0:T(8,128)(2,1)S(1)}, bf16[64,1024]{1,0:T(8,128)(2,1)S(1)}, u32[]{:S(2)}, u32[]{:S(2)}) collective-permute-start(bf16[64,1024]{1,0:T(8,128)(2,1)S(1)} %get-tuple-element.137), channel_id=1, source_target_pairs={{0,4},{1,5},{2,6},{3,7},{4,0},{5,1},{6,2},{7,3},{8,12},{9,13},{10,... | collective-permute-start | bytes 393224 | tf_op jit(solution)/shard_map/ppermute | solution.py:503
  66.3 7.0 %collective-permute-start.24 = (bf16[2,32,1024]{2,1,0:T(8,128)(2,1)S(1)}, bf16[2,32,1024]{2,1,0:T(8,128)(2,1)S(1)}, u32[]{:S(2)}, u32[]{:S(2)}) collective-permute-start(bf16[2,32,1024]{2,1,0:T(8,128)(2,1)S(1)} %get-tuple-element.156), channel_id=1, source_target_pairs={{0,4},{1,5},{2,6},{3,7},{4,0},{5,1},{6,2},{7,3},{8,12},{9,13},{10,... | collective-permute-start | bytes 393224 | tf_op jit(solution)/shard_map/ppermute | solution.py:503
  72.2 5.1 %collective-permute-start.17 = (bf16[2,32,1024]{2,1,0:T(8,128)(2,1)S(1)}, bf16[2,32,1024]{2,1,0:T(8,128)(2,1)S(1)}, u32[]{:S(2)}, u32[]{:S(2)}) collective-permute-start(bf16[2,32,1024]{2,1,0:T(8,128)(2,1)S(1)} %get-tuple-element.139), channel_id=1, source_target_pairs={{0,2},{1,3},{2,0},{3,1},{4,6},{5,7},{6,4},{7,5},{8,10},{9,11},{10,... | collective-permute-start | bytes 393224 | tf_op jit(solution)/shard_map/ppermute | solution.py:503
  73.3 7.4 %collective-permute-start.25 = (bf16[1,32,1024]{2,1,0:T(8,128)(2,1)S(1)}, bf16[1,32,1024]{2,1,0:T(8,128)(2,1)S(1)}, u32[]{:S(2)}, u32[]{:S(2)}) collective-permute-start(bf16[1,32,1024]{2,1,0:T(8,128)(2,1)S(1)} %get-tuple-element.158), channel_id=1, source_target_pairs={{0,12},{1,13},{2,14},{3,15},{4,8},{5,9},{6,10},{7,11},{8,4},{9,5},... | collective-permute-start | bytes 196616 | tf_op jit(solution)/shard_map/ppermute | solution.py:503
  77.2 5.7 %collective-permute-start.18 = (bf16[1,32,1024]{2,1,0:T(8,128)(2,1)S(1)}, bf16[1,32,1024]{2,1,0:T(8,128)(2,1)S(1)}, u32[]{:S(2)}, u32[]{:S(2)}) collective-permute-start(bf16[1,32,1024]{2,1,0:T(8,128)(2,1)S(1)} %get-tuple-element.141), channel_id=1, source_target_pairs={{0,130},{1,131},{2,128},{3,129},{4,134},{5,135},{6,132},{7,133},{8... | collective-permute-start | bytes 196616 | tf_op jit(solution)/shard_map/ppermute | solution.py:531
  83.7 12.4 %all-to-all-start = ((bf16[8,64,128]{2,1,0:T(8,128)(2,1)}), bf16[8,64,128]{2,1,0:T(8,128)(2,1)S(1)}, u32[]{:S(2)}, u32[]{:S(2)}) async-start(bf16[8,64,128]{2,1,0:T(8,128)(2,1)} %shard_map.214), calls=%async_computation | async-start | bytes 262144 | tf_op jit(solution)/shard_map/all_to_all | solution.py:549

commit v9 on v6

--- a/solution.py
+++ b/solution.py
@@ -18,7 +18,6 @@
 GROUPS = WIDTH // GROUP
 PER_GROUP = GROUP // HEAD
 ROOT = HEAD**0.5
-Z_GROUPS = ((0, 3, 4, 7), (1, 2, 5, 6))
 SIDE = 2 * WIDTH
 EPS = 1e-05
 NEG = -1000000000.0
@@ -459,26 +458,18 @@
     send[...] = keep[half:] + got[half:]
 
 
-def kernel_columns(keep_a, got_a, keep_b, got_b, send, keep, blocks):
+def kernel_columns(keep_a, got_a, keep_b, got_b, blocks):
     for rows, held, got in ((slice(0, 32), keep_a, got_a), (slice(32, 64), keep_b, got_b)):
         total = held[0].astype(F32) + got[0].astype(F32)
         for block in range(8):
             qkv = total[:, block * 96 : (block + 1) * 96]
             out = total[:, 768 + block * 32 : 768 + (block + 1) * 32]
             blocks[block, rows] = jnp.concatenate([qkv, out], axis=1).astype(BF16)
-    group = (lax.axis_index("lon") % 8 + 1) // 2 % 2
-    for at, (outer, inner) in enumerate(zip(*Z_GROUPS, strict=True)):
-        keep[at] = blocks[outer + group * (inner - outer)]
-        send[at] = blocks[inner + group * (outer - inner)]
-
-
-def kernel_sum(keep, got, total):
-    total[...] = keep[...] + got[...]
 
 
 def kernel_total(parts, qkv_a, out_a, qkv_b, out_b):
     total = parts[0].astype(F32)
-    for at in range(1, 4):
+    for at in range(1, 8):
         total = total + parts[at].astype(F32)
     for rows, qkv, out in ((slice(0, 32), qkv_a, out_a), (slice(32, 64), qkv_b, out_b)):
         qkv[...] = total[rows, :96]
@@ -557,12 +548,8 @@
     return call(kernel_halve, [(shape, BF16)] * 2, [], (keep, got))
 
 
-def to_z(array):
-    return permute(array, "lon", lambda i: i ^ 1)
-
-
 def exchange_z(messages):
-    groups = [[x_hi * 8 + z for z in group] for x_hi in range(2) for group in Z_GROUPS]
+    groups = [[x_hi * 8 + z for z in range(8)] for x_hi in range(2)]
     return lax.all_to_all(messages, "lon", 0, 0, axis_index_groups=groups, tiled=True)
 
 
@@ -698,11 +685,10 @@
         flops=2 * 10**9, final=(0,),
     )[0]
     got_a, got_b, advanced = lax.optimization_barrier((got_a, got_b, advanced))
-    four = ((4, 64, GROUP), BF16)
-    send, keep = call(
-        kernel_columns, [four] * 2, [((8, 64, GROUP), BF16)], (keep_a, got_a, keep_b, got_b)
-    )
-    parts = exchange_z(call(kernel_sum, [four], [], (keep, to_z(send)))[0])
+    blocks = call(
+        kernel_columns, [((8, 64, GROUP), BF16)], [], (keep_a, got_a, keep_b, got_b)
+    )[0]
+    parts = exchange_z(blocks)
     grads = call(
         kernel_total,
         [((32, 96), F32), ((32, 32), F32)] * 2,

time: 95.5 us -> 92.2 us (0.965)
  waiting for transfers between devices: 23.4 us -> 19.2 us
  blocking collectives: 10.4 us -> 11.5 us
    ppermute x18 -> x17, waiting for transfers between devices: 11.8 us -> 7.5 us  [permute(): lax.ppermute(array, axis, [(i, target(i) % length) for i in range(length)])]
    all_to_all x1, blocking collectives: 10.4 us -> 11.5 us  [exchange_z(): lax.all_to_all(messages, 'lon', 0, 0, axis_index_groups=groups, tiled=True)]
    ppermute x18 -> x17, starting transfers between devices: 25.8 us -> 25.7 us  [permute(): lax.ppermute(array, axis, [(i, target(i) % length) for i in range(length)])]
    pallas_call x20 -> x19, Pallas kernels: 28.6 us -> 28.6 us  [call(): pl.pallas_call(kernel, out_shape=tuple((jax.ShapeDtypeStruct(shape, kind)...]
  transfers between devices with their start and end apart: 24 -> 23, of which waited for: 11 -> 10; matrix products, arithmetic and copies ran while one was open for 0% -> 0% of each run, Pallas kernels for 19% -> 19%
where the time goes in v9:
time: 92.2 us; the launch traced here: 92.1 us
  starting transfers between devices  31.8 us (34%)
  Pallas kernels  28.6 us (31%)
  waiting for transfers between devices  19.2 us (21%)
  blocking collectives  11.5 us (12%)
  between operations  0.93 us (1%)
    pallas_call x19, Pallas kernels, call(): pl.pallas_call(kernel, out_shape=tuple((jax.ShapeDtypeStruct(shape, kind)...  28.6 us
    ppermute x17, starting transfers between devices, permute(): lax.ppermute(array, axis, [(i, target(i) % length) for i in range(length)])  25.7 us
    all_to_all x1, blocking collectives, exchange_z(): lax.all_to_all(messages, 'lon', 0, 0, axis_index_groups=groups, tiled=True)  11.5 us
    ppermute x17, waiting for transfers between devices, permute(): lax.ppermute(array, axis, [(i, target(i) % length) for i in range(length)])  7.5 us
    ppermute x3, waiting for transfers between devices, permute_both(): return lax.ppermute(array, ('lon', 'lat'), pairs)  6.35 us
    ppermute x3, waiting for transfers between devices, to_x(): return lax.ppermute(array, ('lon', 'lat'), pairs)  5.34 us
    ppermute x3, starting transfers between devices, to_x(): return lax.ppermute(array, ('lon', 'lat'), pairs)  4.14 us
    ppermute x3, starting transfers between devices, permute_both(): return lax.ppermute(array, ('lon', 'lat'), pairs)  2 us
  transfers between devices with their start and end apart: 23, of which 10 were waited for; matrix products, arithmetic and copies ran while one was open for 0% of the time, Pallas kernels for 19%

profile of v9, /device:TPU:6, one launch (start us, length us, event | category | flops | bytes accessed | tf_op | source)
XLA Modules:
  0.0 92.1 jit_solution(958907735820285490)
XLA Ops:
  0.6 0.0 copy-start.8
  0.7 0.0 copy-start.9
  0.7 0.0 copy-start.10
  0.7 5.5 %shard_map.199 = (bf16[72,512]{1,0:T(8,128)(2,1)S(1)}, bf16[72,512]{1,0:T(8,128)(2,1)S(1)}, bf16[72,512]{1,0:T(8,128)(2,1)S(1)}, bf16[72,512]{1,0:T(8,128)(2,1)S...) custom-call(bf16[12,6,4,512]{3,2,1,0:T(4,128)(2,1)} %bitcast.6, ...), custom_call_target="tpu_custom_call" | custom-call | flops 7000000000 | bytes 1048576 | tf_op jit(solution)/shard_map/pallas_call | solution.py:491
  6.2 6.8 %collective-permute-start.3 = (bf16[72,512]{1,0:T(8,128)(2,1)S(1)}, bf16[72,512]{1,0:T(8,128)(2,1)S(1)}, u32[]{:S(2)}, u32[]{:S(2)}) collective-permute-start(bf16[72,512]{1,0:T(8,128)(2,1)S(1)} %get-tuple-element.91), channel_id=1, source_target_pairs={{0,240},{16,0},{32,16},{48,32},{64,48},{80,64},{96,80},{112,96},{1... | collective-permute-start | bytes 221192 | tf_op jit(solution)/shard_map/ppermute | solution.py:507
  13.0 0.0 collective-permute-start.4
  13.0 0.2 collective-permute-start.5
  13.2 0.0 copy-start
  13.2 0.0 copy-start.1
  13.2 0.0 copy-start.4
  13.2 0.0 copy-start.6
  13.2 2.9 %shard_map.200 = (bf16[72,512]{1,0:T(8,128)(2,1)S(1)}, bf16[72,512]{1,0:T(8,128)(2,1)S(1)}, bf16[72,512]{1,0:T(8,128)(2,1)S(1)}, bf16[72,512]{1,0:T(8,128)(2,1)S...) custom-call(bf16[12,6,4,512]{3,2,1,0:T(4,128)(2,1)} %bitcast.7, ...), custom_call_target="tpu_custom_call" | custom-call | flops 2000000000 | bytes 1048576 | tf_op jit(solution)/shard_map/pallas_call | solution.py:491
  16.2 2.0 %collective-permute-start = (bf16[72,512]{1,0:T(8,128)(2,1)S(1)}, bf16[72,512]{1,0:T(8,128)(2,1)S(1)}, u32[]{:S(2)}, u32[]{:S(2)}) collective-permute-start(bf16[72,512]{1,0:T(8,128)(2,1)S(1)} %get-tuple-element.87), channel_id=1, source_target_pairs={{0,240},{16,0},{32,16},{48,32},{64,48},{80,64},{96,80},{112,96},{1... | collective-permute-start | bytes 221192 | tf_op jit(solution)/shard_map/ppermute | solution.py:507
  18.2 2.4 %collective-permute-start.1 = (bf16[72,512]{1,0:T(8,128)(2,1)S(1)}, bf16[72,512]{1,0:T(8,128)(2,1)S(1)}, u32[]{:S(2)}, u32[]{:S(2)}) collective-permute-start(bf16[72,512]{1,0:T(8,128)(2,1)S(1)} %get-tuple-element.88), channel_id=1, source_target_pairs={{0,15},{1,0},{2,1},{3,2},{4,3},{5,4},{6,5},{7,6},{8,7},{9,8},{10,9... | collective-permute-start | bytes 221192 | tf_op jit(solution)/shard_map/ppermute | solution.py:507
  20.5 1.2 %collective-permute-start.2 = (bf16[72,512]{1,0:T(8,128)(2,1)S(1)}, bf16[72,512]{1,0:T(8,128)(2,1)S(1)}, u32[]{:S(2)}, u32[]{:S(2)}) collective-permute-start(bf16[72,512]{1,0:T(8,128)(2,1)S(1)} %get-tuple-element.89), channel_id=1, source_target_pairs={{0,255},{1,240},{2,241},{3,242},{4,243},{5,244},{6,245},{7,246},{8... | collective-permute-start | bytes 221192 | tf_op jit(solution)/shard_map/ppermute | solution.py:517
  21.8 3.8 %shard_map.201 = (bf16[72,512]{1,0:T(8,128)(2,1)S(1)}, bf16[72,512]{1,0:T(8,128)(2,1)S(1)}, bf16[72,512]{1,0:T(8,128)(2,1)S(1)}, bf16[72,512]{1,0:T(8,128)(2,1)S...) custom-call(bf16[72,512]{1,0:T(8,128)(2,1)S(1)} %get-tuple-element.9, ...), custom_call_target="tpu_custom_call" | custom-call | flops 5000000000 | bytes 1048576 | tf_op jit(solution)/shard_map/pallas_call | solution.py:491
  25.6 0.0 collective-permute-done.piece1
  25.6 4.4 %shard_map.202 = (bf16[2,72,512]{2,1,0:T(8,128)(2,1)S(1)}, bf16[2,72,512]{2,1,0:T(8,128)(2,1)S(1)}, bf16[2,72,512]{2,1,0:T(8,128)(2,1)S(1)}, bf16[2,72,512]{2,1,...) custom-call(bf16[72,512]{1,0:T(8,128)(2,1)S(1)} %get-tuple-element.86.piece0, ...), custom_call_target="tpu_custom_call" | custom-call | flops 5000000000 | bytes 1048576 | tf_op jit(solution)/shard_map/pallas_call | solution.py:491
  30.0 0.6 collective-permute-start.6
  30.6 0.1 collective-permute-start.7
  30.7 1.0 %collective-permute-start.8 = (bf16[2,72,512]{2,1,0:T(8,128)(2,1)S(1)}, bf16[2,72,512]{2,1,0:T(8,128)(2,1)S(1)}, u32[]{:S(2)}, u32[]{:S(2)}) collective-permute-start(bf16[2,72,512]{2,1,0:T(8,128)(2,1)S(1)} %get-tuple-element.106), channel_id=1, source_target_pairs={{0,16},{16,32},{32,48},{48,64},{64,80},{80,96},{96,112},{112,128},... | collective-permute-start | bytes 442376 | tf_op jit(solution)/shard_map/ppermute | solution.py:507
  31.6 1.3 %shard_map.210 = (bf16[256,2048]{1,0:T(8,128)(2,1)S(1)}, bf16[256,2048]{1,0:T(8,128)(2,1)S(1)}) custom-call(bf16[288,512]{1,0:T(8,128)(2,1)S(1)} %get-tuple-element.133.normed, bf16[2,512,144]{2,1,0:T(8,128)(2,1)S(1)} %get-tuple-element.103.mixed_t, bf16[288,512]{1,0:T(8,128)(2,1)S(1)} %get-tuple-element.134.upstream, ...), custom_call_target="tpu_custom_call" | custom-call | flops 2000000000 | bytes 1048576 | tf_op jit(solution)/shard_map/pallas_call | solution.py:491
  33.0 0.4 collective-permute-start.16
  33.3 6.3 %collective-permute-done.6.back0 = bf16[2,72,512]{2,1,0:T(8,128)(2,1)S(1)} collective-permute-done((bf16[2,72,512]{2,1,0:T(8,128)(2,1)S(1)}, bf16[2,72,512]{2,1,0:T(8,128)(2,1)S(1)}, u32[]{:S(2)}, u32[]{:S(2)}) %collective-permute-start.6) | collective-permute-done | bytes 147488 | tf_op jit(solution)/shard_map/ppermute | solution.py:517
  39.7 0.0 collective-permute-done.7.back1
  39.7 3.1 %collective-permute-done.8.back2 = bf16[2,72,512]{2,1,0:T(8,128)(2,1)S(1)} collective-permute-done((bf16[2,72,512]{2,1,0:T(8,128)(2,1)S(1)}, bf16[2,72,512]{2,1,0:T(8,128)(2,1)S(1)}, u32[]{:S(2)}, u32[]{:S(2)}) %collective-permute-start.8) | collective-permute-done | bytes 147488 | tf_op jit(solution)/shard_map/ppermute | solution.py:507
  42.8 4.1 %shard_map.203 = (bf16[288,512]{1,0:T(8,128)(2,1)S(1)}, bf16[288,1536]{1,0:T(8,128)(2,1)S(1)}, bf16[256,2048]{1,0:T(8,128)(2,1)S(1)}) custom-call(bf16[2,72,512]{2,1,0:T(8,128)(2,1)S(1)} %collective-permute-done.6.back0, bf16[2,72,512]{2,1,0:T(8,128)(2,1)S(1)} %collective-permute-done.7.back1, bf16[2,72,512]{2,1,0:T(8,128)(2,1)S(1)} %collective-permute-done.8.back2, ...), custom_call_target="tpu_custom_call" | custom-call | flops 5000000000 | bytes 1048576 | tf_op jit(solution)/shard_map/pallas_call | solution.py:491
  46.8 0.1 collective-permute-start.9
  46.9 0.7 shard_map.204.keep
  47.6 0.0 copy-start.5
  47.6 0.0 copy-start.7
  47.7 0.0 collective-permute-done.16.got
  47.7 0.1 shard_map.211
  47.8 0.9 collective-permute-start.17
  48.7 1.2 %collective-permute-start.18 = (bf16[2,64,1024]{2,1,0:T(8,128)(2,1)S(1)}, bf16[2,64,1024]{2,1,0:T(8,128)(2,1)S(1)}, u32[]{:S(2)}, u32[]{:S(2)}) collective-permute-start(bf16[2,64,1024]{2,1,0:T(8,128)(2,1)S(1)} %get-tuple-element.141), channel_id=1, source_target_pairs={{0,130},{1,131},{2,128},{3,129},{4,134},{5,135},{6,132},{7,133},{8... | collective-permute-start | bytes 786440 | tf_op jit(solution)/shard_map/ppermute | solution.py:535
  49.9 0.0 collective-permute-done.9.got
  49.9 0.1 shard_map.205
  50.0 1.0 %collective-permute-start.10 = (bf16[2,64,1024]{2,1,0:T(8,128)(2,1)S(1)}, bf16[2,64,1024]{2,1,0:T(8,128)(2,1)S(1)}, u32[]{:S(2)}, u32[]{:S(2)}) collective-permute-start(bf16[2,64,1024]{2,1,0:T(8,128)(2,1)S(1)} %get-tuple-element.117), channel_id=1, source_target_pairs={{0,4},{1,5},{2,6},{3,7},{4,0},{5,1},{6,2},{7,3},{8,12},{9,13},{10,... | collective-permute-start | bytes 786440 | tf_op jit(solution)/shard_map/ppermute | solution.py:507
  51.1 2.7 %collective-permute-start.11 = (bf16[2,64,1024]{2,1,0:T(8,128)(2,1)S(1)}, bf16[2,64,1024]{2,1,0:T(8,128)(2,1)S(1)}, u32[]{:S(2)}, u32[]{:S(2)}) collective-permute-start(bf16[2,64,1024]{2,1,0:T(8,128)(2,1)S(1)} %get-tuple-element.119), channel_id=1, source_target_pairs={{0,12},{1,13},{2,14},{3,15},{4,8},{5,9},{6,10},{7,11},{8,4},{9,5},... | collective-permute-start | bytes 786440 | tf_op jit(solution)/shard_map/ppermute | solution.py:507
  53.8 3.2 %shard_map.207 = bf16[12,6,4,512]{3,2,1,0:T(4,128)(2,1)} custom-call(bf16[288,512]{1,0:T(8,128)(2,1)S(1)} %get-tuple-element.123.inputs, bf16[288,512]{1,0:T(8,128)(2,1)S(1)} %get-tuple-element.111.grad_middle, f32[512]{0:T(512)S(1)} %copy-done.5, bf16[512,1536]{1,0:T(8,128)(2,1)} %qkv_hbm.3, bf16[288,1536]{1,0:T(8,128)(2,1)S(1)} %get-tuple-element.124.d_packed, ...), custom_call_target="tpu_custom_call" | custom-call | flops 4000000000 | bytes 1048576 | tf_op jit(solution)/shard_map/pallas_call | solution.py:491
  57.0 0.0 collective-permute-done.17.got_one
  57.0 1.3 %collective-permute-done.18.got_two = bf16[2,64,1024]{2,1,0:T(8,128)(2,1)S(1)} collective-permute-done((bf16[2,64,1024]{2,1,0:T(8,128)(2,1)S(1)}, bf16[2,64,1024]{2,1,0:T(8,128)(2,1)S(1)}, u32[]{:S(2)}, u32[]{:S(2)}) %collective-permute-start.18) | collective-permute-done | bytes 262176 | tf_op jit(solution)/shard_map/ppermute | solution.py:535
  58.4 0.1 shard_map.212
  58.4 1.4 %collective-permute-start.19 = (bf16[64,1024]{1,0:T(8,128)(2,1)S(1)}, bf16[64,1024]{1,0:T(8,128)(2,1)S(1)}, u32[]{:S(2)}, u32[]{:S(2)}) collective-permute-start(bf16[64,1024]{1,0:T(8,128)(2,1)S(1)} %get-tuple-element.143), channel_id=1, source_target_pairs={{0,130},{1,131},{2,128},{3,129},{4,134},{5,135},{6,132},{7,133},{8... | collective-permute-start | bytes 393224 | tf_op jit(solution)/shard_map/ppermute | solution.py:535
  59.8 0.0 collective-permute-done.10.got_one
  59.8 0.3 collective-permute-done.11.got_two
  60.2 0.1 shard_map.206
  60.2 3.2 %collective-permute-start.12 = (bf16[64,1024]{1,0:T(8,128)(2,1)S(1)}, bf16[64,1024]{1,0:T(8,128)(2,1)S(1)}, u32[]{:S(2)}, u32[]{:S(2)}) collective-permute-start(bf16[64,1024]{1,0:T(8,128)(2,1)S(1)} %get-tuple-element.125), channel_id=1, source_target_pairs={{0,12},{1,13},{2,14},{3,15},{4,8},{5,9},{6,10},{7,11},{8,4},{9,5},... | collective-permute-start | bytes 393224 | tf_op jit(solution)/shard_map/ppermute | solution.py:507
  63.4 1.3 %collective-permute-done.19.got_one = bf16[64,1024]{1,0:T(8,128)(2,1)S(1)} collective-permute-done((bf16[64,1024]{1,0:T(8,128)(2,1)S(1)}, bf16[64,1024]{1,0:T(8,128)(2,1)S(1)}, u32[]{:S(2)}, u32[]{:S(2)}) %collective-permute-start.19) | collective-permute-done | bytes 131104 | tf_op jit(solution)/shard_map/ppermute | solution.py:535
  64.7 0.1 collective-permute-done.20.got_two
  64.8 0.1 shard_map.213
  64.9 0.9 %collective-permute-start.21 = (bf16[2,32,1024]{2,1,0:T(8,128)(2,1)S(1)}, bf16[2,32,1024]{2,1,0:T(8,128)(2,1)S(1)}, u32[]{:S(2)}, u32[]{:S(2)}) collective-permute-start(bf16[2,32,1024]{2,1,0:T(8,128)(2,1)S(1)} %get-tuple-element.147), channel_id=1, source_target_pairs={{0,4},{1,5},{2,6},{3,7},{4,0},{5,1},{6,2},{7,3},{8,12},{9,13},{10,... | collective-permute-start | bytes 393224 | tf_op jit(solution)/shard_map/ppermute | solution.py:507
  65.8 0.7 collective-permute-done.12.got_one
  66.5 2.5 %collective-permute-done.13.got_two = bf16[64,1024]{1,0:T(8,128)(2,1)S(1)} collective-permute-done((bf16[64,1024]{1,0:T(8,128)(2,1)S(1)}, bf16[64,1024]{1,0:T(8,128)(2,1)S(1)}, u32[]{:S(2)}, u32[]{:S(2)}) %collective-permute-start.13) | collective-permute-done | bytes 131104 | tf_op jit(solution)/shard_map/ppermute | solution.py:507
  69.0 0.1 shard_map.208
  69.1 1.8 %collective-permute-start.14 = (bf16[2,32,1024]{2,1,0:T(8,128)(2,1)S(1)}, bf16[2,32,1024]{2,1,0:T(8,128)(2,1)S(1)}, u32[]{:S(2)}, u32[]{:S(2)}) collective-permute-start(bf16[2,32,1024]{2,1,0:T(8,128)(2,1)S(1)} %get-tuple-element.129), channel_id=1, source_target_pairs={{0,2},{1,3},{2,0},{3,1},{4,6},{5,7},{6,4},{7,5},{8,10},{9,11},{10,... | collective-permute-start | bytes 393224 | tf_op jit(solution)/shard_map/ppermute | solution.py:507
  71.0 2.5 %collective-permute-start.22 = (bf16[1,32,1024]{2,1,0:T(8,128)(2,1)S(1)}, bf16[1,32,1024]{2,1,0:T(8,128)(2,1)S(1)}, u32[]{:S(2)}, u32[]{:S(2)}) collective-permute-start(bf16[1,32,1024]{2,1,0:T(8,128)(2,1)S(1)} %get-tuple-element.148), channel_id=1, source_target_pairs={{0,12},{1,13},{2,14},{3,15},{4,8},{5,9},{6,10},{7,11},{8,4},{9,5},... | collective-permute-start | bytes 196616 | tf_op jit(solution)/shard_map/ppermute | solution.py:507
  73.4 0.7 collective-permute-done.14.got
  74.2 1.5 %collective-permute-start.15 = (bf16[1,32,1024]{2,1,0:T(8,128)(2,1)S(1)}, bf16[1,32,1024]{2,1,0:T(8,128)(2,1)S(1)}, u32[]{:S(2)}, u32[]{:S(2)}) collective-permute-start(bf16[1,32,1024]{2,1,0:T(8,128)(2,1)S(1)} %get-tuple-element.132), channel_id=1, source_target_pairs={{0,130},{1,131},{2,128},{3,129},{4,134},{5,135},{6,132},{7,133},{8... | collective-permute-start | bytes 196616 | tf_op jit(solution)/shard_map/ppermute | solution.py:535
  75.7 1.3 %shard_map.215 = bf16[12,6,4,512]{3,2,1,0:T(4,128)(2,1)} custom-call(bf16[2,72,512]{2,1,0:T(8,128)(2,1)S(1)} %collective-permute-done.6.back0, bf16[2,72,512]{2,1,0:T(8,128)(2,1)S(1)} %collective-permute-done.7.back1, bf16[2,72,512]{2,1,0:T(8,128)(2,1)S(1)} %collective-permute-done.8.back2, bf16[2,72,512]{2,1,0:T(8,128)(2,1)S(1)} %get-tuple-element.107.back3, ...), custom_call_target="tpu_custom_call" | custom-call | flops 2000000000 | bytes 1048576 | tf_op jit(solution)/shard_map/pallas_call | solution.py:491
  77.0 2.7 %collective-permute-done.15.got_a = bf16[1,32,1024]{2,1,0:T(8,128)(2,1)S(1)} collective-permute-done((bf16[1,32,1024]{2,1,0:T(8,128)(2,1)S(1)}, bf16[1,32,1024]{2,1,0:T(8,128)(2,1)S(1)}, u32[]{:S(2)}, u32[]{:S(2)}) %collective-permute-start.15) | collective-permute-done | bytes 65568 | tf_op jit(solution)/shard_map/ppermute | solution.py:535
  79.7 0.1 shard_map.216
  79.9 11.5 %all_to_all.5.parts = bf16[8,64,128]{2,1,0:T(8,128)(2,1)S(1)} all-to-all(bf16[8,64,128]{2,1,0:T(8,128)(2,1)S(1)} %shard_map.216), channel_id=1, replica_groups={{0,16,32,48,64,80,96,112},{128,144,160,176,192,208,224,240},{1,17,33,49..., dimensions={0} | all-to-all | bytes 262144 | tf_op jit(solution)/shard_map/all_to_all | solution.py:553
  91.4 0.7 shard_map.217
  (24 shorter events, 0.1 us)
Async XLA Ops:
  0.6 12.5 %copy-start.3 = (s32[192,96]{1,0:T(8,128)S(1)}, s32[192,96]{1,0:T(8,128)}, u32[]{:S(2)}) copy-start(s32[192,96]{1,0:T(8,128)} %ids.1) | copy-start | bytes 221188
  0.6 12.5 %copy-start.8 = (bf16[288,288]{1,0:T(8,128)(2,1)S(1)}, bf16[288,288]{1,0:T(8,128)(2,1)}, u32[]{:S(2)}) copy-start(bf16[288,288]{1,0:T(8,128)(2,1)} %constant.12.clone.sort_hbm.sort) | copy-start | bytes 497668
  0.7 12.5 %copy-start.9 = (bf16[288,288]{1,0:T(8,128)(2,1)S(1)}, bf16[288,288]{1,0:T(8,128)(2,1)}, u32[]{:S(2)}) copy-start(bf16[288,288]{1,0:T(8,128)(2,1)} %constant.10.clone.place_hbm.place) | copy-start | bytes 497668
  0.7 12.5 %copy-start.10 = (s32[144,8]{1,0:T(8,128)S(1)}, s32[144,8]{1,0:T(8,128)}, u32[]{:S(2)}) copy-start(s32[144,8]{1,0:T(8,128)} %constant.14.clone.where_hbm.where) | copy-start | bytes 13828
  6.2 14.3 %collective-permute-start.3 = (bf16[72,512]{1,0:T(8,128)(2,1)S(1)}, bf16[72,512]{1,0:T(8,128)(2,1)S(1)}, u32[]{:S(2)}, u32[]{:S(2)}) collective-permute-start(bf16[72,512]{1,0:T(8,128)(2,1)S(1)} %get-tuple-element.91), channel_id=1, source_target_pairs={{0,240},{16,0},{32,16},{48,32},{64,48},{80,64},{96,80},{112,96},{1... | collective-permute-start | bytes 221192 | tf_op jit(solution)/shard_map/ppermute | solution.py:507
  13.0 8.8 %collective-permute-start.4 = (bf16[72,512]{1,0:T(8,128)(2,1)S(1)}, bf16[72,512]{1,0:T(8,128)(2,1)S(1)}, u32[]{:S(2)}, u32[]{:S(2)}) collective-permute-start(bf16[72,512]{1,0:T(8,128)(2,1)S(1)} %get-tuple-element.92), channel_id=1, source_target_pairs={{0,15},{1,0},{2,1},{3,2},{4,3},{5,4},{6,5},{7,6},{8,7},{9,8},{10,9... | collective-permute-start | bytes 221192 | tf_op jit(solution)/shard_map/ppermute | solution.py:507
  13.0 8.8 %collective-permute-start.5 = (bf16[72,512]{1,0:T(8,128)(2,1)S(1)}, bf16[72,512]{1,0:T(8,128)(2,1)S(1)}, u32[]{:S(2)}, u32[]{:S(2)}) collective-permute-start(bf16[72,512]{1,0:T(8,128)(2,1)S(1)} %get-tuple-element.93), channel_id=1, source_target_pairs={{0,255},{1,240},{2,241},{3,242},{4,243},{5,244},{6,245},{7,246},{8... | collective-permute-start | bytes 221192 | tf_op jit(solution)/shard_map/ppermute | solution.py:517
  13.2 8.6 %copy-start = (bf16[512,1536]{1,0:T(8,128)(2,1)S(1)}, bf16[512,1536]{1,0:T(8,128)(2,1)}, u32[]{:S(2)}) copy-start(bf16[512,1536]{1,0:T(8,128)(2,1)} %qkv.3) | copy-start | bytes 4718596
  13.2 8.6 %copy-start.1 = (bf16[512,512]{1,0:T(8,128)(2,1)S(1)}, bf16[512,512]{1,0:T(8,128)(2,1)}, u32[]{:S(2)}) copy-start(bf16[512,512]{1,0:T(8,128)(2,1)} %out.4) | copy-start | bytes 1572868
  13.2 8.6 %copy-start.4 = (f32[512]{0:T(512)S(1)}, f32[512]{0:T(512)}, u32[]{:S(2)}) copy-start(f32[512]{0:T(512)} %gain.4) | copy-start | bytes 6148
  13.2 8.6 %copy-start.6 = (bf16[288,288]{1,0:T(8,128)(2,1)S(1)}, bf16[288,288]{1,0:T(8,128)(2,1)}, u32[]{:S(2)}) copy-start(bf16[288,288]{1,0:T(8,128)(2,1)} %constant.13.clone.sort_t) | copy-start | bytes 497668
  16.2 9.4 %collective-permute-start = (bf16[72,512]{1,0:T(8,128)(2,1)S(1)}, bf16[72,512]{1,0:T(8,128)(2,1)S(1)}, u32[]{:S(2)}, u32[]{:S(2)}) collective-permute-start(bf16[72,512]{1,0:T(8,128)(2,1)S(1)} %get-tuple-element.87), channel_id=1, source_target_pairs={{0,240},{16,0},{32,16},{48,32},{64,48},{80,64},{96,80},{112,96},{1... | collective-permute-start | bytes 221192 | tf_op jit(solution)/shard_map/ppermute | solution.py:507
  18.2 7.4 %collective-permute-start.1 = (bf16[72,512]{1,0:T(8,128)(2,1)S(1)}, bf16[72,512]{1,0:T(8,128)(2,1)S(1)}, u32[]{:S(2)}, u32[]{:S(2)}) collective-permute-start(bf16[72,512]{1,0:T(8,128)(2,1)S(1)} %get-tuple-element.88), channel_id=1, source_target_pairs={{0,15},{1,0},{2,1},{3,2},{4,3},{5,4},{6,5},{7,6},{8,7},{9,8},{10,9... | collective-permute-start | bytes 221192 | tf_op jit(solution)/shard_map/ppermute | solution.py:507
  20.5 5.1 %collective-permute-start.2 = (bf16[72,512]{1,0:T(8,128)(2,1)S(1)}, bf16[72,512]{1,0:T(8,128)(2,1)S(1)}, u32[]{:S(2)}, u32[]{:S(2)}) collective-permute-start(bf16[72,512]{1,0:T(8,128)(2,1)S(1)} %get-tuple-element.89), channel_id=1, source_target_pairs={{0,255},{1,240},{2,241},{3,242},{4,243},{5,244},{6,245},{7,246},{8... | collective-permute-start | bytes 221192 | tf_op jit(solution)/shard_map/ppermute | solution.py:517
  30.0 9.7 %collective-permute-start.6 = (bf16[2,72,512]{2,1,0:T(8,128)(2,1)S(1)}, bf16[2,72,512]{2,1,0:T(8,128)(2,1)S(1)}, u32[]{:S(2)}, u32[]{:S(2)}) collective-permute-start(bf16[2,72,512]{2,1,0:T(8,128)(2,1)S(1)} %get-tuple-element.104), channel_id=1, source_target_pairs={{0,17},{1,18},{2,19},{3,20},{4,21},{5,22},{6,23},{7,24},{8,25},{9,... | collective-permute-start | bytes 442376 | tf_op jit(solution)/shard_map/ppermute | solution.py:517
  30.6 9.1 %collective-permute-start.7 = (bf16[2,72,512]{2,1,0:T(8,128)(2,1)S(1)}, bf16[2,72,512]{2,1,0:T(8,128)(2,1)S(1)}, u32[]{:S(2)}, u32[]{:S(2)}) collective-permute-start(bf16[2,72,512]{2,1,0:T(8,128)(2,1)S(1)} %get-tuple-element.105), channel_id=1, source_target_pairs={{0,1},{1,2},{2,3},{3,4},{4,5},{5,6},{6,7},{7,8},{8,9},{9,10},{10,1... | collective-permute-start | bytes 442376 | tf_op jit(solution)/shard_map/ppermute | solution.py:507
  30.7 12.1 %collective-permute-start.8 = (bf16[2,72,512]{2,1,0:T(8,128)(2,1)S(1)}, bf16[2,72,512]{2,1,0:T(8,128)(2,1)S(1)}, u32[]{:S(2)}, u32[]{:S(2)}) collective-permute-start(bf16[2,72,512]{2,1,0:T(8,128)(2,1)S(1)} %get-tuple-element.106), channel_id=1, source_target_pairs={{0,16},{16,32},{32,48},{48,64},{64,80},{80,96},{96,112},{112,128},... | collective-permute-start | bytes 442376 | tf_op jit(solution)/shard_map/ppermute | solution.py:507
  31.6 11.1 %copy-start.2 = (bf16[512,512]{1,0:T(8,128)(2,1)S(1)}, bf16[512,512]{1,0:T(8,128)(2,1)}, u32[]{:S(2)}) copy-start(bf16[512,512]{1,0:T(8,128)(2,1)} %out.5) | copy-start | bytes 1572868
  33.0 14.7 %collective-permute-start.16 = (bf16[256,2048]{1,0:T(8,128)(2,1)S(1)}, bf16[256,2048]{1,0:T(8,128)(2,1)S(1)}, u32[]{:S(2)}, u32[]{:S(2)}) collective-permute-start(bf16[256,2048]{1,0:T(8,128)(2,1)S(1)} %get-tuple-element.137), channel_id=1, source_target_pairs={{0,1},{1,0},{2,3},{3,2},{4,5},{5,4},{6,7},{7,6},{8,9},{9,8},{10,11... | collective-permute-start | bytes 3145736 | tf_op jit(solution)/shard_map/ppermute | solution.py:507
  46.8 3.1 %collective-permute-start.9 = (bf16[256,2048]{1,0:T(8,128)(2,1)S(1)}, bf16[256,2048]{1,0:T(8,128)(2,1)S(1)}, u32[]{:S(2)}, u32[]{:S(2)}) collective-permute-start(bf16[256,2048]{1,0:T(8,128)(2,1)S(1)} %get-tuple-element.113), channel_id=1, source_target_pairs={{0,1},{1,0},{2,3},{3,2},{4,5},{5,4},{6,7},{7,6},{8,9},{9,8},{10,11... | collective-permute-start | bytes 3145736 | tf_op jit(solution)/shard_map/ppermute | solution.py:507
  47.6 6.1 %copy-start.5 = (f32[512]{0:T(512)S(1)}, f32[512]{0:T(512)}, u32[]{:S(2)}) copy-start(f32[512]{0:T(512)} %gain.5) | copy-start | bytes 6148
  47.6 6.1 %copy-start.7 = (bf16[288,288]{1,0:T(8,128)(2,1)S(1)}, bf16[288,288]{1,0:T(8,128)(2,1)}, u32[]{:S(2)}) copy-start(bf16[288,288]{1,0:T(8,128)(2,1)} %constant.11.clone.place_t) | copy-start | bytes 497668
  47.8 9.2 %collective-permute-start.17 = (bf16[2,64,1024]{2,1,0:T(8,128)(2,1)S(1)}, bf16[2,64,1024]{2,1,0:T(8,128)(2,1)S(1)}, u32[]{:S(2)}, u32[]{:S(2)}) collective-permute-start(bf16[2,64,1024]{2,1,0:T(8,128)(2,1)S(1)} %get-tuple-element.139), channel_id=1, source_target_pairs={{0,2},{1,3},{2,0},{3,1},{4,6},{5,7},{6,4},{7,5},{8,10},{9,11},{10,... | collective-permute-start | bytes 786440 | tf_op jit(solution)/shard_map/ppermute | solution.py:507
  48.7 9.6 %collective-permute-start.18 = (bf16[2,64,1024]{2,1,0:T(8,128)(2,1)S(1)}, bf16[2,64,1024]{2,1,0:T(8,128)(2,1)S(1)}, u32[]{:S(2)}, u32[]{:S(2)}) collective-permute-start(bf16[2,64,1024]{2,1,0:T(8,128)(2,1)S(1)} %get-tuple-element.141), channel_id=1, source_target_pairs={{0,130},{1,131},{2,128},{3,129},{4,134},{5,135},{6,132},{7,133},{8... | collective-permute-start | bytes 786440 | tf_op jit(solution)/shard_map/ppermute | solution.py:535
  50.0 9.8 %collective-permute-start.10 = (bf16[2,64,1024]{2,1,0:T(8,128)(2,1)S(1)}, bf16[2,64,1024]{2,1,0:T(8,128)(2,1)S(1)}, u32[]{:S(2)}, u32[]{:S(2)}) collective-permute-start(bf16[2,64,1024]{2,1,0:T(8,128)(2,1)S(1)} %get-tuple-element.117), channel_id=1, source_target_pairs={{0,4},{1,5},{2,6},{3,7},{4,0},{5,1},{6,2},{7,3},{8,12},{9,13},{10,... | collective-permute-start | bytes 786440 | tf_op jit(solution)/shard_map/ppermute | solution.py:507
  51.1 9.1 %collective-permute-start.11 = (bf16[2,64,1024]{2,1,0:T(8,128)(2,1)S(1)}, bf16[2,64,1024]{2,1,0:T(8,128)(2,1)S(1)}, u32[]{:S(2)}, u32[]{:S(2)}) collective-permute-start(bf16[2,64,1024]{2,1,0:T(8,128)(2,1)S(1)} %get-tuple-element.119), channel_id=1, source_target_pairs={{0,12},{1,13},{2,14},{3,15},{4,8},{5,9},{6,10},{7,11},{8,4},{9,5},... | collective-permute-start | bytes 786440 | tf_op jit(solution)/shard_map/ppermute | solution.py:507
  58.4 6.3 %collective-permute-start.19 = (bf16[64,1024]{1,0:T(8,128)(2,1)S(1)}, bf16[64,1024]{1,0:T(8,128)(2,1)S(1)}, u32[]{:S(2)}, u32[]{:S(2)}) collective-permute-start(bf16[64,1024]{1,0:T(8,128)(2,1)S(1)} %get-tuple-element.143), channel_id=1, source_target_pairs={{0,130},{1,131},{2,128},{3,129},{4,134},{5,135},{6,132},{7,133},{8... | collective-permute-start | bytes 393224 | tf_op jit(solution)/shard_map/ppermute | solution.py:535
  59.8 5.0 %collective-permute-start.20 = (bf16[64,1024]{1,0:T(8,128)(2,1)S(1)}, bf16[64,1024]{1,0:T(8,128)(2,1)S(1)}, u32[]{:S(2)}, u32[]{:S(2)}) collective-permute-start(bf16[64,1024]{1,0:T(8,128)(2,1)S(1)} %get-tuple-element.145), channel_id=1, source_target_pairs={{0,2},{1,3},{2,0},{3,1},{4,6},{5,7},{6,4},{7,5},{8,10},{9,11},{10,... | collective-permute-start | bytes 393224 | tf_op jit(solution)/shard_map/ppermute | solution.py:507
  60.2 6.3 %collective-permute-start.12 = (bf16[64,1024]{1,0:T(8,128)(2,1)S(1)}, bf16[64,1024]{1,0:T(8,128)(2,1)S(1)}, u32[]{:S(2)}, u32[]{:S(2)}) collective-permute-start(bf16[64,1024]{1,0:T(8,128)(2,1)S(1)} %get-tuple-element.125), channel_id=1, source_target_pairs={{0,12},{1,13},{2,14},{3,15},{4,8},{5,9},{6,10},{7,11},{8,4},{9,5},... | collective-permute-start | bytes 393224 | tf_op jit(solution)/shard_map/ppermute | solution.py:507
  63.4 5.6 %collective-permute-start.13 = (bf16[64,1024]{1,0:T(8,128)(2,1)S(1)}, bf16[64,1024]{1,0:T(8,128)(2,1)S(1)}, u32[]{:S(2)}, u32[]{:S(2)}) collective-permute-start(bf16[64,1024]{1,0:T(8,128)(2,1)S(1)} %get-tuple-element.127), channel_id=1, source_target_pairs={{0,4},{1,5},{2,6},{3,7},{4,0},{5,1},{6,2},{7,3},{8,12},{9,13},{10,... | collective-permute-start | bytes 393224 | tf_op jit(solution)/shard_map/ppermute | solution.py:507
  64.9 6.1 %collective-permute-start.21 = (bf16[2,32,1024]{2,1,0:T(8,128)(2,1)S(1)}, bf16[2,32,1024]{2,1,0:T(8,128)(2,1)S(1)}, u32[]{:S(2)}, u32[]{:S(2)}) collective-permute-start(bf16[2,32,1024]{2,1,0:T(8,128)(2,1)S(1)} %get-tuple-element.147), channel_id=1, source_target_pairs={{0,4},{1,5},{2,6},{3,7},{4,0},{5,1},{6,2},{7,3},{8,12},{9,13},{10,... | collective-permute-start | bytes 393224 | tf_op jit(solution)/shard_map/ppermute | solution.py:507
  69.1 5.1 %collective-permute-start.14 = (bf16[2,32,1024]{2,1,0:T(8,128)(2,1)S(1)}, bf16[2,32,1024]{2,1,0:T(8,128)(2,1)S(1)}, u32[]{:S(2)}, u32[]{:S(2)}) collective-permute-start(bf16[2,32,1024]{2,1,0:T(8,128)(2,1)S(1)} %get-tuple-element.129), channel_id=1, source_target_pairs={{0,2},{1,3},{2,0},{3,1},{4,6},{5,7},{6,4},{7,5},{8,10},{9,11},{10,... | collective-permute-start | bytes 393224 | tf_op jit(solution)/shard_map/ppermute | solution.py:507
  71.0 6.0 %collective-permute-start.22 = (bf16[1,32,1024]{2,1,0:T(8,128)(2,1)S(1)}, bf16[1,32,1024]{2,1,0:T(8,128)(2,1)S(1)}, u32[]{:S(2)}, u32[]{:S(2)}) collective-permute-start(bf16[1,32,1024]{2,1,0:T(8,128)(2,1)S(1)} %get-tuple-element.148), channel_id=1, source_target_pairs={{0,12},{1,13},{2,14},{3,15},{4,8},{5,9},{6,10},{7,11},{8,4},{9,5},... | collective-permute-start | bytes 196616 | tf_op jit(solution)/shard_map/ppermute | solution.py:507
  74.2 5.6 %collective-permute-start.15 = (bf16[1,32,1024]{2,1,0:T(8,128)(2,1)S(1)}, bf16[1,32,1024]{2,1,0:T(8,128)(2,1)S(1)}, u32[]{:S(2)}, u32[]{:S(2)}) collective-permute-start(bf16[1,32,1024]{2,1,0:T(8,128)(2,1)S(1)} %get-tuple-element.132), channel_id=1, source_target_pairs={{0,130},{1,131},{2,128},{3,129},{4,134},{5,135},{6,132},{7,133},{8... | collective-permute-start | bytes 196616 | tf_op jit(solution)/shard_map/ppermute | solution.py:535

commit v10 on v9

--- a/solution.py
+++ b/solution.py
@@ -317,7 +317,7 @@
 
 
 def kernel_forward_b(
-    piece0, piece1, piece2, piece3, query_features, key_features, gain, qkv, out, sort, sort_t,
+    piece0, piece1, piece3, piece2, query_features, key_features, gain, qkv, out, sort, sort_t,
     back0, back1, back2, back3, inputs_out, normed_out, packed, probs, mixed_t,
     scores,
 ):
@@ -332,7 +332,7 @@
 
 
 def kernel_backward_b(
-    piece0, piece1, piece2, piece3, delta0, delta1, delta2, delta3,
+    piece0, piece1, piece3, piece2, delta0, delta1, delta2, delta3,
     inputs, gain, qkv, out, packed, probs, mixed_t, sort, sort_t,
     back0, back1, back2, back3, upstream_out, d_packed,
     d_probs, d_scores,
@@ -358,7 +358,7 @@
 
 
 def kernel_backward_a(
-    back0, back1, back2, back3, upstream, out, packed, probs, mixed_t, normed_t, sort_t,
+    back0, back2, back1, back3, upstream, out, packed, probs, mixed_t, normed_t, sort_t,
     grad_middle_out, d_packed, send,
     d_probs, d_scores,
 ):
@@ -375,7 +375,7 @@
     grads_half(core, normed_t, mixed_t, grad_middle[...], d_packed, keep)
 
 
-def kernel_advanced(back0, back1, back2, back3, middle, place_t, sort_t, advanced):
+def kernel_advanced(back0, back2, back1, back3, middle, place_t, sort_t, advanced):
     delta = join_pieces(sort_t[...], [back[1] for back in (back0, back1, back2, back3)])
     store_grid(advanced, place_t[...], (middle[...].astype(F32) + delta).astype(BF16))
 
@@ -597,8 +597,8 @@
         hbm=(0, 1, 2, 3, 4, 5, 6, 7, 8), copies=9, flops=7 * 10**9,
     )
     diagonal = permute_both(p0, -1)
+    eastern = permute(p2, "lon", lambda i: i - 1)
     below = permute(p1, "lat", lambda i: i - 1)
-    eastern = permute(p2, "lon", lambda i: i - 1)
     c0, c1, c2, c3, upstream_a, normed_a_t, query_b, keys_b = call(
         kernel_cotangent,
         [piece] * 4 + [token, normed_t, query, keys],
@@ -607,13 +607,13 @@
         smem=(5,), hbm=(0,), copies=1, flops=2 * 10**9,
     )
     c_diagonal = permute_both(c0, -1)
+    c_eastern = permute(c2, "lon", lambda i: i - 1)
     c_below = permute(c1, "lat", lambda i: i - 1)
-    c_eastern = permute(c2, "lon", lambda i: i - 1)
     b0, b1, b2, b3, inputs_b, normed_b, packed_b, probs_b, mixed_b = call(
         kernel_forward_b,
         [piece] * 4 + [token] * 2 + [packed, probs, mixed_t],
         [scores],
-        (p3, eastern, below, diagonal, query_b, keys_b, gain_b, qkv_weight_b, out_weight_b, sort, sort_t),
+        (p3, eastern, diagonal, below, query_b, keys_b, gain_b, qkv_weight_b, out_weight_b, sort, sort_t),
         flops=5 * 10**9,
     )
     twin = ((2, PIECE, WIDTH), BF16)
@@ -622,14 +622,14 @@
         [twin] * 4 + [token, packed],
         [scores, probs],
         (
-            c3, c_eastern, c_below, c_diagonal, b0, b1, b2, b3, inputs_b, gain_b, qkv_weight_b,
+            c3, c_eastern, c_diagonal, c_below, b0, b1, b2, b3, inputs_b, gain_b, qkv_weight_b,
             out_weight_b, packed_b, probs_b, mixed_b, sort, sort_t,
         ),
         flops=5 * 10**9,
     )
     d3 = permute_both(d3, 1)
+    d1 = permute(d1, "lon", lambda i: i + 1)
     d2 = permute(d2, "lat", lambda i: i + 1)
-    d1 = permute(d1, "lon", lambda i: i + 1)
     send_b, keep_b = call(
         kernel_grads_b, [half_grads] * 2, [normed_t], (normed_b, mixed_b, upstream_b, d_packed_b),
         flops=2 * 10**9,
@@ -645,7 +645,7 @@
         [token, packed, half_grads],
         [scores, probs],
         (
-            d3, d2, d1, d0, upstream_a, out_weight_a, packed_a, probs_a, mixed_a, normed_a_t,
+            d3, d1, d2, d0, upstream_a, out_weight_a, packed_a, probs_a, mixed_a, normed_a_t,
             sort_t,
         ),
         flops=5 * 10**9,
@@ -681,7 +681,7 @@
     send_a, middle_a = lax.optimization_barrier((send_a, middle_a))
     got_a = to_x(send_a, 3)
     advanced = call(
-        kernel_advanced, [grid], [], (d3, d2, d1, d0, middle_a, place_t, sort_t),
+        kernel_advanced, [grid], [], (d3, d1, d2, d0, middle_a, place_t, sort_t),
         flops=2 * 10**9, final=(0,),
     )[0]
     got_a, got_b, advanced = lax.optimization_barrier((got_a, got_b, advanced))

time: 92.2 us -> 93.6 us (1.015)
  waiting for transfers between devices: 19.2 us -> 22.7 us
  starting transfers between devices: 31.8 us -> 29.7 us
    ppermute x17, starting transfers between devices: 25.7 us -> 23 us  [permute(): lax.ppermute(array, axis, [(i, target(i) % length) for i in range(length)])]
    ppermute x17, waiting for transfers between devices: 7.5 us -> 8.88 us  [permute(): lax.ppermute(array, axis, [(i, target(i) % length) for i in range(length)])]
    ppermute x3, waiting for transfers between devices: 6.35 us -> 7.49 us  [permute_both(): return lax.ppermute(array, ('lon', 'lat'), pairs)]
    ppermute x3, waiting for transfers between devices: 5.34 us -> 6.3 us  [to_x(): return lax.ppermute(array, ('lon', 'lat'), pairs)]
  transfers between devices with their start and end apart: 23 -> 23, of which waited for: 10 -> 11; matrix products, arithmetic and copies ran while one was open for 0% -> 0% of each run, Pallas kernels for 19% -> 19%
where the time goes in v10:
time: 93.6 us; the launch traced here: 93.4 us
  starting transfers between devices  29.7 us (32%)
  Pallas kernels  28.6 us (31%)
  waiting for transfers between devices  22.7 us (24%)
  blocking collectives  11.5 us (12%)
  between operations  0.95 us (1%)
    pallas_call x19, Pallas kernels, call(): pl.pallas_call(kernel, out_shape=tuple((jax.ShapeDtypeStruct(shape, kind)...  28.6 us
    ppermute x17, starting transfers between devices, permute(): lax.ppermute(array, axis, [(i, target(i) % length) for i in range(length)])  23 us
    all_to_all x1, blocking collectives, exchange_z(): lax.all_to_all(messages, 'lon', 0, 0, axis_index_groups=groups, tiled=True)  11.5 us
    ppermute x17, waiting for transfers between devices, permute(): lax.ppermute(array, axis, [(i, target(i) % length) for i in range(length)])  8.88 us
    ppermute x3, waiting for transfers between devices, permute_both(): return lax.ppermute(array, ('lon', 'lat'), pairs)  7.49 us
    ppermute x3, waiting for transfers between devices, to_x(): return lax.ppermute(array, ('lon', 'lat'), pairs)  6.3 us
    ppermute x3, starting transfers between devices, to_x(): return lax.ppermute(array, ('lon', 'lat'), pairs)  4.36 us
    ppermute x3, starting transfers between devices, permute_both(): return lax.ppermute(array, ('lon', 'lat'), pairs)  2.28 us
  transfers between devices with their start and end apart: 23, of which 11 were waited for; matrix products, arithmetic and copies ran while one was open for 0% of the time, Pallas kernels for 19%

profile of v10, /device:TPU:6, one launch (start us, length us, event | category | flops | bytes accessed | tf_op | source)
XLA Modules:
  0.0 93.4 jit_solution(8733377971919055371)
XLA Ops:
  0.6 0.0 copy-start.8
  0.7 0.0 copy-start.9
  0.7 0.0 copy-start.10
  0.7 5.5 %shard_map.199 = (bf16[72,512]{1,0:T(8,128)(2,1)S(1)}, bf16[72,512]{1,0:T(8,128)(2,1)S(1)}, bf16[72,512]{1,0:T(8,128)(2,1)S(1)}, bf16[72,512]{1,0:T(8,128)(2,1)S...) custom-call(bf16[12,6,4,512]{3,2,1,0:T(4,128)(2,1)} %bitcast.6, ...), custom_call_target="tpu_custom_call" | custom-call | flops 7000000000 | bytes 1048576 | tf_op jit(solution)/shard_map/pallas_call | solution.py:491
  6.2 6.8 %collective-permute-start.3 = (bf16[72,512]{1,0:T(8,128)(2,1)S(1)}, bf16[72,512]{1,0:T(8,128)(2,1)S(1)}, u32[]{:S(2)}, u32[]{:S(2)}) collective-permute-start(bf16[72,512]{1,0:T(8,128)(2,1)S(1)} %get-tuple-element.91), channel_id=1, source_target_pairs={{0,240},{16,0},{32,16},{48,32},{64,48},{80,64},{96,80},{112,96},{1... | collective-permute-start | bytes 221192 | tf_op jit(solution)/shard_map/ppermute | solution.py:507
  13.0 0.0 collective-permute-start.4
  13.0 0.7 collective-permute-start.5
  13.7 0.0 copy-start
  13.7 0.0 copy-start.1
  13.7 0.0 copy-start.4
  13.7 0.0 copy-start.6
  13.7 2.9 %shard_map.200 = (bf16[72,512]{1,0:T(8,128)(2,1)S(1)}, bf16[72,512]{1,0:T(8,128)(2,1)S(1)}, bf16[72,512]{1,0:T(8,128)(2,1)S(1)}, bf16[72,512]{1,0:T(8,128)(2,1)S...) custom-call(bf16[12,6,4,512]{3,2,1,0:T(4,128)(2,1)} %bitcast.7, ...), custom_call_target="tpu_custom_call" | custom-call | flops 2000000000 | bytes 1048576 | tf_op jit(solution)/shard_map/pallas_call | solution.py:491
  16.6 1.7 %collective-permute-start = (bf16[72,512]{1,0:T(8,128)(2,1)S(1)}, bf16[72,512]{1,0:T(8,128)(2,1)S(1)}, u32[]{:S(2)}, u32[]{:S(2)}) collective-permute-start(bf16[72,512]{1,0:T(8,128)(2,1)S(1)} %get-tuple-element.87), channel_id=1, source_target_pairs={{0,240},{16,0},{32,16},{48,32},{64,48},{80,64},{96,80},{112,96},{1... | collective-permute-start | bytes 221192 | tf_op jit(solution)/shard_map/ppermute | solution.py:507
  18.3 2.2 %collective-permute-start.1 = (bf16[72,512]{1,0:T(8,128)(2,1)S(1)}, bf16[72,512]{1,0:T(8,128)(2,1)S(1)}, u32[]{:S(2)}, u32[]{:S(2)}) collective-permute-start(bf16[72,512]{1,0:T(8,128)(2,1)S(1)} %get-tuple-element.88), channel_id=1, source_target_pairs={{0,255},{1,240},{2,241},{3,242},{4,243},{5,244},{6,245},{7,246},{8... | collective-permute-start | bytes 221192 | tf_op jit(solution)/shard_map/ppermute | solution.py:517
  20.5 1.9 %collective-permute-start.2 = (bf16[72,512]{1,0:T(8,128)(2,1)S(1)}, bf16[72,512]{1,0:T(8,128)(2,1)S(1)}, u32[]{:S(2)}, u32[]{:S(2)}) collective-permute-start(bf16[72,512]{1,0:T(8,128)(2,1)S(1)} %get-tuple-element.89), channel_id=1, source_target_pairs={{0,15},{1,0},{2,1},{3,2},{4,3},{5,4},{6,5},{7,6},{8,7},{9,8},{10,9... | collective-permute-start | bytes 221192 | tf_op jit(solution)/shard_map/ppermute | solution.py:507
  22.4 0.0 collective-permute-done.4.piece3
  22.4 0.0 collective-permute-done.5.piece2
  22.4 3.8 %shard_map.201 = (bf16[72,512]{1,0:T(8,128)(2,1)S(1)}, bf16[72,512]{1,0:T(8,128)(2,1)S(1)}, bf16[72,512]{1,0:T(8,128)(2,1)S(1)}, bf16[72,512]{1,0:T(8,128)(2,1)S...) custom-call(bf16[72,512]{1,0:T(8,128)(2,1)S(1)} %get-tuple-element.9, ...), custom_call_target="tpu_custom_call" | custom-call | flops 5000000000 | bytes 1048576 | tf_op jit(solution)/shard_map/pallas_call | solution.py:491
  26.2 0.0 collective-permute-done.1.piece3
  26.3 4.4 %shard_map.202 = (bf16[2,72,512]{2,1,0:T(8,128)(2,1)S(1)}, bf16[2,72,512]{2,1,0:T(8,128)(2,1)S(1)}, bf16[2,72,512]{2,1,0:T(8,128)(2,1)S(1)}, bf16[2,72,512]{2,1,...) custom-call(bf16[72,512]{1,0:T(8,128)(2,1)S(1)} %get-tuple-element.86.piece0, ...), custom_call_target="tpu_custom_call" | custom-call | flops 5000000000 | bytes 1048576 | tf_op jit(solution)/shard_map/pallas_call | solution.py:491
  30.6 0.1 collective-permute-start.6
  30.7 1.1 %collective-permute-start.7 = (bf16[2,72,512]{2,1,0:T(8,128)(2,1)S(1)}, bf16[2,72,512]{2,1,0:T(8,128)(2,1)S(1)}, u32[]{:S(2)}, u32[]{:S(2)}) collective-permute-start(bf16[2,72,512]{2,1,0:T(8,128)(2,1)S(1)} %get-tuple-element.105), channel_id=1, source_target_pairs={{0,16},{16,32},{32,48},{48,64},{64,80},{80,96},{96,112},{112,128},... | collective-permute-start | bytes 442376 | tf_op jit(solution)/shard_map/ppermute | solution.py:507
  31.8 1.3 %shard_map.210 = (bf16[256,2048]{1,0:T(8,128)(2,1)S(1)}, bf16[256,2048]{1,0:T(8,128)(2,1)S(1)}) custom-call(bf16[288,512]{1,0:T(8,128)(2,1)S(1)} %get-tuple-element.133.normed, bf16[2,512,144]{2,1,0:T(8,128)(2,1)S(1)} %get-tuple-element.103.mixed_t, bf16[288,512]{1,0:T(8,128)(2,1)S(1)} %get-tuple-element.134.upstream, ...), custom_call_target="tpu_custom_call" | custom-call | flops 2000000000 | bytes 1048576 | tf_op jit(solution)/shard_map/pallas_call | solution.py:491
  33.2 0.4 collective-permute-start.16
  33.6 7.5 %collective-permute-done.6.back0 = bf16[2,72,512]{2,1,0:T(8,128)(2,1)S(1)} collective-permute-done((bf16[2,72,512]{2,1,0:T(8,128)(2,1)S(1)}, bf16[2,72,512]{2,1,0:T(8,128)(2,1)S(1)}, u32[]{:S(2)}, u32[]{:S(2)}) %collective-permute-start.6) | collective-permute-done | bytes 147488 | tf_op jit(solution)/shard_map/ppermute | solution.py:517
  41.1 1.8 %collective-permute-done.7.back2 = bf16[2,72,512]{2,1,0:T(8,128)(2,1)S(1)} collective-permute-done((bf16[2,72,512]{2,1,0:T(8,128)(2,1)S(1)}, bf16[2,72,512]{2,1,0:T(8,128)(2,1)S(1)}, u32[]{:S(2)}, u32[]{:S(2)}) %collective-permute-start.7) | collective-permute-done | bytes 147488 | tf_op jit(solution)/shard_map/ppermute | solution.py:507
  42.9 0.0 collective-permute-done.8.back1
  42.9 4.1 %shard_map.203 = (bf16[288,512]{1,0:T(8,128)(2,1)S(1)}, bf16[288,1536]{1,0:T(8,128)(2,1)S(1)}, bf16[256,2048]{1,0:T(8,128)(2,1)S(1)}) custom-call(bf16[2,72,512]{2,1,0:T(8,128)(2,1)S(1)} %collective-permute-done.6.back0, bf16[2,72,512]{2,1,0:T(8,128)(2,1)S(1)} %collective-permute-done.7.back2, bf16[2,72,512]{2,1,0:T(8,128)(2,1)S(1)} %collective-permute-done.8.back1, ...), custom_call_target="tpu_custom_call" | custom-call | flops 5000000000 | bytes 1048576 | tf_op jit(solution)/shard_map/pallas_call | solution.py:491
  47.0 0.1 collective-permute-start.9
  47.1 0.7 shard_map.204.keep
  47.8 0.0 copy-start.5
  47.8 0.0 copy-start.7
  47.8 0.1 shard_map.211
  48.0 1.5 %collective-permute-start.17 = (bf16[2,64,1024]{2,1,0:T(8,128)(2,1)S(1)}, bf16[2,64,1024]{2,1,0:T(8,128)(2,1)S(1)}, u32[]{:S(2)}, u32[]{:S(2)}) collective-permute-start(bf16[2,64,1024]{2,1,0:T(8,128)(2,1)S(1)} %get-tuple-element.139), channel_id=1, source_target_pairs={{0,2},{1,3},{2,0},{3,1},{4,6},{5,7},{6,4},{7,5},{8,10},{9,11},{10,... | collective-permute-start | bytes 786440 | tf_op jit(solution)/shard_map/ppermute | solution.py:507
  49.4 1.9 %collective-permute-start.18 = (bf16[2,64,1024]{2,1,0:T(8,128)(2,1)S(1)}, bf16[2,64,1024]{2,1,0:T(8,128)(2,1)S(1)}, u32[]{:S(2)}, u32[]{:S(2)}) collective-permute-start(bf16[2,64,1024]{2,1,0:T(8,128)(2,1)S(1)} %get-tuple-element.141), channel_id=1, source_target_pairs={{0,130},{1,131},{2,128},{3,129},{4,134},{5,135},{6,132},{7,133},{8... | collective-permute-start | bytes 786440 | tf_op jit(solution)/shard_map/ppermute | solution.py:535
  51.4 0.0 collective-permute-done.9.got
  51.4 0.1 shard_map.205
  51.5 0.2 collective-permute-start.10
  51.7 2.8 %collective-permute-start.11 = (bf16[2,64,1024]{2,1,0:T(8,128)(2,1)S(1)}, bf16[2,64,1024]{2,1,0:T(8,128)(2,1)S(1)}, u32[]{:S(2)}, u32[]{:S(2)}) collective-permute-start(bf16[2,64,1024]{2,1,0:T(8,128)(2,1)S(1)} %get-tuple-element.119), channel_id=1, source_target_pairs={{0,12},{1,13},{2,14},{3,15},{4,8},{5,9},{6,10},{7,11},{8,4},{9,5},... | collective-permute-start | bytes 786440 | tf_op jit(solution)/shard_map/ppermute | solution.py:507
  54.4 3.2 %shard_map.207 = bf16[12,6,4,512]{3,2,1,0:T(4,128)(2,1)} custom-call(bf16[288,512]{1,0:T(8,128)(2,1)S(1)} %get-tuple-element.123.inputs, bf16[288,512]{1,0:T(8,128)(2,1)S(1)} %get-tuple-element.111.grad_middle, f32[512]{0:T(512)S(1)} %copy-done.5, bf16[512,1536]{1,0:T(8,128)(2,1)} %qkv_hbm.3, bf16[288,1536]{1,0:T(8,128)(2,1)S(1)} %get-tuple-element.124.d_packed, ...), custom_call_target="tpu_custom_call" | custom-call | flops 4000000000 | bytes 1048576 | tf_op jit(solution)/shard_map/pallas_call | solution.py:491
  57.7 1.3 %collective-permute-done.18.got_two = bf16[2,64,1024]{2,1,0:T(8,128)(2,1)S(1)} collective-permute-done((bf16[2,64,1024]{2,1,0:T(8,128)(2,1)S(1)}, bf16[2,64,1024]{2,1,0:T(8,128)(2,1)S(1)}, u32[]{:S(2)}, u32[]{:S(2)}) %collective-permute-start.18) | collective-permute-done | bytes 262176 | tf_op jit(solution)/shard_map/ppermute | solution.py:535
  59.0 0.1 shard_map.212
  59.1 2.3 %collective-permute-start.19 = (bf16[64,1024]{1,0:T(8,128)(2,1)S(1)}, bf16[64,1024]{1,0:T(8,128)(2,1)S(1)}, u32[]{:S(2)}, u32[]{:S(2)}) collective-permute-start(bf16[64,1024]{1,0:T(8,128)(2,1)S(1)} %get-tuple-element.143), channel_id=1, source_target_pairs={{0,130},{1,131},{2,128},{3,129},{4,134},{5,135},{6,132},{7,133},{8... | collective-permute-start | bytes 393224 | tf_op jit(solution)/shard_map/ppermute | solution.py:535
  61.4 0.0 collective-permute-done.11.got_two
  61.4 0.1 shard_map.206
  61.5 2.6 %collective-permute-start.12 = (bf16[64,1024]{1,0:T(8,128)(2,1)S(1)}, bf16[64,1024]{1,0:T(8,128)(2,1)S(1)}, u32[]{:S(2)}, u32[]{:S(2)}) collective-permute-start(bf16[64,1024]{1,0:T(8,128)(2,1)S(1)} %get-tuple-element.125), channel_id=1, source_target_pairs={{0,12},{1,13},{2,14},{3,15},{4,8},{5,9},{6,10},{7,11},{8,4},{9,5},... | collective-permute-start | bytes 393224 | tf_op jit(solution)/shard_map/ppermute | solution.py:507
  64.1 1.3 %collective-permute-done.19.got_one = bf16[64,1024]{1,0:T(8,128)(2,1)S(1)} collective-permute-done((bf16[64,1024]{1,0:T(8,128)(2,1)S(1)}, bf16[64,1024]{1,0:T(8,128)(2,1)S(1)}, u32[]{:S(2)}, u32[]{:S(2)}) %collective-permute-start.19) | collective-permute-done | bytes 131104 | tf_op jit(solution)/shard_map/ppermute | solution.py:535
  65.3 1.0 %collective-permute-done.20.got_two = bf16[64,1024]{1,0:T(8,128)(2,1)S(1)} collective-permute-done((bf16[64,1024]{1,0:T(8,128)(2,1)S(1)}, bf16[64,1024]{1,0:T(8,128)(2,1)S(1)}, u32[]{:S(2)}, u32[]{:S(2)}) %collective-permute-start.20) | collective-permute-done | bytes 131104 | tf_op jit(solution)/shard_map/ppermute | solution.py:507
  66.4 0.1 shard_map.213
  66.4 0.1 collective-permute-start.21
  66.5 1.2 %collective-permute-done.12.got_one = bf16[64,1024]{1,0:T(8,128)(2,1)S(1)} collective-permute-done((bf16[64,1024]{1,0:T(8,128)(2,1)S(1)}, bf16[64,1024]{1,0:T(8,128)(2,1)S(1)}, u32[]{:S(2)}, u32[]{:S(2)}) %collective-permute-start.12) | collective-permute-done | bytes 131104 | tf_op jit(solution)/shard_map/ppermute | solution.py:507
  67.7 2.7 %collective-permute-done.13.got_two = bf16[64,1024]{1,0:T(8,128)(2,1)S(1)} collective-permute-done((bf16[64,1024]{1,0:T(8,128)(2,1)S(1)}, bf16[64,1024]{1,0:T(8,128)(2,1)S(1)}, u32[]{:S(2)}, u32[]{:S(2)}) %collective-permute-start.13) | collective-permute-done | bytes 131104 | tf_op jit(solution)/shard_map/ppermute | solution.py:507
  70.4 0.1 shard_map.208
  70.5 1.1 %collective-permute-start.14 = (bf16[2,32,1024]{2,1,0:T(8,128)(2,1)S(1)}, bf16[2,32,1024]{2,1,0:T(8,128)(2,1)S(1)}, u32[]{:S(2)}, u32[]{:S(2)}) collective-permute-start(bf16[2,32,1024]{2,1,0:T(8,128)(2,1)S(1)} %get-tuple-element.129), channel_id=1, source_target_pairs={{0,2},{1,3},{2,0},{3,1},{4,6},{5,7},{6,4},{7,5},{8,10},{9,11},{10,... | collective-permute-start | bytes 393224 | tf_op jit(solution)/shard_map/ppermute | solution.py:507
  71.6 0.2 collective-permute-done.21.got
  71.9 2.2 %collective-permute-start.22 = (bf16[1,32,1024]{2,1,0:T(8,128)(2,1)S(1)}, bf16[1,32,1024]{2,1,0:T(8,128)(2,1)S(1)}, u32[]{:S(2)}, u32[]{:S(2)}) collective-permute-start(bf16[1,32,1024]{2,1,0:T(8,128)(2,1)S(1)} %get-tuple-element.148), channel_id=1, source_target_pairs={{0,12},{1,13},{2,14},{3,15},{4,8},{5,9},{6,10},{7,11},{8,4},{9,5},... | collective-permute-start | bytes 196616 | tf_op jit(solution)/shard_map/ppermute | solution.py:507
  74.1 1.4 %collective-permute-done.14.got = bf16[2,32,1024]{2,1,0:T(8,128)(2,1)S(1)} collective-permute-done((bf16[2,32,1024]{2,1,0:T(8,128)(2,1)S(1)}, bf16[2,32,1024]{2,1,0:T(8,128)(2,1)S(1)}, u32[]{:S(2)}, u32[]{:S(2)}) %collective-permute-start.14) | collective-permute-done | bytes 131104 | tf_op jit(solution)/shard_map/ppermute | solution.py:507
  75.6 0.1 collective-permute-start.15
  75.7 1.3 %shard_map.215 = bf16[12,6,4,512]{3,2,1,0:T(4,128)(2,1)} custom-call(bf16[2,72,512]{2,1,0:T(8,128)(2,1)S(1)} %collective-permute-done.6.back0, bf16[2,72,512]{2,1,0:T(8,128)(2,1)S(1)} %collective-permute-done.7.back2, bf16[2,72,512]{2,1,0:T(8,128)(2,1)S(1)} %collective-permute-done.8.back1, bf16[2,72,512]{2,1,0:T(8,128)(2,1)S(1)} %get-tuple-element.107.back3, ...), custom_call_target="tpu_custom_call" | custom-call | flops 2000000000 | bytes 1048576 | tf_op jit(solution)/shard_map/pallas_call | solution.py:491
  77.0 0.5 collective-permute-done.22.got_b
  77.4 3.7 %collective-permute-done.15.got_a = bf16[1,32,1024]{2,1,0:T(8,128)(2,1)S(1)} collective-permute-done((bf16[1,32,1024]{2,1,0:T(8,128)(2,1)S(1)}, bf16[1,32,1024]{2,1,0:T(8,128)(2,1)S(1)}, u32[]{:S(2)}, u32[]{:S(2)}) %collective-permute-start.15) | collective-permute-done | bytes 65568 | tf_op jit(solution)/shard_map/ppermute | solution.py:535
  81.1 0.1 shard_map.216
  81.3 11.5 %all_to_all.5.parts = bf16[8,64,128]{2,1,0:T(8,128)(2,1)S(1)} all-to-all(bf16[8,64,128]{2,1,0:T(8,128)(2,1)S(1)} %shard_map.216), channel_id=1, replica_groups={{0,16,32,48,64,80,96,112},{128,144,160,176,192,208,224,240},{1,17,33,49..., dimensions={0} | all-to-all | bytes 262144 | tf_op jit(solution)/shard_map/all_to_all | solution.py:553
  92.7 0.7 shard_map.217
  (24 shorter events, 0.1 us)
Async XLA Ops:
  0.6 13.0 %copy-start.3 = (s32[192,96]{1,0:T(8,128)S(1)}, s32[192,96]{1,0:T(8,128)}, u32[]{:S(2)}) copy-start(s32[192,96]{1,0:T(8,128)} %ids.1) | copy-start | bytes 221188
  0.6 13.0 %copy-start.8 = (bf16[288,288]{1,0:T(8,128)(2,1)S(1)}, bf16[288,288]{1,0:T(8,128)(2,1)}, u32[]{:S(2)}) copy-start(bf16[288,288]{1,0:T(8,128)(2,1)} %constant.12.clone.sort_hbm.sort) | copy-start | bytes 497668
  0.7 13.0 %copy-start.9 = (bf16[288,288]{1,0:T(8,128)(2,1)S(1)}, bf16[288,288]{1,0:T(8,128)(2,1)}, u32[]{:S(2)}) copy-start(bf16[288,288]{1,0:T(8,128)(2,1)} %constant.10.clone.place_hbm.place) | copy-start | bytes 497668
  0.7 13.0 %copy-start.10 = (s32[144,8]{1,0:T(8,128)S(1)}, s32[144,8]{1,0:T(8,128)}, u32[]{:S(2)}) copy-start(s32[144,8]{1,0:T(8,128)} %constant.14.clone.where_hbm.where) | copy-start | bytes 13828
  6.2 14.3 %collective-permute-start.3 = (bf16[72,512]{1,0:T(8,128)(2,1)S(1)}, bf16[72,512]{1,0:T(8,128)(2,1)S(1)}, u32[]{:S(2)}, u32[]{:S(2)}) collective-permute-start(bf16[72,512]{1,0:T(8,128)(2,1)S(1)} %get-tuple-element.91), channel_id=1, source_target_pairs={{0,240},{16,0},{32,16},{48,32},{64,48},{80,64},{96,80},{112,96},{1... | collective-permute-start | bytes 221192 | tf_op jit(solution)/shard_map/ppermute | solution.py:507
  13.0 9.4 %collective-permute-start.4 = (bf16[72,512]{1,0:T(8,128)(2,1)S(1)}, bf16[72,512]{1,0:T(8,128)(2,1)S(1)}, u32[]{:S(2)}, u32[]{:S(2)}) collective-permute-start(bf16[72,512]{1,0:T(8,128)(2,1)S(1)} %get-tuple-element.92), channel_id=1, source_target_pairs={{0,255},{1,240},{2,241},{3,242},{4,243},{5,244},{6,245},{7,246},{8... | collective-permute-start | bytes 221192 | tf_op jit(solution)/shard_map/ppermute | solution.py:517
  13.0 9.4 %collective-permute-start.5 = (bf16[72,512]{1,0:T(8,128)(2,1)S(1)}, bf16[72,512]{1,0:T(8,128)(2,1)S(1)}, u32[]{:S(2)}, u32[]{:S(2)}) collective-permute-start(bf16[72,512]{1,0:T(8,128)(2,1)S(1)} %get-tuple-element.93), channel_id=1, source_target_pairs={{0,15},{1,0},{2,1},{3,2},{4,3},{5,4},{6,5},{7,6},{8,7},{9,8},{10,9... | collective-permute-start | bytes 221192 | tf_op jit(solution)/shard_map/ppermute | solution.py:507
  13.7 8.8 %copy-start = (bf16[512,1536]{1,0:T(8,128)(2,1)S(1)}, bf16[512,1536]{1,0:T(8,128)(2,1)}, u32[]{:S(2)}) copy-start(bf16[512,1536]{1,0:T(8,128)(2,1)} %qkv.3) | copy-start | bytes 4718596
  13.7 8.7 %copy-start.1 = (bf16[512,512]{1,0:T(8,128)(2,1)S(1)}, bf16[512,512]{1,0:T(8,128)(2,1)}, u32[]{:S(2)}) copy-start(bf16[512,512]{1,0:T(8,128)(2,1)} %out.4) | copy-start | bytes 1572868
  13.7 8.7 %copy-start.4 = (f32[512]{0:T(512)S(1)}, f32[512]{0:T(512)}, u32[]{:S(2)}) copy-start(f32[512]{0:T(512)} %gain.4) | copy-start | bytes 6148
  13.7 8.7 %copy-start.6 = (bf16[288,288]{1,0:T(8,128)(2,1)S(1)}, bf16[288,288]{1,0:T(8,128)(2,1)}, u32[]{:S(2)}) copy-start(bf16[288,288]{1,0:T(8,128)(2,1)} %constant.13.clone.sort_t) | copy-start | bytes 497668
  16.6 9.6 %collective-permute-start = (bf16[72,512]{1,0:T(8,128)(2,1)S(1)}, bf16[72,512]{1,0:T(8,128)(2,1)S(1)}, u32[]{:S(2)}, u32[]{:S(2)}) collective-permute-start(bf16[72,512]{1,0:T(8,128)(2,1)S(1)} %get-tuple-element.87), channel_id=1, source_target_pairs={{0,240},{16,0},{32,16},{48,32},{64,48},{80,64},{96,80},{112,96},{1... | collective-permute-start | bytes 221192 | tf_op jit(solution)/shard_map/ppermute | solution.py:507
  18.3 7.9 %collective-permute-start.1 = (bf16[72,512]{1,0:T(8,128)(2,1)S(1)}, bf16[72,512]{1,0:T(8,128)(2,1)S(1)}, u32[]{:S(2)}, u32[]{:S(2)}) collective-permute-start(bf16[72,512]{1,0:T(8,128)(2,1)S(1)} %get-tuple-element.88), channel_id=1, source_target_pairs={{0,255},{1,240},{2,241},{3,242},{4,243},{5,244},{6,245},{7,246},{8... | collective-permute-start | bytes 221192 | tf_op jit(solution)/shard_map/ppermute | solution.py:517
  20.5 5.7 %collective-permute-start.2 = (bf16[72,512]{1,0:T(8,128)(2,1)S(1)}, bf16[72,512]{1,0:T(8,128)(2,1)S(1)}, u32[]{:S(2)}, u32[]{:S(2)}) collective-permute-start(bf16[72,512]{1,0:T(8,128)(2,1)S(1)} %get-tuple-element.89), channel_id=1, source_target_pairs={{0,15},{1,0},{2,1},{3,2},{4,3},{5,4},{6,5},{7,6},{8,7},{9,8},{10,9... | collective-permute-start | bytes 221192 | tf_op jit(solution)/shard_map/ppermute | solution.py:507
  30.6 10.4 %collective-permute-start.6 = (bf16[2,72,512]{2,1,0:T(8,128)(2,1)S(1)}, bf16[2,72,512]{2,1,0:T(8,128)(2,1)S(1)}, u32[]{:S(2)}, u32[]{:S(2)}) collective-permute-start(bf16[2,72,512]{2,1,0:T(8,128)(2,1)S(1)} %get-tuple-element.104), channel_id=1, source_target_pairs={{0,17},{1,18},{2,19},{3,20},{4,21},{5,22},{6,23},{7,24},{8,25},{9,... | collective-permute-start | bytes 442376 | tf_op jit(solution)/shard_map/ppermute | solution.py:517
  30.7 12.2 %collective-permute-start.7 = (bf16[2,72,512]{2,1,0:T(8,128)(2,1)S(1)}, bf16[2,72,512]{2,1,0:T(8,128)(2,1)S(1)}, u32[]{:S(2)}, u32[]{:S(2)}) collective-permute-start(bf16[2,72,512]{2,1,0:T(8,128)(2,1)S(1)} %get-tuple-element.105), channel_id=1, source_target_pairs={{0,16},{16,32},{32,48},{48,64},{64,80},{80,96},{96,112},{112,128},... | collective-permute-start | bytes 442376 | tf_op jit(solution)/shard_map/ppermute | solution.py:507
  31.8 11.1 %collective-permute-start.8 = (bf16[2,72,512]{2,1,0:T(8,128)(2,1)S(1)}, bf16[2,72,512]{2,1,0:T(8,128)(2,1)S(1)}, u32[]{:S(2)}, u32[]{:S(2)}) collective-permute-start(bf16[2,72,512]{2,1,0:T(8,128)(2,1)S(1)} %get-tuple-element.106), channel_id=1, source_target_pairs={{0,1},{1,2},{2,3},{3,4},{4,5},{5,6},{6,7},{7,8},{8,9},{9,10},{10,1... | collective-permute-start | bytes 442376 | tf_op jit(solution)/shard_map/ppermute | solution.py:507
  31.8 11.1 %copy-start.2 = (bf16[512,512]{1,0:T(8,128)(2,1)S(1)}, bf16[512,512]{1,0:T(8,128)(2,1)}, u32[]{:S(2)}) copy-start(bf16[512,512]{1,0:T(8,128)(2,1)} %out.5) | copy-start | bytes 1572868
  33.2 14.6 %collective-permute-start.16 = (bf16[256,2048]{1,0:T(8,128)(2,1)S(1)}, bf16[256,2048]{1,0:T(8,128)(2,1)S(1)}, u32[]{:S(2)}, u32[]{:S(2)}) collective-permute-start(bf16[256,2048]{1,0:T(8,128)(2,1)S(1)} %get-tuple-element.137), channel_id=1, source_target_pairs={{0,1},{1,0},{2,3},{3,2},{4,5},{5,4},{6,7},{7,6},{8,9},{9,8},{10,11... | collective-permute-start | bytes 3145736 | tf_op jit(solution)/shard_map/ppermute | solution.py:507
  47.0 4.4 %collective-permute-start.9 = (bf16[256,2048]{1,0:T(8,128)(2,1)S(1)}, bf16[256,2048]{1,0:T(8,128)(2,1)S(1)}, u32[]{:S(2)}, u32[]{:S(2)}) collective-permute-start(bf16[256,2048]{1,0:T(8,128)(2,1)S(1)} %get-tuple-element.113), channel_id=1, source_target_pairs={{0,1},{1,0},{2,3},{3,2},{4,5},{5,4},{6,7},{7,6},{8,9},{9,8},{10,11... | collective-permute-start | bytes 3145736 | tf_op jit(solution)/shard_map/ppermute | solution.py:507
  47.8 6.7 %copy-start.5 = (f32[512]{0:T(512)S(1)}, f32[512]{0:T(512)}, u32[]{:S(2)}) copy-start(f32[512]{0:T(512)} %gain.5) | copy-start | bytes 6148
  47.8 6.6 %copy-start.7 = (bf16[288,288]{1,0:T(8,128)(2,1)S(1)}, bf16[288,288]{1,0:T(8,128)(2,1)}, u32[]{:S(2)}) copy-start(bf16[288,288]{1,0:T(8,128)(2,1)} %constant.11.clone.place_t) | copy-start | bytes 497668
  48.0 9.7 %collective-permute-start.17 = (bf16[2,64,1024]{2,1,0:T(8,128)(2,1)S(1)}, bf16[2,64,1024]{2,1,0:T(8,128)(2,1)S(1)}, u32[]{:S(2)}, u32[]{:S(2)}) collective-permute-start(bf16[2,64,1024]{2,1,0:T(8,128)(2,1)S(1)} %get-tuple-element.139), channel_id=1, source_target_pairs={{0,2},{1,3},{2,0},{3,1},{4,6},{5,7},{6,4},{7,5},{8,10},{9,11},{10,... | collective-permute-start | bytes 786440 | tf_op jit(solution)/shard_map/ppermute | solution.py:507
  49.4 9.6 %collective-permute-start.18 = (bf16[2,64,1024]{2,1,0:T(8,128)(2,1)S(1)}, bf16[2,64,1024]{2,1,0:T(8,128)(2,1)S(1)}, u32[]{:S(2)}, u32[]{:S(2)}) collective-permute-start(bf16[2,64,1024]{2,1,0:T(8,128)(2,1)S(1)} %get-tuple-element.141), channel_id=1, source_target_pairs={{0,130},{1,131},{2,128},{3,129},{4,134},{5,135},{6,132},{7,133},{8... | collective-permute-start | bytes 786440 | tf_op jit(solution)/shard_map/ppermute | solution.py:535
  51.5 9.9 %collective-permute-start.10 = (bf16[2,64,1024]{2,1,0:T(8,128)(2,1)S(1)}, bf16[2,64,1024]{2,1,0:T(8,128)(2,1)S(1)}, u32[]{:S(2)}, u32[]{:S(2)}) collective-permute-start(bf16[2,64,1024]{2,1,0:T(8,128)(2,1)S(1)} %get-tuple-element.117), channel_id=1, source_target_pairs={{0,4},{1,5},{2,6},{3,7},{4,0},{5,1},{6,2},{7,3},{8,12},{9,13},{10,... | collective-permute-start | bytes 786440 | tf_op jit(solution)/shard_map/ppermute | solution.py:507
  51.7 9.7 %collective-permute-start.11 = (bf16[2,64,1024]{2,1,0:T(8,128)(2,1)S(1)}, bf16[2,64,1024]{2,1,0:T(8,128)(2,1)S(1)}, u32[]{:S(2)}, u32[]{:S(2)}) collective-permute-start(bf16[2,64,1024]{2,1,0:T(8,128)(2,1)S(1)} %get-tuple-element.119), channel_id=1, source_target_pairs={{0,12},{1,13},{2,14},{3,15},{4,8},{5,9},{6,10},{7,11},{8,4},{9,5},... | collective-permute-start | bytes 786440 | tf_op jit(solution)/shard_map/ppermute | solution.py:507
  59.1 6.3 %collective-permute-start.19 = (bf16[64,1024]{1,0:T(8,128)(2,1)S(1)}, bf16[64,1024]{1,0:T(8,128)(2,1)S(1)}, u32[]{:S(2)}, u32[]{:S(2)}) collective-permute-start(bf16[64,1024]{1,0:T(8,128)(2,1)S(1)} %get-tuple-element.143), channel_id=1, source_target_pairs={{0,130},{1,131},{2,128},{3,129},{4,134},{5,135},{6,132},{7,133},{8... | collective-permute-start | bytes 393224 | tf_op jit(solution)/shard_map/ppermute | solution.py:535
  61.4 5.0 %collective-permute-start.20 = (bf16[64,1024]{1,0:T(8,128)(2,1)S(1)}, bf16[64,1024]{1,0:T(8,128)(2,1)S(1)}, u32[]{:S(2)}, u32[]{:S(2)}) collective-permute-start(bf16[64,1024]{1,0:T(8,128)(2,1)S(1)} %get-tuple-element.145), channel_id=1, source_target_pairs={{0,2},{1,3},{2,0},{3,1},{4,6},{5,7},{6,4},{7,5},{8,10},{9,11},{10,... | collective-permute-start | bytes 393224 | tf_op jit(solution)/shard_map/ppermute | solution.py:507
  61.5 6.3 %collective-permute-start.12 = (bf16[64,1024]{1,0:T(8,128)(2,1)S(1)}, bf16[64,1024]{1,0:T(8,128)(2,1)S(1)}, u32[]{:S(2)}, u32[]{:S(2)}) collective-permute-start(bf16[64,1024]{1,0:T(8,128)(2,1)S(1)} %get-tuple-element.125), channel_id=1, source_target_pairs={{0,12},{1,13},{2,14},{3,15},{4,8},{5,9},{6,10},{7,11},{8,4},{9,5},... | collective-permute-start | bytes 393224 | tf_op jit(solution)/shard_map/ppermute | solution.py:507
  64.1 6.4 %collective-permute-start.13 = (bf16[64,1024]{1,0:T(8,128)(2,1)S(1)}, bf16[64,1024]{1,0:T(8,128)(2,1)S(1)}, u32[]{:S(2)}, u32[]{:S(2)}) collective-permute-start(bf16[64,1024]{1,0:T(8,128)(2,1)S(1)} %get-tuple-element.127), channel_id=1, source_target_pairs={{0,4},{1,5},{2,6},{3,7},{4,0},{5,1},{6,2},{7,3},{8,12},{9,13},{10,... | collective-permute-start | bytes 393224 | tf_op jit(solution)/shard_map/ppermute | solution.py:507
  66.4 5.4 %collective-permute-start.21 = (bf16[2,32,1024]{2,1,0:T(8,128)(2,1)S(1)}, bf16[2,32,1024]{2,1,0:T(8,128)(2,1)S(1)}, u32[]{:S(2)}, u32[]{:S(2)}) collective-permute-start(bf16[2,32,1024]{2,1,0:T(8,128)(2,1)S(1)} %get-tuple-element.147), channel_id=1, source_target_pairs={{0,4},{1,5},{2,6},{3,7},{4,0},{5,1},{6,2},{7,3},{8,12},{9,13},{10,... | collective-permute-start | bytes 393224 | tf_op jit(solution)/shard_map/ppermute | solution.py:507
  70.5 5.1 %collective-permute-start.14 = (bf16[2,32,1024]{2,1,0:T(8,128)(2,1)S(1)}, bf16[2,32,1024]{2,1,0:T(8,128)(2,1)S(1)}, u32[]{:S(2)}, u32[]{:S(2)}) collective-permute-start(bf16[2,32,1024]{2,1,0:T(8,128)(2,1)S(1)} %get-tuple-element.129), channel_id=1, source_target_pairs={{0,2},{1,3},{2,0},{3,1},{4,6},{5,7},{6,4},{7,5},{8,10},{9,11},{10,... | collective-permute-start | bytes 393224 | tf_op jit(solution)/shard_map/ppermute | solution.py:507
  71.9 5.6 %collective-permute-start.22 = (bf16[1,32,1024]{2,1,0:T(8,128)(2,1)S(1)}, bf16[1,32,1024]{2,1,0:T(8,128)(2,1)S(1)}, u32[]{:S(2)}, u32[]{:S(2)}) collective-permute-start(bf16[1,32,1024]{2,1,0:T(8,128)(2,1)S(1)} %get-tuple-element.148), channel_id=1, source_target_pairs={{0,12},{1,13},{2,14},{3,15},{4,8},{5,9},{6,10},{7,11},{8,4},{9,5},... | collective-permute-start | bytes 196616 | tf_op jit(solution)/shard_map/ppermute | solution.py:507
  75.6 5.6 %collective-permute-start.15 = (bf16[1,32,1024]{2,1,0:T(8,128)(2,1)S(1)}, bf16[1,32,1024]{2,1,0:T(8,128)(2,1)S(1)}, u32[]{:S(2)}, u32[]{:S(2)}) collective-permute-start(bf16[1,32,1024]{2,1,0:T(8,128)(2,1)S(1)} %get-tuple-element.132), channel_id=1, source_target_pairs={{0,130},{1,131},{2,128},{3,129},{4,134},{5,135},{6,132},{7,133},{8... | collective-permute-start | bytes 196616 | tf_op jit(solution)/shard_map/ppermute | solution.py:535
